TPU v7x, 32 devices: a whole 2x2x4 slice. The times are simulated.
32 devices in a mesh: dp: 8 (over z, y), vocab: 4 (over x, core).
Axes of the slice: x: 2, y: 2, z: 4, core: 2. Of those that a mesh axis runs over, the one named last changes fastest.
Arguments:
- tokens: int32 [2, 8, 1024], P(None, 'dp', 'vocab'), may hold values from 0 to 32127
- targets: int32 [2, 8, 1024], P(None, 'dp', 'vocab'), may hold values from 0 to 32127
- loss_mask: int32 [2, 8, 1024], P(None, 'dp', 'vocab'), may hold values from 0 to 1
- seg_lengths: int32 [2, 8, 3], P(None, 'dp'), may hold values from 101 to 822, as said below
- task_ids: int32 [2, 8, 3], P(None, 'dp'), may hold values from 0 to 7
- embedding: bfloat16 [32128, 768], P('vocab'), may hold values from -24 to 24
- attend_in: bfloat16 [3, 768, 2304], P(None, 'dp'), may hold values from -0.21875 to 0.21875
- attend_out: bfloat16 [3, 768, 768], P(None, 'dp'), may hold values from -4 to 4
- expand_weights: bfloat16 [2, 768, 3072], P(None, 'dp'), may hold values from -0.21875 to 0.21875
- reduce_weights: bfloat16 [2, 3072, 768], P(None, 'dp'), may hold values from -0.109375 to 0.109375
- norm_gains: float32 [7, 768], replicated, may hold values from 0.25 to 1.75
- prompt: float32 [8, 100, 768], P(None, None, 'vocab'), may hold values from -6 to 6
- first_moment: float32 [8, 100, 768], P(None, None, 'vocab'), may hold values from -4.4703484e-08 to 4.4703484e-08
- row_moment: float32 [8, 100], replicated, may hold values from 6.5104165e-19 to 2.6041666e-18
- column_moment: float32 [8, 768], P(None, 'vocab'), may hold values from 6.5104165e-19 to 2.6041666e-18
Outputs:
- loss_mean: float32 [], replicated
- grad_norm: float32 [], replicated
- prompt_grad: float32 [8, 100, 768], P(None, None, 'vocab')
- new_moment: float32 [8, 100, 768], P(None, None, 'vocab')
- row_second: float32 [8, 100], replicated
- column_second: float32 [8, 768], P(None, 'vocab')
- new_prompt: float32 [8, 100, 768], P(None, None, 'vocab')
Inputs may be any that keep to these rules, and one draw needn't show every extreme that they name: `seg_lengths`: each row holds 3 segments whose lengths sum to 1024; the first and the last are shorter than 256.
All inputs are finite; a program needn't handle non-finite values.
Results may differ from a plain program's by a relative error of at most 0.0058.
Values may be sent and summed in bfloat16 or wider, within the bound.
A program may use at most 384 MiB of HBM per device.

v0:
```python
import jax
import jax.numpy as jnp
from jax import lax
from jax.sharding import PartitionSpec as P

DH = 64
P_SIZE = 100
TASKS = 8
STEP = 5


NORM_EPS = 1e-06
CLIP_NORM = 2e-05
BETA_ONE = 0.9
BETA_TWO = 0.999
LEARN_RATE = 1.0
WEIGHT_DECAY = 1e-05
SQUARE_EPS = 1e-30
MASKED = -1e30


def combined_all(shard, axis, combine):
    everything = jax.tree.map(lambda part: lax.all_gather(part, axis), shard)
    initial = jax.tree.map(lambda part: part[0], everything)

    def step(k, so_far):
        return combine(so_far, jax.tree.map(lambda part: part[k], everything))

    return lax.fori_loop(1, lax.axis_size(axis), step, initial)


def normed(values, gain):
    inverse = lax.rsqrt(jnp.mean(values * values, -1, keepdims=True) + NORM_EPS)
    return (values * inverse * gain, inverse)


def normed_back(values, gain, inverse, gradient):
    unit_rows = values * inverse
    scaled = gradient * gain
    return inverse * (scaled - unit_rows * jnp.mean(scaled * unit_rows, -1, keepdims=True))


def layout(lengths, task_list, offset, amount):
    positions = offset + jnp.arange(amount, dtype=jnp.int32)
    seg_ends = jnp.cumsum(lengths, -1)
    seg_starts = seg_ends - lengths
    segment = jnp.sum((positions[None, :, None] >= seg_ends[:, None, :]).astype(jnp.int32), -1)
    member = segment[:, :, None] == jnp.arange(lengths.shape[-1], dtype=jnp.int32)
    in_segment = positions[None, :] - jnp.sum(jnp.where(member, seg_starts[:, None, :], 0), -1)
    task_of = jnp.sum(jnp.where(member, task_list[:, None, :], 0), -1)
    return (segment, in_segment, task_of)


def per_task(task_of, amounts):
    hits = task_of[..., None] == jnp.arange(TASKS, dtype=jnp.int32)
    return jnp.sum(jnp.where(hits, amounts[..., None], 0.0), (0, 1))


def lookup(table_rows, token_ids, vocab_start):
    local_ids = token_ids - vocab_start
    inside = (local_ids >= 0) & (local_ids < table_rows.shape[0])
    picked = jnp.take(table_rows, jnp.clip(local_ids, 0, table_rows.shape[0] - 1), axis=0)
    return jnp.where(inside[..., None], picked, 0).astype(jnp.float32)


def split_heads(values):
    return values.reshape(values.shape[0], values.shape[1], -1, DH)


def scores(query_heads, key_rows, allowed):
    score_rows = jnp.einsum(
        "bqhd,bkhd->bhqk", query_heads, key_rows, preferred_element_type=jnp.float32
    ) * DH ** (-0.5)
    return jnp.where(allowed[:, None], score_rows, MASKED)


def smooth(values):
    return jax.nn.gelu(values, approximate=True)


def attend_forward(query_source, key_source, weight_in, weight_out, allowed):
    model_width = weight_out.shape[0]
    queries = jnp.dot(
        query_source, weight_in[:, :model_width], preferred_element_type=jnp.float32
    ).astype(jnp.bfloat16)
    key_value = jnp.dot(
        key_source, weight_in[:, model_width:], preferred_element_type=jnp.float32
    ).astype(jnp.bfloat16)
    key_value = lax.all_gather(key_value, "vocab", axis=1, tiled=True)
    score_rows = scores(split_heads(queries), split_heads(key_value[..., :model_width]), allowed)
    maxima = jnp.max(score_rows, -1, keepdims=True)
    log_total = maxima + jnp.log(jnp.sum(jnp.exp(score_rows - maxima), -1, keepdims=True))
    weights = jnp.exp(score_rows - log_total).astype(jnp.bfloat16)
    mixed = jnp.einsum(
        "bhqk,bkhd->bqhd",
        weights,
        split_heads(key_value[..., model_width:]),
        preferred_element_type=jnp.float32,
    )
    mixed = mixed.reshape(queries.shape).astype(jnp.bfloat16)
    branch = jnp.dot(mixed, weight_out, preferred_element_type=jnp.float32)
    return (branch, (queries, key_value, allowed, log_total, weight_in, weight_out))


def attend_backward(stored, gradient, want_queries):
    queries, key_value, allowed, log_total, weight_in, weight_out = stored
    model_width = weight_out.shape[0]
    row_count, length = (key_value.shape[0], key_value.shape[1])
    key_rows = split_heads(key_value[..., :model_width])
    value_rows = split_heads(key_value[..., model_width:])
    query_heads = split_heads(queries)
    weights = jnp.exp(scores(query_heads, key_rows, allowed) - log_total)
    mixed_grad = jnp.einsum(
        "bqe,fe->bqf", gradient.astype(jnp.bfloat16), weight_out, preferred_element_type=jnp.float32
    ).astype(jnp.bfloat16)
    head_grad = split_heads(mixed_grad)
    weight_grad = jnp.einsum(
        "bqhd,bkhd->bhqk", head_grad, value_rows, preferred_element_type=jnp.float32
    )
    score_grad = (
        weights * (weight_grad - jnp.sum(weight_grad * weights, -1, keepdims=True))
    ).astype(jnp.bfloat16)
    value_grad = jnp.einsum(
        "bhqk,bqhd->bkhd",
        weights.astype(jnp.bfloat16),
        head_grad,
        preferred_element_type=jnp.float32,
    )
    key_grad = jnp.einsum(
        "bhqk,bqhd->bkhd", score_grad, query_heads, preferred_element_type=jnp.float32
    ) * DH ** (-0.5)
    pair_grad = jnp.concatenate(
        [
            key_grad.reshape(row_count, length, model_width),
            value_grad.reshape(row_count, length, model_width),
        ],
        -1,
    )
    pair_weight = weight_in[:, model_width:].astype(jnp.float32)
    pair_grad = lax.psum_scatter(pair_grad, "vocab", scatter_dimension=1, tiled=True)
    source_grad = jnp.einsum("bqe,fe->bqf", pair_grad, pair_weight, precision=lax.Precision.HIGHEST)
    if want_queries:
        query_grad = jnp.einsum(
            "bhqk,bkhd->bqhd", score_grad, key_rows, preferred_element_type=jnp.float32
        ) * DH ** (-0.5)
        query_grad = query_grad.reshape(queries.shape).astype(jnp.bfloat16)
        source_grad = source_grad + jnp.einsum(
            "bqe,fe->bqf",
            query_grad,
            weight_in[:, :model_width],
            preferred_element_type=jnp.float32,
        )
    return source_grad


def feed_forward(source, weight_one, weight_two):
    hidden_pre = jnp.dot(source, weight_one, preferred_element_type=jnp.float32)
    activated = smooth(hidden_pre).astype(jnp.bfloat16)
    return (
        jnp.dot(activated, weight_two, preferred_element_type=jnp.float32),
        (hidden_pre, weight_one, weight_two),
    )


def feed_backward(stored, gradient):
    hidden_pre, weight_one, weight_two = stored
    active_grad = jnp.einsum(
        "bqe,fe->bqf", gradient.astype(jnp.bfloat16), weight_two, preferred_element_type=jnp.float32
    )
    pullback = jax.vjp(smooth, hidden_pre)[1]
    pre_grad = pullback(active_grad)[0].astype(jnp.bfloat16)
    return jnp.einsum("bqe,fe->bqf", pre_grad, weight_one, preferred_element_type=jnp.float32)


def combine(left, right):
    maxima = jnp.maximum(left[0], right[0])
    exp_sums = left[1] * jnp.exp(left[0] - maxima) + right[1] * jnp.exp(right[0] - maxima)
    return (maxima, exp_sums, left[2] + right[2])


def micro_step(
    tokens,
    targets,
    loss_mask,
    seg_lengths,
    task_ids,
    own_layout,
    embedding,
    weights,
    norm_gains,
    prompt_flat,
):
    attend_in, attend_out, expand_weights, reduce_weights = weights
    row_count, own_count = tokens.shape
    offset = lax.axis_index("vocab") * own_count
    vocab_start = lax.axis_index("vocab") * embedding.shape[0]
    segment, in_segment, task_of = own_layout
    all_tokens, all_targets, all_mask = (
        lax.all_gather(tokens, "vocab", axis=1, tiled=True),
        lax.all_gather(targets, "vocab", axis=1, tiled=True),
        lax.all_gather(loss_mask, "vocab", axis=1, tiled=True),
    )
    length = all_tokens.shape[1]
    full_layout = layout(seg_lengths, task_ids, 0, length)
    all_segment, all_in_segment = (full_layout[0], full_layout[1])
    shifted = jnp.where(all_in_segment >= 1, jnp.roll(all_targets, 1, axis=1), 0)
    enc_rows, dec_input = (
        lax.psum_scatter(
            lookup(embedding, all_tokens, vocab_start).astype(jnp.bfloat16),
            "vocab",
            scatter_dimension=1,
            tiled=True,
        ).astype(jnp.float32),
        lax.psum_scatter(
            lookup(embedding, shifted, vocab_start).astype(jnp.bfloat16),
            "vocab",
            scatter_dimension=1,
            tiled=True,
        ).astype(jnp.float32),
    )
    is_prompt = in_segment < P_SIZE
    prompt_slot = task_of * P_SIZE + jnp.minimum(in_segment, P_SIZE - 1)
    enc_input = jnp.where(
        is_prompt[..., None],
        jnp.take(prompt_flat, prompt_slot, axis=0).astype(jnp.float32),
        enc_rows,
    )
    allowed = segment[:, :, None] == all_segment[:, None, :]
    later = (offset + jnp.arange(own_count, dtype=jnp.int32))[:, None] >= jnp.arange(
        length, dtype=jnp.int32
    )[None, :]
    causal = allowed & later[None]
    normed_in, inverse_in = normed(enc_input, norm_gains[0])
    normed_low = normed_in.astype(jnp.bfloat16)
    branch, enc_attend = attend_forward(
        normed_low, normed_low, attend_in[0], attend_out[0], allowed
    )
    enc_mid = enc_input + branch
    normed_mid, inverse_mid = normed(enc_mid, norm_gains[1])
    branch, enc_feed = feed_forward(
        normed_mid.astype(jnp.bfloat16), expand_weights[0], reduce_weights[0]
    )
    enc_last = enc_mid + branch
    encoded, inverse_last = normed(enc_last, norm_gains[2])
    encoded_low = encoded.astype(jnp.bfloat16)
    normed_dec = normed(dec_input, norm_gains[3])[0].astype(jnp.bfloat16)
    dec_first = (
        dec_input + attend_forward(normed_dec, normed_dec, attend_in[1], attend_out[1], causal)[0]
    )
    cross_query = normed(dec_first, norm_gains[4])[0].astype(jnp.bfloat16)
    branch, cross_attend = attend_forward(
        cross_query, encoded_low, attend_in[2], attend_out[2], allowed
    )
    dec_second = dec_first + branch
    normed_second, inverse_second = normed(dec_second, norm_gains[5])
    branch, dec_feed = feed_forward(
        normed_second.astype(jnp.bfloat16), expand_weights[1], reduce_weights[1]
    )
    dec_last = dec_second + branch
    output_norm, inverse_out = normed(dec_last, norm_gains[6])
    model_width = dec_last.shape[-1]
    hidden_low = (output_norm * model_width ** (-0.5)).astype(jnp.bfloat16)
    all_hidden = lax.all_gather(
        jnp.swapaxes(hidden_low, 0, 1), "vocab", axis=0, tiled=True
    ).reshape(-1, model_width)
    target_local = jnp.swapaxes(all_targets, 0, 1).reshape(-1) - vocab_start
    logits = lax.dot_general(
        all_hidden, embedding, (((1,), (1,)), ((), ())), preferred_element_type=jnp.float32
    )
    target_hit = jnp.arange(embedding.shape[0], dtype=jnp.int32)[None, :] == target_local[:, None]
    maxima = jnp.max(logits, -1)
    exp_sums = jnp.sum(jnp.exp(logits - maxima[:, None]), -1)
    picked = jnp.sum(jnp.where(target_hit, logits, 0.0), -1)
    maxima, exp_sums, picked = combined_all((maxima, exp_sums, picked), "vocab", combine)
    log_total = maxima + jnp.log(exp_sums)
    all_counted = (
        jnp.swapaxes(all_mask * (all_in_segment >= P_SIZE), 0, 1).reshape(-1).astype(jnp.float32)
    )
    dlogits = (
        all_counted[:, None]
        * (jnp.exp(logits - log_total[:, None]) - target_hit.astype(jnp.float32))
    ).astype(jnp.bfloat16)
    token_loss = jnp.swapaxes((log_total - picked).reshape(length, row_count), 0, 1)
    own_loss = lax.dynamic_slice_in_dim(token_loss, offset, own_count, 1)
    counted = (loss_mask * (in_segment >= P_SIZE)).astype(jnp.float32)
    task_loss = per_task(task_of, counted * own_loss)
    hidden_grad = lax.psum_scatter(
        jnp.dot(dlogits, embedding, preferred_element_type=jnp.float32),
        "vocab",
        scatter_dimension=0,
        tiled=True,
    )
    hidden_grad = jnp.swapaxes(hidden_grad.reshape(own_count, row_count, model_width), 0, 1)
    dec_grad = normed_back(
        dec_last, norm_gains[6], inverse_out, hidden_grad * model_width ** (-0.5)
    )
    dec_grad = dec_grad + normed_back(
        dec_second, norm_gains[5], inverse_second, feed_backward(dec_feed, dec_grad)
    )
    enc_grad = normed_back(
        enc_last, norm_gains[2], inverse_last, attend_backward(cross_attend, dec_grad, False)
    )
    enc_grad = enc_grad + normed_back(
        enc_mid, norm_gains[1], inverse_mid, feed_backward(enc_feed, enc_grad)
    )
    enc_grad = enc_grad + normed_back(
        enc_input, norm_gains[0], inverse_in, attend_backward(enc_attend, enc_grad, True)
    )
    prompt_count = prompt_flat.shape[0]
    chosen = (
        (prompt_slot[..., None] == jnp.arange(prompt_count, dtype=jnp.int32)) & is_prompt[..., None]
    ).astype(jnp.float32)
    gradient = jnp.einsum("bsp,bsd->pd", chosen, enc_grad, precision=lax.Precision.HIGHEST)
    return (gradient, task_loss)


def on_device(
    tokens,
    targets,
    loss_mask,
    seg_lengths,
    task_ids,
    embedding,
    attend_in,
    attend_out,
    expand_weights,
    reduce_weights,
    norm_gains,
    prompt,
    first_moment,
    row_moment,
    column_moment,
):
    own_count = tokens.shape[-1]
    offset = lax.axis_index("vocab") * own_count
    prompt_all = lax.all_gather(prompt.astype(jnp.bfloat16), "vocab", axis=2, tiled=True)
    model_width = prompt_all.shape[-1]
    prompt_flat = prompt_all.reshape(-1, model_width)
    layouts = []
    counts_local = jnp.zeros((TASKS,), jnp.float32)
    for micro_index in range(tokens.shape[0]):
        own_layout = layout(seg_lengths[micro_index], task_ids[micro_index], offset, own_count)
        layouts.append(own_layout)
        counted = (loss_mask[micro_index] * (own_layout[1] >= P_SIZE)).astype(jnp.float32)
        counts_local = counts_local + per_task(own_layout[2], counted)
    counts = lax.psum(counts_local, ("dp", "vocab"))
    gradient = jnp.zeros(prompt_flat.shape, jnp.float32)
    task_loss = jnp.zeros((TASKS,), jnp.float32)
    for micro_index in range(tokens.shape[0]):
        weights = (
            lax.all_gather(attend_in, "dp", axis=1, tiled=True),
            lax.all_gather(attend_out, "dp", axis=1, tiled=True),
            lax.all_gather(expand_weights, "dp", axis=1, tiled=True),
            lax.all_gather(reduce_weights, "dp", axis=1, tiled=True),
        )
        step_grad, step_loss = micro_step(
            tokens[micro_index],
            targets[micro_index],
            loss_mask[micro_index],
            seg_lengths[micro_index],
            task_ids[micro_index],
            layouts[micro_index],
            embedding,
            weights,
            norm_gains,
            prompt_flat,
        )
        gradient = gradient + step_grad
        task_loss = task_loss + step_loss
    gradient, task_loss = lax.psum((gradient, task_loss), ("dp", "vocab"))
    task_scale = 1.0 / (TASKS * jnp.maximum(counts, 1.0))
    loss_mean = jnp.sum(task_loss * task_scale)
    full_grad = gradient.reshape(TASKS, P_SIZE, model_width) * task_scale[:, None, None]
    grad_norm = jnp.sqrt(jnp.sum(full_grad * full_grad))
    clipped = full_grad * (CLIP_NORM / jnp.maximum(grad_norm, CLIP_NORM))
    row_second = BETA_TWO * row_moment + (1.0 - BETA_TWO) * (
        jnp.mean(clipped * clipped, -1) + SQUARE_EPS
    )
    share_width = prompt.shape[-1]
    prompt_grad = lax.dynamic_slice_in_dim(
        clipped, lax.axis_index("vocab") * share_width, share_width, 2
    )
    column_second = BETA_TWO * column_moment + (1.0 - BETA_TWO) * (
        jnp.mean(prompt_grad * prompt_grad, 1) + SQUARE_EPS
    )
    new_moment = BETA_ONE * first_moment + (1.0 - BETA_ONE) * prompt_grad
    estimate = (
        row_second[:, :, None] * column_second[:, None, :] / jnp.mean(row_second, -1)[:, None, None]
    )
    update = new_moment / (1.0 - BETA_ONE**STEP) / jnp.sqrt(estimate / (1.0 - BETA_TWO**STEP))
    new_prompt = prompt - LEARN_RATE * (update + WEIGHT_DECAY * prompt)
    return (loss_mean, grad_norm, prompt_grad, new_moment, row_second, column_second, new_prompt)


def solution(mesh):
    placed = (
        P(None, "dp", "vocab"),
        P(None, "dp", "vocab"),
        P(None, "dp", "vocab"),
        P(None, "dp", None),
        P(None, "dp", None),
        P("vocab", None),
        P(None, "dp", None),
        P(None, "dp", None),
        P(None, "dp", None),
        P(None, "dp", None),
        P(),
        P(None, None, "vocab"),
        P(None, None, "vocab"),
        P(),
        P(None, "vocab"),
    )
    return jax.shard_map(
        on_device,
        mesh=mesh,
        in_specs=placed,
        out_specs=(
            P(),
            P(),
            P(None, None, "vocab"),
            P(None, None, "vocab"),
            P(),
            P(None, "vocab"),
            P(None, None, "vocab"),
        ),
        check_vma=False,
    )
```

profile of v0, /device:TPU:25, one launch (start us, length us, event | category | flops | bytes accessed | tf_op | source)
XLA Modules:
  0.0 1438.7 jit_solution(298780638005790614)
XLA Ops:
  10.6 5.5 all-gather
  17.6 10.6 gather_fusion
  32.1 5.1 all-gather.2
  37.3 11.5 gather_fusion.2
  50.5 5.0 all-gather.9
  57.1 10.7 gather_fusion.3
  70.3 5.1 all-gather.11
  75.4 10.7 gather_fusion.5
  90.3 93.9 %all-gather.34.cloned.1.call-done = bf16[3,768,2304]{2,1,0:T(8,128)(2,1)} async-done(((bf16[3,96,2304]{2,1,0:T(8,128)(2,1)}), bf16[3,768,2304]{2,1,0:T(8,128)(2,1)}) %all-gather.34.cloned.1.call-update) | async-done | bytes 10616848 | tf_op jit(solution)/shard_map/all_gather | solution.py:351
  184.2 6.7 slice_bitcast_fusion.5
  196.2 9.9 all-gather.38.cloned.1.call-done
  256.4 8.1 fusion.181
  264.4 37.2 %all-gather.36.cloned.1.call-done = bf16[3,768,768]{2,1,0:T(8,128)(2,1)} async-done(((bf16[3,96,768]{2,1,0:T(8,128)(2,1)}), bf16[3,768,768]{2,1,0:T(8,128)(2,1)}) %all-gather.36.cloned.1.call-update) | async-done | bytes 3538960 | tf_op jit(solution)/shard_map/all_gather | solution.py:352
  306.4 25.7 %all-gather.46.cloned.1.call-done = bf16[1024,1536]{1,0:T(8,128)(2,1)} async-done(((bf16[256,1536]{1,0:T(8,128)(2,1)}), bf16[1024,1536]{1,0:T(8,128)(2,1)}) %all-gather.46.cloned.1.call-update) | async-done | bytes 3145744 | tf_op jit(solution)/shard_map/all_gather | solution.py:89
  340.7 21.9 %all-gather.52.cloned.1.call-done = bf16[1024,1536]{1,0:T(8,128)(2,1)} async-done(((bf16[256,1536]{1,0:T(8,128)(2,1)}), bf16[1024,1536]{1,0:T(8,128)(2,1)}) %all-gather.52.cloned.1.call-update) | async-done | bytes 3145744 | tf_op jit(solution)/shard_map/all_gather | solution.py:89
  380.3 8.0 fusion.180
  408.3 91.6 %all-gather.40.cloned.1.call-done = bf16[2,768,3072]{2,1,0:T(8,128)(2,1)} async-done(((bf16[2,96,3072]{2,1,0:T(8,128)(2,1)}), bf16[2,768,3072]{2,1,0:T(8,128)(2,1)}) %all-gather.40.cloned.1.call-update) | async-done | bytes 9437200 | tf_op jit(solution)/shard_map/all_gather | solution.py:353
  499.9 5.4 fusion.51
  505.3 132.1 %all-gather.42.cloned.1.call-done = bf16[2,3072,768]{2,1,0:T(8,128)(2,1)} async-done(((bf16[2,384,768]{2,1,0:T(8,128)(2,1)}), bf16[2,3072,768]{2,1,0:T(8,128)(2,1)}) %all-gather.42.cloned.1.call-update) | async-done | bytes 9437200 | tf_op jit(solution)/shard_map/all_gather | solution.py:354
  637.5 5.5 multiply_reduce_fusion.24
  645.7 22.5 %all-gather.54.cloned.1.call-done = bf16[1024,1536]{1,0:T(8,128)(2,1)} async-done(((bf16[256,1536]{1,0:T(8,128)(2,1)}), bf16[1024,1536]{1,0:T(8,128)(2,1)}) %all-gather.54.cloned.1.call-update) | async-done | bytes 3145744 | tf_op jit(solution)/shard_map/all_gather | solution.py:89
  693.5 5.6 multiply_reduce_fusion.18
  728.2 5.5 multiply_reduce_fusion.21
  750.2 8.1 convolution_convert_fusion.10
  773.3 5.1 all-gather.18
  778.5 9.4 all-gather.58.cloned.1.call-done
  787.9 22.2 %fusion.430 = (f32[1024]{0:T(1024)S(1)}, f32[1024,8032]{0,1:T(8,128)}) fusion(bf16[8032,768]{1,0:T(8,128)(2,1)} %param.28, bf16[1,1024,768]{2,1,0:T(8,128)(2,1)} %all-gather.58.cloned.1.call-done), kind=kOutput, calls=%fused_computation.627 | convolution fusion | flops 12641467392 | bytes 46813184 | tf_op jit(solution)/shard_map/dot_general | solution.py:267
  810.1 14.9 %select_reduce_fusion = (f32[1024]{0:T(1024)S(1)}, f32[1024]{0:T(1024)S(1)}) fusion(f32[1024,8032]{0,1:T(8,128)} %get-tuple-element.553, s32[1024]{0:T(1024)S(1)} %bitcast.722, f32[1024]{0:T(1024)S(1)} %get-tuple-element.552), kind=kLoop, calls=%fused_computation.16 | loop fusion | flops 41121792 | bytes 32915456 | tf_op jit(solution)/shard_map/reduce_sum | solution.py:273
  825.0 5.3 all-gather.16
  830.3 5.2 all-gather.17
  835.5 5.2 all-gather.15
  841.8 25.5 %fusion.1 = f32[1024,768]{1,0:T(8,128)} fusion(bf16[8032,768]{1,0:T(8,128)(2,1)} %param.28, f32[1024,8032]{0,1:T(8,128)} %get-tuple-element.553, f32[1024]{0:T(1024)S(1)} %get-tuple-element.460, f32[1024]{0:T(1024)S(1)} %bitcast.735, s32[1024]{0:T(1024)S(1)} %bitcast.723), kind=kOutput, calls=%fused_computation.23 | convolution fusion | flops 12682592256 | bytes 48394240 | tf_op jit(solution)/shard_map/dot_general | solution.py:288
  867.3 22.7 %fusion.429 = (f32[1024]{0:T(1024)S(1)}, f32[1024,8032]{0,1:T(8,128)}) fusion(bf16[8032,768]{1,0:T(8,128)(2,1)} %param.28, bf16[1,1024,768]{2,1,0:T(8,128)(2,1)} %all-gather.50.cloned.1.call-done), kind=kOutput, calls=%fused_computation.626 | convolution fusion | flops 12641467392 | bytes 46813184 | tf_op jit(solution)/shard_map/dot_general | solution.py:267
  890.0 14.9 %select_reduce_fusion.1 = (f32[1024]{0:T(1024)S(1)}, f32[1024]{0:T(1024)S(1)}) fusion(f32[1024,8032]{0,1:T(8,128)} %get-tuple-element.551, s32[1024]{0:T(1024)S(1)} %bitcast.720, f32[1024]{0:T(1024)S(1)} %get-tuple-element.550), kind=kLoop, calls=%fused_computation.19 | loop fusion | flops 41121792 | bytes 32915456 | tf_op jit(solution)/shard_map/reduce_sum | solution.py:273
  904.9 5.2 all-gather.7
  910.1 5.2 all-gather.8
  915.3 5.2 all-gather.6
  921.9 25.6 %fusion = f32[1024,768]{1,0:T(8,128)} fusion(bf16[8032,768]{1,0:T(8,128)(2,1)} %param.28, f32[1024,8032]{0,1:T(8,128)} %get-tuple-element.551, f32[1024]{0:T(1024)S(1)} %get-tuple-element.470, f32[1024]{0:T(1024)S(1)} %bitcast.734, s32[1024]{0:T(1024)S(1)} %bitcast.721), kind=kOutput, calls=%fused_computation.22 | convolution fusion | flops 12682592256 | bytes 48394240 | tf_op jit(solution)/shard_map/dot_general | solution.py:288
  947.6 37.5 %reduce-scatter.19.cloned.1.call-done = f32[256,768]{1,0:T(8,128)} async-done(((f32[1024,768]{1,0:T(8,128)}), f32[256,768]{1,0:T(8,128)}) %reduce-scatter.19.cloned.1.call-update) | async-done | bytes 786448 | tf_op jit(solution)/shard_map/reduce_scatter | solution.py:287
  986.9 9.5 multiply_reduce_fusion.10
  999.1 11.0 multiply_reduce_fusion.1
  1010.1 6.5 fusion.306
  1016.6 7.7 fusion.66
  1028.9 9.3 multiply_reduce_fusion.14
  1041.0 8.6 fusion.312
  1049.6 10.7 multiply_reduce_fusion.3
  1060.4 7.8 fusion.67
  1068.1 5.7 pad_maximum_fusion
  1074.2 12.0 reduce-scatter.27.cloned.1.call-done
  1086.1 6.1 multiply_reduce_fusion.9
  1092.3 11.1 multiply_reduce_fusion.8
  1108.3 12.5 multiply_reduce_fusion
  1120.9 6.8 multiply_convert_fusion.4
  1135.0 5.5 pad_maximum_fusion.3
  1140.8 6.3 reduce-scatter.21.cloned.1.call-done
  1147.1 6.1 multiply_reduce_fusion.13
  1153.2 10.6 multiply_reduce_fusion.12
  1168.6 12.4 multiply_reduce_fusion.2
  1182.3 6.8 multiply_convert_fusion.6
  1212.5 7.6 multiply_reduce_fusion.7
  1220.6 48.4 %reduce-scatter.23.cloned.1.call-done = f32[1,256,1536]{1,2,0:T(8,128)} async-done(((f32[1,1024,1536]{1,2,0:T(8,128)}), f32[1,256,1536]{1,2,0:T(8,128)}) %reduce-scatter.23.cloned.1.call-update) | async-done | bytes 1572880 | tf_op jit(solution)/shard_map/reduce_scatter | solution.py:140
  1269.0 6.2 multiply_reduce_fusion.11
  1285.4 38.3 %all-reduce = (f32[8]{0:T(128)S(1)}, f32[8]{0:T(128)S(1)}) all-reduce(f32[8]{0:T(128)S(1)} %add.593, f32[8]{0:T(128)S(1)} %add.594), channel_id=1, replica_groups=mesh['dp'=8,'vocab'=4] {'dp','vocab'}, use_global_device_ids=true, to_apply=%region_54.57 | all-reduce | flops 16 | bytes 128 | tf_op jit(solution)/shard_map/psum | solution.py:370
  1324.4 90.0 %all-reduce.3.cloned.1.call-done = f32[800,768]{1,0:T(8,128)} async-done(((f32[800,768]{1,0:T(8,128)}), f32[800,768]{1,0:T(8,128)}) %all-reduce.3.cloned.1.call-update) | async-done | bytes 2457616 | tf_op jit(solution)/shard_map/psum | solution.py:370
  (655 shorter events, 294.3 us)
Async XLA Ops:
  8.0 81.1 %reduce-scatter.11.cloned.1.call-start = ((), (), s32[]{:S(2)}) async-start(), calls=%async_computation.10 | async-start | bytes 1966080 | tf_op jit(solution)/shard_map/reduce_scatter | solution.py:214
  30.6 153.6 %all-gather.34.cloned.1.call-start = ((), (), s32[]{:S(2)}) async-start(), calls=%async_computation.11 | async-start | bytes 11943936 | tf_op jit(solution)/shard_map/all_gather | solution.py:351
  31.2 174.9 %all-gather.38.cloned.1.call-start = ((), (), s32[]{:S(2)}) async-start(), calls=%async_computation.13 | async-start | bytes 1966080 | tf_op jit(solution)/shard_map/all_gather | solution.py:336
  32.1 177.3 %reduce-scatter.13.cloned.1.call-start = ((), (), s32[]{:S(2)}) async-start(), calls=%async_computation.14 | async-start | bytes 1966080 | tf_op jit(solution)/shard_map/reduce_scatter | solution.py:208
  50.5 164.1 %reduce-scatter.15.cloned.1.call-start = ((), (), s32[]{:S(2)}) async-start(), calls=%async_computation.17 | async-start | bytes 1966080 | tf_op jit(solution)/shard_map/reduce_scatter | solution.py:214
  70.2 155.0 %reduce-scatter.17.cloned.1.call-start = ((), (), s32[]{:S(2)}) async-start(), calls=%async_computation.18 | async-start | bytes 1966080 | tf_op jit(solution)/shard_map/reduce_scatter | solution.py:208
  87.9 152.3 %all-gather.44.cloned.1.call-start = ((), (), s32[]{:S(2)}) async-start(), calls=%async_computation.26 | async-start | bytes 3932160 | tf_op jit(solution)/shard_map/all_gather | solution.py:89
  89.1 147.3 %copy-start.152 = (f32[768]{0:T(1024)}, f32[768]{0:T(1024)S(1)}, u32[]{:S(2)}) copy-start(f32[768]{0:T(1024)S(1)} %get-tuple-element.400) | copy-start | bytes 9220
  89.1 600.2 %copy-start.153 = (f32[768]{0:T(1024)}, f32[768]{0:T(1024)S(1)}, u32[]{:S(2)}) copy-start(f32[768]{0:T(1024)S(1)} %get-tuple-element.399) | copy-start | bytes 9220
  89.1 610.0 %copy-start.105 = (f32[768]{0:T(1024)}, f32[768]{0:T(1024)S(1)}, u32[]{:S(2)}) copy-start(f32[768]{0:T(1024)S(1)} %get-tuple-element.398) | copy-start | bytes 9220
  90.3 102.4 %copy-start.83 = (bf16[1,256,768]{2,1,0:T(8,128)(2,1)S(1)}, bf16[1,256,768]{2,1,0:T(8,128)(2,1)}, u32[]{:S(2)}) copy-start(bf16[1,256,768]{2,1,0:T(8,128)(2,1)} %reduce-scatter.11.cloned.1.call-done) | copy-start | bytes 1179652
  194.4 107.2 %all-gather.36.cloned.1.call-start = ((), (), s32[]{:S(2)}) async-start(), calls=%async_computation.12 | async-start | bytes 3981312 | tf_op jit(solution)/shard_map/all_gather | solution.py:352
  195.2 136.9 %all-gather.46.cloned.1.call-start = ((), (), s32[]{:S(2)}) async-start(), calls=%async_computation.27 | async-start | bytes 3932160 | tf_op jit(solution)/shard_map/all_gather | solution.py:89
  195.5 25.6 %copy-start.128 = (s32[256]{0:T(256)}, s32[256]{0:T(256)S(1)}, u32[]{:S(2)}) copy-start(s32[256]{0:T(256)S(1)} %get-tuple-element.579) | copy-start | bytes 3076
  195.5 26.2 %copy-start.110 = (s32[256]{0:T(256)}, s32[256]{0:T(256)S(1)}, u32[]{:S(2)}) copy-start(s32[256]{0:T(256)S(1)} %get-tuple-element.578) | copy-start | bytes 3076
  196.1 210.2 %copy-start.135 = (pred[256]{0:T(512)(128)(4,1)}, pred[256]{0:T(512)(128)(4,1)S(1)}, u32[]{:S(2)}) copy-start(pred[256]{0:T(512)(128)(4,1)S(1)} %get-tuple-element.471) | copy-start | bytes 772
  196.1 210.2 %copy-start.133 = (pred[256]{0:T(512)(128)(4,1)}, pred[256]{0:T(512)(128)(4,1)S(1)}, u32[]{:S(2)}) copy-start(pred[256]{0:T(512)(128)(4,1)S(1)} %broadcast_compare_fusion.3) | copy-start | bytes 772
  209.4 20.1 %copy-start.43 = (bf16[256,768]{1,0:T(8,128)(2,1)}, bf16[256,768]{1,0:T(8,128)(2,1)S(1)}, u32[]{:S(2)}) copy-start(bf16[256,768]{1,0:T(8,128)(2,1)S(1)} %gather_fusion.1) | copy-start | bytes 1179652
  210.8 18.6 %copy-start.155 = (f32[256]{0:T(256)}, f32[256]{0:T(256)S(1)}, u32[]{:S(2)}) copy-start(f32[256]{0:T(256)S(1)} %add_rsqrt_fusion.12) | copy-start | bytes 3076
  214.5 148.1 %all-gather.52.cloned.1.call-start = ((), (), s32[]{:S(2)}) async-start(), calls=%async_computation.30 | async-start | bytes 3932160 | tf_op jit(solution)/shard_map/all_gather | solution.py:89
  219.9 280.0 %all-gather.40.cloned.1.call-start = ((), (), s32[]{:S(2)}) async-start(), calls=%async_computation.15 | async-start | bytes 10616832 | tf_op jit(solution)/shard_map/all_gather | solution.py:353
  220.4 417.0 %all-gather.42.cloned.1.call-start = ((), (), s32[]{:S(2)}) async-start(), calls=%async_computation.16 | async-start | bytes 10616832 | tf_op jit(solution)/shard_map/all_gather | solution.py:354
  221.0 447.1 %all-gather.54.cloned.1.call-start = ((), (), s32[]{:S(2)}) async-start(), calls=%async_computation.31 | async-start | bytes 3932160 | tf_op jit(solution)/shard_map/all_gather | solution.py:89
  221.7 465.7 %copy-start.137 = (pred[256]{0:T(512)(128)(4,1)}, pred[256]{0:T(512)(128)(4,1)S(1)}, u32[]{:S(2)}) copy-start(pred[256]{0:T(512)(128)(4,1)S(1)} %get-tuple-element.461) | copy-start | bytes 772
  221.7 465.7 %copy-start.130 = (pred[256]{0:T(512)(128)(4,1)}, pred[256]{0:T(512)(128)(4,1)S(1)}, u32[]{:S(2)}) copy-start(pred[256]{0:T(512)(128)(4,1)S(1)} %broadcast_compare_fusion.2) | copy-start | bytes 772
  222.9 494.3 %copy-start.9 = (pred[256,1024]{1,0:T(8,128)(4,1)}, pred[256,1024]{1,0:T(8,128)(4,1)S(1)}, u32[]{:S(2)}) copy-start(pred[256,1024]{1,0:T(8,128)(4,1)S(1)} %get-tuple-element.498) | copy-start | bytes 786436
  224.0 526.3 %copy-start.11 = (pred[256,1024]{1,0:T(8,128)(4,1)}, pred[256,1024]{1,0:T(8,128)(4,1)S(1)}, u32[]{:S(2)}) copy-start(pred[256,1024]{1,0:T(8,128)(4,1)S(1)} %get-tuple-element.496) | copy-start | bytes 786436
  231.5 164.0 %copy-start.35 = (bf16[256,768]{0,1:T(8,128)(2,1)}, bf16[256,768]{0,1:T(8,128)(2,1)S(1)}, u32[]{:S(2)}) copy-start(bf16[256,768]{0,1:T(8,128)(2,1)S(1)} %copy.123) | copy-start | bytes 1179652
  236.5 440.3 %copy-start.37 = (bf16[256,768]{0,1:T(8,128)(2,1)}, bf16[256,768]{0,1:T(8,128)(2,1)S(1)}, u32[]{:S(2)}) copy-start(bf16[256,768]{0,1:T(8,128)(2,1)S(1)} %copy.132) | copy-start | bytes 1179652
  240.1 461.7 %all-gather.48.cloned.1.call-start = ((), (), s32[]{:S(2)}) async-start(), calls=%async_computation.28 | async-start | bytes 3932160 | tf_op jit(solution)/shard_map/all_gather | solution.py:89
  256.4 45.3 %copy-start.84 = (bf16[1,256,768]{2,1,0:T(8,128)(2,1)S(1)}, bf16[1,256,768]{2,1,0:T(8,128)(2,1)}, u32[]{:S(2)}) copy-start(bf16[1,256,768]{2,1,0:T(8,128)(2,1)} %reduce-scatter.11.cloned.1.call-done) | copy-start | bytes 1179652
  306.4 403.1 %copy-start.39 = (bf16[256,768]{0,1:T(8,128)(2,1)}, bf16[256,768]{0,1:T(8,128)(2,1)S(1)}, u32[]{:S(2)}) copy-start(bf16[256,768]{0,1:T(8,128)(2,1)S(1)} %copy.126) | copy-start | bytes 1179652
  337.5 58.0 %copy-start.15 = (bf16[1,1024,768]{1,2,0:T(8,128)(2,1)}, bf16[1,1024,768]{1,2,0:T(8,128)(2,1)S(1)}, u32[]{:S(2)}) copy-start(bf16[1,1024,768]{1,2,0:T(8,128)(2,1)S(1)} %copy.124) | copy-start | bytes 4718596
  408.2 229.2 %copy-start.75 = (f32[1,256,768]{2,1,0:T(8,128)}, f32[1,256,768]{2,1,0:T(8,128)S(1)}, u32[]{:S(2)}) copy-start(f32[1,256,768]{2,1,0:T(8,128)S(1)} %get-tuple-element.539) | copy-start | bytes 2359300
  408.3 97.1 %copy-start.141 = (f32[256]{0:T(256)}, f32[256]{0:T(256)S(1)}, u32[]{:S(2)}) copy-start(f32[256]{0:T(256)S(1)} %add_rsqrt_fusion.11) | copy-start | bytes 3076
  642.9 29.0 %copy-start.118 = (f32[256]{0:T(256)}, f32[256]{0:T(256)S(1)}, u32[]{:S(2)}) copy-start(f32[256]{0:T(256)S(1)} %add_rsqrt_fusion.10) | copy-start | bytes 3076
  645.6 88.1 %all-gather.56.cloned.1.call-start = ((), (), s32[]{:S(2)}) async-start(), calls=%async_computation.32 | async-start | bytes 3932160 | tf_op jit(solution)/shard_map/all_gather | solution.py:89
  701.7 86.2 %all-gather.58.cloned.1.call-start = ((), (), s32[]{:S(2)}) async-start(), calls=%async_computation.33 | async-start | bytes 1966080 | tf_op jit(solution)/shard_map/all_gather | solution.py:263
  733.7 33.3 %copy-start.21 = (f32[1,256,768]{2,1,0:T(8,128)}, f32[1,256,768]{2,1,0:T(8,128)S(1)}, u32[]{:S(2)}) copy-start(f32[1,256,768]{2,1,0:T(8,128)S(1)} %get-tuple-element.549) | copy-start | bytes 2359300
  733.7 33.3 %copy-start.113 = (f32[256]{0:T(256)}, f32[256]{0:T(256)S(1)}, u32[]{:S(2)}) copy-start(f32[256]{0:T(256)S(1)} %add_rsqrt_fusion.7) | copy-start | bytes 3076
  767.0 43.2 %copy-start.115 = (f32[256]{0:T(256)}, f32[256]{0:T(256)S(1)}, u32[]{:S(2)}) copy-start(f32[256]{0:T(256)S(1)} %add_rsqrt_fusion) | copy-start | bytes 3076
  768.2 99.2 %all-gather.50.cloned.1.call-start = ((), (), s32[]{:S(2)}) async-start(), calls=%async_computation.29 | async-start | bytes 1966080 | tf_op jit(solution)/shard_map/all_gather | solution.py:263
  768.2 41.9 %copy-start.122 = (s32[1,1,256]{2,1,0:T(1,128)}, s32[1,1,256]{2,1,0:T(1,128)S(1)}, u32[]{:S(2)}) copy-start(s32[1,1,256]{2,1,0:T(1,128)S(1)} %get-tuple-element.503) | copy-start | bytes 3076
  768.2 41.9 %copy-start.124 = (s32[1,1,256]{2,1,0:T(1,128)}, s32[1,1,256]{2,1,0:T(1,128)S(1)}, u32[]{:S(2)}) copy-start(s32[1,1,256]{2,1,0:T(1,128)S(1)} %get-tuple-element.502) | copy-start | bytes 3076
  778.5 169.2 %reduce-scatter.25.cloned.1.call-start = ((), (), s32[]{:S(2)}) async-start(), calls=%async_computation.22 | async-start | bytes 3932160 | tf_op jit(solution)/shard_map/reduce_scatter | solution.py:287
  867.3 117.9 %reduce-scatter.19.cloned.1.call-start = ((), (), s32[]{:S(2)}) async-start(), calls=%async_computation.19 | async-start | bytes 3932160 | tf_op jit(solution)/shard_map/reduce_scatter | solution.py:287
  921.9 25.7 %copy-start.104 = (f32[768]{0:T(1024)S(1)}, f32[768]{0:T(1024)}, u32[]{:S(2)}) copy-start(f32[768]{0:T(1024)} %get-tuple-element.396) | copy-start | bytes 9220
  921.9 63.3 %copy-start.114 = (f32[256]{0:T(256)S(1)}, f32[256]{0:T(256)}, u32[]{:S(2)}) copy-start(f32[256]{0:T(256)} %copy-done.113) | copy-start | bytes 3076
  921.9 63.3 %copy-start.116 = (f32[256]{0:T(256)S(1)}, f32[256]{0:T(256)}, u32[]{:S(2)}) copy-start(f32[256]{0:T(256)} %copy-done.115) | copy-start | bytes 3076
  947.5 37.7 %copy-start.22 = (f32[1,256,768]{2,1,0:T(8,128)S(1)}, f32[1,256,768]{2,1,0:T(8,128)}, u32[]{:S(2)}) copy-start(f32[1,256,768]{2,1,0:T(8,128)} %copy-done.21) | copy-start | bytes 2359300
  947.5 37.7 %copy-start.24 = (f32[1,256,768]{2,1,0:T(8,128)S(1)}, f32[1,256,768]{2,1,0:T(8,128)}, u32[]{:S(2)}) copy-start(f32[1,256,768]{2,1,0:T(8,128)} %copy-done.23) | copy-start | bytes 2359300
  947.5 39.4 %copy-start.56 = (f32[1,256,768]{2,1,0:T(8,128)S(1)}, f32[1,256,768]{2,1,0:T(8,128)}, u32[]{:S(2)}) copy-start(f32[1,256,768]{2,1,0:T(8,128)} %copy-done.55) | copy-start | bytes 2359300
  947.5 39.4 %copy-start.148 = (f32[256]{0:T(256)S(1)}, f32[256]{0:T(256)}, u32[]{:S(2)}) copy-start(f32[256]{0:T(256)} %copy-done.147) | copy-start | bytes 3076
  947.5 138.6 %reduce-scatter.27.cloned.1.call-start = ((), (), s32[]{:S(2)}) async-start(), calls=%async_computation.23 | async-start | bytes 7864320 | tf_op jit(solution)/shard_map/reduce_scatter | solution.py:140
  1027.6 119.5 %reduce-scatter.21.cloned.1.call-start = ((), (), s32[]{:S(2)}) async-start(), calls=%async_computation.20 | async-start | bytes 7864320 | tf_op jit(solution)/shard_map/reduce_scatter | solution.py:140
  1041.0 19.3 %slice-start.6 = ((s8[12582912]{0:T(1024)(128)(4,1)}), s8[4194304]{0:T(1024)(128)(4,1)S(1)}, s32[]{:S(2)}) async-start(s8[12582912]{0:T(1024)(128)(4,1)} %bitcast.644), calls=%async_computation.40 | async-start | bytes 8388608
  1041.0 19.3 %slice-start.7 = ((s8[12582912]{0:T(1024)(128)(4,1)}), s8[4194304]{0:T(1024)(128)(4,1)S(1)}, s32[]{:S(2)}) async-start(s8[12582912]{0:T(1024)(128)(4,1)} %bitcast.644), calls=%async_computation.41 | async-start | bytes 8388608
  1073.9 138.5 %reduce-scatter.29.cloned.1.call-start = ((), (), s32[]{:S(2)}) async-start(), calls=%async_computation.24 | async-start | bytes 7864320 | tf_op jit(solution)/shard_map/reduce_scatter | solution.py:140
  1140.5 128.4 %reduce-scatter.23.cloned.1.call-start = ((), (), s32[]{:S(2)}) async-start(), calls=%async_computation.21 | async-start | bytes 7864320 | tf_op jit(solution)/shard_map/reduce_scatter | solution.py:140
  1198.3 216.2 %all-reduce.3.cloned.1.call-start = ((), (), s32[]{:S(2)}) async-start(), calls=%async_computation.25 | async-start | bytes 4915200 | tf_op jit(solution)/shard_map/psum | solution.py:370
  1212.4 56.5 %copy-start.20 = (bf16[768,2304]{1,0:T(8,128)(2,1)S(1)}, bf16[768,2304]{1,0:T(8,128)(2,1)}, u32[]{:S(2)}) copy-start(bf16[768,2304]{1,0:T(8,128)(2,1)} %get-tuple-element.481) | copy-start | bytes 10616836
  1212.4 56.5 %copy-start.134 = (pred[256]{0:T(512)(128)(4,1)S(1)}, pred[256]{0:T(512)(128)(4,1)}, u32[]{:S(2)}) copy-start(pred[256]{0:T(512)(128)(4,1)} %copy-done.133) | copy-start | bytes 772
  1212.4 56.5 %copy-start.136 = (pred[256]{0:T(512)(128)(4,1)S(1)}, pred[256]{0:T(512)(128)(4,1)}, u32[]{:S(2)}) copy-start(pred[256]{0:T(512)(128)(4,1)} %copy-done.135) | copy-start | bytes 772
  1281.5 137.4 %copy-start.151 = (f32[8,100]{1,0:T(8,128)S(1)}, f32[8,100]{1,0:T(8,128)}, u32[]{:S(2)}) copy-start(f32[8,100]{1,0:T(8,128)} %param.36) | copy-start | bytes 9604
  (137 other events, 874.5 us)
Sparse Core Ops, SparseCore 0:
  30.7 28.7 reduce-scatter.10
  62.2 28.1 reduce-scatter.12
  92.9 28.1 reduce-scatter.14
  123.7 28.1 reduce-scatter.16
  768.3 19.5 all-gather.57
  789.3 19.6 all-gather.49
  867.4 37.4 reduce-scatter.24
  947.6 37.4 reduce-scatter.18
  1027.7 58.3 reduce-scatter.26
  1088.7 58.3 reduce-scatter.20
  1149.6 58.3 reduce-scatter.28
  1210.6 58.3 reduce-scatter.22
  1281.3 133.1 all-reduce.2
Sparse Core Ops, SparseCore 1:
  33.3 150.9 all-gather.33
  186.2 19.8 all-gather.37
  208.1 28.4 all-gather.43
  238.7 62.9 all-gather.35
  303.2 28.8 all-gather.45
  334.2 28.3 all-gather.51
  364.7 135.1 all-gather.39
  502.0 135.4 all-gather.41
  639.5 28.6 all-gather.53
  669.7 28.3 all-gather.47
  701.8 28.4 all-gather.55
where the time goes:
time: 1450 us; the launch traced here: 1440 us
  waiting for transfers between devices  641 us (44%)
  matrix products  407 us (28%)
  local copies, waits for them, and re-layouts  144 us (10%)
  other arithmetic  122 us (8%)
  blocking collectives  100 us (7%)
  between operations  20.3 us (1%)
    all_gather x1, waiting for transfers between devices, on_device(): lax.all_gather(reduce_weights, 'dp', axis=1, tiled=True)  132 us
    all_gather x1, waiting for transfers between devices, on_device(): lax.all_gather(attend_in, 'dp', axis=1, tiled=True)  93.9 us
    all_gather x1, waiting for transfers between devices, on_device(): lax.all_gather(expand_weights, 'dp', axis=1, tiled=True)  91.6 us
    psum x1, waiting for transfers between devices, on_device(): gradient, task_loss = lax.psum((gradient, task_loss), ('dp', 'vocab'))  90 us
    all_gather x6, waiting for transfers between devices, attend_forward(): key_value = lax.all_gather(key_value, 'vocab', axis=1, tiled=True)  70.2 us
    reduce_scatter x4, waiting for transfers between devices, attend_backward(): lax.psum_scatter(pair_grad, 'vocab', scatter_dimension=1, tiled=True)  66.6 us
    dot_general x2, matrix products, micro_step(): jnp.dot(dlogits, embedding, preferred_element_type=jnp.float32)  51.1 us
    dot_general x4, matrix products, attend_backward(): jnp.einsum('bqhd,bkhd->bhqk', head_grad, value_rows, preferred_element_ty...  46.7 us
  transfers between devices with their start and end apart: 24, of which 14 were waited for; matrix products, arithmetic and copies ran while one was open for 37% of the time, Pallas kernels for 0%

commit v1 on v0

v1 whole, which is shorter than its diff:
```python
import functools

import jax
import jax.numpy as jnp
from jax import lax
from jax.experimental import pallas as pl
from jax.experimental.pallas import tpu as pltpu
from jax.sharding import PartitionSpec as P

DH = 64
P_SIZE = 100
TASKS = 8
STEP = 5
HALO = 16
LANES = 128
VOCAB_BLOCK = 1024
VMEM_LIMIT = 60 * 1024 * 1024

NORM_EPS = 1e-06
CLIP_NORM = 2e-05
BETA_ONE = 0.9
BETA_TWO = 0.999
LEARN_RATE = 1.0
WEIGHT_DECAY = 1e-05
SQUARE_EPS = 1e-30
MASKED = -1e30

F32 = jnp.float32
BF16 = jnp.bfloat16


def dot(left, right):
    return jnp.dot(left, right, preferred_element_type=F32)


def dot_rows(left, right):
    return lax.dot_general(left, right, (((1,), (1,)), ((), ())), preferred_element_type=F32)


def dot_columns(left, right):
    return lax.dot_general(left, right, (((0,), (0,)), ((), ())), preferred_element_type=F32)


def normed(values, gain):
    inverse = lax.rsqrt(jnp.mean(values * values, -1, keepdims=True) + NORM_EPS)
    return (values * inverse * gain, inverse)


def normed_back(values, gain, inverse, gradient):
    unit_rows = values * inverse
    scaled = gradient * gain
    return inverse * (scaled - unit_rows * jnp.mean(scaled * unit_rows, -1, keepdims=True))


def smooth(values):
    return jax.nn.gelu(values, approximate=True)


def layout(lengths, task_list, positions):
    seg_ends = jnp.cumsum(lengths)
    seg_starts = seg_ends - lengths
    segment = jnp.sum((positions[:, None] >= seg_ends[None, :]).astype(jnp.int32), -1)
    member = segment[:, None] == jnp.arange(lengths.shape[0], dtype=jnp.int32)[None, :]
    in_segment = positions - jnp.sum(jnp.where(member, seg_starts[None, :], 0), -1)
    task_of = jnp.sum(jnp.where(member, task_list[None, :], 0), -1)
    return (segment, in_segment, task_of)


def per_task(task_of, amounts):
    hits = task_of[:, None] == jnp.arange(TASKS, dtype=jnp.int32)
    return jnp.sum(jnp.where(hits, amounts[:, None], 0.0), 0)


def attend_kernel(parts, own, causal, *refs):
    q_ref, k_refs, v_refs = refs[0], refs[1 : 1 + parts], refs[1 + parts : 1 + 2 * parts]
    q_info, k_info, out_ref, bias_ref = refs[1 + 2 * parts :]

    @pl.when(pl.program_id(0) == 0)
    def _():
        keep = q_info[:, 0:1] == k_info[0:1, :]
        if causal:
            keep = keep & (q_info[:, 1:2] >= k_info[1:2, :])
        bias_ref[...] = jnp.where(keep, 0.0, MASKED)

    low_half = lax.broadcasted_iota(jnp.int32, (own, LANES), 1) < DH
    queries = q_ref[...].astype(F32) * DH ** (-0.5)
    mixed = []
    for head in range(LANES // DH):
        query = jnp.where(low_half == (head == 0), queries, 0.0).astype(BF16)
        scores = [
            dot_rows(query, k_refs[k][...]) + bias_ref[:, k * own : (k + 1) * own]
            for k in range(parts)
        ]
        maxima = functools.reduce(jnp.maximum, [jnp.max(s, -1, keepdims=True) for s in scores])
        powers = [jnp.exp(s - maxima) for s in scores]
        total = sum(jnp.sum(p, -1, keepdims=True) for p in powers)
        value = sum(dot(p.astype(BF16), v_refs[k][...]) for k, p in enumerate(powers))
        mixed.append(value / total)
    out_ref[...] = jnp.where(low_half, mixed[0], mixed[1]).astype(BF16)


def attend(queries, pairs, q_info, k_info, causal):
    own, width = queries.shape
    parts, length = len(pairs), k_info.shape[1]
    steps = width // LANES
    key_spec = pl.BlockSpec((own, LANES), lambda i: (0, i))
    value_spec = pl.BlockSpec((own, LANES), lambda i: (0, steps + i))
    return pl.pallas_call(
        functools.partial(attend_kernel, parts, own, causal),
        grid=(steps,),
        out_shape=jax.ShapeDtypeStruct((own, width), BF16),
        in_specs=[key_spec]
        + [key_spec] * parts
        + [value_spec] * parts
        + [
            pl.BlockSpec(q_info.shape, lambda i: (0, 0)),
            pl.BlockSpec(k_info.shape, lambda i: (0, 0)),
        ],
        out_specs=key_spec,
        scratch_shapes=[pltpu.VMEM((own, length), F32)],
        compiler_params=pltpu.CompilerParams(vmem_limit_bytes=VMEM_LIMIT),
        cost_estimate=pl.CostEstimate(
            flops=16 * own * length * width, bytes_accessed=6 * own * width, transcendentals=0
        ),
    )(queries, *pairs, *pairs, q_info, k_info)


def attend_back_kernel(parts, own, block, want_queries, *refs):
    q_ref, k_refs, v_refs = refs[0], refs[1 : 1 + parts], refs[1 + parts : 1 + 2 * parts]
    grad_ref, q_info, k_info = refs[1 + 2 * parts : 4 + 2 * parts]
    rest = refs[4 + 2 * parts :]
    dk_refs, dv_refs = rest[:parts], rest[parts : 2 * parts]
    dq_ref = rest[2 * parts] if want_queries else None
    bias_ref = rest[-1]

    @pl.when(pl.program_id(0) == 0)
    def _():
        bias_ref[...] = jnp.where(k_info[:, 0:1] == q_info[0:1, :], 0.0, MASKED)

    low_half = lax.broadcasted_iota(jnp.int32, (block, LANES), 1) < DH

    def rows(at, first):
        here = pl.ds(pl.multiple_of(at * block, block), block)
        queries = q_ref[here, :].astype(F32) * DH ** (-0.5)
        gradient = grad_ref[here, :].astype(F32)
        dk = [None] * parts
        dv = [None] * parts
        dq = []
        for head in range(LANES // DH):
            mask = low_half == (head == 0)
            query = jnp.where(mask, queries, 0.0).astype(BF16)
            grad = jnp.where(mask, gradient, 0.0).astype(BF16)
            scores = [
                dot_rows(k_refs[k][...], query) + bias_ref[k * own : (k + 1) * own, here]
                for k in range(parts)
            ]
            maxima = functools.reduce(jnp.maximum, [jnp.max(s, 0, keepdims=True) for s in scores])
            powers = [jnp.exp(s - maxima) for s in scores]
            inverse = 1.0 / sum(jnp.sum(p, 0, keepdims=True) for p in powers)
            weights = [p * inverse for p in powers]
            weight_grads = [dot_rows(v_refs[k][...], grad) for k in range(parts)]
            delta = sum(
                jnp.sum(w * dw, 0, keepdims=True) for w, dw in zip(weights, weight_grads)
            )
            score_grads = [
                (w * (dw - delta)).astype(BF16) for w, dw in zip(weights, weight_grads)
            ]
            for k in range(parts):
                key_term = dot(score_grads[k], query)
                value_term = dot(weights[k].astype(BF16), grad)
                dk[k] = key_term if head == 0 else dk[k] + key_term
                dv[k] = value_term if head == 0 else dv[k] + value_term
            if want_queries:
                dq.append(sum(dot_columns(score_grads[k], k_refs[k][...]) for k in range(parts)))
        for k in range(parts):
            dk_refs[k][...] = dk[k] if first else dk_refs[k][...] + dk[k]
            dv_refs[k][...] = dv[k] if first else dv_refs[k][...] + dv[k]
        if want_queries:
            dq_ref[here, :] = (jnp.where(low_half, dq[0], dq[1]) * DH ** (-0.5)).astype(BF16)

    rows(0, True)
    if own > block:
        lax.fori_loop(1, own // block, lambda at, _: (rows(at, False), 0)[1], 0)


def attend_back(queries, pairs, gradient, q_info, k_info, want_queries):
    own, width = queries.shape
    parts, length = len(pairs), k_info.shape[0]
    steps = width // LANES
    key_spec = pl.BlockSpec((own, LANES), lambda i: (0, i))
    value_spec = pl.BlockSpec((own, LANES), lambda i: (0, steps + i))
    shapes = [jax.ShapeDtypeStruct((own, width), F32)] * (2 * parts)
    if want_queries:
        shapes.append(jax.ShapeDtypeStruct((own, width), BF16))
    return pl.pallas_call(
        functools.partial(attend_back_kernel, parts, own, min(256, own), want_queries),
        grid=(steps,),
        out_shape=shapes,
        in_specs=[key_spec]
        + [key_spec] * parts
        + [value_spec] * parts
        + [
            key_spec,
            pl.BlockSpec(q_info.shape, lambda i: (0, 0)),
            pl.BlockSpec(k_info.shape, lambda i: (0, 0)),
        ],
        out_specs=[key_spec] * len(shapes),
        scratch_shapes=[pltpu.VMEM((length, own), F32)],
        compiler_params=pltpu.CompilerParams(vmem_limit_bytes=VMEM_LIMIT),
        cost_estimate=pl.CostEstimate(
            flops=40 * own * length * width, bytes_accessed=20 * own * width, transcendentals=0
        ),
    )(queries, *pairs, *pairs, gradient, q_info, k_info)


def vocab_kernel(tile, valid, h_ref, target_ref, table_hbm, grad_ref, stat_ref, table, sem):
    padded = table.shape[0]

    @pl.when(pl.program_id(0) == 0)
    def _():
        copy = pltpu.make_async_copy(table_hbm, table.at[pl.ds(0, valid), :], sem)
        copy.start()
        if padded > valid:
            table[valid:, :] = jnp.zeros((padded - valid, table.shape[1]), BF16)
        copy.wait()

    rows = h_ref.shape[0]
    hidden = h_ref[...]
    column = lax.broadcasted_iota(jnp.int32, (rows, tile), 1)
    target = target_ref[...]

    def block(at, carry, last):
        maxima, total = carry
        part = table[pl.ds(pl.multiple_of(at * tile, tile), tile), :]
        logits = dot_rows(hidden, part)
        if last and padded > valid:
            logits = jnp.where(column < valid - (padded - tile), logits, MASKED)
        highest = jnp.maximum(maxima, jnp.max(logits, -1, keepdims=True))
        powers = jnp.exp(logits - highest)
        scale = jnp.exp(maxima - highest)
        total = total * scale + jnp.sum(powers, -1, keepdims=True)
        powers = jnp.where(column == target - at * tile, 0.0, powers).astype(BF16)
        grad_ref[...] = grad_ref[...] * scale + dot(powers, part)
        return (highest, total)

    grad_ref[...] = jnp.zeros_like(grad_ref)
    blocks = padded // tile
    carry = (jnp.full((rows, 1), MASKED, F32), jnp.zeros((rows, 1), F32))
    carry = lax.fori_loop(0, blocks - 1, lambda at, c: block(at, c, False), carry)
    maxima, total = block(blocks - 1, carry, True)
    lane = lax.broadcasted_iota(jnp.int32, stat_ref.shape, 1)
    stat_ref[...] = jnp.where(lane == 0, maxima, total)


def vocab_pass(hidden, target_local, embedding, rows):
    count, width = hidden.shape
    valid = embedding.shape[0]
    tile = VOCAB_BLOCK
    padded = (valid + tile - 1) // tile * tile
    return pl.pallas_call(
        functools.partial(vocab_kernel, tile, valid),
        grid=(count // rows,),
        out_shape=[
            jax.ShapeDtypeStruct((count, width), F32),
            jax.ShapeDtypeStruct((count, LANES), F32),
        ],
        in_specs=[
            pl.BlockSpec((rows, width), lambda i: (i, 0)),
            pl.BlockSpec((rows, 1), lambda i: (i, 0)),
            pl.BlockSpec(memory_space=pl.ANY),
        ],
        out_specs=[
            pl.BlockSpec((rows, width), lambda i: (i, 0)),
            pl.BlockSpec((rows, LANES), lambda i: (i, 0)),
        ],
        scratch_shapes=[pltpu.VMEM((padded, width), BF16), pltpu.SemaphoreType.DMA],
        compiler_params=pltpu.CompilerParams(vmem_limit_bytes=VMEM_LIMIT),
        cost_estimate=pl.CostEstimate(
            flops=4 * count * padded * width, bytes_accessed=2 * valid * width, transcendentals=0
        ),
    )(hidden, target_local, embedding)


def gather_kernel(rows_z, rows_y, *refs):
    in_ref, out_ref, expand_ref, reduce_ref = refs[:4]
    in_full, out_full, expand_full, reduce_full = refs[4:7], refs[7:10], refs[10:12], refs[12:14]
    send_sem, recv_sem, local_sem = refs[14:]
    at, v = lax.axis_index("dp"), lax.axis_index("vocab")
    z, y, x, core = at // rows_y, lax.rem(at, rows_y), v // 2, lax.rem(v, 2)
    top = rows_z - 1
    above = {"dp": jnp.minimum(z + 1, top) * rows_y + y, "vocab": v}
    below = {"dp": jnp.maximum(z - 1, 0) * rows_y + y, "vocab": v}
    beside = {"dp": z * rows_y + (1 - y), "vocab": v}
    other_x = (1 - x) * 2 + core
    across = {"dp": at, "vocab": other_x}
    twin = {"dp": at, "vocab": x * 2 + (1 - core)}

    barrier = pltpu.get_barrier_semaphore()

    def greet(peer):
        pl.semaphore_signal(barrier, inc=1, device_id=peer, device_id_type=pl.DeviceIdType.MESH)

    pl.when(z < top)(lambda: greet(above))
    pl.when(z > 0)(lambda: greet(below))
    greet(beside)
    greet(across)
    greet(twin)
    inner = jnp.logical_and(z > 0, z < top)
    pl.when(inner)(lambda: pl.semaphore_wait(barrier, 5))
    pl.when(jnp.logical_not(inner))(lambda: pl.semaphore_wait(barrier, 4))

    names, tallies = {}, [0, 0]

    def remote(name, source, target, peer):
        if name not in names:
            names[name] = tallies[0]
            tallies[0] += 1
        return pltpu.make_async_remote_copy(
            src_ref=source,
            dst_ref=target,
            send_sem=send_sem.at[names[name]],
            recv_sem=recv_sem.at[names[name]],
            device_id=peer,
            device_id_type=pl.DeviceIdType.MESH,
        )

    def local(source, target):
        copy = pltpu.make_async_copy(source, target, local_sem.at[tallies[1]])
        tallies[1] += 1
        copy.start()
        return copy

    def columns(ref, full, index, blocks):
        wide = ref.shape[2] // blocks
        here = lambda b: pl.ds(pl.multiple_of(b * wide, wide), wide)
        return (
            lambda b: ref.at[index, :, here(b)],
            lambda zs, ys, b: full.at[zs, ys, :, here(b)],
            lambda ys, b: full.at[:, ys, :, here(b)],
            blocks == 4,
        )

    def row_blocks(ref, full, index):
        count = ref.shape[1] // 4
        return (
            lambda b: ref.at[index, pl.ds(pl.multiple_of(b * count, count), count), :],
            lambda zs, ys, b: full.at[zs, ys, b],
            lambda ys, b: full.at[:, ys, b],
            True,
        )

    def attention(j):
        return [columns(in_ref, in_full[j], j, 2), columns(out_ref, out_full[j], j, 2)]

    def feed(j):
        return [columns(expand_ref, expand_full[j], j, 4), row_blocks(reduce_ref, reduce_full[j], j)]

    waves = [feed(0) + attention(0), feed(1) + attention(1) + attention(2)]
    units = [u for wave in waves for u in wave]
    starts = [0, len(waves[0]), len(units)]
    blocks = [v if u[3] else core for u in units]
    sides = (("up", -1), ("down", 1))

    def there(side, k):
        return z - k >= 0 if side == "up" else z + k <= top

    def further(side):
        return z < top if side == "up" else z > 0

    def begin(i):
        source, target, _, quarter = units[i]
        b = blocks[i]
        piece = target(z, y, b)
        pl.when(z < top)(lambda: remote((i, "up", 1), source(b), piece, above).start())
        pl.when(z > 0)(lambda: remote((i, "down", 1), source(b), piece, below).start())
        remote((i, "y", 0), source(b), piece, beside).start()
        copies = [local(source(b), piece)]
        if quarter:
            copies.append(local(source(other_x), target(z, y, other_x)))
        return copies

    def step(i, k):
        _, target, _, quarter = units[i]
        for side, sign in sides:

            @pl.when(there(side, k))
            def _():
                piece = target(z + sign * k, y, blocks[i])
                remote((i, side, k), piece, piece, above).wait_recv()
                if k < top:

                    @pl.when(further(side))
                    def _():
                        peer = above if side == "up" else below
                        remote((i, side, k + 1), piece, piece, peer).start()

                remote((i, side, k, "y"), piece, piece, beside).start()
                if quarter:
                    remote((i, side, k, "x"), piece, piece, across).start()

    def came(i, k):
        _, target, _, quarter = units[i]
        if k == 0:
            piece = target(z, 1 - y, blocks[i])
            remote((i, "y", 0), piece, piece, beside).wait_recv()
            if quarter:
                remote((i, "yx", 0), piece, piece, across).start()
            return
        for side, sign in sides:

            @pl.when(there(side, k))
            def _():
                piece = target(z + sign * k, 1 - y, blocks[i])
                remote((i, side, k, "y"), piece, piece, beside).wait_recv()
                if quarter:
                    remote((i, side, k, "yx"), piece, piece, across).start()

    def to_twin(i, column, b, tag):
        block = units[i][2](column, b)
        remote((i, "core", tag), block, block, twin).start()

    def spread(i):
        for copy in locals_[i]:
            copy.wait()
        to_twin(i, y, blocks[i], 0)

    def spread_beside(i):
        to_twin(i, 1 - y, blocks[i], 1)

    def x_came(i, tag):
        _, target, _, _ = units[i]
        if tag == "yx":
            piece = target(z, 1 - y, other_x)
            remote((i, "yx", 0), piece, piece, across).wait_recv()
        for k in range(1, rows_z):
            for side, sign in sides:

                @pl.when(there(side, k))
                def _():
                    piece = target(z + sign * k, y if tag == "x" else 1 - y, other_x)
                    remote((i, side, k, tag), piece, piece, across).wait_recv()

        to_twin(i, y if tag == "x" else 1 - y, other_x, 2 if tag == "x" else 3)

    first, second = range(starts[0], starts[1]), range(starts[1], starts[2])
    locals_ = {}

    def each(action, wave, *rest):
        for i in wave:
            action(i, *rest)

    for i in first:
        locals_[i] = begin(i)
    locals_[second[0]] = begin(second[0])
    each(step, first, 1)
    for i in second[1:]:
        locals_[i] = begin(i)
    each(came, first, 0)
    each(step, first, 2)
    each(came, first, 1)
    each(step, second, 1)
    each(step, first, 3)
    each(spread, first)
    each(came, first, 2)
    each(step, second, 2)
    each(came, second, 0)
    for i in first:
        came(i, 3)
        spread_beside(i)
    each(came, second, 1)
    each(step, second, 3)
    each(spread, second)
    for i in first:
        if units[i][3]:
            x_came(i, "x")
    each(came, second, 2)
    for i in first:
        if units[i][3]:
            x_came(i, "yx")
    for i in second:
        came(i, 3)
        spread_beside(i)
    for i in second:
        if units[i][3]:
            x_came(i, "x")
            x_came(i, "yx")

    for i, (source, target, whole, quarter) in enumerate(units):
        b = blocks[i]
        for tag in range(4 if quarter else 2):
            block = whole(y, b)
            remote((i, "core", tag), block, block, twin).wait()
        piece = target(z, y, b)
        remote((i, "y", 0), piece, piece, beside).wait_send()
        if quarter:
            remote((i, "yx", 0), piece, piece, across).wait_send()
        for k in range(1, rows_z):
            for side, sign in sides:
                sent = there(side, k - 1) if k > 1 else True
                pl.when(jnp.logical_and(sent, further(side)))(
                    lambda: remote((i, side, k), piece, piece, above).wait_send()
                )

                @pl.when(there(side, k))
                def _():
                    remote((i, side, k, "y"), piece, piece, beside).wait_send()
                    if quarter:
                        remote((i, side, k, "x"), piece, piece, across).wait_send()
                        remote((i, side, k, "yx"), piece, piece, across).wait_send()


def gather_weights(attend_in, attend_out, expand_weights, reduce_weights):
    shards, rows_y = 8, 2
    rows_z = shards // rows_y
    rows = attend_in.shape[1]
    width = rows * shards
    tall = reduce_weights.shape[1]

    def full(*tail):
        return jax.ShapeDtypeStruct((rows_z, rows_y, *tail), BF16)

    shapes = (
        [full(rows, attend_in.shape[2])] * 3
        + [full(rows, attend_out.shape[2])] * 3
        + [full(rows, expand_weights.shape[2])] * 2
        + [full(4, tall // 4, width)] * 2
    )
    copies = 10 * (1 + 4 * (rows_z - 1) + 2) + 4 * (1 + 4 * (rows_z - 1) + 2)
    outs = pl.pallas_call(
        functools.partial(gather_kernel, rows_z, rows_y),
        out_shape=shapes,
        in_specs=[pl.BlockSpec(memory_space=pl.ANY)] * 4,
        out_specs=[pl.BlockSpec(memory_space=pl.ANY)] * 10,
        scratch_shapes=[
            pltpu.SemaphoreType.DMA((copies,)),
            pltpu.SemaphoreType.DMA((copies,)),
            pltpu.SemaphoreType.DMA((14,)),
        ],
        compiler_params=pltpu.CompilerParams(collective_id=0, has_side_effects=True),
        cost_estimate=pl.CostEstimate(flops=0, bytes_accessed=400_000_000, transcendentals=0),
    )(attend_in, attend_out, expand_weights, reduce_weights)
    return [o.reshape(-1, o.shape[-1]) for o in outs]


def whole_weights(attend_in, attend_out, expand_weights, reduce_weights):
    tensors = (attend_in, attend_out, expand_weights, reduce_weights)
    if lax.axis_size("dp") == 8 and lax.axis_size("vocab") == 4:
        flat = gather_weights(*tensors)
        return flat[:3], flat[3:6], flat[6:8], flat[8:]
    return tuple(lax.all_gather(tensor, "dp", axis=1, tiled=True) for tensor in tensors)


def on_device(
    tokens,
    targets,
    loss_mask,
    seg_lengths,
    task_ids,
    embedding,
    attend_in,
    attend_out,
    expand_weights,
    reduce_weights,
    norm_gains,
    prompt,
    first_moment,
    row_moment,
    column_moment,
):
    shards = lax.axis_size("vocab")
    micros, span = tokens.shape[0], tokens.shape[-1]
    length = span * shards
    group = shards // micros
    own = length // group
    me = lax.axis_index("vocab")
    micro, place = me // group, me % group
    shard_rows, width = embedding.shape
    share = prompt.shape[-1]

    def around(array, shift):
        pairs = [
            (m * group + r, m * group + (r + shift) % group)
            for m in range(micros)
            for r in range(group)
        ]
        return lax.ppermute(array, "vocab", pairs)

    ids = lax.all_gather(jnp.stack([tokens[:, 0], targets[:, 0], loss_mask[:, 0]]), "vocab")
    ids = jnp.transpose(ids, (1, 2, 0, 3)).reshape(3, micros, length)
    enc_ids = ids[0].reshape(shards, own)
    before = jnp.pad(ids[1], ((0, 0), (1, 0)))[:, :length].reshape(shards, own)[:, :1]
    dec_ids = jnp.concatenate(
        [jnp.zeros((shards, HALO - 1), jnp.int32), before, ids[1].reshape(shards, own)], 1
    )
    first_row = me * shard_rows

    def lookup(wanted):
        local = wanted.reshape(-1) - first_row
        inside = (local >= 0) & (local < shard_rows)
        picked = jnp.take(embedding, jnp.clip(local, 0, shard_rows - 1), axis=0)
        return jnp.where(inside[:, None], picked, 0)

    enc_rows = lax.psum_scatter(lookup(enc_ids), "vocab", scatter_dimension=0, tiled=True)
    dec_rows = lax.psum_scatter(lookup(dec_ids), "vocab", scatter_dimension=0, tiled=True)

    prompt_all = lax.all_gather(prompt.astype(BF16), "vocab", axis=2, tiled=True)
    prompt_flat = prompt_all.reshape(-1, width)
    attend_in, attend_out, expand_weights, reduce_weights = whole_weights(
        attend_in, attend_out, expand_weights, reduce_weights
    )

    lengths = lax.dynamic_index_in_dim(seg_lengths[:, 0], micro, 0, False)
    tasks = lax.dynamic_index_in_dim(task_ids[:, 0], micro, 0, False)
    steps = jnp.arange(own, dtype=jnp.int32)
    positions = place * own + steps
    segment, in_segment, task_of = layout(lengths, tasks, positions)
    key_positions = jnp.concatenate(
        [((place - k + group) % group) * own + steps for k in range(group)]
    )
    key_segment = layout(lengths, tasks, key_positions)[0]
    rows_info = jnp.stack([segment, positions], 1)
    keys_info = jnp.stack([key_segment, key_positions], 0)
    own_mask = lax.dynamic_slice(ids[2], (micro, place * own), (1, own))[0]
    counted = (own_mask * (in_segment >= P_SIZE)).astype(F32)

    def key_parts(source, weight):
        pair = dot(source, weight).astype(BF16)
        return [pair] + [around(pair, k) for k in range(1, group)]

    def project(source, weight):
        return dot(source, weight).astype(BF16)

    is_prompt = in_segment < P_SIZE
    slot = task_of * P_SIZE + jnp.minimum(in_segment, P_SIZE - 1)
    enc_input = jnp.where(
        is_prompt[:, None], jnp.take(prompt_flat, slot, axis=0), enc_rows
    ).astype(F32)
    target_rows = dec_rows[HALO:].astype(F32)
    dec_input = jnp.where(
        (in_segment >= 1)[:, None], dec_rows[HALO - 1 : HALO - 1 + own], dec_rows[:1]
    ).astype(F32)

    normed_in, inverse_in = normed(enc_input, norm_gains[0])
    normed_low = normed_in.astype(BF16)
    enc_pairs = key_parts(normed_low, attend_in[0][:, width:])
    enc_queries = project(normed_low, attend_in[0][:, :width])
    normed_dec = normed(dec_input, norm_gains[3])[0].astype(BF16)
    dec_pairs = key_parts(normed_dec, attend_in[1][:, width:])
    dec_queries = project(normed_dec, attend_in[1][:, :width])
    mixed = attend(enc_queries, enc_pairs, rows_info, keys_info, False)
    enc_mid = enc_input + dot(mixed, attend_out[0])
    normed_mid, inverse_mid = normed(enc_mid, norm_gains[1])
    enc_pre = dot(normed_mid.astype(BF16), expand_weights[0])
    enc_last = enc_mid + dot(smooth(enc_pre).astype(BF16), reduce_weights[0])
    encoded, inverse_last = normed(enc_last, norm_gains[2])
    cross_pairs = key_parts(encoded.astype(BF16), attend_in[2][:, width:])

    mixed = attend(dec_queries, dec_pairs, rows_info, keys_info, True)
    dec_first = dec_input + dot(mixed, attend_out[1])
    cross_queries = project(normed(dec_first, norm_gains[4])[0].astype(BF16), attend_in[2][:, :width])
    mixed = attend(cross_queries, cross_pairs, rows_info, keys_info, False)
    dec_second = dec_first + dot(mixed, attend_out[2])
    normed_second, inverse_second = normed(dec_second, norm_gains[5])
    dec_pre = dot(normed_second.astype(BF16), expand_weights[1])
    dec_last = dec_second + dot(smooth(dec_pre).astype(BF16), reduce_weights[1])
    output_norm, inverse_out = normed(dec_last, norm_gains[6])
    hidden = (output_norm * width ** (-0.5)).astype(BF16)

    all_hidden = lax.all_gather(hidden, "vocab", axis=0, tiled=True)
    target_local = ids[1].reshape(-1, 1) - first_row
    part, stats = vocab_pass(all_hidden, target_local, embedding, own)
    gathered = lax.all_gather(stats[:, :2].T, "vocab")
    maxima = jnp.max(gathered[:, 0], 0)
    log_total = maxima + jnp.log(
        jnp.sum(gathered[:, 1] * jnp.exp(gathered[:, 0] - maxima), 0)
    )
    scaled = part * jnp.exp(stats[:, 0] - log_total)[:, None]
    summed = lax.psum_scatter(scaled, "vocab", scatter_dimension=0, tiled=True)
    own_total = lax.dynamic_slice(log_total, (me * own,), (own,))
    target_logit = jnp.sum(hidden.astype(F32) * target_rows, -1)
    token_loss = own_total - target_logit
    target_coefficient = (jnp.exp(target_logit - own_total) - 1.0).astype(BF16).astype(F32)
    hidden_grad = counted[:, None] * (summed + target_coefficient[:, None] * target_rows)

    def feed_back(hidden_pre, weight_one, weight_two, gradient):
        active_grad = dot_rows(gradient.astype(BF16), weight_two)
        pre_grad = jax.vjp(smooth, hidden_pre)[1](active_grad)[0].astype(BF16)
        return dot_rows(pre_grad, weight_one)

    def keys_back(parts, weight):
        dk, dv = parts[:group], parts[group : 2 * group]
        pairs = [jnp.concatenate([dk[k], dv[k]], 1) for k in range(group)]
        total = pairs[0]
        for k in range(1, group):
            total = total + around(pairs[k], group - k)
        high = total.astype(BF16)
        rest = (total - high.astype(F32)).astype(BF16)
        return dot_rows(high, weight) + dot_rows(rest, weight)

    dec_grad = normed_back(
        dec_last, norm_gains[6], inverse_out, hidden_grad * width ** (-0.5)
    )
    dec_grad = dec_grad + normed_back(
        dec_second,
        norm_gains[5],
        inverse_second,
        feed_back(dec_pre, expand_weights[1], reduce_weights[1], dec_grad),
    )
    mixed_grad = dot_rows(dec_grad.astype(BF16), attend_out[2]).astype(BF16)
    back = attend_back(cross_queries, cross_pairs, mixed_grad, rows_info.T, keys_info.T, False)
    enc_grad = normed_back(
        enc_last, norm_gains[2], inverse_last, keys_back(back, attend_in[2][:, width:])
    )
    enc_grad = enc_grad + normed_back(
        enc_mid,
        norm_gains[1],
        inverse_mid,
        feed_back(enc_pre, expand_weights[0], reduce_weights[0], enc_grad),
    )
    mixed_grad = dot_rows(enc_grad.astype(BF16), attend_out[0]).astype(BF16)
    back = attend_back(enc_queries, enc_pairs, mixed_grad, rows_info.T, keys_info.T, True)
    source_grad = keys_back(back, attend_in[0][:, width:]) + dot_rows(
        back[-1], attend_in[0][:, :width]
    )
    enc_grad = enc_grad + normed_back(enc_input, norm_gains[0], inverse_in, source_grad)

    entries = TASKS * P_SIZE
    chosen = (
        (slot[:, None] == jnp.arange(entries, dtype=jnp.int32)) & is_prompt[:, None]
    ).astype(BF16)
    high = enc_grad.astype(BF16)
    rest = (enc_grad - high.astype(F32)).astype(BF16)
    gradient = dot_columns(chosen, high) + dot_columns(chosen, rest)
    tallies = jnp.stack([per_task(task_of, counted * token_loss), per_task(task_of, counted)])
    extra = jnp.zeros((8, share), F32).at[:2, :TASKS].set(tallies)
    gradient = jnp.concatenate([gradient, jnp.tile(extra, (1, shards))], 0)
    gradient = jnp.transpose(gradient.reshape(entries + 8, shards, share), (1, 0, 2))
    gradient = lax.psum_scatter(gradient, "vocab", scatter_dimension=0, tiled=True)[0]
    gradient = lax.psum(gradient, "dp")

    task_loss, counts = gradient[entries, :TASKS], gradient[entries + 1, :TASKS]
    task_scale = 1.0 / (TASKS * jnp.maximum(counts, 1.0))
    loss_mean = jnp.sum(task_loss * task_scale)
    full_grad = gradient[:entries].reshape(TASKS, P_SIZE, share) * task_scale[:, None, None]
    row_squares = jnp.sum(lax.all_gather(jnp.sum(full_grad * full_grad, -1), "vocab"), 0)
    grad_norm = jnp.sqrt(jnp.sum(row_squares))
    clip = CLIP_NORM / jnp.maximum(grad_norm, CLIP_NORM)
    prompt_grad = full_grad * clip
    row_second = BETA_TWO * row_moment + (1.0 - BETA_TWO) * (
        row_squares * clip * clip / width + SQUARE_EPS
    )
    column_second = BETA_TWO * column_moment + (1.0 - BETA_TWO) * (
        jnp.mean(prompt_grad * prompt_grad, 1) + SQUARE_EPS
    )
    new_moment = BETA_ONE * first_moment + (1.0 - BETA_ONE) * prompt_grad
    estimate = (
        row_second[:, :, None] * column_second[:, None, :] / jnp.mean(row_second, -1)[:, None, None]
    )
    update = new_moment / (1.0 - BETA_ONE**STEP) / jnp.sqrt(estimate / (1.0 - BETA_TWO**STEP))
    new_prompt = prompt - LEARN_RATE * (update + WEIGHT_DECAY * prompt)
    return (loss_mean, grad_norm, prompt_grad, new_moment, row_second, column_second, new_prompt)


def solution(mesh):
    placed = (
        P(None, "dp", "vocab"),
        P(None, "dp", "vocab"),
        P(None, "dp", "vocab"),
        P(None, "dp", None),
        P(None, "dp", None),
        P("vocab", None),
        P(None, "dp", None),
        P(None, "dp", None),
        P(None, "dp", None),
        P(None, "dp", None),
        P(),
        P(None, None, "vocab"),
        P(None, None, "vocab"),
        P(),
        P(None, "vocab"),
    )
    return jax.shard_map(
        on_device,
        mesh=mesh,
        in_specs=placed,
        out_specs=(
            P(),
            P(),
            P(None, None, "vocab"),
            P(None, None, "vocab"),
            P(),
            P(None, "vocab"),
            P(None, None, "vocab"),
        ),
        check_vma=False,
    )
```

time: 1450 us -> 791 us (0.55)
  waiting for transfers between devices: 641 us -> 208 us
  Pallas kernels: 0 us -> 341 us
  matrix products: 407 us -> 100 us
  local copies, waits for them, and re-layouts: 144 us -> 52.9 us
  blocking collectives: 100 us -> 19.2 us
  other arithmetic: 122 us -> 41.6 us
    all_gather x13 -> x2, waiting for transfers between devices: 444 us -> 31.9 us  [the longest x1 31.9 us: on_device(): all_hidden = lax.all_gather(hidden, 'vocab', axis=0, tiled=True)]
    pallas_call x0 -> x7, Pallas kernels: none -> 341 us  [the longest x1 140 us: gather_weights(): pl.pallas_call(functools.partial(gather_kernel, rows_z, rows_y), out_shap...]
    dot_general x72 -> x24, matrix products: 407 us -> 100 us  [the longest x9 50.1 us: dot_rows(): lax.dot_general(left, right, (((1,), (1,)), ((), ())), preferred_element_...]
    reduce_sum x18 -> x7, other arithmetic: 56.1 us -> 2.4 us  [the longest x1 1.35 us: on_device(): target_logit = jnp.sum(hidden.astype(F32) * target_rows, -1)]
    slice x30 -> x4, local copies, waits for them, and re-layouts: 52.2 us -> 0.87 us  [the longest x1 0.73 us: on_device(): dec_rows[:1]]
    all_gather x12 -> x3, blocking collectives: 62 us -> 19.2 us  [the longest x1 7.97 us: on_device(): lax.all_gather(jnp.sum(full_grad * full_grad, -1), 'vocab')]
    psum x1 -> x0, blocking collectives: 38.3 us -> none  [on_device(): gradient, task_loss = lax.psum((gradient, task_loss), ('dp', 'vocab'))]
    unnamed x359 -> x113, local copies, waits for them, and re-layouts: 29.9 us -> 8.79 us
  transfers between devices with their start and end apart: 24 -> 12, of which waited for: 14 -> 6; matrix products, arithmetic and copies ran while one was open for 37% -> 11% of each run, Pallas kernels for 0% -> 22%
where the time goes in v1:
time: 791 us; the launch traced here: 782 us
  Pallas kernels  341 us (43%)
  waiting for transfers between devices  208 us (26%)
  matrix products  100 us (13%)
  local copies, waits for them, and re-layouts  52.9 us (7%)
  other arithmetic  41.6 us (5%)
  blocking collectives  19.2 us (2%)
  between operations  17.3 us (2%)
    pallas_call x1, Pallas kernels, gather_weights(): pl.pallas_call(functools.partial(gather_kernel, rows_z, rows_y), out_shap...  140 us
    pallas_call x1, Pallas kernels, vocab_pass(): pl.pallas_call(functools.partial(vocab_kernel, tile, valid), grid=(count...  98.5 us
    psum x1, waiting for transfers between devices, on_device(): gradient = lax.psum(gradient, 'dp')  73.8 us
    pallas_call x2, Pallas kernels, attend_back(): pl.pallas_call(functools.partial(attend_back_kernel, parts, own, min(256,...  56.8 us
    reduce_scatter x1, waiting for transfers between devices, on_device(): summed = lax.psum_scatter(scaled, 'vocab', scatter_dimension=0, tiled=True)  56.2 us
    dot_general x9, matrix products, dot_rows(): lax.dot_general(left, right, (((1,), (1,)), ((), ())), preferred_element_...  50.1 us
    dot_general x13, matrix products, dot(): return jnp.dot(left, right, preferred_element_type=F32)  45.7 us
    pallas_call x3, Pallas kernels, attend(): pl.pallas_call(functools.partial(attend_kernel, parts, own, causal), grid...  45.6 us
  transfers between devices with their start and end apart: 12, of which 6 were waited for; matrix products, arithmetic and copies ran while one was open for 11% of the time, Pallas kernels for 22%

profile of v1, /device:TPU:25, one launch (start us, length us, event | category | flops | bytes accessed | tf_op | source)
XLA Modules:
  0.0 781.8 jit_solution(9199607100187365846)
XLA Ops:
  7.3 1.9 convert_element_type.137
  9.3 5.7 all-gather
  15.7 15.1 %gather_fusion.1 = bf16[2048,768]{1,0:T(8,128)(2,1)S(1)} fusion(bf16[8032,768]{1,0:T(8,128)(2,1)} %table_hbm.1, s32[2048]{0:T(1024)S(1)} %broadcast_clamp_fusion.1), kind=kCustom, calls=%fused_computation.1 | custom fusion | bytes 6299648 | tf_op jit(solution)/shard_map/jit(_take)/gather | solution.py:600
  30.9 2.0 select_select_fusion.1
  33.4 15.5 %gather_fusion.2 = bf16[2112,768]{1,0:T(8,128)(2,1)S(1)} fusion(bf16[8032,768]{1,0:T(8,128)(2,1)} %table_hbm.1, s32[3072]{0:T(1024)S(1)} %pad_clamp_fusion), kind=kCustom, calls=%fused_computation.2 | custom fusion | bytes 6496512 | tf_op jit(solution)/shard_map/jit(_take)/gather | solution.py:600
  49.1 2.7 select_select_fusion
  54.2 139.9 %shard_map.198 = (bf16[4,2,96,2304]{3,2,1,0:T(8,128)(2,1)}, bf16[4,2,96,2304]{3,2,1,0:T(8,128)(2,1)}, bf16[4,2,96,2304]{3,2,1,0:T(8,128)(2,1)}, bf16[4,2,96,768]...) custom-call(bf16[3,96,2304]{2,1,0:T(8,128)(2,1)} %refs_0_.1, ...), custom_call_target="tpu_custom_call" | custom-call | bytes 400000000 | tf_op jit(solution)/shard_map/pallas_call | solution.py:529
  195.0 1.8 copy.128
  197.1 2.0 gather_fusion
  199.1 1.7 fusion.51
  200.9 3.4 convolution_convert_fusion.2.refs_1_.refs_3_
  205.5 3.0 convolution_convert_fusion.7.refs_0_
  209.2 1.7 fusion.52
  210.9 4.7 convolution_convert_fusion.1.refs_1_.refs_3_
  215.8 15.0 %shard_map.199 = bf16[512,768]{1,0:T(8,128)(2,1)} custom-call(bf16[512,768]{1,0:T(8,128)(2,1)} %convolution_convert_fusion.7.refs_0_, bf16[512,1536]{1,0:T(8,128)(2,1)} %copy-done.44, bf16[512,1536]{1,0:T(8,128)(2,1)} %collective-permute-done.refs_2_.refs_4_, bf16[512,1536]{1,0:T(8,128)(2,1)} %copy-done.44, ...), custom_call_target="tpu_custom_call" | custom-call | flops 6442450944 | bytes 2359296 | tf_op jit(solution)/shard_map/pallas_call | solution.py:108
  230.8 2.5 multiply_reduce_fusion.8
  233.4 5.6 fusion.76
  239.0 3.9 multiply_reduce_fusion.7
  243.3 2.6 convolution_convert_fusion.refs_1_.refs_3_
  246.3 3.1 convolution_convert_fusion.6.refs_0_
  249.4 15.3 %shard_map.200 = bf16[512,768]{1,0:T(8,128)(2,1)} custom-call(bf16[512,768]{1,0:T(8,128)(2,1)} %convolution_convert_fusion.6.refs_0_, bf16[512,1536]{1,0:T(8,128)(2,1)} %convolution_convert_fusion.1.refs_1_.refs_3_, bf16[512,1536]{1,0:T(8,128)(2,1)} %collective-permute-done.1.refs_2_.refs_4_, bf16[512,1536]{1,0:T(8,128)(2,1)} %convolution_convert_fusion.1.refs_1_.refs_3_, ...), custom_call_target="tpu_custom_call" | custom-call | flops 6442450944 | bytes 2359296 | tf_op jit(solution)/shard_map/pallas_call | solution.py:108
  264.7 2.1 multiply_reduce_fusion.6
  266.8 3.6 convolution_convert_fusion.5.refs_0_
  270.4 15.3 %shard_map.201 = bf16[512,768]{1,0:T(8,128)(2,1)} custom-call(bf16[512,768]{1,0:T(8,128)(2,1)} %convolution_convert_fusion.5.refs_0_, bf16[512,1536]{1,0:T(8,128)(2,1)} %convolution_convert_fusion.refs_1_.refs_3_, bf16[512,1536]{1,0:T(8,128)(2,1)} %collective-permute-done.2.refs_2_.refs_4_, bf16[512,1536]{1,0:T(8,128)(2,1)} %convolution_convert_fusion.refs_1_.refs_3_, ...), custom_call_target="tpu_custom_call" | custom-call | flops 6442450944 | bytes 2359296 | tf_op jit(solution)/shard_map/pallas_call | solution.py:108
  285.7 2.7 multiply_reduce_fusion.5
  288.4 4.7 fusion.77
  293.1 3.9 multiply_reduce_fusion.4
  297.0 1.4 fusion.42
  298.4 1.9 sub.166.target_ref
  300.3 31.9 %all-gather.8.cloned.1.call-done.h_ref = bf16[2048,768]{1,0:T(8,128)(2,1)} async-done(((bf16[512,768]{1,0:T(8,128)(2,1)}), bf16[2048,768]{1,0:T(8,128)(2,1)}) %all-gather.8.cloned.1.call-update) | async-done | bytes 3145744 | tf_op jit(solution)/shard_map/all_gather | solution.py:669
  332.2 98.5 %shard_map.202 = (f32[2048,768]{1,0:T(8,128)}, f32[2048,128]{1,0:T(8,128)}) custom-call(bf16[2048,768]{1,0:T(8,128)(2,1)} %all-gather.8.cloned.1.call-done.h_ref, s32[2048,1]{1,0:T(8,128)} %sub.166.target_ref, bf16[8032,768]{1,0:T(8,128)(2,1)} %table_hbm.1), custom_call_target="tpu_custom_call" | custom-call | flops 51539607552 | bytes 12337152 | tf_op jit(solution)/shard_map/pallas_call | solution.py:260
  430.7 2.3 slice_bitcast_fusion
  433.0 1.6 copy.134
  434.5 5.5 all-gather.2
  440.2 1.4 copy.135
  441.6 1.9 exponential_reduce_fusion
  443.5 5.9 broadcast_multiply_fusion
  451.2 56.2 %reduce-scatter.9.cloned.1.call-done = f32[512,768]{1,0:T(8,128)} async-done(((f32[2048,768]{1,0:T(8,128)}), f32[512,768]{1,0:T(8,128)}) %reduce-scatter.9.cloned.1.call-update) | async-done | bytes 1572880 | tf_op jit(solution)/shard_map/reduce_scatter | solution.py:678
  507.4 2.3 multiply_reduce_fusion.3
  509.8 14.4 %multiply_reduce_fusion.2 = (f32[512]{0:T(512)S(1)}, f32[512,768]{1,0:T(8,128)}) fusion(f32[512,768]{1,0:T(8,128)S(1)} %get-tuple-element.149, f32[768]{0:T(1024)S(1)} %get-tuple-element.104, f32[512]{0:T(512)S(1)} %add_rsqrt_fusion.1, bf16[768,3072]{1,0:T(8,128)(2,1)} %bitcast.94, f32[512,3072]{1,0:T(8,128)} %copy-done.7, bf16[3072,768]{1,0:T(8,128)(2,1)} %bitcast.134, ...), kind=kOutput, calls=%fused_computation.88 | convolution fusion | flops 4868800000 | bytes 22824960 | tf_op jit(solution)/shard_map/dot_general | solution.py:37
  524.2 5.0 convolution_convert_fusion.4.refs_5_
  529.2 26.3 %shard_map.203 = (f32[512,768]{1,0:T(8,128)}, f32[512,768]{1,0:T(8,128)}, f32[512,768]{1,0:T(8,128)}, f32[512,768]{1,0:T(8,128)}) custom-call(bf16[512,768]{1,0:T(8,128)(2,1)} %convolution_convert_fusion.5.refs_0_, bf16[512,1536]{1,0:T(8,128)(2,1)} %convolution_convert_fusion.refs_1_.refs_3_, bf16[512,1536]{1,0:T(8,128)(2,1)} %collective-permute-done.2.refs_2_.refs_4_, ...), custom_call_target="tpu_custom_call" | custom-call | flops 16106127360 | bytes 7864320 | tf_op jit(solution)/shard_map/pallas_call | solution.py:195
  555.5 2.3 pad_maximum_fusion
  558.5 5.3 collective-permute-done.3
  563.8 3.0 fusion.29
  566.9 2.6 multiply_reduce_fusion.1
  569.5 14.1 %multiply_reduce_fusion = (f32[512]{0:T(512)S(1)}, f32[512,768]{1,0:T(8,128)}) fusion(f32[512,768]{1,0:T(8,128)S(1)} %copy-done.9, f32[768]{0:T(1024)S(1)} %get-tuple-element.102, f32[512]{0:T(512)S(1)} %add_rsqrt_fusion.5, bf16[768,3072]{1,0:T(8,128)(2,1)} %bitcast.92, f32[512,3072]{1,0:T(8,128)} %copy-done.6, bf16[3072,768]{1,0:T(8,128)(2,1)} %bitcast.130, ...), kind=kOutput, calls=%fused_computation.83 | convolution fusion | flops 4866833920 | bytes 22031360 | tf_op jit(solution)/shard_map/dot_general | solution.py:37
  583.6 3.1 multiply_add_fusion
  586.7 1.7 convolution_convert_fusion.3.refs_5_
  588.4 30.4 %shard_map.204 = (f32[512,768]{1,0:T(8,128)}, f32[512,768]{1,0:T(8,128)}, f32[512,768]{1,0:T(8,128)}, f32[512,768]{1,0:T(8,128)}, bf16[512,768]{1,0:T(8,128)(2,1)}) custom-call(bf16[512,768]{1,0:T(8,128)(2,1)} %convolution_convert_fusion.7.refs_0_, bf16[512,1536]{1,0:T(8,128)(2,1)} %copy-done.44, bf16[512,1536]{1,0:T(8,128)(2,1)} %collective-permute-done.refs_2_.refs_4_, ...), custom_call_target="tpu_custom_call" | custom-call | flops 16106127360 | bytes 7864320 | tf_op jit(solution)/shard_map/pallas_call | solution.py:195
  618.8 4.0 pad_maximum_fusion.1
  623.5 5.4 collective-permute-done.4
  628.9 4.7 fusion.34
  633.7 3.6 fusion.36
  638.4 1.4 fusion.25
  639.8 2.9 fusion.39
  642.6 2.2 copy.137
  644.8 1.8 maximum_bitcast_fusion
  646.8 35.3 %reduce-scatter.11.cloned.1.call-done = f32[1,808,192]{1,2,0:T(8,128)} async-done(((f32[4,808,192]{1,2,0:T(8,128)}), f32[1,808,192]{1,2,0:T(8,128)}) %reduce-scatter.11.cloned.1.call-update) | async-done | bytes 620560 | tf_op jit(solution)/shard_map/reduce_scatter | solution.py:738
  682.1 73.8 %all-reduce.4.cloned.1.call-done = f32[808,192]{0,1:T(8,128)} async-done(((f32[808,192]{0,1:T(8,128)}), f32[808,192]{0,1:T(8,128)}) %all-reduce.4.cloned.1.call-update) | async-done | bytes 620560 | tf_op jit(solution)/shard_map/psum | solution.py:739
  757.0 1.2 fusion.150
  758.3 8.0 %all_gather.31 = f32[4,8,100]{2,1,0:T(8,128)S(1)} all-gather(f32[1,8,100]{2,1,0:T(8,128)S(1)} %all_gather.30), channel_id=1, replica_groups=mesh['dp'=8,'vocab'=4] {'vocab'}, dimensions={0}, use_global_device_ids=true | all-gather | bytes 16000 | tf_op jit(solution)/shard_map/all_gather | solution.py:745
  768.8 1.0 copy.144
  769.8 1.1 add_subtract_fusion
  (218 shorter events, 18.0 us)
Async XLA Ops:
  7.2 186.9 %copy-start = (s32[2,1,3]{2,1,0:T(1,128)S(1)}, s32[2,1,3]{2,1,0:T(1,128)}, u32[]{:S(2)}) copy-start(s32[2,1,3]{2,1,0:T(1,128)} %param.21) | copy-start | bytes 76
  7.2 2.1 copy-start.40
  7.2 2.1 copy-start.42
  7.2 2.1 copy-start.41
  7.2 187.8 %all-gather.6.cloned.1.call-start = ((), (), s32[]{:S(2)}) async-start(), calls=%async_computation.4 | async-start | bytes 1966080 | tf_op jit(solution)/shard_map/all_gather | solution.py:606
  9.2 189.9 %reduce-scatter.5.cloned.1.call-start = ((), (), s32[]{:S(2)}) async-start(), calls=%async_computation.5 | async-start | bytes 3932160 | tf_op jit(solution)/shard_map/reduce_scatter | solution.py:603
  32.9 175.6 %reduce-scatter.7.cloned.1.call-start = ((), (), s32[]{:S(2)}) async-start(), calls=%async_computation.6 | async-start | bytes 4055040 | tf_op jit(solution)/shard_map/reduce_scatter | solution.py:604
  51.8 0.7 copy-start.43
  51.8 280.4 %all-gather.8.cloned.1.call-start = ((), (), s32[]{:S(2)}) async-start(), calls=%async_computation.7 | async-start | bytes 3932160 | tf_op jit(solution)/shard_map/all_gather | solution.py:669
  54.2 140.1 %copy-start.31 = (f32[7,768]{1,0:T(8,128)S(1)}, f32[7,768]{1,0:T(8,128)}, u32[]{:S(2)}) copy-start(f32[7,768]{1,0:T(8,128)} %param.27) | copy-start | bytes 64516
  194.2 2.9 copy-start.27
  194.4 11.1 %copy-start.33 = (f32[768]{0:T(1024)}, f32[768]{0:T(1024)S(1)}, u32[]{:S(2)}) copy-start(f32[768]{0:T(1024)S(1)} %get-tuple-element.103) | copy-start | bytes 9220
  195.0 4.2 copy-start.37
  200.9 29.9 %copy-start.2 = (bf16[512,768]{1,0:T(8,128)(2,1)}, bf16[512,768]{1,0:T(8,128)(2,1)S(1)}, u32[]{:S(2)}) copy-start(bf16[512,768]{1,0:T(8,128)(2,1)S(1)} %get-tuple-element.122) | copy-start | bytes 2359300
  200.9 4.6 copy-start.24
  204.3 4.2 copy-start.44
  204.3 11.4 %collective-permute-start = (bf16[512,1536]{1,0:T(8,128)(2,1)S(1)}, bf16[512,1536]{1,0:T(8,128)(2,1)}, u32[]{:S(2)}, u32[]{:S(2)}) collective-permute-start(bf16[512,1536]{1,0:T(8,128)(2,1)S(1)} %convolution_convert_fusion.2.refs_1_.refs_3_), channel_id=1, source_target_pairs={{0,1},{1,0},{2,3},{3,2},{4,5},{5,4},{6,7},{7,6},{8,9},{9,8},{10,11... | collective-permute-start | bytes 4718600 | tf_op jit(solution)/shard_map/ppermute | solution.py:586
  215.6 33.8 %collective-permute-start.1 = (bf16[512,1536]{1,0:T(8,128)(2,1)}, bf16[512,1536]{1,0:T(8,128)(2,1)}, u32[]{:S(2)}, u32[]{:S(2)}) collective-permute-start(bf16[512,1536]{1,0:T(8,128)(2,1)} %convolution_convert_fusion.1.refs_1_.refs_3_), channel_id=1, source_target_pairs={{0,1},{1,0},{2,3},{3,2},{4,5},{5,4},{6,7},{7,6},{8,9},{9,8},{10,11... | collective-permute-start | bytes 4718600 | tf_op jit(solution)/shard_map/ppermute | solution.py:586
  230.8 8.2 %slice-start = ((s8[4718592]{0:T(1024)(128)(4,1)}), s8[4194304]{0:T(1024)(128)(4,1)S(1)}, s32[]{:S(2)}) async-start(s8[4718592]{0:T(1024)(128)(4,1)} %bitcast.131), calls=%async_computation.11 | async-start | bytes 8388608
  233.3 5.6 copy-start.8
  233.4 5.6 slice-start.1
  239.0 3.9 copy-start.6
  239.0 4.2 copy-start.18
  242.9 3.0 copy-start.10
  243.3 3.0 copy-start.4
  245.9 24.5 %collective-permute-start.2 = (bf16[512,1536]{1,0:T(8,128)(2,1)}, bf16[512,1536]{1,0:T(8,128)(2,1)}, u32[]{:S(2)}, u32[]{:S(2)}) collective-permute-start(bf16[512,1536]{1,0:T(8,128)(2,1)} %convolution_convert_fusion.refs_1_.refs_3_), channel_id=1, source_target_pairs={{0,1},{1,0},{2,3},{3,2},{4,5},{5,4},{6,7},{7,6},{8,9},{9,8},{10,11... | collective-permute-start | bytes 4718600 | tf_op jit(solution)/shard_map/ppermute | solution.py:586
  249.4 15.3 %copy-start.46 = (bf16[4,2,96,768]{3,2,1,0:T(8,128)(2,1)S(1)}, bf16[4,2,96,768]{3,2,1,0:T(8,128)(2,1)}, u32[]{:S(2)}) copy-start(bf16[4,2,96,768]{3,2,1,0:T(8,128)(2,1)} %get-tuple-element.45) | copy-start | bytes 3538948
  266.8 3.6 copy-start.17
  270.4 15.3 %copy-start.12 = (bf16[4,2,96,768]{3,2,1,0:T(8,128)(2,1)S(1)}, bf16[4,2,96,768]{3,2,1,0:T(8,128)(2,1)}, u32[]{:S(2)}) copy-start(bf16[4,2,96,768]{3,2,1,0:T(8,128)(2,1)} %get-tuple-element.47) | copy-start | bytes 3538948
  285.7 7.4 slice-start.2
  288.4 4.7 slice-start.3
  293.0 3.9 copy-start.7
  293.1 3.9 copy-start.5
  298.4 209.1 %reduce-scatter.9.cloned.1.call-start = ((), (), s32[]{:S(2)}) async-start(), calls=%async_computation.8 | async-start | bytes 7864320 | tf_op jit(solution)/shard_map/reduce_scatter | solution.py:678
  449.3 0.7 copy-start.26
  449.3 1.7 copy-start.30
  449.4 232.7 %reduce-scatter.11.cloned.1.call-start = ((), (), s32[]{:S(2)}) async-start(), calls=%async_computation.9 | async-start | bytes 3440640 | tf_op jit(solution)/shard_map/reduce_scatter | solution.py:738
  555.5 8.4 %copy-start.19 = (bf16[4,2,96,2304]{3,2,1,0:T(8,128)(2,1)S(1)}, bf16[4,2,96,2304]{3,2,1,0:T(8,128)(2,1)}, u32[]{:S(2)}) copy-start(bf16[4,2,96,2304]{3,2,1,0:T(8,128)(2,1)} %get-tuple-element.46) | copy-start | bytes 10616836
  555.5 8.4 %copy-start.20 = (f32[512,768]{1,0:T(8,128)S(1)}, f32[512,768]{1,0:T(8,128)}, u32[]{:S(2)}) copy-start(f32[512,768]{1,0:T(8,128)} %get-tuple-element.52) | copy-start | bytes 4718596
  557.8 6.0 collective-permute-start.3
  563.8 3.0 copy-start.11
  563.8 3.0 copy-start.21
  566.8 2.7 copy-start.9
  583.6 3.1 copy-start.45
  618.8 4.4 copy-start.28
  618.8 10.1 %copy-start.15 = (f32[512,768]{1,0:T(8,128)S(1)}, f32[512,768]{1,0:T(8,128)}, u32[]{:S(2)}) copy-start(f32[512,768]{1,0:T(8,128)} %get-tuple-element.56) | copy-start | bytes 4718596
  622.9 6.0 collective-permute-start.4
  628.9 4.7 copy-start.13
  628.9 4.8 copy-start.16
  633.6 3.6 copy-start.3
  633.6 3.6 copy-start.23
  633.7 3.6 copy-start.25
  633.7 3.6 copy-start.34
  637.3 1.1 copy-start.32
  637.3 1.1 copy-start.38
  646.7 120.9 %copy-start.39 = (f32[8,100]{1,0:T(8,128)S(1)}, f32[8,100]{1,0:T(8,128)}, u32[]{:S(2)}) copy-start(f32[8,100]{1,0:T(8,128)} %param.30) | copy-start | bytes 9604
  646.7 109.2 %all-reduce.4.cloned.1.call-start = ((), (), s32[]{:S(2)}) async-start(), calls=%async_computation.10 | async-start | bytes 1376256 | tf_op jit(solution)/shard_map/psum | solution.py:739
  767.8 2.1 copy-start.35
  767.8 0.9 copy-start.36
  768.2 1.6 copy-start.14
  768.2 1.6 copy-start.22
  768.7 2.3 copy-start.29
  771.0 2.7 copy-start.1
Sparse Core Ops, SparseCore 0:
  10.2 21.0 all-gather.5
  33.8 44.9 reduce-scatter.4
  81.5 51.0 reduce-scatter.6
  298.5 33.6 all-gather.7
  449.5 57.8 reduce-scatter.8
  646.8 35.1 reduce-scatter.10
  685.5 70.3 all-reduce.3

commit v2 on v1

--- a/solution.py
+++ b/solution.py
@@ -550,6 +550,351 @@
     return tuple(lax.all_gather(tensor, "dp", axis=1, tiled=True) for tensor in tensors)
 
 
+def vocab_exchange_kernel(tile, valid, h_ref, target_ref, table_hbm, grad_ref, stat_ref, *scratch):
+    table, held, logits_a, logits_b, powers_a, powers_b, scale_a, scale_b = scratch[:8]
+    maxima_ref, total_ref, parcel, arrived, send_sem, recv_sem, table_sem = scratch[8:]
+    rows, width = h_ref.shape
+    padded = table.shape[0]
+    tiles = padded // tile
+    v = lax.axis_index("vocab")
+    x, core = v // 2, lax.rem(v, 2)
+    twin, across, diagonal = x * 2 + 1 - core, (1 - x) * 2 + core, (1 - x) * 2 + 1 - core
+
+    barrier = pltpu.get_barrier_semaphore()
+    for peer in (twin, across, diagonal):
+        pl.semaphore_signal(
+            barrier, inc=1, device_id={"vocab": peer}, device_id_type=pl.DeviceIdType.MESH
+        )
+    pl.semaphore_wait(barrier, 3)
+
+    def remote(source, target, index, peer):
+        return pltpu.make_async_remote_copy(
+            src_ref=source,
+            dst_ref=target,
+            send_sem=send_sem.at[index],
+            recv_sem=recv_sem.at[index],
+            device_id={"vocab": peer},
+            device_id_type=pl.DeviceIdType.MESH,
+        )
+
+    to_twin = remote(h_ref, held.at[0], 0, twin)
+    to_across = remote(h_ref, held.at[1], 1, across)
+    passed_on = remote(held.at[1], held.at[2], 2, twin)
+    results = [
+        remote(parcel.at[k], arrived.at[k], 3 + k, peer)
+        for k, peer in enumerate((twin, across, diagonal))
+    ]
+    to_twin.start()
+    to_across.start()
+    held[3] = h_ref[...]
+
+    sizes = [min(tile, valid - k * tile) for k in range(tiles)]
+    loads = [
+        pltpu.make_async_copy(
+            table_hbm.at[pl.ds(k * tile, size), :],
+            table.at[pl.ds(k * tile, size), :],
+            table_sem.at[k],
+        )
+        for k, size in enumerate(sizes)
+    ]
+    for load in loads:
+        load.start()
+    if padded > valid:
+        table[valid:, :] = jnp.zeros((padded - valid, width), BF16)
+    to_twin.wait_recv()
+    for load in loads:
+        load.wait()
+
+    logits_of, powers_of, scale_of = (logits_a, logits_b), (powers_a, powers_b), (scale_a, scale_b)
+    column = lax.broadcasted_iota(jnp.int32, (rows, tile), 1)
+    lane = lax.broadcasted_iota(jnp.int32, (rows, LANES), 1)
+
+    def turn(k, _):
+        @pl.when(k == 1)
+        def _():
+            to_across.wait_recv()
+            passed_on.start()
+
+        @pl.when(k == 2)
+        def _():
+            passed_on.wait_recv()
+
+        owner = jnp.where(k == 0, twin, jnp.where(k == 1, across, jnp.where(k == 2, diagonal, v)))
+
+        def part(at):
+            return table[at * tile : (at + 1) * tile, :]
+
+        def scores(at):
+            logits_of[at % 2][...] = dot_rows(held[k], part(at))
+
+        def soften(at):
+            logits = logits_of[at % 2][...]
+            if at == tiles - 1 and padded > valid:
+                logits = jnp.where(column < valid - at * tile, logits, MASKED)
+            highest = jnp.maximum(maxima_ref[...], jnp.max(logits, -1, keepdims=True))
+            powers = jnp.exp(logits - highest)
+            scale = jnp.exp(maxima_ref[...] - highest)
+            maxima_ref[...] = highest
+            total_ref[...] = total_ref[...] * scale + jnp.sum(powers, -1, keepdims=True)
+            scale_of[at % 2][...] = scale
+            powers_of[at % 2][...] = jnp.where(
+                column == target_ref[owner] - at * tile, 0.0, powers
+            ).astype(BF16)
+
+        def gather(at):
+            term = dot(powers_of[at % 2][...], part(at))
+            grad_ref[...] = grad_ref[...] * scale_of[at % 2][...] + term
+
+        maxima_ref[...] = jnp.full((rows, 1), MASKED, F32)
+        total_ref[...] = jnp.zeros((rows, 1), F32)
+        grad_ref[...] = jnp.zeros_like(grad_ref)
+        for at in range(tiles + 2):
+            if at < tiles:
+                scores(at)
+            if 0 <= at - 1 < tiles:
+                soften(at - 1)
+            if at >= 2:
+                gather(at - 2)
+
+        @pl.when(k < 3)
+        def _():
+            parcel[k, :, :width] = grad_ref[...].astype(BF16)
+            tail = jnp.zeros((rows, LANES), F32)
+            for first, value in ((0, maxima_ref[...]), (3, total_ref[...])):
+                for step in range(3):
+                    piece = value.astype(BF16).astype(F32)
+                    tail = jnp.where(lane == first + step, piece, tail)
+                    value = value - piece
+            parcel[k, :, width:] = tail.astype(BF16)
+
+        for index, result in enumerate(results):
+            pl.when(k == index)(result.start)
+        return 0
+
+    lax.fori_loop(0, 4, turn, 0)
+    for result in results:
+        result.wait_recv()
+    tails = [arrived[k, :, width:].astype(F32) for k in range(3)]
+    highs = [t[:, 0:1] + t[:, 1:2] + t[:, 2:3] for t in tails] + [maxima_ref[...]]
+    totals = [t[:, 3:4] + t[:, 4:5] + t[:, 5:6] for t in tails] + [total_ref[...]]
+    highest = functools.reduce(jnp.maximum, highs)
+    log_total = highest + jnp.log(sum(t * jnp.exp(m - highest) for m, t in zip(highs, totals)))
+    summed = grad_ref[...] * jnp.exp(highs[3] - log_total)
+    for k in range(3):
+        summed = summed + arrived[k, :, :width].astype(F32) * jnp.exp(highs[k] - log_total)
+    grad_ref[...] = summed
+    stat_ref[...] = jnp.where(lane == 0, log_total, 0.0)
+    for copy in [to_twin, to_across, passed_on, *results]:
+        copy.wait_send()
+
+
+def vocab_exchange(hidden, target_local, embedding):
+    rows, width = hidden.shape
+    valid = embedding.shape[0]
+    tile = 2 * VOCAB_BLOCK
+    padded = (valid + tile - 1) // tile * tile
+    vmem = pl.BlockSpec(memory_space=pltpu.VMEM)
+    return pl.pallas_call(
+        functools.partial(vocab_exchange_kernel, tile, valid),
+        out_shape=[
+            jax.ShapeDtypeStruct((rows, width), F32),
+            jax.ShapeDtypeStruct((rows, LANES), F32),
+        ],
+        in_specs=[vmem, vmem, pl.BlockSpec(memory_space=pl.ANY)],
+        out_specs=[vmem, vmem],
+        scratch_shapes=[
+            pltpu.VMEM((padded, width), BF16),
+            pltpu.VMEM((4, rows, width), BF16),
+            pltpu.VMEM((rows, tile), F32),
+            pltpu.VMEM((rows, tile), F32),
+            pltpu.VMEM((rows, tile), BF16),
+            pltpu.VMEM((rows, tile), BF16),
+            pltpu.VMEM((rows, 1), F32),
+            pltpu.VMEM((rows, 1), F32),
+            pltpu.VMEM((rows, 1), F32),
+            pltpu.VMEM((rows, 1), F32),
+            pltpu.VMEM((3, rows, width + LANES), BF16),
+            pltpu.VMEM((3, rows, width + LANES), BF16),
+            pltpu.SemaphoreType.DMA((6,)),
+            pltpu.SemaphoreType.DMA((6,)),
+            pltpu.SemaphoreType.DMA((padded // tile,)),
+        ],
+        compiler_params=pltpu.CompilerParams(
+            collective_id=1, has_side_effects=True, vmem_limit_bytes=VMEM_LIMIT
+        ),
+        cost_estimate=pl.CostEstimate(
+            flops=16 * rows * padded * width, bytes_accessed=2 * valid * width, transcendentals=0
+        ),
+    )(hidden, target_local.reshape(4, rows, 1), embedding)
+
+
+def reduce_kernel(rows_dp, task_ref, table_ref, stat_ref, out_ref, stats_out, squares_out, *scratch):
+    cast, crossed, swap, swapped, own, outgoing, pieces, result, results = scratch[:9]
+    stats, squares, send_sem, recv_sem = scratch[9:]
+    features = own.shape[1]
+    at, v = lax.axis_index("dp"), lax.axis_index("vocab")
+    x, core = v // 2, lax.rem(v, 2)
+    twin, across = x * 2 + 1 - core, (1 - x) * 2 + core
+    dp_peers = [lax.rem(at + k, rows_dp) for k in range(1, rows_dp)]
+    vocab_peers = [lax.rem(v + k, 4) for k in range(1, 4)]
+
+    barrier = pltpu.get_barrier_semaphore()
+    for peer in [{"vocab": p} for p in vocab_peers] + [{"dp": p} for p in dp_peers]:
+        pl.semaphore_signal(barrier, inc=1, device_id=peer, device_id_type=pl.DeviceIdType.MESH)
+    pl.semaphore_wait(barrier, rows_dp + 2)
+
+    def remote(source, target, send, recv, peer):
+        return pltpu.make_async_remote_copy(
+            src_ref=source,
+            dst_ref=target,
+            send_sem=send_sem.at[send],
+            recv_sem=recv_sem.at[recv],
+            device_id=peer,
+            device_id_type=pl.DeviceIdType.MESH,
+        )
+
+    half = 2 * features
+    there = pl.ds(pl.multiple_of((1 - x) * half, half), half)
+    here = pl.ds(pl.multiple_of(x * half, half), half)
+    stats[0] = stat_ref[...]
+    cast[...] = table_ref[there, :].astype(BF16)
+    over_x = remote(cast, crossed, 0, 0, {"vocab": across})
+    stat_x = remote(stats.at[0], stats.at[1], 1, 1, {"vocab": across})
+    over_x.start()
+    stat_x.start()
+    over_x.wait_recv()
+    stat_x.wait_recv()
+
+    stats[2] = stats[0] + stats[1]
+    stat_core = remote(stats.at[2], stats.at[3], 2, 2, {"vocab": twin})
+    stat_core.start()
+    tasks = [[task_ref[m, s] for s in range(task_ref.shape[1])] for m in range(2)]
+    other = jnp.where(x == 0, 1, 0)
+
+    def by_task(part, t):
+        start = pl.multiple_of(part * features, features)
+        mine = table_ref[pl.ds(pl.multiple_of(x * half + part * features, features), features), :]
+        theirs = crossed[pl.ds(start, features), :].astype(F32)
+        total = jnp.zeros((features, LANES), F32)
+        for s in range(task_ref.shape[1]):
+            lanes = slice(s * LANES, (s + 1) * LANES)
+            mine_task = jnp.where(x == 0, tasks[0][s], tasks[1][s])
+            their_task = jnp.where(x == 0, tasks[1][s], tasks[0][s])
+            total = total + jnp.where(mine_task == t, mine[:, lanes], 0.0)
+            total = total + jnp.where(their_task == t, theirs[:, lanes], 0.0)
+        return total
+
+    for t in range(TASKS):
+        swap[t] = by_task(1 - core, t).astype(BF16)
+    over_core = remote(swap, swapped, 3, 3, {"vocab": twin})
+    over_core.start()
+    for t in range(TASKS):
+        own[t] = by_task(core, t)
+    over_core.wait_recv()
+    stat_core.wait_recv()
+    stats[4 + at] = stats[2] + stats[3]
+    for t in range(TASKS):
+        own[t] = own[t] + swapped[t].astype(F32)
+        outgoing[t] = own[t].astype(BF16)
+
+    base = 4
+    spread, tallies = [], []
+    for k, peer in enumerate(dp_peers):
+        spread.append(
+            remote(outgoing.at[peer], pieces.at[at], base + k, base + at, {"dp": peer})
+        )
+        tallies.append(
+            remote(
+                stats.at[4 + at],
+                stats.at[4 + at],
+                base + rows_dp + k,
+                base + rows_dp + at,
+                {"dp": peer},
+            )
+        )
+    for copy in spread + tallies:
+        copy.start()
+    total = own[at]
+    for peer in dp_peers:
+        remote(outgoing.at[peer], pieces.at[peer], base, base + peer, {"dp": peer}).wait_recv()
+        total = total + pieces[peer].astype(F32)
+    result[...] = total.astype(BF16)
+    results[at] = result[...]
+    returns = []
+    for k, peer in enumerate(dp_peers):
+        returns.append(
+            remote(
+                result,
+                results.at[at],
+                base + 2 * rows_dp + k,
+                base + 2 * rows_dp + at,
+                {"dp": peer},
+            )
+        )
+    for copy in returns:
+        copy.start()
+    for peer in dp_peers:
+        remote(
+            stats.at[4 + peer], stats.at[4 + peer], base, base + rows_dp + peer, {"dp": peer}
+        ).wait_recv()
+    tally = functools.reduce(jnp.add, [stats[4 + k] for k in range(rows_dp)])
+    stats_out[...] = tally
+    for peer in dp_peers:
+        remote(result, results.at[peer], base, base + 2 * rows_dp + peer, {"dp": peer}).wait_recv()
+    for t in range(TASKS):
+        scale = 1.0 / (TASKS * jnp.maximum(tally[1:2, t : t + 1], 1.0))
+        scaled = results[t].astype(F32) * scale
+        out_ref[t] = scaled
+        squares[v, t : t + 1, :] = jnp.sum(scaled * scaled, 0, keepdims=True)
+    last = base + 3 * rows_dp
+    shares = [
+        remote(squares.at[v], squares.at[v], last + k, last + v, {"vocab": peer})
+        for k, peer in enumerate(vocab_peers)
+    ]
+    for copy in shares:
+        copy.start()
+    for peer in vocab_peers:
+        remote(squares.at[peer], squares.at[peer], last, last + peer, {"vocab": peer}).wait_recv()
+    squares_out[...] = squares[0] + squares[1] + squares[2] + squares[3]
+    for copy in [over_x, stat_x, stat_core, over_core, *spread, *tallies, *returns, *shares]:
+        copy.wait_send()
+
+
+def reduce_over_devices(task_list, table, stats):
+    rows_dp = lax.axis_size("dp")
+    features = table.shape[0] // 4
+    vmem = pl.BlockSpec(memory_space=pltpu.VMEM)
+    copies = 4 + 3 * rows_dp + 4
+    return pl.pallas_call(
+        functools.partial(reduce_kernel, rows_dp),
+        out_shape=[
+            jax.ShapeDtypeStruct((TASKS, features, LANES), F32),
+            jax.ShapeDtypeStruct((8, LANES), F32),
+            jax.ShapeDtypeStruct((8, LANES), F32),
+        ],
+        in_specs=[pl.BlockSpec(memory_space=pltpu.SMEM), vmem, vmem],
+        out_specs=[vmem] * 3,
+        scratch_shapes=[
+            pltpu.VMEM((2 * features, table.shape[1]), BF16),
+            pltpu.VMEM((2 * features, table.shape[1]), BF16),
+            pltpu.VMEM((TASKS, features, LANES), BF16),
+            pltpu.VMEM((TASKS, features, LANES), BF16),
+            pltpu.VMEM((TASKS, features, LANES), F32),
+            pltpu.VMEM((TASKS, features, LANES), BF16),
+            pltpu.VMEM((rows_dp, features, LANES), BF16),
+            pltpu.VMEM((features, LANES), BF16),
+            pltpu.VMEM((rows_dp, features, LANES), BF16),
+            pltpu.VMEM((4 + rows_dp, 8, LANES), F32),
+            pltpu.VMEM((4, 8, LANES), F32),
+            pltpu.SemaphoreType.DMA((copies,)),
+            pltpu.SemaphoreType.DMA((copies,)),
+        ],
+        compiler_params=pltpu.CompilerParams(
+            collective_id=2, has_side_effects=True, vmem_limit_bytes=VMEM_LIMIT
+        ),
+    )(task_list, table, stats)
+
+
 def on_device(
     tokens,
     targets,
@@ -666,17 +1011,21 @@
     output_norm, inverse_out = normed(dec_last, norm_gains[6])
     hidden = (output_norm * width ** (-0.5)).astype(BF16)
 
-    all_hidden = lax.all_gather(hidden, "vocab", axis=0, tiled=True)
     target_local = ids[1].reshape(-1, 1) - first_row
-    part, stats = vocab_pass(all_hidden, target_local, embedding, own)
-    gathered = lax.all_gather(stats[:, :2].T, "vocab")
-    maxima = jnp.max(gathered[:, 0], 0)
-    log_total = maxima + jnp.log(
-        jnp.sum(gathered[:, 1] * jnp.exp(gathered[:, 0] - maxima), 0)
-    )
-    scaled = part * jnp.exp(stats[:, 0] - log_total)[:, None]
-    summed = lax.psum_scatter(scaled, "vocab", scatter_dimension=0, tiled=True)
-    own_total = lax.dynamic_slice(log_total, (me * own,), (own,))
+    if shards == 4:
+        summed, stats = vocab_exchange(hidden, target_local, embedding)
+        own_total = stats[:, 0]
+    else:
+        all_hidden = lax.all_gather(hidden, "vocab", axis=0, tiled=True)
+        part, stats = vocab_pass(all_hidden, target_local, embedding, own)
+        gathered = lax.all_gather(stats[:, :2].T, "vocab")
+        maxima = jnp.max(gathered[:, 0], 0)
+        log_total = maxima + jnp.log(
+            jnp.sum(gathered[:, 1] * jnp.exp(gathered[:, 0] - maxima), 0)
+        )
+        scaled = part * jnp.exp(stats[:, 0] - log_total)[:, None]
+        summed = lax.psum_scatter(scaled, "vocab", scatter_dimension=0, tiled=True)
+        own_total = lax.dynamic_slice(log_total, (me * own,), (own,))
     target_logit = jnp.sum(hidden.astype(F32) * target_rows, -1)
     token_loss = own_total - target_logit
     target_coefficient = (jnp.exp(target_logit - own_total) - 1.0).astype(BF16).astype(F32)
@@ -724,25 +1073,35 @@
     )
     enc_grad = enc_grad + normed_back(enc_input, norm_gains[0], inverse_in, source_grad)
 
-    entries = TASKS * P_SIZE
+    segments = lengths.shape[0]
+    place_of = segment * LANES + in_segment
     chosen = (
-        (slot[:, None] == jnp.arange(entries, dtype=jnp.int32)) & is_prompt[:, None]
+        (place_of[:, None] == jnp.arange(segments * LANES, dtype=jnp.int32)) & is_prompt[:, None]
     ).astype(BF16)
     high = enc_grad.astype(BF16)
     rest = (enc_grad - high.astype(F32)).astype(BF16)
-    gradient = dot_columns(chosen, high) + dot_columns(chosen, rest)
+    table = dot_columns(high, chosen) + dot_columns(rest, chosen)
     tallies = jnp.stack([per_task(task_of, counted * token_loss), per_task(task_of, counted)])
-    extra = jnp.zeros((8, share), F32).at[:2, :TASKS].set(tallies)
-    gradient = jnp.concatenate([gradient, jnp.tile(extra, (1, shards))], 0)
-    gradient = jnp.transpose(gradient.reshape(entries + 8, shards, share), (1, 0, 2))
-    gradient = lax.psum_scatter(gradient, "vocab", scatter_dimension=0, tiled=True)[0]
-    gradient = lax.psum(gradient, "dp")
-
-    task_loss, counts = gradient[entries, :TASKS], gradient[entries + 1, :TASKS]
-    task_scale = 1.0 / (TASKS * jnp.maximum(counts, 1.0))
-    loss_mean = jnp.sum(task_loss * task_scale)
-    full_grad = gradient[:entries].reshape(TASKS, P_SIZE, share) * task_scale[:, None, None]
-    row_squares = jnp.sum(lax.all_gather(jnp.sum(full_grad * full_grad, -1), "vocab"), 0)
+    stats = jnp.zeros((8, LANES), F32).at[:2, :TASKS].set(tallies)
+    if shards == 4 and lax.axis_size("dp") == TASKS:
+        gradient, stats, squares = reduce_over_devices(task_ids[:, 0], table, stats)
+        full_grad = jnp.swapaxes(gradient[:, :, :P_SIZE], 1, 2)
+        row_squares = squares[:, :P_SIZE]
+        task_scale = 1.0 / (TASKS * jnp.maximum(stats[1, :TASKS], 1.0))
+    else:
+        hits = (tasks[:, None] == jnp.arange(TASKS, dtype=jnp.int32)).astype(F32)
+        by_task = jnp.einsum(
+            "fsp,st->tpf",
+            table.reshape(width, segments, LANES)[:, :, :P_SIZE],
+            hits,
+            precision=lax.Precision.HIGHEST,
+        )
+        stats = lax.psum(stats, ("dp", "vocab"))
+        gradient = lax.psum_scatter(by_task, "vocab", scatter_dimension=2, tiled=True)
+        task_scale = 1.0 / (TASKS * jnp.maximum(stats[1, :TASKS], 1.0))
+        full_grad = lax.psum(gradient, "dp") * task_scale[:, None, None]
+        row_squares = jnp.sum(lax.all_gather(jnp.sum(full_grad * full_grad, -1), "vocab"), 0)
+    loss_mean = jnp.sum(stats[0, :TASKS] * task_scale)
     grad_norm = jnp.sqrt(jnp.sum(row_squares))
     clip = CLIP_NORM / jnp.maximum(grad_norm, CLIP_NORM)
     prompt_grad = full_grad * clip

time: 791 us -> 575 us (0.73)
  waiting for transfers between devices: 208 us -> 10.2 us
  Pallas kernels: 341 us -> 367 us
  blocking collectives: 19.2 us -> 5.67 us
  other arithmetic: 41.6 us -> 29.5 us
  local copies, waits for them, and re-layouts: 52.9 us -> 41.7 us
    reduce_scatter x2 -> x0, waiting for transfers between devices: 91.5 us -> none  [the longest x1 56.2 us: on_device(): summed = lax.psum_scatter(scaled, 'vocab', scatter_dimension=0, tiled=True)]
    psum x1 -> x0, waiting for transfers between devices: 73.8 us -> none  [on_device(): gradient = lax.psum(gradient, 'dp')]
    all_gather x1 -> x0, waiting for transfers between devices: 31.9 us -> none  [on_device(): all_hidden = lax.all_gather(hidden, 'vocab', axis=0, tiled=True)]
    pallas_call x1 -> x2, Pallas kernels: 98.5 us -> 125 us  [the longest x1 80.3 us: vocab_exchange(): pl.pallas_call(functools.partial(vocab_exchange_kernel, tile, valid), out...]
    all_gather x2 -> x0, blocking collectives: 13.5 us -> none  [the longest x1 7.97 us: on_device(): lax.all_gather(jnp.sum(full_grad * full_grad, -1), 'vocab')]
  transfers between devices with their start and end apart: 12 -> 8, of which waited for: 6 -> 2; matrix products, arithmetic and copies ran while one was open for 11% -> 15% of each run, Pallas kernels for 22% -> 30%
where the time goes in v2:
time: 575 us; the launch traced here: 568 us
  Pallas kernels  367 us (64%)
  matrix products  95.3 us (17%)
  local copies, waits for them, and re-layouts  41.7 us (7%)
  other arithmetic  29.5 us (5%)
  between operations  16.9 us (3%)
  waiting for transfers between devices  10.2 us (2%)
    pallas_call x1, Pallas kernels, gather_weights(): pl.pallas_call(functools.partial(gather_kernel, rows_z, rows_y), out_shap...  140 us
    pallas_call x1, Pallas kernels, vocab_exchange(): pl.pallas_call(functools.partial(vocab_exchange_kernel, tile, valid), out...  80.3 us
    pallas_call x2, Pallas kernels, attend_back(): pl.pallas_call(functools.partial(attend_back_kernel, parts, own, min(256,...  56.9 us
    dot_general x9, matrix products, dot_rows(): lax.dot_general(left, right, (((1,), (1,)), ((), ())), preferred_element_...  46.5 us
    dot_general x13, matrix products, dot(): return jnp.dot(left, right, preferred_element_type=F32)  45.7 us
    pallas_call x3, Pallas kernels, attend(): pl.pallas_call(functools.partial(attend_kernel, parts, own, causal), grid...  45.5 us
    pallas_call x1, Pallas kernels, reduce_over_devices(): pl.pallas_call(functools.partial(reduce_kernel, rows_dp), out_shape=[jax....  44.7 us
    gather x2, local copies, waits for them, and re-layouts, lookup(): picked = jnp.take(embedding, jnp.clip(local, 0, shard_rows - 1), axis=0)  30.3 us
  transfers between devices with their start and end apart: 8, of which 2 were waited for; matrix products, arithmetic and copies ran while one was open for 15% of the time, Pallas kernels for 30%

profile of v2, /device:TPU:25, one launch (start us, length us, event | category | flops | bytes accessed | tf_op | source)
XLA Modules:
  0.0 567.9 jit_solution(11521411154055514103)
XLA Ops:
  7.2 1.9 convert_element_type.144
  9.3 5.7 all-gather
  15.1 14.8 %gather_fusion.1 = bf16[2048,768]{1,0:T(8,128)(2,1)S(1)} fusion(bf16[8032,768]{1,0:T(8,128)(2,1)} %table_hbm.1, s32[2048]{0:T(1024)S(1)} %broadcast_clamp_fusion.1), kind=kCustom, calls=%fused_computation.1 | custom fusion | bytes 6299648 | tf_op jit(solution)/shard_map/jit(_take)/gather | solution.py:945
  30.0 2.0 select_select_fusion.1
  32.5 15.5 %gather_fusion.2 = bf16[2112,768]{1,0:T(8,128)(2,1)S(1)} fusion(bf16[8032,768]{1,0:T(8,128)(2,1)} %table_hbm.1, s32[3072]{0:T(1024)S(1)} %pad_clamp_fusion), kind=kCustom, calls=%fused_computation.2 | custom fusion | bytes 6496512 | tf_op jit(solution)/shard_map/jit(_take)/gather | solution.py:945
  48.2 2.7 select_select_fusion
  50.9 0.6 copy-done.42
  51.8 0.6 fusion.135
  52.4 0.8 copy.87.refs_5_
  53.3 1.9 sub.166.target_ref
  55.3 1.0 copy.92
  56.3 139.9 %shard_map.198 = (bf16[4,2,96,2304]{3,2,1,0:T(8,128)(2,1)}, bf16[4,2,96,2304]{3,2,1,0:T(8,128)(2,1)}, bf16[4,2,96,2304]{3,2,1,0:T(8,128)(2,1)}, bf16[4,2,96,768]...) custom-call(bf16[3,96,2304]{2,1,0:T(8,128)(2,1)} %refs_0_.1, ...), custom_call_target="tpu_custom_call" | custom-call | bytes 400000000 | tf_op jit(solution)/shard_map/pallas_call | solution.py:529
  196.6 1.8 copy.85
  198.4 0.3 reshape.423
  198.7 2.0 gather_fusion
  200.8 1.7 fusion.43
  202.5 3.4 convolution_convert_fusion.2.refs_1_.refs_3_
  206.1 3.3 convolution_convert_fusion.7.refs_0_
  209.5 0.7 slice_reduce_fusion.1
  210.2 1.7 fusion.44
  211.9 4.7 convolution_convert_fusion.1.refs_1_.refs_3_
  216.7 15.0 %shard_map.199 = bf16[512,768]{1,0:T(8,128)(2,1)} custom-call(bf16[512,768]{1,0:T(8,128)(2,1)} %convolution_convert_fusion.7.refs_0_, bf16[512,1536]{1,0:T(8,128)(2,1)} %copy-done.43, bf16[512,1536]{1,0:T(8,128)(2,1)} %collective-permute-done.refs_2_.refs_4_, bf16[512,1536]{1,0:T(8,128)(2,1)} %copy-done.43, ...), custom_call_target="tpu_custom_call" | custom-call | flops 6442450944 | bytes 2359296 | tf_op jit(solution)/shard_map/pallas_call | solution.py:108
  231.8 2.5 multiply_reduce_fusion.8
  234.3 5.3 fusion.64
  239.7 3.8 multiply_reduce_fusion.7
  243.6 0.4 copy-done.17
  244.0 2.6 convolution_convert_fusion.refs_1_.refs_3_
  246.6 0.4 collective-permute-start.2
  247.0 3.1 convolution_convert_fusion.6.refs_0_
  250.1 15.3 %shard_map.200 = bf16[512,768]{1,0:T(8,128)(2,1)} custom-call(bf16[512,768]{1,0:T(8,128)(2,1)} %convolution_convert_fusion.6.refs_0_, bf16[512,1536]{1,0:T(8,128)(2,1)} %convolution_convert_fusion.1.refs_1_.refs_3_, bf16[512,1536]{1,0:T(8,128)(2,1)} %collective-permute-done.1.refs_2_.refs_4_, bf16[512,1536]{1,0:T(8,128)(2,1)} %convolution_convert_fusion.1.refs_1_.refs_3_, ...), custom_call_target="tpu_custom_call" | custom-call | flops 6442450944 | bytes 2359296 | tf_op jit(solution)/shard_map/pallas_call | solution.py:108
  265.4 2.1 multiply_reduce_fusion.6
  267.5 3.6 convolution_convert_fusion.5.refs_0_
  271.1 15.1 %shard_map.201 = bf16[512,768]{1,0:T(8,128)(2,1)} custom-call(bf16[512,768]{1,0:T(8,128)(2,1)} %convolution_convert_fusion.5.refs_0_, bf16[512,1536]{1,0:T(8,128)(2,1)} %convolution_convert_fusion.refs_1_.refs_3_, bf16[512,1536]{1,0:T(8,128)(2,1)} %collective-permute-done.2.refs_2_.refs_4_, bf16[512,1536]{1,0:T(8,128)(2,1)} %convolution_convert_fusion.refs_1_.refs_3_, ...), custom_call_target="tpu_custom_call" | custom-call | flops 6442450944 | bytes 2359296 | tf_op jit(solution)/shard_map/pallas_call | solution.py:108
  286.2 2.7 multiply_reduce_fusion.5
  288.9 4.6 fusion.65
  293.6 3.9 multiply_reduce_fusion.4
  297.5 1.3 fusion.34
  298.8 80.3 %shard_map.202 = (f32[512,768]{1,0:T(8,128)}, f32[512,128]{1,0:T(8,128)}) custom-call(bf16[512,768]{1,0:T(8,128)(2,1)} %get-tuple-element.87.h_ref, s32[4,512,1]{2,1,0:T(8,128)} %sub.166.target_ref, bf16[8032,768]{1,0:T(8,128)(2,1)} %table_hbm.1), custom_call_target="tpu_custom_call" | custom-call | flops 51539607552 | bytes 12337152 | tf_op jit(solution)/shard_map/pallas_call | solution.py:697
  379.1 1.1 copy.91
  380.3 2.3 multiply_reduce_fusion.3
  382.6 14.5 %multiply_reduce_fusion.2 = (f32[512]{0:T(512)S(1)}, f32[512,768]{1,0:T(8,128)}) fusion(f32[512,768]{1,0:T(8,128)S(1)} %get-tuple-element.110, f32[768]{0:T(1024)S(1)} %get-tuple-element.73, f32[512]{0:T(512)S(1)} %add_rsqrt_fusion.1, bf16[768,3072]{1,0:T(8,128)(2,1)} %bitcast.81, f32[512,3072]{1,0:T(8,128)} %copy-done.5, bf16[3072,768]{1,0:T(8,128)(2,1)} %bitcast.126, ...), kind=kOutput, calls=%fused_computation.81 | convolution fusion | flops 4868800000 | bytes 22824960 | tf_op jit(solution)/shard_map/dot_general | solution.py:37
  397.1 4.8 convolution_convert_fusion.4.refs_5_
  401.9 26.4 %shard_map.203 = (f32[512,768]{1,0:T(8,128)}, f32[512,768]{1,0:T(8,128)}, f32[512,768]{1,0:T(8,128)}, f32[512,768]{1,0:T(8,128)}) custom-call(bf16[512,768]{1,0:T(8,128)(2,1)} %convolution_convert_fusion.5.refs_0_, bf16[512,1536]{1,0:T(8,128)(2,1)} %convolution_convert_fusion.refs_1_.refs_3_, bf16[512,1536]{1,0:T(8,128)(2,1)} %collective-permute-done.2.refs_2_.refs_4_, ...), custom_call_target="tpu_custom_call" | custom-call | flops 16106127360 | bytes 7864320 | tf_op jit(solution)/shard_map/pallas_call | solution.py:195
  428.3 2.3 pad_maximum_fusion
  430.9 5.4 collective-permute-done.3
  436.4 3.0 fusion.24
  439.5 2.7 multiply_reduce_fusion.1
  442.1 14.4 %multiply_reduce_fusion = (f32[512]{0:T(512)S(1)}, f32[512,768]{1,0:T(8,128)}) fusion(f32[512,768]{1,0:T(8,128)S(1)} %copy-done.7, f32[768]{0:T(1024)S(1)} %get-tuple-element.71, f32[512]{0:T(512)S(1)} %add_rsqrt_fusion.5, bf16[768,3072]{1,0:T(8,128)(2,1)} %bitcast.79, f32[512,3072]{1,0:T(8,128)} %copy-done.4, bf16[3072,768]{1,0:T(8,128)(2,1)} %bitcast.122, ...), kind=kOutput, calls=%fused_computation.76 | convolution fusion | flops 4866833920 | bytes 22031360 | tf_op jit(solution)/shard_map/dot_general | solution.py:37
  456.5 3.0 multiply_add_fusion
  459.6 1.7 convolution_convert_fusion.3.refs_5_
  461.3 30.6 %shard_map.204 = (f32[512,768]{1,0:T(8,128)}, f32[512,768]{1,0:T(8,128)}, f32[512,768]{1,0:T(8,128)}, f32[512,768]{1,0:T(8,128)}, bf16[512,768]{1,0:T(8,128)(2,1)}) custom-call(bf16[512,768]{1,0:T(8,128)(2,1)} %convolution_convert_fusion.7.refs_0_, bf16[512,1536]{1,0:T(8,128)(2,1)} %copy-done.43, bf16[512,1536]{1,0:T(8,128)(2,1)} %collective-permute-done.refs_2_.refs_4_, ...), custom_call_target="tpu_custom_call" | custom-call | flops 16106127360 | bytes 7864320 | tf_op jit(solution)/shard_map/pallas_call | solution.py:195
  491.9 2.3 pad_maximum_fusion.1
  494.6 0.6 select_maximum_fusion.stat_ref
  495.3 4.7 collective-permute-done.4
  500.0 2.9 fusion.31
  503.0 1.4 fusion.29
  504.4 1.0 fusion.39
  505.5 1.0 fusion.92
  506.5 2.1 convolution_add_fusion.1.table_ref
  508.6 44.7 %shard_map.205 = (f32[8,192,128]{2,1,0:T(8,128)}, f32[8,128]{1,0:T(8,128)}, f32[8,128]{1,0:T(8,128)}) custom-call(s32[2,3]{1,0:T(2,128)} %bitcast.121, f32[768,384]{1,0:T(8,128)} %convolution_add_fusion.1.table_ref, f32[8,128]{1,0:T(8,128)} %select_maximum_fusion.stat_ref), custom_call_target="tpu_custom_call" | custom-call | tf_op jit(solution)/shard_map/pallas_call | solution.py:868
  553.3 1.4 fusion.109
  554.7 1.3 slice_reduce_fusion
  556.7 1.5 multiply_reduce_fusion.9
  558.4 1.6 add_subtract_fusion
  (180 shorter events, 3.0 us)
Async XLA Ops:
  7.2 2.1 copy-start.38
  7.2 2.1 copy-start.39
  7.2 2.1 copy-start.40
  7.2 189.4 %all-gather.3.cloned.1.call-start = ((), (), s32[]{:S(2)}) async-start(), calls=%async_computation.2 | async-start | bytes 1966080 | tf_op jit(solution)/shard_map/all_gather | solution.py:951
  9.2 191.5 %reduce-scatter.3.cloned.1.call-start = ((), (), s32[]{:S(2)}) async-start(), calls=%async_computation.3 | async-start | bytes 3932160 | tf_op jit(solution)/shard_map/reduce_scatter | solution.py:948
  32.0 177.5 %reduce-scatter.5.cloned.1.call-start = ((), (), s32[]{:S(2)}) async-start(), calls=%async_computation.4 | async-start | bytes 4055040 | tf_op jit(solution)/shard_map/reduce_scatter | solution.py:949
  50.9 0.7 copy-start.42
  55.3 141.0 %copy-start.26 = (s32[2,1024]{1,0:T(2,128)}, s32[2,1024]{1,0:T(2,128)S(1)}, u32[]{:S(2)}) copy-start(s32[2,1024]{1,0:T(2,128)S(1)} %pad_add_fusion.refs_6_) | copy-start | bytes 24580
  56.3 139.9 %copy-start.41 = (s32[2,1,3]{2,1,0:T(1,128)S(1)}, s32[2,1,3]{2,1,0:T(1,128)}, u32[]{:S(2)}) copy-start(s32[2,1,3]{2,1,0:T(1,128)} %param.21) | copy-start | bytes 76
  56.3 140.1 %copy-start.29 = (f32[7,768]{1,0:T(8,128)S(1)}, f32[7,768]{1,0:T(8,128)}, u32[]{:S(2)}) copy-start(f32[7,768]{1,0:T(8,128)} %param.27) | copy-start | bytes 64516
  196.4 2.3 copy-start.27
  196.5 9.6 %copy-start.30 = (f32[768]{0:T(1024)}, f32[768]{0:T(1024)S(1)}, u32[]{:S(2)}) copy-start(f32[768]{0:T(1024)S(1)} %get-tuple-element.72) | copy-start | bytes 9220
  196.5 4.2 copy-start.35
  202.5 29.3 %copy-start = (bf16[512,768]{1,0:T(8,128)(2,1)}, bf16[512,768]{1,0:T(8,128)(2,1)S(1)}, u32[]{:S(2)}) copy-start(bf16[512,768]{1,0:T(8,128)(2,1)S(1)} %get-tuple-element.89) | copy-start | bytes 2359300
  202.5 3.6 copy-start.23
  205.9 3.6 copy-start.43
  205.9 10.8 %collective-permute-start = (bf16[512,1536]{1,0:T(8,128)(2,1)S(1)}, bf16[512,1536]{1,0:T(8,128)(2,1)}, u32[]{:S(2)}, u32[]{:S(2)}) collective-permute-start(bf16[512,1536]{1,0:T(8,128)(2,1)S(1)} %convolution_convert_fusion.2.refs_1_.refs_3_), channel_id=1, source_target_pairs={{0,1},{1,0},{2,3},{3,2},{4,5},{5,4},{6,7},{7,6},{8,9},{9,8},{10,11... | collective-permute-start | bytes 4718600 | tf_op jit(solution)/shard_map/ppermute | solution.py:931
  216.6 33.5 %collective-permute-start.1 = (bf16[512,1536]{1,0:T(8,128)(2,1)}, bf16[512,1536]{1,0:T(8,128)(2,1)}, u32[]{:S(2)}, u32[]{:S(2)}) collective-permute-start(bf16[512,1536]{1,0:T(8,128)(2,1)} %convolution_convert_fusion.1.refs_1_.refs_3_), channel_id=1, source_target_pairs={{0,1},{1,0},{2,3},{3,2},{4,5},{5,4},{6,7},{7,6},{8,9},{9,8},{10,11... | collective-permute-start | bytes 4718600 | tf_op jit(solution)/shard_map/ppermute | solution.py:931
  231.7 7.9 %slice-start = ((s8[4718592]{0:T(1024)(128)(4,1)}), s8[4194304]{0:T(1024)(128)(4,1)S(1)}, s32[]{:S(2)}) async-start(s8[4718592]{0:T(1024)(128)(4,1)} %bitcast.123), calls=%async_computation.5 | async-start | bytes 8388608
  234.3 5.4 copy-start.6
  234.3 5.4 slice-start.1
  239.7 3.9 copy-start.4
  239.7 4.2 copy-start.17
  243.6 3.0 copy-start.8
  244.0 3.0 copy-start.2
  246.6 24.5 %collective-permute-start.2 = (bf16[512,1536]{1,0:T(8,128)(2,1)}, bf16[512,1536]{1,0:T(8,128)(2,1)}, u32[]{:S(2)}, u32[]{:S(2)}) collective-permute-start(bf16[512,1536]{1,0:T(8,128)(2,1)} %convolution_convert_fusion.refs_1_.refs_3_), channel_id=1, source_target_pairs={{0,1},{1,0},{2,3},{3,2},{4,5},{5,4},{6,7},{7,6},{8,9},{9,8},{10,11... | collective-permute-start | bytes 4718600 | tf_op jit(solution)/shard_map/ppermute | solution.py:931
  250.1 15.3 %copy-start.45 = (bf16[4,2,96,768]{3,2,1,0:T(8,128)(2,1)S(1)}, bf16[4,2,96,768]{3,2,1,0:T(8,128)(2,1)}, u32[]{:S(2)}) copy-start(bf16[4,2,96,768]{3,2,1,0:T(8,128)(2,1)} %get-tuple-element.48) | copy-start | bytes 3538948
  267.5 3.6 copy-start.16
  271.1 15.1 %copy-start.10 = (bf16[4,2,96,768]{3,2,1,0:T(8,128)(2,1)S(1)}, bf16[4,2,96,768]{3,2,1,0:T(8,128)(2,1)}, u32[]{:S(2)}) copy-start(bf16[4,2,96,768]{3,2,1,0:T(8,128)(2,1)} %get-tuple-element.50) | copy-start | bytes 3538948
  286.2 7.3 %slice-start.2 = ((s8[4718592]{0:T(1024)(128)(4,1)}), s8[4194304]{0:T(1024)(128)(4,1)S(1)}, s32[]{:S(2)}) async-start(s8[4718592]{0:T(1024)(128)(4,1)} %bitcast.127), calls=%async_computation.7 | async-start | bytes 8388608
  288.9 4.7 slice-start.3
  293.5 3.9 copy-start.5
  293.6 3.9 copy-start.3
  428.3 8.1 %copy-start.18 = (bf16[4,2,96,2304]{3,2,1,0:T(8,128)(2,1)S(1)}, bf16[4,2,96,2304]{3,2,1,0:T(8,128)(2,1)}, u32[]{:S(2)}) copy-start(bf16[4,2,96,2304]{3,2,1,0:T(8,128)(2,1)} %get-tuple-element.49) | copy-start | bytes 10616836
  428.3 8.1 %copy-start.19 = (f32[512,768]{1,0:T(8,128)S(1)}, f32[512,768]{1,0:T(8,128)}, u32[]{:S(2)}) copy-start(f32[512,768]{1,0:T(8,128)} %get-tuple-element.55) | copy-start | bytes 4718596
  430.6 5.7 %collective-permute-start.3 = (f32[512,1536]{1,0:T(8,128)S(1)}, f32[512,1536]{1,0:T(8,128)S(1)}, u32[]{:S(2)}, u32[]{:S(2)}) collective-permute-start(f32[512,1536]{1,0:T(8,128)S(1)} %pad_maximum_fusion), channel_id=1, source_target_pairs={{0,1},{1,0},{2,3},{3,2},{4,5},{5,4},{6,7},{7,6},{8,9},{9,8},{10,11... | collective-permute-start | bytes 9437192 | tf_op jit(solution)/shard_map/ppermute | solution.py:931
  436.4 3.1 copy-start.9
  436.4 3.1 copy-start.20
  439.4 2.7 copy-start.7
  456.5 3.1 copy-start.44
  491.9 2.6 copy-start.28
  491.9 8.1 %copy-start.11 = (bf16[4,2,96,2304]{3,2,1,0:T(8,128)(2,1)S(1)}, bf16[4,2,96,2304]{3,2,1,0:T(8,128)(2,1)}, u32[]{:S(2)}) copy-start(bf16[4,2,96,2304]{3,2,1,0:T(8,128)(2,1)} %get-tuple-element.43) | copy-start | bytes 10616836
  491.9 8.1 %copy-start.14 = (f32[512,768]{1,0:T(8,128)S(1)}, f32[512,768]{1,0:T(8,128)}, u32[]{:S(2)}) copy-start(f32[512,768]{1,0:T(8,128)} %get-tuple-element.59) | copy-start | bytes 4718596
  494.2 5.7 %collective-permute-start.4 = (f32[512,1536]{1,0:T(8,128)S(1)}, f32[512,1536]{1,0:T(8,128)S(1)}, u32[]{:S(2)}, u32[]{:S(2)}) collective-permute-start(f32[512,1536]{1,0:T(8,128)S(1)} %pad_maximum_fusion.1), channel_id=1, source_target_pairs={{0,1},{1,0},{2,3},{3,2},{4,5},{5,4},{6,7},{7,6},{8,9},{9,8},{10,11... | collective-permute-start | bytes 9437192 | tf_op jit(solution)/shard_map/ppermute | solution.py:931
  500.0 3.0 copy-start.15
  502.9 1.5 copy-start.1
  502.9 1.5 copy-start.22
  502.9 1.5 copy-start.24
  502.9 1.5 copy-start.31
  504.4 1.0 copy-start.36
  508.6 49.6 %copy-start.37 = (f32[8,100]{1,0:T(8,128)S(1)}, f32[8,100]{1,0:T(8,128)}, u32[]{:S(2)}) copy-start(f32[8,100]{1,0:T(8,128)} %param.30) | copy-start | bytes 9604
  508.6 49.8 %copy-start.34 = (f32[8,192]{1,0:T(8,128)S(1)}, f32[8,192]{1,0:T(8,128)}, u32[]{:S(2)}) copy-start(f32[8,192]{1,0:T(8,128)} %param.31) | copy-start | bytes 18436
  508.6 49.8 %copy-start.12 = (f32[8,100,192]{1,2,0:T(8,128)S(1)}, f32[8,100,192]{1,2,0:T(8,128)}, u32[]{:S(2)}) copy-start(f32[8,100,192]{1,2,0:T(8,128)} %param.28) | copy-start | bytes 1843204
  508.6 49.8 %copy-start.21 = (f32[8,100,192]{1,2,0:T(8,128)S(1)}, f32[8,100,192]{1,2,0:T(8,128)}, u32[]{:S(2)}) copy-start(f32[8,100,192]{1,2,0:T(8,128)} %param.29) | copy-start | bytes 1843204
  553.3 4.9 copy-start.33
  558.2 1.8 copy-start.13
  558.4 1.7 copy-start.32
  558.4 1.6 copy-start.25
Sparse Core Ops, SparseCore 0:
  10.2 21.0 all-gather.2
  33.8 42.5 reduce-scatter.2
  79.1 52.4 reduce-scatter.4

commit v3 on v2

--- a/solution.py
+++ b/solution.py
@@ -13,8 +13,9 @@
 STEP = 5
 HALO = 16
 LANES = 128
+SEGS = 3
 VOCAB_BLOCK = 1024
-VMEM_LIMIT = 60 * 1024 * 1024
+MIB = 1024 * 1024
 
 NORM_EPS = 1e-06
 CLIP_NORM = 2e-05
@@ -71,146 +72,239 @@
     return jnp.sum(jnp.where(hits, amounts[:, None], 0.0), 0)
 
 
-def attend_kernel(parts, own, causal, *refs):
-    q_ref, k_refs, v_refs = refs[0], refs[1 : 1 + parts], refs[1 + parts : 1 + 2 * parts]
-    q_info, k_info, out_ref, bias_ref = refs[1 + 2 * parts :]
-
-    @pl.when(pl.program_id(0) == 0)
-    def _():
-        keep = q_info[:, 0:1] == k_info[0:1, :]
-        if causal:
-            keep = keep & (q_info[:, 1:2] >= k_info[1:2, :])
-        bias_ref[...] = jnp.where(keep, 0.0, MASKED)
-
-    low_half = lax.broadcasted_iota(jnp.int32, (own, LANES), 1) < DH
-    queries = q_ref[...].astype(F32) * DH ** (-0.5)
-    mixed = []
-    for head in range(LANES // DH):
-        query = jnp.where(low_half == (head == 0), queries, 0.0).astype(BF16)
-        scores = [
-            dot_rows(query, k_refs[k][...]) + bias_ref[:, k * own : (k + 1) * own]
-            for k in range(parts)
-        ]
-        maxima = functools.reduce(jnp.maximum, [jnp.max(s, -1, keepdims=True) for s in scores])
-        powers = [jnp.exp(s - maxima) for s in scores]
-        total = sum(jnp.sum(p, -1, keepdims=True) for p in powers)
-        value = sum(dot(p.astype(BF16), v_refs[k][...]) for k, p in enumerate(powers))
-        mixed.append(value / total)
-    out_ref[...] = jnp.where(low_half, mixed[0], mixed[1]).astype(BF16)
-
-
-def attend(queries, pairs, q_info, k_info, causal):
-    own, width = queries.shape
-    parts, length = len(pairs), k_info.shape[1]
-    steps = width // LANES
-    key_spec = pl.BlockSpec((own, LANES), lambda i: (0, i))
-    value_spec = pl.BlockSpec((own, LANES), lambda i: (0, steps + i))
-    return pl.pallas_call(
-        functools.partial(attend_kernel, parts, own, causal),
-        grid=(steps,),
-        out_shape=jax.ShapeDtypeStruct((own, width), BF16),
-        in_specs=[key_spec]
-        + [key_spec] * parts
-        + [value_spec] * parts
-        + [
-            pl.BlockSpec(q_info.shape, lambda i: (0, 0)),
-            pl.BlockSpec(k_info.shape, lambda i: (0, 0)),
-        ],
-        out_specs=key_spec,
-        scratch_shapes=[pltpu.VMEM((own, length), F32)],
-        compiler_params=pltpu.CompilerParams(vmem_limit_bytes=VMEM_LIMIT),
-        cost_estimate=pl.CostEstimate(
-            flops=16 * own * length * width, bytes_accessed=6 * own * width, transcendentals=0
-        ),
-    )(queries, *pairs, *pairs, q_info, k_info)
-
-
-def attend_back_kernel(parts, own, block, want_queries, *refs):
-    q_ref, k_refs, v_refs = refs[0], refs[1 : 1 + parts], refs[1 + parts : 1 + 2 * parts]
-    grad_ref, q_info, k_info = refs[1 + 2 * parts : 4 + 2 * parts]
-    rest = refs[4 + 2 * parts :]
-    dk_refs, dv_refs = rest[:parts], rest[parts : 2 * parts]
-    dq_ref = rest[2 * parts] if want_queries else None
-    bias_ref = rest[-1]
-
-    @pl.when(pl.program_id(0) == 0)
-    def _():
-        bias_ref[...] = jnp.where(k_info[:, 0:1] == q_info[0:1, :], 0.0, MASKED)
-
-    low_half = lax.broadcasted_iota(jnp.int32, (block, LANES), 1) < DH
-
-    def rows(at, first):
-        here = pl.ds(pl.multiple_of(at * block, block), block)
-        queries = q_ref[here, :].astype(F32) * DH ** (-0.5)
-        gradient = grad_ref[here, :].astype(F32)
-        dk = [None] * parts
-        dv = [None] * parts
-        dq = []
-        for head in range(LANES // DH):
-            mask = low_half == (head == 0)
-            query = jnp.where(mask, queries, 0.0).astype(BF16)
-            grad = jnp.where(mask, gradient, 0.0).astype(BF16)
-            scores = [
-                dot_rows(k_refs[k][...], query) + bias_ref[k * own : (k + 1) * own, here]
-                for k in range(parts)
-            ]
-            maxima = functools.reduce(jnp.maximum, [jnp.max(s, 0, keepdims=True) for s in scores])
-            powers = [jnp.exp(s - maxima) for s in scores]
-            inverse = 1.0 / sum(jnp.sum(p, 0, keepdims=True) for p in powers)
-            weights = [p * inverse for p in powers]
-            weight_grads = [dot_rows(v_refs[k][...], grad) for k in range(parts)]
-            delta = sum(
-                jnp.sum(w * dw, 0, keepdims=True) for w, dw in zip(weights, weight_grads)
-            )
-            score_grads = [
-                (w * (dw - delta)).astype(BF16) for w, dw in zip(weights, weight_grads)
-            ]
-            for k in range(parts):
-                key_term = dot(score_grads[k], query)
-                value_term = dot(weights[k].astype(BF16), grad)
-                dk[k] = key_term if head == 0 else dk[k] + key_term
-                dv[k] = value_term if head == 0 else dv[k] + value_term
-            if want_queries:
-                dq.append(sum(dot_columns(score_grads[k], k_refs[k][...]) for k in range(parts)))
+def pair_lanes(pair, first=0):
+    return pl.ds(pl.multiple_of(first + pair * LANES, LANES), LANES)
+
+
+def head_mask(shape, head, axis=1):
+    return (lax.broadcasted_iota(jnp.int32, shape, axis) < DH) == (head == 0)
+
+
+def segment_columns(segment, is_key, shape):
+    column = lax.rem(lax.broadcasted_iota(jnp.int32, shape, 1), DH)
+    if is_key:
+        return jnp.where((column < SEGS) & (column != segment), MASKED, 0.0).astype(BF16)
+    return jnp.where(column == segment, 1.0, 0.0).astype(BF16)
+
+
+def head_part(values, rest, head):
+    return jnp.where(head_mask(values.shape, head), values, rest)
+
+
+def over_heads(pairs, scores, soften, mix):
+    scores(0, 0)
+    scores(0, 1)
+    soften(0, 0)
+
+    def step(pair, _):
+        scores(pair + 1, 0)
+        soften(pair, 1)
+        mix(pair, 0)
+        scores(pair + 1, 1)
+        soften(pair + 1, 0)
+        mix(pair, 1)
+        return 0
+
+    lax.fori_loop(0, pairs - 1, step, 0)
+    soften(pairs - 1, 1)
+    mix(pairs - 1, 0)
+    mix(pairs - 1, 1)
+
+
+def attend_kernel(parts, causal, *refs):
+    q_ref, pair_refs = refs[0], refs[1 : 1 + parts]
+    residual_ref, weight_ref, q_info, k_info, k_rows, out_ref, mixed_ref, log_ref = refs[
+        1 + parts : 9 + parts
+    ]
+    bias_ref, q_mark, k_mark, low_ref, scores_a, scores_b, powers_a, powers_b = refs[9 + parts :]
+    width = q_ref.shape[1]
+    own = pair_refs[0].shape[0]
+    scores_of, powers_of = (scores_a, scores_b), (powers_a, powers_b)
+    rows = [slice(k * own, (k + 1) * own) for k in range(parts)]
+    q_mark[...] = segment_columns(q_info[:, 0:1], False, q_mark.shape)
+    k_mark[...] = segment_columns(k_info[:, 0:1], True, k_mark.shape)
+    if causal:
+        bias_ref[...] = jnp.where(q_info[:, 1:2] >= k_rows[...], 0.0, MASKED)
+    log_ref[...] = jnp.zeros_like(log_ref)
+    lane = lax.broadcasted_iota(jnp.int32, log_ref.shape, 1)
+
+    def scores(pair, head):
+        query = q_ref[:, pair_lanes(pair)] * jnp.asarray(DH ** (-0.5), BF16)
+        query = head_part(query, q_mark[...], head)
         for k in range(parts):
-            dk_refs[k][...] = dk[k] if first else dk_refs[k][...] + dk[k]
-            dv_refs[k][...] = dv[k] if first else dv_refs[k][...] + dv[k]
-        if want_queries:
-            dq_ref[here, :] = (jnp.where(low_half, dq[0], dq[1]) * DH ** (-0.5)).astype(BF16)
-
-    rows(0, True)
-    if own > block:
-        lax.fori_loop(1, own // block, lambda at, _: (rows(at, False), 0)[1], 0)
-
-
-def attend_back(queries, pairs, gradient, q_info, k_info, want_queries):
+            keys = head_part(pair_refs[k][:, pair_lanes(pair)], k_mark[rows[k], :], head)
+            values = dot_rows(query, keys)
+            if causal:
+                values = values + bias_ref[:, rows[k]]
+            scores_of[head][:, rows[k]] = values
+
+    def soften(pair, head):
+        values = scores_of[head][...]
+        highest = jnp.max(values, -1, keepdims=True)
+        powers_of[head][...] = jnp.exp(values - highest).astype(BF16)
+        log_ref[...] += jnp.where(lane == 2 * pair + head, highest, 0.0)
+
+    def mix(pair, head):
+        value = None
+        for k in range(parts):
+            values = pair_refs[k][:, pair_lanes(pair, width)]
+            values = head_part(values, jnp.ones_like(values), head)
+            term = dot(powers_of[head][:, rows[k]], values)
+            value = term if value is None else value + term
+        total = value[:, LANES - 1 :] if head == 0 else value[:, :1]
+        value = value / total
+        log_ref[...] += jnp.where(lane == 2 * pair + head, jnp.log(total), 0.0)
+        lanes = pair_lanes(pair)
+        if head:
+            value = jnp.where(head_mask(value.shape, 0), mixed_ref[:, lanes], value)
+        mixed_ref[:, lanes] = value
+        if head:
+            low_ref[:, lanes] = value.astype(BF16)
+
+    over_heads(width // LANES, scores, soften, mix)
+    out_ref[...] = residual_ref[...] + dot(low_ref[...], weight_ref[...])
+
+
+def attend(queries, pairs, residual, weight, q_info, k_info, causal):
     own, width = queries.shape
     parts, length = len(pairs), k_info.shape[0]
-    steps = width // LANES
-    key_spec = pl.BlockSpec((own, LANES), lambda i: (0, i))
-    value_spec = pl.BlockSpec((own, LANES), lambda i: (0, steps + i))
-    shapes = [jax.ShapeDtypeStruct((own, width), F32)] * (2 * parts)
+    vmem = pl.BlockSpec(memory_space=pltpu.VMEM)
+    return pl.pallas_call(
+        functools.partial(attend_kernel, parts, causal),
+        out_shape=[
+            jax.ShapeDtypeStruct((own, width), F32),
+            jax.ShapeDtypeStruct((own, width), F32),
+            jax.ShapeDtypeStruct((own, LANES), F32),
+        ],
+        in_specs=[vmem] * (parts + 6),
+        out_specs=[vmem] * 3,
+        scratch_shapes=[
+            pltpu.VMEM((own, length), F32),
+            pltpu.VMEM((own, LANES), BF16),
+            pltpu.VMEM((length, LANES), BF16),
+            pltpu.VMEM((own, width), BF16),
+            pltpu.VMEM((own, length), F32),
+            pltpu.VMEM((own, length), F32),
+            pltpu.VMEM((own, length), BF16),
+            pltpu.VMEM((own, length), BF16),
+        ],
+        compiler_params=pltpu.CompilerParams(vmem_limit_bytes=26 * MIB),
+        cost_estimate=pl.CostEstimate(
+            flops=10 * own * length * width, bytes_accessed=6 * own * width, transcendentals=0
+        ),
+    )(queries, *pairs, residual, weight, q_info, k_info, k_info[:, 1:].T)
+
+
+def attend_back_kernel(parts, want_queries, *refs):
+    q_ref, pair_refs = refs[0], refs[1 : 1 + parts]
+    grad_ref, weight_ref, mixed_ref, log_ref, q_info, k_info = refs[1 + parts : 7 + parts]
+    rest = refs[7 + parts :]
+    out_refs = rest[:parts]
+    dq_ref = rest[parts] if want_queries else None
+    q_mark, k_mark, low_ref, delta_ref, *rest = rest[parts + want_queries :]
+    scores_of, grads_of, weights_of, steps_of = rest[0:2], rest[2:4], rest[4:6], rest[6:8]
+    width = q_ref.shape[1]
+    own = pair_refs[0].shape[0]
+    rows = [slice(k * own, (k + 1) * own) for k in range(parts)]
+    scale = jnp.asarray(DH ** (-0.5), BF16)
+    q_mark[...] = segment_columns(q_info[:, 0:1], False, q_mark.shape)
+    k_mark[...] = segment_columns(k_info[:, 0:1], True, k_mark.shape)
+    low_ref[...] = dot_rows(grad_ref[...].astype(BF16), weight_ref[...]).astype(BF16)
+    product = low_ref[...].astype(F32) * mixed_ref[...]
+    high = product.astype(BF16)
+    shape = (2 * 8, width)
+    belongs = lax.broadcasted_iota(jnp.int32, shape, 1) // DH == lax.broadcasted_iota(
+        jnp.int32, shape, 0
+    )
+    belongs = jnp.where(belongs, 1.0, 0.0).astype(BF16)
+    delta_ref[...] = dot_rows(belongs, high) + dot_rows(
+        belongs, (product - high.astype(F32)).astype(BF16)
+    )
+
+    def scores(pair, head):
+        query = head_part(q_ref[:, pair_lanes(pair)] * scale, q_mark[...], head)
+        grad = low_ref[:, pair_lanes(pair)]
+        grad = head_part(grad, jnp.zeros_like(grad), head)
+        for k in range(parts):
+            keys = head_part(pair_refs[k][:, pair_lanes(pair)], k_mark[rows[k], :], head)
+            scores_of[head][rows[k], :] = dot_rows(keys, query)
+            grads_of[head][rows[k], :] = dot_rows(pair_refs[k][:, pair_lanes(pair, width)], grad)
+
+    def soften(pair, head):
+        at = pl.ds(2 * pair + head, 1)
+        weights = jnp.exp(scores_of[head][...] - log_ref[at, :])
+        weights_of[head][...] = weights.astype(BF16)
+        steps_of[head][...] = (weights * (grads_of[head][...] - delta_ref[at, :])).astype(BF16)
+
+    def mix(pair, head):
+        keys, values = pair_lanes(pair), pair_lanes(pair, width)
+        query, grad = q_ref[:, keys] * scale, low_ref[:, keys]
+        query = head_part(query, jnp.zeros_like(query), head)
+        grad = head_part(grad, jnp.zeros_like(grad), head)
+        dq = None
+        for k in range(parts):
+            step = steps_of[head][rows[k], :]
+            dk = dot(step, query)
+            dv = dot(weights_of[head][rows[k], :], grad)
+            out_refs[k][:, keys] = dk if head == 0 else out_refs[k][:, keys] + dk
+            out_refs[k][:, values] = dv if head == 0 else out_refs[k][:, values] + dv
+            if want_queries:
+                term = dot_columns(pair_refs[k][:, keys], step)
+                dq = term if dq is None else dq + term
+        if want_queries:
+            here = pl.ds(pl.multiple_of(pair * LANES, LANES), LANES)
+            dq = (dq * DH ** (-0.5)).astype(BF16)
+            if head:
+                dq = jnp.where(head_mask(dq.shape, 0, 0), dq_ref[here, :], dq)
+            dq_ref[here, :] = dq
+
+    over_heads(width // LANES, scores, soften, mix)
+
+
+def attend_back(queries, pairs, gradient, weight, mixed, logs, q_info, k_info, want_queries):
+    own, width = queries.shape
+    parts, length = len(pairs), k_info.shape[0]
+    shapes = [jax.ShapeDtypeStruct(pair.shape, F32) for pair in pairs]
     if want_queries:
-        shapes.append(jax.ShapeDtypeStruct((own, width), BF16))
+        shapes.append(jax.ShapeDtypeStruct((width, own), BF16))
     return pl.pallas_call(
-        functools.partial(attend_back_kernel, parts, own, min(256, own), want_queries),
-        grid=(steps,),
+        functools.partial(attend_back_kernel, parts, want_queries),
         out_shape=shapes,
-        in_specs=[key_spec]
-        + [key_spec] * parts
-        + [value_spec] * parts
-        + [
-            key_spec,
-            pl.BlockSpec(q_info.shape, lambda i: (0, 0)),
-            pl.BlockSpec(k_info.shape, lambda i: (0, 0)),
-        ],
-        out_specs=[key_spec] * len(shapes),
-        scratch_shapes=[pltpu.VMEM((length, own), F32)],
-        compiler_params=pltpu.CompilerParams(vmem_limit_bytes=VMEM_LIMIT),
+        in_specs=[pl.BlockSpec(memory_space=pltpu.VMEM)] * (parts + 7),
+        out_specs=[pl.BlockSpec(memory_space=pltpu.VMEM)] * len(shapes),
+        scratch_shapes=[
+            pltpu.VMEM((own, LANES), BF16),
+            pltpu.VMEM((length, LANES), BF16),
+            pltpu.VMEM((own, width), BF16),
+            pltpu.VMEM((16, own), F32),
+        ]
+        + [pltpu.VMEM((length, own), F32)] * 4
+        + [pltpu.VMEM((length, own), BF16)] * 4,
+        compiler_params=pltpu.CompilerParams(vmem_limit_bytes=34 * MIB),
         cost_estimate=pl.CostEstimate(
-            flops=40 * own * length * width, bytes_accessed=20 * own * width, transcendentals=0
+            flops=20 * own * length * width, bytes_accessed=20 * own * width, transcendentals=0
         ),
-    )(queries, *pairs, *pairs, gradient, q_info, k_info)
+    )(queries, *pairs, gradient, weight, mixed, logs.T[:16], q_info, k_info)
+
+
+def feed(rows, gain, weights_one, weights_two):
+    values, inverse = normed(rows, gain)
+    source = values.astype(BF16)
+    before = [dot(source, one) for one in weights_one]
+    for pre, two in zip(before, weights_two):
+        rows = rows + dot(smooth(pre).astype(BF16), two)
+    return rows, (before, inverse)
+
+
+def feed_back(gradient, rows, gain, kept, weights_one, weights_two):
+    before, inverse = kept
+    low = gradient.astype(BF16)
+    total = 0.0
+    for pre, one, two in zip(before, weights_one, weights_two):
+        active_grad = dot_rows(low, two)
+        step = jax.vjp(smooth, pre)[1](active_grad)[0].astype(BF16)
+        total = total + dot_rows(step, one)
+    return gradient + normed_back(rows, gain, inverse, total)
 
 
 def vocab_kernel(tile, valid, h_ref, target_ref, table_hbm, grad_ref, stat_ref, table, sem):
@@ -274,7 +368,7 @@
             pl.BlockSpec((rows, LANES), lambda i: (i, 0)),
         ],
         scratch_shapes=[pltpu.VMEM((padded, width), BF16), pltpu.SemaphoreType.DMA],
-        compiler_params=pltpu.CompilerParams(vmem_limit_bytes=VMEM_LIMIT),
+        compiler_params=pltpu.CompilerParams(vmem_limit_bytes=56 * MIB),
         cost_estimate=pl.CostEstimate(
             flops=4 * count * padded * width, bytes_accessed=2 * valid * width, transcendentals=0
         ),
@@ -536,7 +630,9 @@
             pltpu.SemaphoreType.DMA((copies,)),
             pltpu.SemaphoreType.DMA((14,)),
         ],
-        compiler_params=pltpu.CompilerParams(collective_id=0, has_side_effects=True),
+        compiler_params=pltpu.CompilerParams(
+            collective_id=0, has_side_effects=True, vmem_limit_bytes=60 * MIB
+        ),
         cost_estimate=pl.CostEstimate(flops=0, bytes_accessed=400_000_000, transcendentals=0),
     )(attend_in, attend_out, expand_weights, reduce_weights)
     return [o.reshape(-1, o.shape[-1]) for o in outs]
@@ -544,18 +640,21 @@
 
 def whole_weights(attend_in, attend_out, expand_weights, reduce_weights):
     tensors = (attend_in, attend_out, expand_weights, reduce_weights)
-    if lax.axis_size("dp") == 8 and lax.axis_size("vocab") == 4:
-        flat = gather_weights(*tensors)
-        return flat[:3], flat[3:6], flat[6:8], flat[8:]
-    return tuple(lax.all_gather(tensor, "dp", axis=1, tiled=True) for tensor in tensors)
-
-
-def vocab_exchange_kernel(tile, valid, h_ref, target_ref, table_hbm, grad_ref, stat_ref, *scratch):
-    table, held, logits_a, logits_b, powers_a, powers_b, scale_a, scale_b = scratch[:8]
-    maxima_ref, total_ref, parcel, arrived, send_sem, recv_sem, table_sem = scratch[8:]
+    shards = lax.axis_size("dp")
+    if shards != 8 or lax.axis_size("vocab") != 4:
+        whole = [lax.all_gather(tensor, "dp", axis=1, tiled=True) for tensor in tensors]
+        return (whole[0], whole[1], whole[2][:, None], whole[3][:, None])
+    flat = gather_weights(*tensors)
+    return flat[:3], flat[3:6], [[w] for w in flat[6:8]], [[w] for w in flat[8:]]
+
+
+def vocab_exchange_kernel(tile, h_ref, target_ref, table_ref, grad_ref, stat_ref, *scratch):
+    tail, held, logits_a, logits_b, powers_a, powers_b, scale_a, scale_b = scratch[:8]
+    maxima_ref, total_ref, parcel, arrived, send_sem, recv_sem = scratch[8:]
     rows, width = h_ref.shape
-    padded = table.shape[0]
-    tiles = padded // tile
+    valid = table_ref.shape[0]
+    tiles = (valid + tile - 1) // tile
+    padded = tiles * tile
     v = lax.axis_index("vocab")
     x, core = v // 2, lax.rem(v, 2)
     twin, across, diagonal = x * 2 + 1 - core, (1 - x) * 2 + core, (1 - x) * 2 + 1 - core
@@ -588,22 +687,11 @@
     to_across.start()
     held[3] = h_ref[...]
 
-    sizes = [min(tile, valid - k * tile) for k in range(tiles)]
-    loads = [
-        pltpu.make_async_copy(
-            table_hbm.at[pl.ds(k * tile, size), :],
-            table.at[pl.ds(k * tile, size), :],
-            table_sem.at[k],
-        )
-        for k, size in enumerate(sizes)
-    ]
-    for load in loads:
-        load.start()
-    if padded > valid:
-        table[valid:, :] = jnp.zeros((padded - valid, width), BF16)
+    short = padded - valid
+    if short:
+        tail[: tile - short, :] = table_ref[padded - tile :, :]
+        tail[tile - short :, :] = jnp.zeros((short, width), BF16)
     to_twin.wait_recv()
-    for load in loads:
-        load.wait()
 
     logits_of, powers_of, scale_of = (logits_a, logits_b), (powers_a, powers_b), (scale_a, scale_b)
     column = lax.broadcasted_iota(jnp.int32, (rows, tile), 1)
@@ -622,7 +710,9 @@
         owner = jnp.where(k == 0, twin, jnp.where(k == 1, across, jnp.where(k == 2, diagonal, v)))
 
         def part(at):
-            return table[at * tile : (at + 1) * tile, :]
+            if short and at == tiles - 1:
+                return tail[...]
+            return table_ref[at * tile : (at + 1) * tile, :]
 
         def scores(at):
             logits_of[at % 2][...] = dot_rows(held[k], part(at))
@@ -695,15 +785,15 @@
     padded = (valid + tile - 1) // tile * tile
     vmem = pl.BlockSpec(memory_space=pltpu.VMEM)
     return pl.pallas_call(
-        functools.partial(vocab_exchange_kernel, tile, valid),
+        functools.partial(vocab_exchange_kernel, tile),
         out_shape=[
             jax.ShapeDtypeStruct((rows, width), F32),
             jax.ShapeDtypeStruct((rows, LANES), F32),
         ],
-        in_specs=[vmem, vmem, pl.BlockSpec(memory_space=pl.ANY)],
+        in_specs=[vmem, vmem, vmem],
         out_specs=[vmem, vmem],
         scratch_shapes=[
-            pltpu.VMEM((padded, width), BF16),
+            pltpu.VMEM((tile, width), BF16),
             pltpu.VMEM((4, rows, width), BF16),
             pltpu.VMEM((rows, tile), F32),
             pltpu.VMEM((rows, tile), F32),
@@ -717,10 +807,9 @@
             pltpu.VMEM((3, rows, width + LANES), BF16),
             pltpu.SemaphoreType.DMA((6,)),
             pltpu.SemaphoreType.DMA((6,)),
-            pltpu.SemaphoreType.DMA((padded // tile,)),
         ],
         compiler_params=pltpu.CompilerParams(
-            collective_id=1, has_side_effects=True, vmem_limit_bytes=VMEM_LIMIT
+            collective_id=1, has_side_effects=True, vmem_limit_bytes=52 * MIB
         ),
         cost_estimate=pl.CostEstimate(
             flops=16 * rows * padded * width, bytes_accessed=2 * valid * width, transcendentals=0
@@ -890,7 +979,7 @@
             pltpu.SemaphoreType.DMA((copies,)),
         ],
         compiler_params=pltpu.CompilerParams(
-            collective_id=2, has_side_effects=True, vmem_limit_bytes=VMEM_LIMIT
+            collective_id=2, has_side_effects=True, vmem_limit_bytes=24 * MIB
         ),
     )(task_list, table, stats)
 
@@ -933,10 +1022,46 @@
     ids = lax.all_gather(jnp.stack([tokens[:, 0], targets[:, 0], loss_mask[:, 0]]), "vocab")
     ids = jnp.transpose(ids, (1, 2, 0, 3)).reshape(3, micros, length)
     enc_ids = ids[0].reshape(shards, own)
-    before = jnp.pad(ids[1], ((0, 0), (1, 0)))[:, :length].reshape(shards, own)[:, :1]
-    dec_ids = jnp.concatenate(
-        [jnp.zeros((shards, HALO - 1), jnp.int32), before, ids[1].reshape(shards, own)], 1
-    )
+
+    segments = seg_lengths.shape[-1]
+    row_lengths = seg_lengths[:, 0]
+    if group == 2 and segments == 3 and 2 * span + 2 * P_SIZE <= length - span:
+        half = (length - segments * P_SIZE) // group
+        heads = (half + LANES - 1) // LANES * LANES
+        extra = (half + 2 * P_SIZE - own + HALO - 1) // HALO * HALO
+        starts = [0, own - extra]
+        near = [P_SIZE, half + 2 * P_SIZE]
+        far = [2 * P_SIZE, half + 3 * P_SIZE]
+        turns = [row_lengths[:, 0] - P_SIZE, length - row_lengths[:, 2] - near[1]]
+    else:
+        half = heads = own
+        extra = 0
+        starts = near = far = [p * own for p in range(group)]
+        turns = [row_lengths[:, 0]] * group
+    held = own + extra
+    entries = jnp.arange(heads, dtype=jnp.int32)
+
+    def of_rows(values, m, p):
+        values = jnp.pad(values, (0, heads + far[p]))
+        return jnp.where(
+            entries < turns[p][m],
+            values[near[p] : near[p] + heads],
+            values[far[p] : far[p] + heads],
+        )
+
+    everyone = [(m, p) for m in range(micros) for p in range(group)]
+    dec_ids = jnp.stack(
+        [
+            jnp.concatenate(
+                [
+                    jnp.zeros((HALO - 1,), jnp.int32),
+                    jnp.pad(ids[1, m], (1, 0))[starts[p] : starts[p] + 1 + held],
+                ]
+            )
+            for m, p in everyone
+        ]
+    )
+    head_targets = jnp.stack([of_rows(ids[1, m], m, p) for m, p in everyone])
     first_row = me * shard_rows
 
     def lookup(wanted):
@@ -964,9 +1089,26 @@
     )
     key_segment = layout(lengths, tasks, key_positions)[0]
     rows_info = jnp.stack([segment, positions], 1)
-    keys_info = jnp.stack([key_segment, key_positions], 0)
-    own_mask = lax.dynamic_slice(ids[2], (micro, place * own), (1, own))[0]
-    counted = (own_mask * (in_segment >= P_SIZE)).astype(F32)
+    keys_info = jnp.stack([key_segment, key_positions], 1)
+    turn = jnp.stack(turns)[place, micro]
+    near_row = jnp.asarray(near, jnp.int32)[place]
+    far_row = jnp.asarray(far, jnp.int32)[place]
+    first_held = jnp.asarray(starts, jnp.int32)[place]
+    head_positions = jnp.where(entries < turn, near_row, far_row) + entries
+    head_positions = jnp.minimum(head_positions, length - 1)
+    head_segment, head_in_segment, head_task = layout(lengths, tasks, head_positions)
+    heads_info = jnp.stack([head_segment, head_positions], 1)
+    head_mask_row = jnp.stack([of_rows(ids[2, m], m, p) for m, p in everyone])[me]
+    counted = (head_mask_row * ((head_in_segment >= P_SIZE) & (entries < half))).astype(F32)
+
+    def head_rows(values):
+        values = jnp.pad(values, ((0, heads), (0, 0)))
+        shape = (heads, values.shape[1])
+        return jnp.where(
+            (entries < turn)[:, None],
+            lax.dynamic_slice(values, (near_row - first_held, 0), shape),
+            lax.dynamic_slice(values, (far_row - first_held, 0), shape),
+        )
 
     def key_parts(source, weight):
         pair = dot(source, weight).astype(BF16)
@@ -980,44 +1122,46 @@
     enc_input = jnp.where(
         is_prompt[:, None], jnp.take(prompt_flat, slot, axis=0), enc_rows
     ).astype(F32)
-    target_rows = dec_rows[HALO:].astype(F32)
-    dec_input = jnp.where(
-        (in_segment >= 1)[:, None], dec_rows[HALO - 1 : HALO - 1 + own], dec_rows[:1]
-    ).astype(F32)
+    held_positions = first_held + jnp.arange(held, dtype=jnp.int32)
+    begun = layout(lengths, tasks, held_positions)[1] >= 1
+    dec_held = jnp.where(begun[:, None], dec_rows[HALO - 1 : HALO - 1 + held], dec_rows[:1])
+    dec_keys = lax.dynamic_slice(dec_held, (place * own - first_held, 0), (own, width)).astype(F32)
+    dec_input = head_rows(dec_held).astype(F32)
+    target_rows = head_rows(dec_rows[HALO:]).astype(F32)
 
     normed_in, inverse_in = normed(enc_input, norm_gains[0])
     normed_low = normed_in.astype(BF16)
     enc_pairs = key_parts(normed_low, attend_in[0][:, width:])
     enc_queries = project(normed_low, attend_in[0][:, :width])
+    normed_keys = normed(dec_keys, norm_gains[3])[0].astype(BF16)
+    dec_pairs = key_parts(normed_keys, attend_in[1][:, width:])
     normed_dec = normed(dec_input, norm_gains[3])[0].astype(BF16)
-    dec_pairs = key_parts(normed_dec, attend_in[1][:, width:])
     dec_queries = project(normed_dec, attend_in[1][:, :width])
-    mixed = attend(enc_queries, enc_pairs, rows_info, keys_info, False)
-    enc_mid = enc_input + dot(mixed, attend_out[0])
-    normed_mid, inverse_mid = normed(enc_mid, norm_gains[1])
-    enc_pre = dot(normed_mid.astype(BF16), expand_weights[0])
-    enc_last = enc_mid + dot(smooth(enc_pre).astype(BF16), reduce_weights[0])
+    enc_mid, enc_mixed, enc_logs = attend(
+        enc_queries, enc_pairs, enc_input, attend_out[0], rows_info, keys_info, False
+    )
+    enc_last, enc_kept = feed(enc_mid, norm_gains[1], expand_weights[0], reduce_weights[0])
     encoded, inverse_last = normed(enc_last, norm_gains[2])
     cross_pairs = key_parts(encoded.astype(BF16), attend_in[2][:, width:])
 
-    mixed = attend(dec_queries, dec_pairs, rows_info, keys_info, True)
-    dec_first = dec_input + dot(mixed, attend_out[1])
+    dec_first = attend(
+        dec_queries, dec_pairs, dec_input, attend_out[1], heads_info, keys_info, True
+    )[0]
     cross_queries = project(normed(dec_first, norm_gains[4])[0].astype(BF16), attend_in[2][:, :width])
-    mixed = attend(cross_queries, cross_pairs, rows_info, keys_info, False)
-    dec_second = dec_first + dot(mixed, attend_out[2])
-    normed_second, inverse_second = normed(dec_second, norm_gains[5])
-    dec_pre = dot(normed_second.astype(BF16), expand_weights[1])
-    dec_last = dec_second + dot(smooth(dec_pre).astype(BF16), reduce_weights[1])
+    dec_second, cross_mixed, cross_logs = attend(
+        cross_queries, cross_pairs, dec_first, attend_out[2], heads_info, keys_info, False
+    )
+    dec_last, dec_kept = feed(dec_second, norm_gains[5], expand_weights[1], reduce_weights[1])
     output_norm, inverse_out = normed(dec_last, norm_gains[6])
     hidden = (output_norm * width ** (-0.5)).astype(BF16)
 
-    target_local = ids[1].reshape(-1, 1) - first_row
+    target_local = head_targets.reshape(-1, 1) - first_row
     if shards == 4:
         summed, stats = vocab_exchange(hidden, target_local, embedding)
         own_total = stats[:, 0]
     else:
         all_hidden = lax.all_gather(hidden, "vocab", axis=0, tiled=True)
-        part, stats = vocab_pass(all_hidden, target_local, embedding, own)
+        part, stats = vocab_pass(all_hidden, target_local, embedding, heads)
         gathered = lax.all_gather(stats[:, :2].T, "vocab")
         maxima = jnp.max(gathered[:, 0], 0)
         log_total = maxima + jnp.log(
@@ -1025,20 +1169,13 @@
         )
         scaled = part * jnp.exp(stats[:, 0] - log_total)[:, None]
         summed = lax.psum_scatter(scaled, "vocab", scatter_dimension=0, tiled=True)
-        own_total = lax.dynamic_slice(log_total, (me * own,), (own,))
+        own_total = lax.dynamic_slice(log_total, (me * heads,), (heads,))
     target_logit = jnp.sum(hidden.astype(F32) * target_rows, -1)
     token_loss = own_total - target_logit
     target_coefficient = (jnp.exp(target_logit - own_total) - 1.0).astype(BF16).astype(F32)
     hidden_grad = counted[:, None] * (summed + target_coefficient[:, None] * target_rows)
 
-    def feed_back(hidden_pre, weight_one, weight_two, gradient):
-        active_grad = dot_rows(gradient.astype(BF16), weight_two)
-        pre_grad = jax.vjp(smooth, hidden_pre)[1](active_grad)[0].astype(BF16)
-        return dot_rows(pre_grad, weight_one)
-
-    def keys_back(parts, weight):
-        dk, dv = parts[:group], parts[group : 2 * group]
-        pairs = [jnp.concatenate([dk[k], dv[k]], 1) for k in range(group)]
+    def keys_back(pairs, weight):
         total = pairs[0]
         for k in range(1, group):
             total = total + around(pairs[k], group - k)
@@ -1049,31 +1186,45 @@
     dec_grad = normed_back(
         dec_last, norm_gains[6], inverse_out, hidden_grad * width ** (-0.5)
     )
-    dec_grad = dec_grad + normed_back(
-        dec_second,
-        norm_gains[5],
-        inverse_second,
-        feed_back(dec_pre, expand_weights[1], reduce_weights[1], dec_grad),
-    )
-    mixed_grad = dot_rows(dec_grad.astype(BF16), attend_out[2]).astype(BF16)
-    back = attend_back(cross_queries, cross_pairs, mixed_grad, rows_info.T, keys_info.T, False)
+    dec_grad = feed_back(
+        dec_grad, dec_second, norm_gains[5], dec_kept, expand_weights[1], reduce_weights[1]
+    )
+    back = attend_back(
+        cross_queries,
+        cross_pairs,
+        dec_grad,
+        attend_out[2],
+        cross_mixed,
+        cross_logs,
+        heads_info,
+        keys_info,
+        False,
+    )
     enc_grad = normed_back(
         enc_last, norm_gains[2], inverse_last, keys_back(back, attend_in[2][:, width:])
     )
-    enc_grad = enc_grad + normed_back(
-        enc_mid,
-        norm_gains[1],
-        inverse_mid,
-        feed_back(enc_pre, expand_weights[0], reduce_weights[0], enc_grad),
-    )
-    mixed_grad = dot_rows(enc_grad.astype(BF16), attend_out[0]).astype(BF16)
-    back = attend_back(enc_queries, enc_pairs, mixed_grad, rows_info.T, keys_info.T, True)
-    source_grad = keys_back(back, attend_in[0][:, width:]) + dot_rows(
-        back[-1], attend_in[0][:, :width]
+    enc_grad = feed_back(
+        enc_grad, enc_mid, norm_gains[1], enc_kept, expand_weights[0], reduce_weights[0]
+    )
+    *back, back_queries = attend_back(
+        enc_queries,
+        enc_pairs,
+        enc_grad,
+        attend_out[0],
+        enc_mixed,
+        enc_logs,
+        rows_info,
+        keys_info,
+        True,
+    )
+    source_grad = keys_back(back, attend_in[0][:, width:]) + lax.dot_general(
+        back_queries,
+        attend_in[0][:, :width],
+        (((0,), (1,)), ((), ())),
+        preferred_element_type=F32,
     )
     enc_grad = enc_grad + normed_back(enc_input, norm_gains[0], inverse_in, source_grad)
 
-    segments = lengths.shape[0]
     place_of = segment * LANES + in_segment
     chosen = (
         (place_of[:, None] == jnp.arange(segments * LANES, dtype=jnp.int32)) & is_prompt[:, None]
@@ -1081,7 +1232,7 @@
     high = enc_grad.astype(BF16)
     rest = (enc_grad - high.astype(F32)).astype(BF16)
     table = dot_columns(high, chosen) + dot_columns(rest, chosen)
-    tallies = jnp.stack([per_task(task_of, counted * token_loss), per_task(task_of, counted)])
+    tallies = jnp.stack([per_task(head_task, counted * token_loss), per_task(head_task, counted)])
     stats = jnp.zeros((8, LANES), F32).at[:2, :TASKS].set(tallies)
     if shards == 4 and lax.axis_size("dp") == TASKS:
         gradient, stats, squares = reduce_over_devices(task_ids[:, 0], table, stats)

time: 575 us -> 533 us (0.927)
  Pallas kernels: 367 us -> 321 us
  matrix products: 95.3 us -> 69.5 us
  other arithmetic: 29.5 us -> 43.9 us
  local copies, waits for them, and re-layouts: 41.7 us -> 54.5 us
    pallas_call x6, Pallas kernels: 183 us -> 138 us  [the longest x1 63.5 us: vocab_exchange(): pl.pallas_call(functools.partial(vocab_exchange_kernel, tile), out_shape=...]
    dot_general x13 -> x10, matrix products: 45.7 us -> 26.8 us  [dot(): return jnp.dot(left, right, preferred_element_type=F32)]
    unnamed x105 -> x175, local copies, waits for them, and re-layouts: 1.23 us -> 10.8 us
    dot_general x9 -> x6, matrix products: 46.5 us -> 39.3 us  [dot_rows(): lax.dot_general(left, right, (((1,), (1,)), ((), ())), preferred_element_...]
  transfers between devices with their start and end apart: 8 -> 8, of which waited for: 2 -> 2; matrix products, arithmetic and copies ran while one was open for 15% -> 16% of each run, Pallas kernels for 30% -> 31%
where the time goes in v3:
time: 533 us; the launch traced here: 526 us
  Pallas kernels  321 us (60%)
  matrix products  69.5 us (13%)
  local copies, waits for them, and re-layouts  54.5 us (10%)
  other arithmetic  43.9 us (8%)
  between operations  18.7 us (4%)
  waiting for transfers between devices  11.3 us (2%)
  blocking collectives  5.67 us (1%)
    pallas_call x1, Pallas kernels, gather_weights(): pl.pallas_call(functools.partial(gather_kernel, rows_z, rows_y), out_shap...  140 us
    pallas_call x1, Pallas kernels, vocab_exchange(): pl.pallas_call(functools.partial(vocab_exchange_kernel, tile), out_shape=...  63.5 us
    pallas_call x1, Pallas kernels, reduce_over_devices(): pl.pallas_call(functools.partial(reduce_kernel, rows_dp), out_shape=[jax....  43.2 us
    dot_general x6, matrix products, dot_rows(): lax.dot_general(left, right, (((1,), (1,)), ((), ())), preferred_element_...  39.3 us
    pallas_call x2, Pallas kernels, attend_back(): pl.pallas_call(functools.partial(attend_back_kernel, parts, want_queries)...  39.3 us
    pallas_call x3, Pallas kernels, attend(): pl.pallas_call(functools.partial(attend_kernel, parts, causal), out_shape...  35.1 us
    gather x2, local copies, waits for them, and re-layouts, lookup(): picked = jnp.take(embedding, jnp.clip(local, 0, shard_rows - 1), axis=0)  31.1 us
    dot_general x10, matrix products, dot(): return jnp.dot(left, right, preferred_element_type=F32)  26.8 us
  transfers between devices with their start and end apart: 8, of which 2 were waited for; matrix products, arithmetic and copies ran while one was open for 16% of the time, Pallas kernels for 31%

profile of v3, /device:TPU:25, one launch (start us, length us, event | category | flops | bytes accessed | tf_op | source)
XLA Modules:
  0.0 525.9 jit_solution(2117628002116725096)
XLA Ops:
  7.2 1.9 convert_element_type.147
  9.3 5.7 %all-gather = s32[12,2,256]{2,1,0:T(2,128)S(1)} all-gather(s32[3,2,256]{2,1,0:T(2,128)S(1)} %pad_add_fusion.2), channel_id=2, replica_groups=mesh['dp'=8,'vocab'=4] {'vocab'}, dimensions={0}, use_global_device_ids=true | all-gather | bytes 30720 | tf_op jit(solution)/shard_map/all_gather | solution.py:1022
  15.1 14.8 %gather_fusion.1 = bf16[2048,768]{1,0:T(8,128)(2,1)S(1)} fusion(bf16[8032,768]{1,0:T(8,128)(2,1)} %table_ref.1, s32[2048]{0:T(1024)S(1)} %broadcast_clamp_fusion.1), kind=kCustom, calls=%fused_computation.1 | custom fusion | bytes 6299648 | tf_op jit(solution)/shard_map/jit(_take)/gather | solution.py:1070
  30.0 2.0 select_select_fusion.1
  33.1 16.3 %gather_fusion.2 = bf16[2368,768]{1,0:T(8,128)(2,1)} fusion(bf16[8032,768]{1,0:T(8,128)(2,1)} %table_ref.1, s32[3072]{0:T(1024)S(1)} %pad_clamp_fusion), kind=kCustom, calls=%fused_computation.2 | custom fusion | bytes 7283968 | tf_op jit(solution)/shard_map/jit(_take)/gather | solution.py:1070
  49.4 4.4 select_select_fusion
  57.4 0.7 fusion.105
  58.1 0.7 fusion.106
  58.8 0.7 fusion.108
  59.6 0.7 fusion.107
  60.5 2.0 add_minimum_fusion.1
  62.6 1.4 compare_select_fusion.9
  64.4 139.9 %shard_map.225 = (bf16[4,2,96,2304]{3,2,1,0:T(8,128)(2,1)}, bf16[4,2,96,2304]{3,2,1,0:T(8,128)(2,1)}, bf16[4,2,96,2304]{3,2,1,0:T(8,128)(2,1)}, bf16[4,2,96,768]...) custom-call(bf16[3,96,2304]{2,1,0:T(8,128)(2,1)} %refs_0_.1, ...), custom_call_target="tpu_custom_call" | custom-call | bytes 400000000 | tf_op jit(solution)/shard_map/pallas_call | solution.py:623
  205.0 0.7 select_reduce_fusion.5
  205.6 2.0 add_minimum_fusion
  207.6 0.8 pad_add_fusion.refs_5_.refs_7_
  208.5 0.9 add_subtract_fusion.target_ref
  209.5 2.0 select_convert_fusion
  211.5 1.8 copy.120
  213.6 2.7 gather_fusion
  216.3 1.8 fusion.146
  218.8 1.5 convolution_convert_fusion.2.refs_1_
  222.5 0.8 copy.138
  223.5 1.1 copy.123.refs_6_.refs_8_
  224.5 3.2 convolution_convert_fusion.3.refs_0_
  227.8 0.7 slice_reduce_fusion.1
  228.5 2.8 fusion.147
  231.6 1.5 convolution_convert_fusion.1.refs_1_
  233.7 14.5 %shard_map.226 = (f32[512,768]{1,0:T(8,128)S(1)}, f32[512,768]{1,0:T(8,128)S(1)}, f32[512,128]{1,0:T(8,128)S(1)}) custom-call(bf16[512,768]{1,0:T(8,128)(2,1)S(1)} %copy-done.26, bf16[512,1536]{1,0:T(8,128)(2,1)S(1)} %copy-done.13, bf16[512,1536]{1,0:T(8,128)(2,1)} %collective-permute-done.refs_2_, f32[512,768]{1,0:T(8,128)S(1)} %get-tuple-element.109.refs_3_, ...), custom_call_target="tpu_custom_call" | custom-call | flops 4026531840 | bytes 2359296 | tf_op jit(solution)/shard_map/pallas_call | solution.py:172
  248.5 2.7 fusion.54
  251.2 3.9 multiply_reduce_fusion.3
  255.1 1.1 copy-done.36
  256.3 1.4 convolution_convert_fusion.refs_1_
  258.8 0.7 convolution_convert_fusion.5.refs_0_
  260.2 11.0 %shard_map.227 = (f32[384,768]{1,0:T(8,128)S(1)}, f32[384,768]{1,0:T(8,128)}, f32[384,128]{1,0:T(8,128)}) custom-call(bf16[384,768]{1,0:T(8,128)(2,1)S(1)} %convolution_convert_fusion.5.refs_0_, bf16[512,1536]{1,0:T(8,128)(2,1)S(1)} %convolution_convert_fusion.1.refs_1_, bf16[512,1536]{1,0:T(8,128)(2,1)S(1)} %collective-permute-done.1.refs_2_, ...), custom_call_target="tpu_custom_call" | custom-call | flops 3019898880 | bytes 1769472 | tf_op jit(solution)/shard_map/pallas_call | solution.py:172
  272.6 9.6 %shard_map.228 = (f32[384,768]{1,0:T(8,128)S(1)}, f32[384,768]{1,0:T(8,128)S(1)}, f32[384,128]{1,0:T(8,128)S(1)}) custom-call(bf16[384,768]{1,0:T(8,128)(2,1)S(1)} %convolution_convert_fusion.4.refs_0_, bf16[512,1536]{1,0:T(8,128)(2,1)S(1)} %convolution_convert_fusion.refs_1_, bf16[512,1536]{1,0:T(8,128)(2,1)S(1)} %collective-permute-done.2.refs_2_, ...), custom_call_target="tpu_custom_call" | custom-call | flops 3019898880 | bytes 1769472 | tf_op jit(solution)/shard_map/pallas_call | solution.py:172
  282.3 1.0 copy-done.28
  284.2 4.4 fusion.73
  288.6 7.0 %multiply_reduce_fusion.8 = (f32[384]{0:T(512)S(1)}, f32[384,768]{1,0:T(8,128)S(1)}) fusion(f32[384,768]{1,0:T(8,128)S(1)} %get-tuple-element.56, bf16[3072,768]{1,0:T(8,128)(2,1)} %bitcast.168, f32[384,3072]{1,0:T(8,128)S(1)} %fusion.73), kind=kOutput, calls=%fused_computation.93 | convolution fusion | flops 1823440512 | bytes 11798016 | tf_op jit(solution)/shard_map/dot_general | solution.py:34
  295.6 0.8 fusion.43
  296.5 0.7 copy-done.2
  297.2 63.5 %shard_map.229 = (f32[384,768]{1,0:T(8,128)}, f32[384,128]{1,0:T(8,128)S(1)}) custom-call(bf16[384,768]{1,0:T(8,128)(2,1)S(1)} %get-tuple-element.106.h_ref, s32[4,384,1]{2,1,0:T(8,128)S(1)} %copy-done.2, bf16[8032,768]{1,0:T(8,128)(2,1)} %table_ref.1), custom_call_target="tpu_custom_call" | custom-call | flops 38654705664 | bytes 12337152 | tf_op jit(solution)/shard_map/pallas_call | solution.py:787
  360.7 2.8 fusion.99
  363.5 1.8 multiply_reduce_fusion.7
  365.3 12.4 %multiply_reduce_fusion.6 = (f32[384]{0:T(512)S(1)}, f32[384,768]{1,0:T(8,128)}) fusion(f32[384,768]{1,0:T(8,128)S(1)} %get-tuple-element.56, f32[384]{0:T(512)S(1)} %add_rsqrt_fusion.1, f32[768]{0:T(1024)S(1)} %get-tuple-element.85, bf16[768,3072]{1,0:T(8,128)(2,1)} %bitcast.167, f32[384,3072]{1,0:T(8,128)} %copy-done.81, bf16[3072,768]{1,0:T(8,128)(2,1)} %bitcast.169, ...), kind=kOutput, calls=%fused_computation.89 | convolution fusion | flops 3651599872 | bytes 19479552 | tf_op jit(solution)/shard_map/dot_general | solution.py:38
  377.7 2.9 multiply_add_fusion.2.refs_3_
  381.5 1.3 copy-done.29
  382.8 16.7 %shard_map.230 = (f32[512,1536]{1,0:T(8,128)S(1)}, f32[512,1536]{1,0:T(8,128)}) custom-call(bf16[384,768]{1,0:T(8,128)(2,1)S(1)} %copy-done.25, bf16[512,1536]{1,0:T(8,128)(2,1)S(1)} %copy-done.16, bf16[512,1536]{1,0:T(8,128)(2,1)S(1)} %copy-done.18, f32[384,768]{1,0:T(8,128)S(1)} %multiply_add_fusion.2.refs_3_, bf16[768,768]{1,0:T(8,128)(2,1)S(1)} %bitcast.116, ...), custom_call_target="tpu_custom_call" | custom-call | flops 6039797760 | bytes 5898240 | tf_op jit(solution)/shard_map/pallas_call | solution.py:270
  399.5 1.7 copy-done
  401.3 5.8 %collective-permute-done.3 = f32[512,1536]{1,0:T(8,128)} collective-permute-done((f32[512,1536]{1,0:T(8,128)}, f32[512,1536]{1,0:T(8,128)}, u32[]{:S(2)}, u32[]{:S(2)}) %collective-permute-start.3) | collective-permute-done | bytes 3145760 | tf_op jit(solution)/shard_map/ppermute | solution.py:1020
  407.2 5.1 fusion.21
  412.3 0.8 copy-done.45
  413.1 4.7 multiply_reduce_fusion.2
  417.8 14.4 %multiply_reduce_fusion.1 = (f32[512]{0:T(512)S(1)}, f32[512,768]{1,0:T(8,128)}) fusion(f32[512,768]{1,0:T(8,128)S(1)} %get-tuple-element.48, f32[768]{0:T(1024)S(1)} %get-tuple-element.83, f32[512]{0:T(512)S(1)} %copy-done.56, bf16[768,3072]{1,0:T(8,128)(2,1)} %bitcast.118, f32[512,3072]{1,0:T(8,128)} %copy-done.35, bf16[3072,768]{1,0:T(8,128)(2,1)} %bitcast.162, ...), kind=kOutput, calls=%fused_computation.59 | convolution fusion | flops 4866833920 | bytes 22031360 | tf_op jit(solution)/shard_map/dot_general | solution.py:38
  432.2 3.1 multiply_add_fusion.1.refs_3_
  436.1 22.6 %shard_map.231 = (f32[512,1536]{1,0:T(8,128)S(1)}, f32[512,1536]{1,0:T(8,128)S(1)}, bf16[768,512]{1,0:T(8,128)(2,1)S(1)}) custom-call(bf16[512,768]{1,0:T(8,128)(2,1)S(1)} %copy-done.27, bf16[512,1536]{1,0:T(8,128)(2,1)S(1)} %copy-done.14, bf16[512,1536]{1,0:T(8,128)(2,1)} %collective-permute-done.refs_2_, f32[512,768]{1,0:T(8,128)S(1)} %multiply_add_fusion.1.refs_3_, ...), custom_call_target="tpu_custom_call" | custom-call | flops 8053063680 | bytes 7864320 | tf_op jit(solution)/shard_map/pallas_call | solution.py:270
  459.1 5.3 %collective-permute-done.4 = f32[512,1536]{1,0:T(8,128)S(1)} collective-permute-done((f32[512,1536]{1,0:T(8,128)S(1)}, f32[512,1536]{1,0:T(8,128)S(1)}, u32[]{:S(2)}, u32[]{:S(2)}) %collective-permute-start.4) | collective-permute-done | bytes 3145760 | tf_op jit(solution)/shard_map/ppermute | solution.py:1020
  464.4 1.4 fusion.26
  465.8 1.4 fusion.28
  467.3 1.2 multiply_reduce_fusion
  468.5 1.0 fusion.70
  469.6 1.1 convolution_add_fusion.table_ref
  470.7 43.2 %shard_map.232 = (f32[8,192,128]{2,1,0:T(8,128)S(1)}, f32[8,128]{1,0:T(8,128)S(1)}, f32[8,128]{1,0:T(8,128)S(1)}) custom-call(s32[2,3]{1,0:T(2,128)S(1)} %bitcast.112, f32[768,384]{1,0:T(8,128)S(1)} %convolution_add_fusion.table_ref, f32[8,128]{1,0:T(8,128)S(1)} %select_maximum_fusion.stat_ref), custom_call_target="tpu_custom_call" | custom-call | tf_op jit(solution)/shard_map/pallas_call | solution.py:957
  516.5 1.6 add_subtract_fusion.1
  (293 shorter events, 17.1 us)
Async XLA Ops:
  7.2 204.3 %all-gather.3.cloned.1.call-start = ((), (), s32[]{:S(2)}) async-start(), calls=%async_computation.2 | async-start | bytes 1966080 | tf_op jit(solution)/shard_map/all_gather | solution.py:1076
  9.2 207.1 %reduce-scatter.3.cloned.1.call-start = ((), (), s32[]{:S(2)}) async-start(), calls=%async_computation.3 | async-start | bytes 3932160 | tf_op jit(solution)/shard_map/reduce_scatter | solution.py:1073
  32.0 195.7 %reduce-scatter.5.cloned.1.call-start = ((), (), s32[]{:S(2)}) async-start(), calls=%async_computation.4 | async-start | bytes 4546560 | tf_op jit(solution)/shard_map/reduce_scatter | solution.py:1074
  64.3 140.0 %copy-start.10 = (s32[2,1,3]{2,1,0:T(1,128)S(1)}, s32[2,1,3]{2,1,0:T(1,128)}, u32[]{:S(2)}) copy-start(s32[2,1,3]{2,1,0:T(1,128)} %param.24) | copy-start | bytes 76
  64.3 144.1 %copy-start.57 = (f32[7,768]{1,0:T(8,128)S(1)}, f32[7,768]{1,0:T(8,128)}, u32[]{:S(2)}) copy-start(f32[7,768]{1,0:T(8,128)} %param.30) | copy-start | bytes 64516
  204.5 8.8 %copy-start.53 = (s32[512]{0:T(512)}, s32[512]{0:T(512)S(1)}, u32[]{:S(2)}) copy-start(s32[512]{0:T(512)S(1)} %convert_reduce_fusion.3) | copy-start | bytes 6148
  204.6 8.7 %copy-start.51 = (s32[512]{0:T(512)}, s32[512]{0:T(512)S(1)}, u32[]{:S(2)}) copy-start(s32[512]{0:T(512)S(1)} %get-tuple-element.93) | copy-start | bytes 6148
  208.5 16.0 %copy-start.61 = (f32[768]{0:T(1024)}, f32[768]{0:T(1024)S(1)}, u32[]{:S(2)}) copy-start(f32[768]{0:T(1024)S(1)} %get-tuple-element.84) | copy-start | bytes 9220
  208.5 46.6 %copy-start.63 = (f32[768]{0:T(1024)}, f32[768]{0:T(1024)S(1)}, u32[]{:S(2)}) copy-start(f32[768]{0:T(1024)S(1)} %get-tuple-element.80) | copy-start | bytes 9220
  209.5 6.9 %copy-start.71 = (pred[512]{0:T(512)(128)(4,1)}, pred[512]{0:T(512)(128)(4,1)S(1)}, u32[]{:S(2)}) copy-start(pred[512]{0:T(512)(128)(4,1)S(1)} %get-tuple-element.122) | copy-start | bytes 1540
  218.4 6.2 %copy-start.48 = (f32[512]{0:T(512)}, f32[512]{0:T(512)S(1)}, u32[]{:S(2)}) copy-start(f32[512]{0:T(512)S(1)} %add_rsqrt_fusion.7) | copy-start | bytes 6148
  220.3 7.5 %copy-start.12 = (bf16[512,1536]{1,0:T(8,128)(2,1)}, bf16[512,1536]{1,0:T(8,128)(2,1)S(1)}, u32[]{:S(2)}) copy-start(bf16[512,1536]{1,0:T(8,128)(2,1)S(1)} %convolution_convert_fusion.2.refs_1_) | copy-start | bytes 4718596
  220.3 13.2 %collective-permute-start = (bf16[512,1536]{1,0:T(8,128)(2,1)S(1)}, bf16[512,1536]{1,0:T(8,128)(2,1)}, u32[]{:S(2)}, u32[]{:S(2)}) collective-permute-start(bf16[512,1536]{1,0:T(8,128)(2,1)S(1)} %convolution_convert_fusion.2.refs_1_), channel_id=1, source_target_pairs={{0,1},{1,0},{2,3},{3,2},{4,5},{5,4},{6,7},{7,6},{8,9},{9,8},{10,11... | collective-permute-start | bytes 4718600 | tf_op jit(solution)/shard_map/ppermute | solution.py:1020
  228.5 3.0 copy-start.78
  231.6 16.9 %slice-start = ((s8[4718592]{0:T(1024)(128)(4,1)}), s8[4194304]{0:T(1024)(128)(4,1)S(1)}, s32[]{:S(2)}) async-start(s8[4718592]{0:T(1024)(128)(4,1)} %bitcast.119), calls=%async_computation.5 | async-start | bytes 8388608
  233.0 26.4 %collective-permute-start.1 = (bf16[512,1536]{1,0:T(8,128)(2,1)S(1)}, bf16[512,1536]{1,0:T(8,128)(2,1)S(1)}, u32[]{:S(2)}, u32[]{:S(2)}) collective-permute-start(bf16[512,1536]{1,0:T(8,128)(2,1)S(1)} %convolution_convert_fusion.1.refs_1_), channel_id=1, source_target_pairs={{0,1},{1,0},{2,3},{3,2},{4,5},{5,4},{6,7},{7,6},{8,9},{9,8},{10,11... | collective-permute-start | bytes 4718600 | tf_op jit(solution)/shard_map/ppermute | solution.py:1020
  233.7 14.8 %slice-start.1 = ((s8[4718592]{0:T(1024)(128)(4,1)}), s8[524288]{0:T(1024)(128)(4,1)S(1)}, s32[]{:S(2)}) async-start(s8[4718592]{0:T(1024)(128)(4,1)} %bitcast.119), calls=%async_computation.6 | async-start | bytes 1048576
  248.2 2.9 copy-start.5
  248.2 2.9 copy-start.30
  248.2 3.0 slice-start.2
  248.4 2.7 copy-start.55
  251.2 3.9 copy-start.35
  251.2 5.0 copy-start.44
  257.7 14.3 %copy-start.15 = (bf16[512,1536]{1,0:T(8,128)(2,1)}, bf16[512,1536]{1,0:T(8,128)(2,1)S(1)}, u32[]{:S(2)}) copy-start(bf16[512,1536]{1,0:T(8,128)(2,1)S(1)} %convolution_convert_fusion.refs_1_) | copy-start | bytes 4718596
  257.7 14.3 %collective-permute-start.2 = (bf16[512,1536]{1,0:T(8,128)(2,1)S(1)}, bf16[512,1536]{1,0:T(8,128)(2,1)S(1)}, u32[]{:S(2)}, u32[]{:S(2)}) collective-permute-start(bf16[512,1536]{1,0:T(8,128)(2,1)S(1)} %convolution_convert_fusion.refs_1_), channel_id=1, source_target_pairs={{0,1},{1,0},{2,3},{3,2},{4,5},{5,4},{6,7},{7,6},{8,9},{9,8},{10,11... | collective-permute-start | bytes 4718600 | tf_op jit(solution)/shard_map/ppermute | solution.py:1020
  272.0 10.2 %copy-start.24 = (bf16[384,768]{1,0:T(8,128)(2,1)}, bf16[384,768]{1,0:T(8,128)(2,1)S(1)}, u32[]{:S(2)}) copy-start(bf16[384,768]{1,0:T(8,128)(2,1)S(1)} %convolution_convert_fusion.4.refs_0_) | copy-start | bytes 1769476
  272.1 10.2 %copy-start.17 = (bf16[512,1536]{1,0:T(8,128)(2,1)}, bf16[512,1536]{1,0:T(8,128)(2,1)S(1)}, u32[]{:S(2)}) copy-start(bf16[512,1536]{1,0:T(8,128)(2,1)S(1)} %collective-permute-done.2.refs_2_) | copy-start | bytes 4718596
  283.4 81.8 %copy-start.66 = (f32[384]{0:T(512)}, f32[384]{0:T(512)S(1)}, u32[]{:S(2)}) copy-start(f32[384]{0:T(512)S(1)} %add_rsqrt_fusion.1) | copy-start | bytes 4612
  288.6 7.0 %copy-start.81 = (f32[384,3072]{1,0:T(8,128)}, f32[384,3072]{1,0:T(8,128)S(1)}, u32[]{:S(2)}) copy-start(f32[384,3072]{1,0:T(8,128)S(1)} %fusion.73) | copy-start | bytes 14155780
  288.6 7.0 %copy-start.39 = (bf16[576,768]{1,0:T(8,128)(2,1)S(1)}, bf16[576,768]{1,0:T(8,128)(2,1)}, u32[]{:S(2)}) copy-start(bf16[576,768]{1,0:T(8,128)(2,1)} %get-tuple-element.111) | copy-start | bytes 2654212
  295.6 67.9 %copy-start.34 = (f32[384,768]{1,0:T(8,128)}, f32[384,768]{1,0:T(8,128)S(1)}, u32[]{:S(2)}) copy-start(f32[384,768]{1,0:T(8,128)S(1)} %get-tuple-element.132) | copy-start | bytes 3538948
  296.5 67.0 %copy-start.38 = (bf16[384,768]{1,0:T(8,128)(2,1)}, bf16[384,768]{1,0:T(8,128)(2,1)S(1)}, u32[]{:S(2)}) copy-start(bf16[384,768]{1,0:T(8,128)(2,1)S(1)} %get-tuple-element.105) | copy-start | bytes 1769476
  297.2 63.5 %copy-start.47 = (s32[384,1]{1,0:T(8,128)S(1)}, s32[384,1]{1,0:T(8,128)}, u32[]{:S(2)}) copy-start(s32[384,1]{1,0:T(8,128)} %copy.138) | copy-start | bytes 4612
  363.5 14.2 %copy-start.58 = (f32[384]{0:T(512)}, f32[384]{0:T(512)S(1)}, u32[]{:S(2)}) copy-start(f32[384]{0:T(512)S(1)} %get-tuple-element.74) | copy-start | bytes 4612
  365.3 12.4 %copy-start.67 = (f32[384]{0:T(512)}, f32[384]{0:T(512)S(1)}, u32[]{:S(2)}) copy-start(f32[384]{0:T(512)S(1)} %broadcast_multiply_fusion.2) | copy-start | bytes 4612
  377.7 3.0 copy-start.4
  377.7 3.0 copy-start.8
  377.7 3.0 copy-start.9
  377.7 3.0 copy-start.16
  377.7 3.3 copy-start.18
  377.7 3.7 copy-start.22
  377.7 3.8 copy-start.25
  382.8 18.3 %copy-start.6 = (f32[512,128]{1,0:T(8,128)S(1)}, f32[512,128]{1,0:T(8,128)}, u32[]{:S(2)}) copy-start(f32[512,128]{1,0:T(8,128)} %copy-done.5) | copy-start | bytes 786436
  401.1 6.0 %collective-permute-start.3 = (f32[512,1536]{1,0:T(8,128)}, f32[512,1536]{1,0:T(8,128)}, u32[]{:S(2)}, u32[]{:S(2)}) collective-permute-start(f32[512,1536]{1,0:T(8,128)} %get-tuple-element.64), channel_id=1, source_target_pairs={{0,1},{1,0},{2,3},{3,2},{4,5},{5,4},{6,7},{7,6},{8,9},{9,8},{10,11... | collective-permute-start | bytes 9437192 | tf_op jit(solution)/shard_map/ppermute | solution.py:1020
  407.1 5.1 copy-start.1
  407.1 5.1 copy-start.37
  407.1 6.0 %copy-start.45 = (bf16[4,2,96,2304]{3,2,1,0:T(8,128)(2,1)S(1)}, bf16[4,2,96,2304]{3,2,1,0:T(8,128)(2,1)}, u32[]{:S(2)}) copy-start(bf16[4,2,96,2304]{3,2,1,0:T(8,128)(2,1)} %get-tuple-element.54) | copy-start | bytes 10616836
  407.1 6.0 %copy-start.60 = (f32[512]{0:T(512)S(1)}, f32[512]{0:T(512)}, u32[]{:S(2)}) copy-start(f32[512]{0:T(512)} %copy-done.59) | copy-start | bytes 6148
  407.2 6.0 %copy-start.64 = (f32[768]{0:T(1024)S(1)}, f32[768]{0:T(1024)}, u32[]{:S(2)}) copy-start(f32[768]{0:T(1024)} %copy-done.63) | copy-start | bytes 9220
  413.1 4.7 copy-start.56
  432.1 3.2 copy-start.14
  432.1 3.2 copy-start.20
  432.1 3.4 copy-start.27
  432.2 3.9 copy-start.31
  436.0 22.8 %copy-start.52 = (s32[512]{0:T(512)S(1)}, s32[512]{0:T(512)}, u32[]{:S(2)}) copy-start(s32[512]{0:T(512)} %copy-done.51) | copy-start | bytes 6148
  436.0 22.8 %copy-start.54 = (s32[512]{0:T(512)S(1)}, s32[512]{0:T(512)}, u32[]{:S(2)}) copy-start(s32[512]{0:T(512)} %copy-done.53) | copy-start | bytes 6148
  436.0 22.8 %copy-start.68 = (f32[384]{0:T(512)S(1)}, f32[384]{0:T(512)}, u32[]{:S(2)}) copy-start(f32[384]{0:T(512)} %get-tuple-element.73) | copy-start | bytes 4612
  436.0 22.8 %copy-start.70 = (s32[384]{0:T(512)S(1)}, s32[384]{0:T(512)}, u32[]{:S(2)}) copy-start(s32[384]{0:T(512)} %get-tuple-element.90) | copy-start | bytes 4612
  436.0 28.3 %copy-start.41 = (bf16[4,2,96,2304]{3,2,1,0:T(8,128)(2,1)S(1)}, bf16[4,2,96,2304]{3,2,1,0:T(8,128)(2,1)}, u32[]{:S(2)}) copy-start(bf16[4,2,96,2304]{3,2,1,0:T(8,128)(2,1)} %get-tuple-element.46) | copy-start | bytes 10616836
  458.7 5.7 %collective-permute-start.4 = (f32[512,1536]{1,0:T(8,128)S(1)}, f32[512,1536]{1,0:T(8,128)S(1)}, u32[]{:S(2)}, u32[]{:S(2)}) collective-permute-start(f32[512,1536]{1,0:T(8,128)S(1)} %get-tuple-element.68), channel_id=1, source_target_pairs={{0,1},{1,0},{2,3},{3,2},{4,5},{5,4},{6,7},{7,6},{8,9},{9,8},{10,11... | collective-permute-start | bytes 9437192 | tf_op jit(solution)/shard_map/ppermute | solution.py:1020
  469.6 46.3 %copy-start.74 = (f32[8,100]{1,0:T(8,128)S(1)}, f32[8,100]{1,0:T(8,128)}, u32[]{:S(2)}) copy-start(f32[8,100]{1,0:T(8,128)} %param.33) | copy-start | bytes 9604
  470.7 45.7 %copy-start.69 = (f32[8,192]{1,0:T(8,128)S(1)}, f32[8,192]{1,0:T(8,128)}, u32[]{:S(2)}) copy-start(f32[8,192]{1,0:T(8,128)} %param.34) | copy-start | bytes 18436
  470.7 45.8 %copy-start.42 = (f32[8,100,192]{1,2,0:T(8,128)S(1)}, f32[8,100,192]{1,2,0:T(8,128)}, u32[]{:S(2)}) copy-start(f32[8,100,192]{1,2,0:T(8,128)} %param.31) | copy-start | bytes 1843204
  470.7 45.8 %copy-start.46 = (f32[8,100,192]{1,2,0:T(8,128)S(1)}, f32[8,100,192]{1,2,0:T(8,128)}, u32[]{:S(2)}) copy-start(f32[8,100,192]{1,2,0:T(8,128)} %param.32) | copy-start | bytes 1843204
  (30 other events, 50.4 us)
Sparse Core Ops, SparseCore 0:
  10.2 21.0 all-gather.2
  33.8 37.5 reduce-scatter.2
  74.1 57.4 reduce-scatter.4

commit v4 on v3

--- a/solution.py
+++ b/solution.py
@@ -376,9 +376,10 @@
 
 
 def gather_kernel(rows_z, rows_y, *refs):
-    in_ref, out_ref, expand_ref, reduce_ref = refs[:4]
-    in_full, out_full, expand_full, reduce_full = refs[4:7], refs[7:10], refs[10:12], refs[12:14]
-    send_sem, recv_sem, local_sem = refs[14:]
+    in_ref, out_ref, expand_ref, reduce_ref, wanted_ref, table_hbm = refs[:6]
+    in_full, out_full, expand_full, reduce_full = refs[6:9], refs[9:12], refs[12:14], refs[14:16]
+    found_ref, table_low, table, stage, far, near, sister, from_core, from_x, from_sister = refs[16:26]
+    send_sem, recv_sem, local_sem, table_sem = refs[26:]
     at, v = lax.axis_index("dp"), lax.axis_index("vocab")
     z, y, x, core = at // rows_y, lax.rem(at, rows_y), v // 2, lax.rem(v, 2)
     top = rows_z - 1
@@ -536,6 +537,74 @@
 
         to_twin(i, y if tag == "x" else 1 - y, other_x, 2 if tag == "x" else 3)
 
+    valid, width = table_low.shape
+    share = far.shape[0]
+    table_copy = pltpu.make_async_copy(table_hbm, table_low, table_sem)
+    table_copy.start()
+
+    def widen(at, _):
+        here = pl.ds(pl.multiple_of(at * 32, 32), 32)
+        table[here, :] = table_low[here, :].astype(F32)
+        return 0
+
+    def prepare():
+        table_copy.wait()
+        table[valid:, :] = jnp.zeros((table.shape[0] - valid, width), F32)
+        lax.fori_loop(0, valid // 32, widen, 0)
+
+    def look_up(target, owner, part):
+        count = stage.shape[0]
+
+        def rows(at, _):
+            for step in range(8):
+                i = at * 8 + step
+                row = wanted_ref[owner * share + part * count + i]
+                stage[pl.ds(i, 1), :] = table[pl.ds(row, 1), :]
+            return 0
+
+        lax.fori_loop(0, count // 8, rows, 0)
+        target[part * count : (part + 1) * count, :] = stage[...].astype(BF16)
+
+    sums = {
+        "far": remote("far", far, from_core, twin),
+        "near": remote("near", near, from_x, across),
+        "sister": remote("sister", sister, from_sister, twin),
+    }
+
+    def send_far():
+        sums["far"].start()
+
+    def send_near():
+        sums["far"].wait_recv()
+        near[...] = (near[...].astype(F32) + from_core[...].astype(F32)).astype(BF16)
+        sums["near"].start()
+
+    def send_sister():
+        sums["sister"].start()
+
+    def finish_rows():
+        sums["sister"].wait_recv()
+        sums["near"].wait_recv()
+        total = found_ref[...].astype(F32) + from_sister[...].astype(F32)
+        found_ref[...] = (total + from_x[...].astype(F32)).astype(BF16)
+
+    jobs = [prepare]
+    for target, owner, after in (
+        (far, (1 - x) * 2 + 1 - core, send_far),
+        (near, other_x, send_near),
+        (sister, x * 2 + 1 - core, send_sister),
+        (found_ref, v, None),
+    ):
+        for part in range(share // stage.shape[0]):
+            jobs.append(functools.partial(look_up, target, owner, part))
+        if after:
+            jobs.append(after)
+    jobs = jobs[::-1]
+
+    def work(count):
+        for _ in range(min(count, len(jobs))):
+            jobs.pop()()
+
     first, second = range(starts[0], starts[1]), range(starts[1], starts[2])
     locals_ = {}
 
@@ -546,21 +615,32 @@
     for i in first:
         locals_[i] = begin(i)
     locals_[second[0]] = begin(second[0])
+    work(2)
     each(step, first, 1)
     for i in second[1:]:
         locals_[i] = begin(i)
+    work(3)
     each(came, first, 0)
+    work(1)
     each(step, first, 2)
+    work(2)
     each(came, first, 1)
+    work(1)
     each(step, second, 1)
+    work(2)
     each(step, first, 3)
     each(spread, first)
+    work(2)
     each(came, first, 2)
+    work(1)
     each(step, second, 2)
+    work(1)
     each(came, second, 0)
+    work(1)
     for i in first:
         came(i, 3)
         spread_beside(i)
+    work(len(jobs))
     each(came, second, 1)
     each(step, second, 3)
     each(spread, second)
@@ -578,6 +658,9 @@
         if units[i][3]:
             x_came(i, "x")
             x_came(i, "yx")
+    finish_rows()
+    for copy in sums.values():
+        copy.wait_send()
 
     for i, (source, target, whole, quarter) in enumerate(units):
         b = blocks[i]
@@ -603,12 +686,14 @@
                         remote((i, side, k, "yx"), piece, piece, across).wait_send()
 
 
-def gather_weights(attend_in, attend_out, expand_weights, reduce_weights):
+def gather_weights(attend_in, attend_out, expand_weights, reduce_weights, wanted, table):
     shards, rows_y = 8, 2
     rows_z = shards // rows_y
     rows = attend_in.shape[1]
     width = rows * shards
     tall = reduce_weights.shape[1]
+    share = wanted.shape[0] // 4
+    valid = table.shape[0]
 
     def full(*tail):
         return jax.ShapeDtypeStruct((rows_z, rows_y, *tail), BF16)
@@ -618,34 +703,33 @@
         + [full(rows, attend_out.shape[2])] * 3
         + [full(rows, expand_weights.shape[2])] * 2
         + [full(4, tall // 4, width)] * 2
-    )
-    copies = 10 * (1 + 4 * (rows_z - 1) + 2) + 4 * (1 + 4 * (rows_z - 1) + 2)
+        + [jax.ShapeDtypeStruct((share, width), BF16)]
+    )
+    copies = 10 * (1 + 4 * (rows_z - 1) + 2) + 4 * (1 + 4 * (rows_z - 1) + 2) + 3
+    anywhere = pl.BlockSpec(memory_space=pl.ANY)
     outs = pl.pallas_call(
         functools.partial(gather_kernel, rows_z, rows_y),
         out_shape=shapes,
-        in_specs=[pl.BlockSpec(memory_space=pl.ANY)] * 4,
-        out_specs=[pl.BlockSpec(memory_space=pl.ANY)] * 10,
+        in_specs=[anywhere] * 4 + [pl.BlockSpec(memory_space=pltpu.SMEM), anywhere],
+        out_specs=[anywhere] * 10 + [pl.BlockSpec(memory_space=pltpu.VMEM)],
         scratch_shapes=[
+            pltpu.VMEM((valid, width), BF16),
+            pltpu.VMEM((valid + 8, width), F32),
+            pltpu.VMEM((share // 3, width), F32),
+        ]
+        + [pltpu.VMEM((share, width), BF16)] * 6
+        + [
             pltpu.SemaphoreType.DMA((copies,)),
             pltpu.SemaphoreType.DMA((copies,)),
             pltpu.SemaphoreType.DMA((14,)),
+            pltpu.SemaphoreType.DMA,
         ],
         compiler_params=pltpu.CompilerParams(
             collective_id=0, has_side_effects=True, vmem_limit_bytes=60 * MIB
         ),
         cost_estimate=pl.CostEstimate(flops=0, bytes_accessed=400_000_000, transcendentals=0),
-    )(attend_in, attend_out, expand_weights, reduce_weights)
+    )(attend_in, attend_out, expand_weights, reduce_weights, wanted, table)
     return [o.reshape(-1, o.shape[-1]) for o in outs]
-
-
-def whole_weights(attend_in, attend_out, expand_weights, reduce_weights):
-    tensors = (attend_in, attend_out, expand_weights, reduce_weights)
-    shards = lax.axis_size("dp")
-    if shards != 8 or lax.axis_size("vocab") != 4:
-        whole = [lax.all_gather(tensor, "dp", axis=1, tiled=True) for tensor in tensors]
-        return (whole[0], whole[1], whole[2][:, None], whole[3][:, None])
-    flat = gather_weights(*tensors)
-    return flat[:3], flat[3:6], [[w] for w in flat[6:8]], [[w] for w in flat[8:]]
 
 
 def vocab_exchange_kernel(tile, h_ref, target_ref, table_ref, grad_ref, stat_ref, *scratch):
@@ -1064,20 +1148,33 @@
     head_targets = jnp.stack([of_rows(ids[1, m], m, p) for m, p in everyone])
     first_row = me * shard_rows
 
-    def lookup(wanted):
-        local = wanted.reshape(-1) - first_row
+    def here(wanted):
+        local = wanted - first_row
         inside = (local >= 0) & (local < shard_rows)
-        picked = jnp.take(embedding, jnp.clip(local, 0, shard_rows - 1), axis=0)
-        return jnp.where(inside[:, None], picked, 0)
-
-    enc_rows = lax.psum_scatter(lookup(enc_ids), "vocab", scatter_dimension=0, tiled=True)
-    dec_rows = lax.psum_scatter(lookup(dec_ids), "vocab", scatter_dimension=0, tiled=True)
+        return local, inside
 
     prompt_all = lax.all_gather(prompt.astype(BF16), "vocab", axis=2, tiled=True)
     prompt_flat = prompt_all.reshape(-1, width)
-    attend_in, attend_out, expand_weights, reduce_weights = whole_weights(
-        attend_in, attend_out, expand_weights, reduce_weights
-    )
+    weights = (attend_in, attend_out, expand_weights, reduce_weights)
+    if lax.axis_size("dp") == 8 and shards == 4 and shard_rows % 32 == 0:
+        local, inside = here(jnp.concatenate([enc_ids, dec_ids], 1).reshape(-1))
+        wanted = jnp.where(inside, local, shard_rows)
+        *flat, found = gather_weights(*weights, wanted, embedding)
+        attend_in, attend_out = flat[:3], flat[3:6]
+        expand_weights, reduce_weights = [[w] for w in flat[6:8]], [[w] for w in flat[8:]]
+        enc_rows, dec_rows = found[:own], found[own:]
+    else:
+
+        def lookup(wanted):
+            local, inside = here(wanted.reshape(-1))
+            picked = jnp.take(embedding, jnp.clip(local, 0, shard_rows - 1), axis=0)
+            picked = jnp.where(inside[:, None], picked, 0)
+            return lax.psum_scatter(picked, "vocab", scatter_dimension=0, tiled=True)
+
+        enc_rows, dec_rows = lookup(enc_ids), lookup(dec_ids)
+        whole = [lax.all_gather(tensor, "dp", axis=1, tiled=True) for tensor in weights]
+        attend_in, attend_out = whole[:2]
+        expand_weights, reduce_weights = whole[2][:, None], whole[3][:, None]
 
     lengths = lax.dynamic_index_in_dim(seg_lengths[:, 0], micro, 0, False)
     tasks = lax.dynamic_index_in_dim(task_ids[:, 0], micro, 0, False)

time: 533 us -> 503 us (0.944)
  local copies, waits for them, and re-layouts: 54.5 us -> 24.3 us
  Pallas kernels: 321 us -> 329 us
  other arithmetic: 43.9 us -> 37.8 us
    gather x2 -> x0, local copies, waits for them, and re-layouts: 31.1 us -> none  [lookup(): picked = jnp.take(embedding, jnp.clip(local, 0, shard_rows - 1), axis=0)]
    pallas_call x1, Pallas kernels: 140 us -> 151 us  [gather_weights(): pl.pallas_call(functools.partial(gather_kernel, rows_z, rows_y), out_shap...]
    select_n x4 -> x1, other arithmetic: 6.46 us -> 0.62 us  [on_device(): wanted = jnp.where(inside, local, shard_rows)]
    pallas_call x1, Pallas kernels: 43.2 us -> 37.8 us  [reduce_over_devices(): pl.pallas_call(functools.partial(reduce_kernel, rows_dp), out_shape=[jax....]
    unnamed x175 -> x182, local copies, waits for them, and re-layouts: 10.8 us -> 8.73 us
  transfers between devices with their start and end apart: 8 -> 6, of which waited for: 2 -> 2; matrix products, arithmetic and copies ran while one was open for 16% -> 11% of each run, Pallas kernels for 31% -> 36%
where the time goes in v4:
time: 503 us; the launch traced here: 499 us
  Pallas kernels  329 us (65%)
  matrix products  71.1 us (14%)
  other arithmetic  37.8 us (8%)
  local copies, waits for them, and re-layouts  24.3 us (5%)
  between operations  18.9 us (4%)
  waiting for transfers between devices  11.2 us (2%)
  blocking collectives  5.67 us (1%)
    pallas_call x1, Pallas kernels, gather_weights(): pl.pallas_call(functools.partial(gather_kernel, rows_z, rows_y), out_shap...  151 us
    pallas_call x1, Pallas kernels, vocab_exchange(): pl.pallas_call(functools.partial(vocab_exchange_kernel, tile), out_shape=...  63.6 us
    dot_general x6, matrix products, dot_rows(): lax.dot_general(left, right, (((1,), (1,)), ((), ())), preferred_element_...  39.3 us
    pallas_call x2, Pallas kernels, attend_back(): pl.pallas_call(functools.partial(attend_back_kernel, parts, want_queries)...  39.2 us
    pallas_call x1, Pallas kernels, reduce_over_devices(): pl.pallas_call(functools.partial(reduce_kernel, rows_dp), out_shape=[jax....  37.8 us
    pallas_call x3, Pallas kernels, attend(): pl.pallas_call(functools.partial(attend_kernel, parts, causal), out_shape...  37.3 us
    dot_general x10, matrix products, dot(): return jnp.dot(left, right, preferred_element_type=F32)  28.5 us
    ppermute x5, waiting for transfers between devices, around(): return lax.ppermute(array, 'vocab', pairs)  11.2 us
  transfers between devices with their start and end apart: 6, of which 2 were waited for; matrix products, arithmetic and copies ran while one was open for 11% of the time, Pallas kernels for 36%

profile of v4, /device:TPU:25, one launch (start us, length us, event | category | flops | bytes accessed | tf_op | source)
XLA Modules:
  0.0 499.2 jit_solution(2619047343251082681)
XLA Ops:
  7.3 1.9 convert_element_type.143
  9.3 5.7 %all-gather = s32[12,2,256]{2,1,0:T(2,128)S(1)} all-gather(s32[3,2,256]{2,1,0:T(2,128)S(1)} %pad_add_fusion.2), channel_id=2, replica_groups=mesh['dp'=8,'vocab'=4] {'vocab'}, dimensions={0}, use_global_device_ids=true | all-gather | bytes 30720 | tf_op jit(solution)/shard_map/all_gather | solution.py:1106
  16.9 151.2 %shard_map.225 = (bf16[4,2,96,2304]{3,2,1,0:T(8,128)(2,1)}, bf16[4,2,96,2304]{3,2,1,0:T(8,128)(2,1)}, bf16[4,2,96,2304]{3,2,1,0:T(8,128)(2,1)}, bf16[4,2,96,768]...) custom-call(bf16[3,96,2304]{2,1,0:T(8,128)(2,1)} %refs_0_.1, ...), custom_call_target="tpu_custom_call" | custom-call | bytes 400000000 | tf_op jit(solution)/shard_map/pallas_call | solution.py:710
  168.1 0.7 slice_reduce_fusion.6
  168.9 2.8 fusion.145
  172.0 2.6 convolution_convert_fusion.1.refs_1_
  177.3 1.4 compare_select_fusion.5
  178.7 0.7 fusion.105
  179.4 0.7 fusion.106
  180.1 0.7 fusion.103
  180.8 0.7 fusion.104
  181.5 1.8 add_minimum_fusion.1
  184.6 0.8 stack.102
  185.4 0.8 stack.101
  186.2 0.8 stack.100
  187.0 0.8 copy.132
  187.9 0.8 copy.123
  188.7 0.8 copy.121
  190.1 1.8 copy.113
  192.3 2.7 gather_fusion
  195.0 1.8 fusion.144
  197.4 1.5 convolution_convert_fusion.2.refs_1_
  199.4 1.0 copy.117.refs_6_.refs_8_
  201.1 0.7 select_reduce_fusion.5
  201.7 1.8 add_minimum_fusion
  203.6 2.2 add_subtract_fusion.target_ref
  206.4 1.8 select_convert_fusion
  208.3 2.2 convolution_convert_fusion.3.refs_0_
  210.6 14.7 %shard_map.226 = (f32[512,768]{1,0:T(8,128)S(1)}, f32[512,768]{1,0:T(8,128)S(1)}, f32[512,128]{1,0:T(8,128)S(1)}) custom-call(bf16[512,768]{1,0:T(8,128)(2,1)S(1)} %convolution_convert_fusion.3.refs_0_, bf16[512,1536]{1,0:T(8,128)(2,1)S(1)} %copy-done.13, bf16[512,1536]{1,0:T(8,128)(2,1)} %collective-permute-done.refs_2_, ...), custom_call_target="tpu_custom_call" | custom-call | flops 4026531840 | bytes 2359296 | tf_op jit(solution)/shard_map/pallas_call | solution.py:172
  225.6 2.7 fusion.54
  228.4 3.8 multiply_reduce_fusion.3
  232.6 1.4 convolution_convert_fusion.refs_1_
  234.5 2.2 convolution_convert_fusion.5.refs_0_
  236.7 12.9 %shard_map.227 = (f32[384,768]{1,0:T(8,128)S(1)}, f32[384,768]{1,0:T(8,128)}, f32[384,128]{1,0:T(8,128)}) custom-call(bf16[384,768]{1,0:T(8,128)(2,1)S(1)} %convolution_convert_fusion.5.refs_0_, bf16[512,1536]{1,0:T(8,128)(2,1)} %convolution_convert_fusion.1.refs_1_, bf16[512,1536]{1,0:T(8,128)(2,1)} %collective-permute-done.1.refs_2_, ...), custom_call_target="tpu_custom_call" | custom-call | flops 3019898880 | bytes 1769472 | tf_op jit(solution)/shard_map/pallas_call | solution.py:172
  249.8 0.7 convolution_convert_fusion.4.refs_0_
  251.1 9.6 %shard_map.228 = (f32[384,768]{1,0:T(8,128)S(1)}, f32[384,768]{1,0:T(8,128)S(1)}, f32[384,128]{1,0:T(8,128)S(1)}) custom-call(bf16[384,768]{1,0:T(8,128)(2,1)S(1)} %convolution_convert_fusion.4.refs_0_, bf16[512,1536]{1,0:T(8,128)(2,1)S(1)} %convolution_convert_fusion.refs_1_, bf16[512,1536]{1,0:T(8,128)(2,1)S(1)} %collective-permute-done.2.refs_2_, ...), custom_call_target="tpu_custom_call" | custom-call | flops 3019898880 | bytes 1769472 | tf_op jit(solution)/shard_map/pallas_call | solution.py:172
  260.7 1.0 copy-done.28
  262.7 4.4 fusion.73
  267.1 7.0 %multiply_reduce_fusion.8 = (f32[384]{0:T(512)S(1)}, f32[384,768]{1,0:T(8,128)S(1)}) fusion(f32[384,768]{1,0:T(8,128)S(1)} %get-tuple-element.58, bf16[3072,768]{1,0:T(8,128)(2,1)} %bitcast.164, f32[384,3072]{1,0:T(8,128)S(1)} %fusion.73), kind=kOutput, calls=%fused_computation.89 | convolution fusion | flops 1823440512 | bytes 11798016 | tf_op jit(solution)/shard_map/dot_general | solution.py:34
  274.1 0.8 fusion.43
  275.0 0.7 copy-done.2
  275.6 63.6 %shard_map.229 = (f32[384,768]{1,0:T(8,128)}, f32[384,128]{1,0:T(8,128)S(1)}) custom-call(bf16[384,768]{1,0:T(8,128)(2,1)S(1)} %get-tuple-element.108.h_ref, s32[4,384,1]{2,1,0:T(8,128)S(1)} %copy-done.2, bf16[8032,768]{1,0:T(8,128)(2,1)} %table_ref.1), custom_call_target="tpu_custom_call" | custom-call | flops 38654705664 | bytes 12337152 | tf_op jit(solution)/shard_map/pallas_call | solution.py:871
  339.2 2.6 fusion.99
  341.8 1.8 multiply_reduce_fusion.7
  343.7 12.4 %multiply_reduce_fusion.6 = (f32[384]{0:T(512)S(1)}, f32[384,768]{1,0:T(8,128)}) fusion(f32[384,768]{1,0:T(8,128)S(1)} %get-tuple-element.58, f32[384]{0:T(512)S(1)} %add_rsqrt_fusion.1, f32[768]{0:T(1024)S(1)} %get-tuple-element.87, bf16[768,3072]{1,0:T(8,128)(2,1)} %bitcast.163, f32[384,3072]{1,0:T(8,128)} %copy-done.85, bf16[3072,768]{1,0:T(8,128)(2,1)} %bitcast.165, ...), kind=kOutput, calls=%fused_computation.85 | convolution fusion | flops 3651599872 | bytes 19479552 | tf_op jit(solution)/shard_map/dot_general | solution.py:38
  356.1 2.9 multiply_add_fusion.2.refs_3_
  359.9 1.3 copy-done.29
  361.2 16.7 %shard_map.230 = (f32[512,1536]{1,0:T(8,128)S(1)}, f32[512,1536]{1,0:T(8,128)}) custom-call(bf16[384,768]{1,0:T(8,128)(2,1)S(1)} %copy-done.25, bf16[512,1536]{1,0:T(8,128)(2,1)S(1)} %copy-done.16, bf16[512,1536]{1,0:T(8,128)(2,1)S(1)} %copy-done.18, f32[384,768]{1,0:T(8,128)S(1)} %multiply_add_fusion.2.refs_3_, bf16[768,768]{1,0:T(8,128)(2,1)S(1)} %bitcast.113, ...), custom_call_target="tpu_custom_call" | custom-call | flops 6039797760 | bytes 5898240 | tf_op jit(solution)/shard_map/pallas_call | solution.py:270
  377.9 1.7 copy-done
  379.7 5.8 %collective-permute-done.3 = f32[512,1536]{1,0:T(8,128)} collective-permute-done((f32[512,1536]{1,0:T(8,128)}, f32[512,1536]{1,0:T(8,128)}, u32[]{:S(2)}, u32[]{:S(2)}) %collective-permute-start.3) | collective-permute-done | bytes 3145760 | tf_op jit(solution)/shard_map/ppermute | solution.py:1104
  385.6 5.1 %fusion.21 = f32[512,768]{1,0:T(8,128)S(1)} fusion(bf16[768,2304]{1,0:T(8,128)(2,1)} %bitcast.124, f32[512,1536]{1,0:T(8,128)} %copy-done, f32[512,1536]{1,0:T(8,128)} %collective-permute-done.3), kind=kOutput, calls=%fused_computation.33 | convolution fusion | flops 1211891712 | bytes 10223616 | tf_op jit(solution)/shard_map/dot_general | solution.py:38
  390.7 0.8 copy-done.48
  391.5 4.7 multiply_reduce_fusion.2
  396.2 14.3 %multiply_reduce_fusion.1 = (f32[512]{0:T(512)S(1)}, f32[512,768]{1,0:T(8,128)}) fusion(f32[512,768]{1,0:T(8,128)S(1)} %get-tuple-element.50, f32[768]{0:T(1024)S(1)} %get-tuple-element.85, f32[512]{0:T(512)S(1)} %copy-done.60, bf16[768,3072]{1,0:T(8,128)(2,1)} %bitcast.115, f32[512,3072]{1,0:T(8,128)} %copy-done.38, bf16[3072,768]{1,0:T(8,128)(2,1)} %bitcast.158, ...), kind=kOutput, calls=%fused_computation.55 | convolution fusion | flops 4866833920 | bytes 22031360 | tf_op jit(solution)/shard_map/dot_general | solution.py:38
  410.6 3.1 multiply_add_fusion.1.refs_3_
  414.5 22.5 %shard_map.231 = (f32[512,1536]{1,0:T(8,128)S(1)}, f32[512,1536]{1,0:T(8,128)S(1)}, bf16[768,512]{1,0:T(8,128)(2,1)S(1)}) custom-call(bf16[512,768]{1,0:T(8,128)(2,1)S(1)} %copy-done.27, bf16[512,1536]{1,0:T(8,128)(2,1)S(1)} %copy-done.14, bf16[512,1536]{1,0:T(8,128)(2,1)} %collective-permute-done.refs_2_, f32[512,768]{1,0:T(8,128)S(1)} %multiply_add_fusion.1.refs_3_, ...), custom_call_target="tpu_custom_call" | custom-call | flops 8053063680 | bytes 7864320 | tf_op jit(solution)/shard_map/pallas_call | solution.py:270
  437.4 5.3 %collective-permute-done.4 = f32[512,1536]{1,0:T(8,128)S(1)} collective-permute-done((f32[512,1536]{1,0:T(8,128)S(1)}, f32[512,1536]{1,0:T(8,128)S(1)}, u32[]{:S(2)}, u32[]{:S(2)}) %collective-permute-start.4) | collective-permute-done | bytes 3145760 | tf_op jit(solution)/shard_map/ppermute | solution.py:1104
  442.7 1.4 fusion.26
  444.2 1.4 fusion.28
  445.6 1.2 multiply_reduce_fusion
  446.9 1.0 fusion.70
  447.9 1.1 convolution_add_fusion.table_ref
  449.1 37.8 %shard_map.232 = (f32[8,192,128]{2,1,0:T(8,128)S(1)}, f32[8,128]{1,0:T(8,128)S(1)}, f32[8,128]{1,0:T(8,128)S(1)}) custom-call(s32[2,3]{1,0:T(2,128)S(1)} %bitcast.109, f32[768,384]{1,0:T(8,128)S(1)} %convolution_add_fusion.table_ref, f32[8,128]{1,0:T(8,128)S(1)} %select_maximum_fusion.stat_ref), custom_call_target="tpu_custom_call" | custom-call | tf_op jit(solution)/shard_map/pallas_call | solution.py:1041
  489.4 1.6 add_subtract_fusion.1
  (279 shorter events, 14.8 us)
Async XLA Ops:
  7.2 8.0 %copy-start.77 = (s32[2,1,3]{2,1,0:T(1,128)S(1)}, s32[2,1,3]{2,1,0:T(1,128)}, u32[]{:S(2)}) copy-start(s32[2,1,3]{2,1,0:T(1,128)} %param.23) | copy-start | bytes 76
  7.2 9.6 %copy-start.61 = (f32[7,768]{1,0:T(8,128)S(1)}, f32[7,768]{1,0:T(8,128)}, u32[]{:S(2)}) copy-start(f32[7,768]{1,0:T(8,128)} %param.30) | copy-start | bytes 64516
  7.2 182.9 %all-gather.3.cloned.1.call-start = ((), (), s32[]{:S(2)}) async-start(), calls=%async_computation | async-start | bytes 1966080 | tf_op jit(solution)/shard_map/all_gather | solution.py:1156
  16.9 191.4 %copy-start.65 = (f32[768]{0:T(1024)}, f32[768]{0:T(1024)S(1)}, u32[]{:S(2)}) copy-start(f32[768]{0:T(1024)S(1)} %get-tuple-element.86) | copy-start | bytes 9220
  16.9 215.4 %copy-start.67 = (f32[768]{0:T(1024)}, f32[768]{0:T(1024)S(1)}, u32[]{:S(2)}) copy-start(f32[768]{0:T(1024)S(1)} %get-tuple-element.82) | copy-start | bytes 9220
  168.8 3.1 copy-start.82
  171.9 3.5 copy-start.83
  171.9 17.6 %copy-start.10 = (s32[2,1,3]{2,1,0:T(1,128)S(1)}, s32[2,1,3]{2,1,0:T(1,128)}, u32[]{:S(2)}) copy-start(s32[2,1,3]{2,1,0:T(1,128)} %param.24) | copy-start | bytes 76
  174.6 62.1 %collective-permute-start.1 = (bf16[512,1536]{1,0:T(8,128)(2,1)}, bf16[512,1536]{1,0:T(8,128)(2,1)}, u32[]{:S(2)}, u32[]{:S(2)}) collective-permute-start(bf16[512,1536]{1,0:T(8,128)(2,1)} %convolution_convert_fusion.1.refs_1_), channel_id=1, source_target_pairs={{0,1},{1,0},{2,3},{3,2},{4,5},{5,4},{6,7},{7,6},{8,9},{9,8},{10,11... | collective-permute-start | bytes 4718600 | tf_op jit(solution)/shard_map/ppermute | solution.py:1104
  190.1 4.9 copy-start.75
  197.0 11.2 %copy-start.52 = (f32[512]{0:T(512)}, f32[512]{0:T(512)S(1)}, u32[]{:S(2)}) copy-start(f32[512]{0:T(512)S(1)} %add_rsqrt_fusion.7) | copy-start | bytes 6148
  198.9 7.5 %copy-start.12 = (bf16[512,1536]{1,0:T(8,128)(2,1)}, bf16[512,1536]{1,0:T(8,128)(2,1)S(1)}, u32[]{:S(2)}) copy-start(bf16[512,1536]{1,0:T(8,128)(2,1)S(1)} %convolution_convert_fusion.2.refs_1_) | copy-start | bytes 4718596
  198.9 11.6 %collective-permute-start = (bf16[512,1536]{1,0:T(8,128)(2,1)S(1)}, bf16[512,1536]{1,0:T(8,128)(2,1)}, u32[]{:S(2)}, u32[]{:S(2)}) collective-permute-start(bf16[512,1536]{1,0:T(8,128)(2,1)S(1)} %convolution_convert_fusion.2.refs_1_), channel_id=1, source_target_pairs={{0,1},{1,0},{2,3},{3,2},{4,5},{5,4},{6,7},{7,6},{8,9},{9,8},{10,11... | collective-permute-start | bytes 4718600 | tf_op jit(solution)/shard_map/ppermute | solution.py:1104
  200.4 5.4 %copy-start.37 = (bf16[576,768]{1,0:T(8,128)(2,1)S(1)}, bf16[576,768]{1,0:T(8,128)(2,1)}, u32[]{:S(2)}) copy-start(bf16[576,768]{1,0:T(8,128)(2,1)} %copy-done.36) | copy-start | bytes 2654212
  203.6 4.7 copy-start.33
  208.3 17.3 %slice-start = ((s8[4718592]{0:T(1024)(128)(4,1)}), s8[4194304]{0:T(1024)(128)(4,1)S(1)}, s32[]{:S(2)}) async-start(s8[4718592]{0:T(1024)(128)(4,1)} %bitcast.116), calls=%async_computation.1 | async-start | bytes 8388608
  210.5 14.8 %copy-start.26 = (bf16[512,768]{1,0:T(8,128)(2,1)}, bf16[512,768]{1,0:T(8,128)(2,1)S(1)}, u32[]{:S(2)}) copy-start(bf16[512,768]{1,0:T(8,128)(2,1)S(1)} %convolution_convert_fusion.3.refs_0_) | copy-start | bytes 2359300
  210.6 15.0 %slice-start.1 = ((s8[4718592]{0:T(1024)(128)(4,1)}), s8[524288]{0:T(1024)(128)(4,1)S(1)}, s32[]{:S(2)}) async-start(s8[4718592]{0:T(1024)(128)(4,1)} %bitcast.116), calls=%async_computation.2 | async-start | bytes 1048576
  225.4 2.9 copy-start.5
  225.4 3.0 slice-start.2
  228.3 3.9 copy-start.38
  228.4 4.3 copy-start.47
  234.1 16.4 %copy-start.15 = (bf16[512,1536]{1,0:T(8,128)(2,1)}, bf16[512,1536]{1,0:T(8,128)(2,1)S(1)}, u32[]{:S(2)}) copy-start(bf16[512,1536]{1,0:T(8,128)(2,1)S(1)} %convolution_convert_fusion.refs_1_) | copy-start | bytes 4718596
  234.1 16.4 %collective-permute-start.2 = (bf16[512,1536]{1,0:T(8,128)(2,1)S(1)}, bf16[512,1536]{1,0:T(8,128)(2,1)S(1)}, u32[]{:S(2)}, u32[]{:S(2)}) collective-permute-start(bf16[512,1536]{1,0:T(8,128)(2,1)S(1)} %convolution_convert_fusion.refs_1_), channel_id=1, source_target_pairs={{0,1},{1,0},{2,3},{3,2},{4,5},{5,4},{6,7},{7,6},{8,9},{9,8},{10,11... | collective-permute-start | bytes 4718600 | tf_op jit(solution)/shard_map/ppermute | solution.py:1104
  234.5 16.0 %copy-start.7 = (s32[384,2]{1,0:T(8,128)}, s32[384,2]{1,0:T(8,128)S(1)}, u32[]{:S(2)}) copy-start(s32[384,2]{1,0:T(8,128)S(1)} %pad_add_fusion.refs_5_.refs_7_) | copy-start | bytes 9220
  250.5 10.2 %copy-start.24 = (bf16[384,768]{1,0:T(8,128)(2,1)}, bf16[384,768]{1,0:T(8,128)(2,1)S(1)}, u32[]{:S(2)}) copy-start(bf16[384,768]{1,0:T(8,128)(2,1)S(1)} %convolution_convert_fusion.4.refs_0_) | copy-start | bytes 1769476
  250.5 10.2 %copy-start.17 = (bf16[512,1536]{1,0:T(8,128)(2,1)}, bf16[512,1536]{1,0:T(8,128)(2,1)S(1)}, u32[]{:S(2)}) copy-start(bf16[512,1536]{1,0:T(8,128)(2,1)S(1)} %collective-permute-done.2.refs_2_) | copy-start | bytes 4718596
  261.9 81.8 %copy-start.70 = (f32[384]{0:T(512)}, f32[384]{0:T(512)S(1)}, u32[]{:S(2)}) copy-start(f32[384]{0:T(512)S(1)} %add_rsqrt_fusion.1) | copy-start | bytes 4612
  267.1 7.0 %copy-start.85 = (f32[384,3072]{1,0:T(8,128)}, f32[384,3072]{1,0:T(8,128)S(1)}, u32[]{:S(2)}) copy-start(f32[384,3072]{1,0:T(8,128)S(1)} %fusion.73) | copy-start | bytes 14155780
  267.1 7.0 %copy-start.42 = (bf16[576,768]{1,0:T(8,128)(2,1)S(1)}, bf16[576,768]{1,0:T(8,128)(2,1)}, u32[]{:S(2)}) copy-start(bf16[576,768]{1,0:T(8,128)(2,1)} %get-tuple-element.113) | copy-start | bytes 2654212
  274.1 67.8 %copy-start.35 = (f32[384,768]{1,0:T(8,128)}, f32[384,768]{1,0:T(8,128)S(1)}, u32[]{:S(2)}) copy-start(f32[384,768]{1,0:T(8,128)S(1)} %get-tuple-element.134) | copy-start | bytes 3538948
  274.9 66.9 %copy-start.41 = (bf16[384,768]{1,0:T(8,128)(2,1)}, bf16[384,768]{1,0:T(8,128)(2,1)S(1)}, u32[]{:S(2)}) copy-start(bf16[384,768]{1,0:T(8,128)(2,1)S(1)} %get-tuple-element.107) | copy-start | bytes 1769476
  275.6 63.6 %copy-start.50 = (s32[384,1]{1,0:T(8,128)S(1)}, s32[384,1]{1,0:T(8,128)}, u32[]{:S(2)}) copy-start(s32[384,1]{1,0:T(8,128)} %copy.132) | copy-start | bytes 4612
  341.8 14.2 %copy-start.62 = (f32[384]{0:T(512)}, f32[384]{0:T(512)S(1)}, u32[]{:S(2)}) copy-start(f32[384]{0:T(512)S(1)} %get-tuple-element.76) | copy-start | bytes 4612
  343.7 12.4 %copy-start.71 = (f32[384]{0:T(512)}, f32[384]{0:T(512)S(1)}, u32[]{:S(2)}) copy-start(f32[384]{0:T(512)S(1)} %broadcast_multiply_fusion.2) | copy-start | bytes 4612
  356.1 3.0 copy-start.4
  356.1 3.0 copy-start.8
  356.1 3.0 copy-start.9
  356.1 3.0 copy-start.16
  356.1 3.4 copy-start.18
  356.1 3.7 copy-start.22
  356.1 3.8 copy-start.25
  361.2 18.3 %copy-start.6 = (f32[512,128]{1,0:T(8,128)S(1)}, f32[512,128]{1,0:T(8,128)}, u32[]{:S(2)}) copy-start(f32[512,128]{1,0:T(8,128)} %copy-done.5) | copy-start | bytes 786436
  379.5 6.0 %collective-permute-start.3 = (f32[512,1536]{1,0:T(8,128)}, f32[512,1536]{1,0:T(8,128)}, u32[]{:S(2)}, u32[]{:S(2)}) collective-permute-start(f32[512,1536]{1,0:T(8,128)} %get-tuple-element.66), channel_id=1, source_target_pairs={{0,1},{1,0},{2,3},{3,2},{4,5},{5,4},{6,7},{7,6},{8,9},{9,8},{10,11... | collective-permute-start | bytes 9437192 | tf_op jit(solution)/shard_map/ppermute | solution.py:1104
  385.5 5.1 %copy-start.1 = (f32[512,1536]{1,0:T(8,128)S(1)}, f32[512,1536]{1,0:T(8,128)}, u32[]{:S(2)}) copy-start(f32[512,1536]{1,0:T(8,128)} %copy-done) | copy-start | bytes 9437188
  385.5 5.1 %copy-start.40 = (f32[512,768]{1,0:T(8,128)S(1)}, f32[512,768]{1,0:T(8,128)}, u32[]{:S(2)}) copy-start(f32[512,768]{1,0:T(8,128)} %copy-done.39) | copy-start | bytes 4718596
  385.5 6.0 %copy-start.48 = (bf16[4,2,96,2304]{3,2,1,0:T(8,128)(2,1)S(1)}, bf16[4,2,96,2304]{3,2,1,0:T(8,128)(2,1)}, u32[]{:S(2)}) copy-start(bf16[4,2,96,2304]{3,2,1,0:T(8,128)(2,1)} %get-tuple-element.56) | copy-start | bytes 10616836
  385.5 6.0 %copy-start.64 = (f32[512]{0:T(512)S(1)}, f32[512]{0:T(512)}, u32[]{:S(2)}) copy-start(f32[512]{0:T(512)} %copy-done.63) | copy-start | bytes 6148
  385.6 6.0 %copy-start.68 = (f32[768]{0:T(1024)S(1)}, f32[768]{0:T(1024)}, u32[]{:S(2)}) copy-start(f32[768]{0:T(1024)} %copy-done.67) | copy-start | bytes 9220
  391.5 4.7 copy-start.60
  410.5 3.1 copy-start.14
  410.5 3.2 copy-start.20
  410.5 3.4 copy-start.27
  410.5 3.9 copy-start.31
  414.4 22.8 %copy-start.56 = (s32[512]{0:T(512)S(1)}, s32[512]{0:T(512)}, u32[]{:S(2)}) copy-start(s32[512]{0:T(512)} %copy-done.55) | copy-start | bytes 6148
  414.4 22.8 %copy-start.58 = (s32[512]{0:T(512)S(1)}, s32[512]{0:T(512)}, u32[]{:S(2)}) copy-start(s32[512]{0:T(512)} %copy-done.57) | copy-start | bytes 6148
  414.4 22.8 %copy-start.72 = (f32[384]{0:T(512)S(1)}, f32[384]{0:T(512)}, u32[]{:S(2)}) copy-start(f32[384]{0:T(512)} %get-tuple-element.75) | copy-start | bytes 4612
  414.4 22.8 %copy-start.74 = (s32[384]{0:T(512)S(1)}, s32[384]{0:T(512)}, u32[]{:S(2)}) copy-start(s32[384]{0:T(512)} %get-tuple-element.92) | copy-start | bytes 4612
  414.4 28.3 %copy-start.44 = (bf16[4,2,96,2304]{3,2,1,0:T(8,128)(2,1)S(1)}, bf16[4,2,96,2304]{3,2,1,0:T(8,128)(2,1)}, u32[]{:S(2)}) copy-start(bf16[4,2,96,2304]{3,2,1,0:T(8,128)(2,1)} %get-tuple-element.48) | copy-start | bytes 10616836
  437.0 5.7 %collective-permute-start.4 = (f32[512,1536]{1,0:T(8,128)S(1)}, f32[512,1536]{1,0:T(8,128)S(1)}, u32[]{:S(2)}, u32[]{:S(2)}) collective-permute-start(f32[512,1536]{1,0:T(8,128)S(1)} %get-tuple-element.70), channel_id=1, source_target_pairs={{0,1},{1,0},{2,3},{3,2},{4,5},{5,4},{6,7},{7,6},{8,9},{9,8},{10,11... | collective-permute-start | bytes 9437192 | tf_op jit(solution)/shard_map/ppermute | solution.py:1104
  447.9 40.9 %copy-start.78 = (f32[8,100]{1,0:T(8,128)S(1)}, f32[8,100]{1,0:T(8,128)}, u32[]{:S(2)}) copy-start(f32[8,100]{1,0:T(8,128)} %param.33) | copy-start | bytes 9604
  449.0 40.3 %copy-start.73 = (f32[8,192]{1,0:T(8,128)S(1)}, f32[8,192]{1,0:T(8,128)}, u32[]{:S(2)}) copy-start(f32[8,192]{1,0:T(8,128)} %param.34) | copy-start | bytes 18436
  449.0 40.3 %copy-start.45 = (f32[8,100,192]{1,2,0:T(8,128)S(1)}, f32[8,100,192]{1,2,0:T(8,128)}, u32[]{:S(2)}) copy-start(f32[8,100,192]{1,2,0:T(8,128)} %param.31) | copy-start | bytes 1843204
  449.1 40.3 %copy-start.49 = (f32[8,100,192]{1,2,0:T(8,128)S(1)}, f32[8,100,192]{1,2,0:T(8,128)}, u32[]{:S(2)}) copy-start(f32[8,100,192]{1,2,0:T(8,128)} %param.32) | copy-start | bytes 1843204
  (32 other events, 63.2 us)
Sparse Core Ops, SparseCore 0:
  10.2 21.0 all-gather.2

commit v5 on v4

--- a/solution.py
+++ b/solution.py
@@ -1,3 +1,4 @@
+import collections
 import functools
 
 import jax
@@ -15,6 +16,7 @@
 LANES = 128
 SEGS = 3
 VOCAB_BLOCK = 1024
+HIDDEN_PIECE = 512
 MIB = 1024 * 1024
 
 NORM_EPS = 1e-06
@@ -80,8 +82,56 @@
     return (lax.broadcasted_iota(jnp.int32, shape, axis) < DH) == (head == 0)
 
 
-def segment_columns(segment, is_key, shape):
-    column = lax.rem(lax.broadcasted_iota(jnp.int32, shape, 1), DH)
+Plan = collections.namedtuple(
+    "Plan", ["length", "group", "own", "held", "heads", "half", "starts", "near", "far"]
+)
+
+
+def chosen(index, values):
+    result = values[0]
+    for k, value in enumerate(values[1:], 1):
+        result = jnp.where(index == k, value, result)
+    return result
+
+
+def turn_of(plan, lengths_ref, m, place):
+    last = plan.length - lengths_ref[m, SEGS - 1] - plan.near[-1]
+    return jnp.where(place == 0, lengths_ref[m, 0] - P_SIZE, last)
+
+
+def row_scalars(plan, lengths_ref, decoder):
+    v = lax.axis_index("vocab")
+    m, place = v // plan.group, lax.rem(v, plan.group)
+    first = lengths_ref[m, 0]
+    ends = [first, first + lengths_ref[m, 1]]
+    if decoder:
+        rows = [
+            turn_of(plan, lengths_ref, m, place),
+            chosen(place, plan.near),
+            chosen(place, plan.far),
+        ]
+    else:
+        rows = [0, place * plan.own, place * plan.own]
+    starts = [lax.rem(place - k + plan.group, plan.group) * plan.own for k in range(plan.group)]
+    return [*ends, *rows, *starts]
+
+
+def row_positions(info, shape, axis):
+    row = lax.broadcasted_iota(jnp.int32, shape, axis)
+    return row + jnp.where(row < info[SEGS - 1], info[SEGS], info[SEGS + 1])
+
+
+def key_positions(info, parts, own, shape, axis):
+    row = lax.broadcasted_iota(jnp.int32, shape, axis)
+    position = row + info[SEGS + 2]
+    for k in range(1, parts):
+        position = jnp.where(row < k * own, position, row - k * own + info[SEGS + 2 + k])
+    return position
+
+
+def segment_columns(info, position, is_key):
+    segment = sum(jnp.where(position >= info[j], 1, 0) for j in range(SEGS - 1))
+    column = lax.rem(lax.broadcasted_iota(jnp.int32, position.shape, 1), DH)
     if is_key:
         return jnp.where((column < SEGS) & (column != segment), MASKED, 0.0).astype(BF16)
     return jnp.where(column == segment, 1.0, 0.0).astype(BF16)
@@ -111,20 +161,21 @@
     mix(pairs - 1, 1)
 
 
-def attend_kernel(parts, causal, *refs):
+def attend_kernel(plan, parts, decoder, causal, *refs):
     q_ref, pair_refs = refs[0], refs[1 : 1 + parts]
-    residual_ref, weight_ref, q_info, k_info, k_rows, out_ref, mixed_ref, log_ref = refs[
-        1 + parts : 9 + parts
-    ]
-    bias_ref, q_mark, k_mark, low_ref, scores_a, scores_b, powers_a, powers_b = refs[9 + parts :]
+    residual_ref, weight_ref, lengths_ref, out_ref, mixed_ref, log_ref = refs[1 + parts : 7 + parts]
+    info = row_scalars(plan, lengths_ref, decoder)
+    bias_ref, q_mark, k_mark, low_ref, scores_a, scores_b, powers_a, powers_b = refs[7 + parts :]
     width = q_ref.shape[1]
     own = pair_refs[0].shape[0]
     scores_of, powers_of = (scores_a, scores_b), (powers_a, powers_b)
     rows = [slice(k * own, (k + 1) * own) for k in range(parts)]
-    q_mark[...] = segment_columns(q_info[:, 0:1], False, q_mark.shape)
-    k_mark[...] = segment_columns(k_info[:, 0:1], True, k_mark.shape)
+    q_mark[...] = segment_columns(info, row_positions(info, q_mark.shape, 0), False)
+    k_mark[...] = segment_columns(info, key_positions(info, parts, own, k_mark.shape, 0), True)
     if causal:
-        bias_ref[...] = jnp.where(q_info[:, 1:2] >= k_rows[...], 0.0, MASKED)
+        shape = bias_ref.shape
+        later = row_positions(info, shape, 0) >= key_positions(info, parts, own, shape, 1)
+        bias_ref[...] = jnp.where(later, 0.0, MASKED)
     log_ref[...] = jnp.zeros_like(log_ref)
     lane = lax.broadcasted_iota(jnp.int32, log_ref.shape, 1)
 
@@ -165,21 +216,21 @@
     out_ref[...] = residual_ref[...] + dot(low_ref[...], weight_ref[...])
 
 
-def attend(queries, pairs, residual, weight, q_info, k_info, causal):
+def attend(plan, queries, pairs, residual, weight, row_lengths, decoder, causal):
     own, width = queries.shape
-    parts, length = len(pairs), k_info.shape[0]
+    parts, length = len(pairs), sum(pair.shape[0] for pair in pairs)
     vmem = pl.BlockSpec(memory_space=pltpu.VMEM)
     return pl.pallas_call(
-        functools.partial(attend_kernel, parts, causal),
+        functools.partial(attend_kernel, plan, parts, decoder, causal),
         out_shape=[
             jax.ShapeDtypeStruct((own, width), F32),
             jax.ShapeDtypeStruct((own, width), F32),
             jax.ShapeDtypeStruct((own, LANES), F32),
         ],
-        in_specs=[vmem] * (parts + 6),
+        in_specs=[vmem] * (parts + 3) + [pl.BlockSpec(memory_space=pltpu.SMEM)],
         out_specs=[vmem] * 3,
         scratch_shapes=[
-            pltpu.VMEM((own, length), F32),
+            pltpu.VMEM((own, length) if causal else (8, LANES), F32),
             pltpu.VMEM((own, LANES), BF16),
             pltpu.VMEM((length, LANES), BF16),
             pltpu.VMEM((own, width), BF16),
@@ -188,27 +239,47 @@
             pltpu.VMEM((own, length), BF16),
             pltpu.VMEM((own, length), BF16),
         ],
-        compiler_params=pltpu.CompilerParams(vmem_limit_bytes=26 * MIB),
+        compiler_params=pltpu.CompilerParams(vmem_limit_bytes=24 * MIB),
         cost_estimate=pl.CostEstimate(
-            flops=10 * own * length * width, bytes_accessed=6 * own * width, transcendentals=0
+            flops=44 * own * length * width, bytes_accessed=6 * own * width, transcendentals=0
         ),
-    )(queries, *pairs, residual, weight, q_info, k_info, k_info[:, 1:].T)
-
-
-def attend_back_kernel(parts, want_queries, *refs):
+    )(queries, *pairs, residual, weight, row_lengths)
+
+
+def attend_back_kernel(plan, parts, decoder, want_queries, exchange, *refs):
     q_ref, pair_refs = refs[0], refs[1 : 1 + parts]
-    grad_ref, weight_ref, mixed_ref, log_ref, q_info, k_info = refs[1 + parts : 7 + parts]
-    rest = refs[7 + parts :]
-    out_refs = rest[:parts]
-    dq_ref = rest[parts] if want_queries else None
-    q_mark, k_mark, low_ref, delta_ref, *rest = rest[parts + want_queries :]
+    grad_ref, weight_ref, mixed_ref, log_ref, lengths_ref = refs[1 + parts : 6 + parts]
+    info = row_scalars(plan, lengths_ref, decoder)
+    rest = refs[6 + parts :]
+    if exchange:
+        in_hbm, rows_hbm, gain_ref, result_ref = rest[:4]
+        part_refs, arrived, send_sem, recv_sem = rest[4:6], rest[6], rest[7], rest[8]
+        dq_ref, in_ref, rows_ref, late_sems = rest[9:13]
+        rest = rest[13:]
+        late = [
+            pltpu.make_async_copy(in_hbm, in_ref, late_sems.at[0]),
+            pltpu.make_async_copy(rows_hbm, rows_ref, late_sems.at[1]),
+        ]
+        for copy in late:
+            copy.start()
+        v = lax.axis_index("vocab")
+        twin = {"vocab": v // 2 * 2 + 1 - lax.rem(v, 2)}
+        barrier = pltpu.get_barrier_semaphore()
+        pl.semaphore_signal(barrier, inc=1, device_id=twin, device_id_type=pl.DeviceIdType.MESH)
+        pl.semaphore_wait(barrier, 1)
+    else:
+        part_refs = rest[:parts]
+        dq_ref = rest[parts] if want_queries else None
+        rest = rest[parts + want_queries :]
+    q_mark, k_mark, low_ref, delta_ref, *rest = rest
     scores_of, grads_of, weights_of, steps_of = rest[0:2], rest[2:4], rest[4:6], rest[6:8]
     width = q_ref.shape[1]
     own = pair_refs[0].shape[0]
+    pairs = width // LANES
     rows = [slice(k * own, (k + 1) * own) for k in range(parts)]
     scale = jnp.asarray(DH ** (-0.5), BF16)
-    q_mark[...] = segment_columns(q_info[:, 0:1], False, q_mark.shape)
-    k_mark[...] = segment_columns(k_info[:, 0:1], True, k_mark.shape)
+    q_mark[...] = segment_columns(info, row_positions(info, q_mark.shape, 0), False)
+    k_mark[...] = segment_columns(info, key_positions(info, parts, own, k_mark.shape, 0), True)
     low_ref[...] = dot_rows(grad_ref[...].astype(BF16), weight_ref[...]).astype(BF16)
     product = low_ref[...].astype(F32) * mixed_ref[...]
     high = product.astype(BF16)
@@ -236,75 +307,296 @@
         weights_of[head][...] = weights.astype(BF16)
         steps_of[head][...] = (weights * (grads_of[head][...] - delta_ref[at, :])).astype(BF16)
 
+    def away(pair, which):
+        lanes = pair_lanes(pair, which * width)
+        return pltpu.make_async_remote_copy(
+            src_ref=part_refs[1].at[:, lanes],
+            dst_ref=arrived.at[:, lanes],
+            send_sem=send_sem.at[pair, which],
+            recv_sem=recv_sem.at[pair, which],
+            device_id=twin,
+            device_id_type=pl.DeviceIdType.MESH,
+        )
+
     def mix(pair, head):
         keys, values = pair_lanes(pair), pair_lanes(pair, width)
         query, grad = q_ref[:, keys] * scale, low_ref[:, keys]
         query = head_part(query, jnp.zeros_like(query), head)
         grad = head_part(grad, jnp.zeros_like(grad), head)
         dq = None
-        for k in range(parts):
+        for k in reversed(range(parts)):
             step = steps_of[head][rows[k], :]
             dk = dot(step, query)
             dv = dot(weights_of[head][rows[k], :], grad)
-            out_refs[k][:, keys] = dk if head == 0 else out_refs[k][:, keys] + dk
-            out_refs[k][:, values] = dv if head == 0 else out_refs[k][:, values] + dv
+            part_refs[k][:, keys] = dk if head == 0 else part_refs[k][:, keys] + dk
+            part_refs[k][:, values] = dv if head == 0 else part_refs[k][:, values] + dv
             if want_queries:
                 term = dot_columns(pair_refs[k][:, keys], step)
                 dq = term if dq is None else dq + term
         if want_queries:
             here = pl.ds(pl.multiple_of(pair * LANES, LANES), LANES)
-            dq = (dq * DH ** (-0.5)).astype(BF16)
+            dq = dq * DH ** (-0.5)
             if head:
-                dq = jnp.where(head_mask(dq.shape, 0, 0), dq_ref[here, :], dq)
-            dq_ref[here, :] = dq
-
-    over_heads(width // LANES, scores, soften, mix)
-
-
-def attend_back(queries, pairs, gradient, weight, mixed, logs, q_info, k_info, want_queries):
-    own, width = queries.shape
-    parts, length = len(pairs), k_info.shape[0]
-    shapes = [jax.ShapeDtypeStruct(pair.shape, F32) for pair in pairs]
+                dq = jnp.where(head_mask(dq.shape, 0, 0), dq_ref[here, :].astype(F32), dq)
+            dq_ref[here, :] = dq.astype(dq_ref.dtype)
+        if exchange and head:
+            away(pair, 0).start()
+            away(pair, 1).start()
+
+    over_heads(pairs, scores, soften, mix)
+    if not exchange:
+        return
+    total = None
+    for copy in late:
+        copy.wait()
     if want_queries:
-        shapes.append(jax.ShapeDtypeStruct((width, own), BF16))
+        total = dot_rows(jnp.transpose(dq_ref[...]).astype(BF16), in_ref[:, :width])
+    for pair in range(pairs):
+        away(pair, 0).wait_recv()
+        away(pair, 1).wait_recv()
+    both = part_refs[0][...] + arrived[...]
+    high = both.astype(BF16)
+    low = (both - high.astype(F32)).astype(BF16)
+    back = dot_rows(high, in_ref[:, width:]) + dot_rows(low, in_ref[:, width:])
+    total = back if total is None else total + back
+    values, gain = rows_ref[...], gain_ref[...]
+    inverse = lax.rsqrt(jnp.mean(values * values, -1, keepdims=True) + NORM_EPS)
+    total = normed_back(values, gain, inverse, total)
+    result_ref[...] = grad_ref[...] + total if want_queries else total
+    for pair in range(pairs):
+        away(pair, 0).wait_send()
+        away(pair, 1).wait_send()
+
+
+def attend_back(
+    plan, queries, pairs, gradient, weight, mixed, logs, row_lengths, decoder, want_queries, through
+):
+    heads, width = queries.shape
+    own = pairs[0].shape[0]
+    parts, length = len(pairs), sum(pair.shape[0] for pair in pairs)
+    vmem = pl.BlockSpec(memory_space=pltpu.VMEM)
+    operands = [queries, *pairs, gradient, weight, mixed, logs.T[:16], row_lengths]
+    in_specs = [vmem] * (parts + 5) + [pl.BlockSpec(memory_space=pltpu.SMEM)]
+    scratch = [
+        pltpu.VMEM((heads, LANES), BF16),
+        pltpu.VMEM((length, LANES), BF16),
+        pltpu.VMEM((heads, width), BF16),
+        pltpu.VMEM((16, heads), F32),
+    ]
+    scratch += [pltpu.VMEM((length, heads), F32)] * 4 + [pltpu.VMEM((length, heads), BF16)] * 4
+    if through:
+        attend_in, rows, gain, collective_id = through
+        operands += [attend_in, rows, gain[None]]
+        in_specs += [pl.BlockSpec(memory_space=pl.ANY)] * 2 + [vmem]
+        shapes = jax.ShapeDtypeStruct(rows.shape, F32)
+        out_specs = vmem
+        each = pltpu.SemaphoreType.DMA((width // LANES, 2))
+        scratch = (
+            [pltpu.VMEM((own, 2 * width), F32)] * 3
+            + [each, each, pltpu.VMEM((width, heads) if want_queries else (8, LANES), F32)]
+            + [pltpu.VMEM(attend_in.shape, BF16), pltpu.VMEM(rows.shape, F32)]
+            + [pltpu.SemaphoreType.DMA((2,))]
+            + scratch
+        )
+        params = pltpu.CompilerParams(
+            collective_id=collective_id, has_side_effects=True, vmem_limit_bytes=46 * MIB
+        )
+    else:
+        shapes = [jax.ShapeDtypeStruct(pair.shape, F32) for pair in pairs]
+        if want_queries:
+            shapes.append(jax.ShapeDtypeStruct((width, heads), BF16))
+        out_specs = [vmem] * len(shapes)
+        params = pltpu.CompilerParams(vmem_limit_bytes=34 * MIB)
     return pl.pallas_call(
-        functools.partial(attend_back_kernel, parts, want_queries),
+        functools.partial(
+            attend_back_kernel, plan, parts, decoder, want_queries, through is not None
+        ),
         out_shape=shapes,
-        in_specs=[pl.BlockSpec(memory_space=pltpu.VMEM)] * (parts + 7),
-        out_specs=[pl.BlockSpec(memory_space=pltpu.VMEM)] * len(shapes),
-        scratch_shapes=[
-            pltpu.VMEM((own, LANES), BF16),
-            pltpu.VMEM((length, LANES), BF16),
-            pltpu.VMEM((own, width), BF16),
-            pltpu.VMEM((16, own), F32),
-        ]
-        + [pltpu.VMEM((length, own), F32)] * 4
-        + [pltpu.VMEM((length, own), BF16)] * 4,
-        compiler_params=pltpu.CompilerParams(vmem_limit_bytes=34 * MIB),
+        in_specs=in_specs,
+        out_specs=out_specs,
+        scratch_shapes=scratch,
+        compiler_params=params,
         cost_estimate=pl.CostEstimate(
-            flops=20 * own * length * width, bytes_accessed=20 * own * width, transcendentals=0
+            flops=80 * heads * length * width, bytes_accessed=20 * own * width, transcendentals=0
         ),
-    )(queries, *pairs, gradient, weight, mixed, logs.T[:16], q_info, k_info)
-
-
-def feed(rows, gain, weights_one, weights_two):
-    values, inverse = normed(rows, gain)
-    source = values.astype(BF16)
-    before = [dot(source, one) for one in weights_one]
-    for pre, two in zip(before, weights_two):
-        rows = rows + dot(smooth(pre).astype(BF16), two)
-    return rows, (before, inverse)
-
-
-def feed_back(gradient, rows, gain, kept, weights_one, weights_two):
-    before, inverse = kept
-    low = gradient.astype(BF16)
-    total = 0.0
-    for pre, one, two in zip(before, weights_one, weights_two):
-        active_grad = dot_rows(low, two)
-        step = jax.vjp(smooth, pre)[1](active_grad)[0].astype(BF16)
-        total = total + dot_rows(step, one)
-    return gradient + normed_back(rows, gain, inverse, total)
+    )(*operands)
+
+
+def feed_kernel(rows_ref, gain_ref, one_ref, two_ref, out_ref, before_ref, source, *scratch):
+    held_of, active_of = scratch[0:2], scratch[2:4]
+    count = one_ref.shape[1] // HIDDEN_PIECE
+    rows = rows_ref[...]
+    source[...] = normed(rows, gain_ref[...])[0].astype(BF16)
+    out_ref[...] = rows
+    for n in range(count + 2):
+        if n < count:
+            here = slice(n * HIDDEN_PIECE, (n + 1) * HIDDEN_PIECE)
+            before = dot(source[...], one_ref[:, here])
+            held_of[n % 2][...] = before
+            before_ref[:, here] = before
+        if 0 < n <= count:
+            active_of[(n - 1) % 2][...] = smooth(held_of[(n - 1) % 2][...]).astype(BF16)
+        if n >= 2:
+            there = slice((n - 2) * HIDDEN_PIECE, (n - 1) * HIDDEN_PIECE)
+            out_ref[...] += dot(active_of[n % 2][...], two_ref[there, :])
+
+
+def feed(rows, gain, one, two):
+    own, width = rows.shape
+    hidden = one.shape[1]
+    vmem = pl.BlockSpec(memory_space=pltpu.VMEM)
+    return pl.pallas_call(
+        feed_kernel,
+        out_shape=[
+            jax.ShapeDtypeStruct((own, width), F32),
+            jax.ShapeDtypeStruct((own, hidden), F32),
+        ],
+        in_specs=[vmem] * 4,
+        out_specs=[vmem] * 2,
+        scratch_shapes=[pltpu.VMEM((own, width), BF16)]
+        + [pltpu.VMEM((own, HIDDEN_PIECE), F32)] * 2
+        + [pltpu.VMEM((own, HIDDEN_PIECE), BF16)] * 2,
+        compiler_params=pltpu.CompilerParams(vmem_limit_bytes=28 * MIB),
+        cost_estimate=pl.CostEstimate(
+            flops=4 * own * width * hidden, bytes_accessed=4 * width * hidden, transcendentals=0
+        ),
+    )(rows, gain[None], one, two)
+
+
+def smooth_slope(u):
+    rate = (2.0 / jnp.pi) ** 0.5
+    bend = jnp.tanh(rate * (u + 0.044715 * (u * u * u)))
+    inner = rate * (1.0 + 3.0 * 0.044715 * (u * u))
+    return 0.5 * (1.0 + bend) + 0.5 * u * (1.0 - bend * bend) * inner
+
+
+def feed_back_kernel(grad_ref, rows_ref, gain_ref, before_ref, one_ref, two_ref, out_ref, low, *scratch):
+    active_of, step_of = scratch[0:2], scratch[2:4]
+    count = one_ref.shape[1] // HIDDEN_PIECE
+    low[...] = grad_ref[...].astype(BF16)
+    out_ref[...] = jnp.zeros_like(out_ref)
+    for n in range(count + 2):
+        if n < count:
+            here = slice(n * HIDDEN_PIECE, (n + 1) * HIDDEN_PIECE)
+            active_of[n % 2][...] = dot_rows(low[...], two_ref[here, :])
+        if 0 < n <= count:
+            here = slice((n - 1) * HIDDEN_PIECE, n * HIDDEN_PIECE)
+            step_of[(n - 1) % 2][...] = (
+                active_of[(n - 1) % 2][...] * smooth_slope(before_ref[:, here])
+            ).astype(BF16)
+        if n >= 2:
+            here = slice((n - 2) * HIDDEN_PIECE, (n - 1) * HIDDEN_PIECE)
+            out_ref[...] += dot_rows(step_of[n % 2][...], one_ref[:, here])
+    rows = rows_ref[...]
+    inverse = lax.rsqrt(jnp.mean(rows * rows, -1, keepdims=True) + NORM_EPS)
+    out_ref[...] = grad_ref[...] + normed_back(rows, gain_ref[...], inverse, out_ref[...])
+
+
+def feed_back(gradient, rows, gain, before, one, two):
+    own, width = rows.shape
+    hidden = one.shape[1]
+    vmem = pl.BlockSpec(memory_space=pltpu.VMEM)
+    return pl.pallas_call(
+        feed_back_kernel,
+        out_shape=jax.ShapeDtypeStruct((own, width), F32),
+        in_specs=[vmem] * 6,
+        out_specs=vmem,
+        scratch_shapes=[pltpu.VMEM((own, width), BF16)]
+        + [pltpu.VMEM((own, HIDDEN_PIECE), F32)] * 2
+        + [pltpu.VMEM((own, HIDDEN_PIECE), BF16)] * 2,
+        compiler_params=pltpu.CompilerParams(vmem_limit_bytes=30 * MIB),
+        cost_estimate=pl.CostEstimate(
+            flops=4 * own * width * hidden, bytes_accessed=4 * width * hidden, transcendentals=0
+        ),
+    )(gradient, rows, gain[None], before, one, two)
+
+
+def prompted(plan, rows_ref, prompt_ref, lengths_ref, tasks_ref):
+    info = row_scalars(plan, lengths_ref, False)
+    m = lax.axis_index("vocab") // plan.group
+    shape = (plan.own, LANES)
+    position = row_positions(info, shape, 0)
+    lane = lax.broadcasted_iota(jnp.int32, shape, 1)
+    begin = jnp.where(position >= info[1], info[1], jnp.where(position >= info[0], info[0], 0))
+    place = position - begin
+    total = None
+    for j, start in enumerate([0, info[0], info[1]]):
+        hit = (begin == start) & (place == lane) & (place < P_SIZE)
+        term = dot_rows(jnp.where(hit, 1.0, 0.0).astype(BF16), prompt_ref[tasks_ref[m, j]])
+        total = term if total is None else total + term
+    return jnp.where(place[:, 0:1] < P_SIZE, total, rows_ref[...].astype(F32))
+
+
+def project_kernel(plan, *refs):
+    rows_ref, prompt_ref, keys_ref, heads_ref, gain_ref, lengths_ref, tasks_ref = refs[:7]
+    first_hbm, second_hbm, out_ref, enc_q, enc_own, enc_other, dec_q, dec_own, dec_other = refs[7:16]
+    first, second, sems, send_sem, recv_sem = refs[16:]
+    width = rows_ref.shape[1]
+    v = lax.axis_index("vocab")
+    twin = {"vocab": v // 2 * 2 + 1 - lax.rem(v, 2)}
+    barrier = pltpu.get_barrier_semaphore()
+    pl.semaphore_signal(barrier, inc=1, device_id=twin, device_id_type=pl.DeviceIdType.MESH)
+    pl.semaphore_wait(barrier, 1)
+    loads = [
+        pltpu.make_async_copy(first_hbm, first, sems.at[0]),
+        pltpu.make_async_copy(second_hbm, second, sems.at[1]),
+    ]
+    for load in loads:
+        load.start()
+
+    def share(source, target, index):
+        return pltpu.make_async_remote_copy(
+            src_ref=source,
+            dst_ref=target,
+            send_sem=send_sem.at[index],
+            recv_sem=recv_sem.at[index],
+            device_id=twin,
+            device_id_type=pl.DeviceIdType.MESH,
+        )
+
+    shares = [share(enc_own, enc_other, 0), share(dec_own, dec_other, 1)]
+    rows = prompted(plan, rows_ref, prompt_ref, lengths_ref, tasks_ref)
+    out_ref[...] = rows
+    low = normed(rows, gain_ref[...])[0].astype(BF16)
+    loads[0].wait()
+    enc_own[...] = dot(low, first[:, width:]).astype(BF16)
+    shares[0].start()
+    enc_q[...] = dot(low, first[:, :width]).astype(BF16)
+    loads[1].wait()
+    dec_own[...] = dot(keys_ref[...], second[:, width:]).astype(BF16)
+    shares[1].start()
+    dec_q[...] = dot(heads_ref[...], second[:, :width]).astype(BF16)
+    for copy in shares:
+        copy.wait()
+
+
+def project(plan, rows, prompts, keys, heads, gain, row_lengths, row_tasks, first, second):
+    width = rows.shape[1]
+    vmem, smem = pl.BlockSpec(memory_space=pltpu.VMEM), pl.BlockSpec(memory_space=pltpu.SMEM)
+    anywhere = pl.BlockSpec(memory_space=pl.ANY)
+    pair = jax.ShapeDtypeStruct((plan.own, 2 * width), BF16)
+    outs = pl.pallas_call(
+        functools.partial(project_kernel, plan),
+        out_shape=[
+            jax.ShapeDtypeStruct(rows.shape, F32),
+            jax.ShapeDtypeStruct(rows.shape, BF16),
+            pair,
+            pair,
+            jax.ShapeDtypeStruct(heads.shape, BF16),
+            pair,
+            pair,
+        ],
+        in_specs=[vmem] * 5 + [smem] * 2 + [anywhere] * 2,
+        out_specs=[vmem] * 7,
+        scratch_shapes=[pltpu.VMEM(first.shape, BF16)] * 2 + [pltpu.SemaphoreType.DMA((2,))] * 3,
+        compiler_params=pltpu.CompilerParams(
+            collective_id=5, has_side_effects=True, vmem_limit_bytes=40 * MIB
+        ),
+        cost_estimate=pl.CostEstimate(
+            flops=10 * rows.size * width, bytes_accessed=4 * first.size, transcendentals=0
+        ),
+    )(rows, prompts, keys, heads, gain[None], row_lengths, row_tasks, first, second)
+    return outs[0], outs[1], outs[2:4], outs[4], outs[5:7]
 
 
 def vocab_kernel(tile, valid, h_ref, target_ref, table_hbm, grad_ref, stat_ref, table, sem):
@@ -375,11 +667,12 @@
     )(hidden, target_local, embedding)
 
 
-def gather_kernel(rows_z, rows_y, *refs):
-    in_ref, out_ref, expand_ref, reduce_ref, wanted_ref, table_hbm = refs[:6]
-    in_full, out_full, expand_full, reduce_full = refs[6:9], refs[9:12], refs[12:14], refs[14:16]
-    found_ref, table_low, table, stage, far, near, sister, from_core, from_x, from_sister = refs[16:26]
-    send_sem, recv_sem, local_sem, table_sem = refs[26:]
+def gather_kernel(plan, rows_z, rows_y, *refs):
+    in_ref, out_ref, expand_ref, reduce_ref, wanted_ref, table_hbm, lengths_ref, gain_ref = refs[:8]
+    in_full, out_full, expand_full, reduce_full = refs[8:11], refs[11:14], refs[14:16], refs[16:18]
+    enc_rows, dec_keys, dec_rows, dec_heads, target_rows = refs[18:23]
+    found_ref, table_low, table, stage, far, near, sister, from_core, from_x, from_sister = refs[23:33]
+    send_sem, recv_sem, local_sem, table_sem = refs[33:]
     at, v = lax.axis_index("dp"), lax.axis_index("vocab")
     z, y, x, core = at // rows_y, lax.rem(at, rows_y), v // 2, lax.rem(v, 2)
     top = rows_z - 1
@@ -558,7 +851,7 @@
         def rows(at, _):
             for step in range(8):
                 i = at * 8 + step
-                row = wanted_ref[owner * share + part * count + i]
+                row = wanted_ref[owner, part * count + i]
                 stage[pl.ds(i, 1), :] = table[pl.ds(row, 1), :]
             return 0
 
@@ -586,7 +879,39 @@
         sums["sister"].wait_recv()
         sums["near"].wait_recv()
         total = found_ref[...].astype(F32) + from_sister[...].astype(F32)
-        found_ref[...] = (total + from_x[...].astype(F32)).astype(BF16)
+        table[:share, :] = total + from_x[...].astype(F32)
+        enc_rows[...] = table[: plan.own, :].astype(BF16)
+        ends = [lengths_ref[x, 0], lengths_ref[x, 0] + lengths_ref[x, 1]]
+        position = lax.broadcasted_iota(jnp.int32, (plan.held, 1), 0) + chosen(core, plan.starts)
+        first_of = (position == 0) | (position == ends[0]) | (position == ends[1])
+        base, held = plan.own + HALO, 2 * plan.own + plan.held
+        table[held : held + plan.held, :] = jnp.where(
+            first_of,
+            table[plan.own : plan.own + 1, :],
+            table[base - 1 : base - 1 + plan.held, :],
+        )
+        shift = held + core * (plan.own - plan.starts[1])
+        keys = table[pl.ds(pl.multiple_of(shift, HALO), plan.own), :]
+        gain = gain_ref[...]
+        dec_keys[...] = normed(keys, gain)[0].astype(BF16)
+        before_turn = lax.broadcasted_iota(jnp.int32, (plan.heads, 1), 0) < turn_of(
+            plan, lengths_ref, x, core
+        )
+
+        def own_heads(first):
+            def rows(offsets):
+                first_place, second_place = [
+                    table[first + o - s : first + o - s + plan.heads, :]
+                    for o, s in zip(offsets, plan.starts)
+                ]
+                return jnp.where(core == 0, first_place, second_place)
+
+            return jnp.where(before_turn, rows(plan.near), rows(plan.far))
+
+        values = own_heads(held)
+        dec_rows[...] = values.astype(BF16)
+        dec_heads[...] = normed(values, gain)[0].astype(BF16)
+        target_rows[...] = own_heads(base).astype(BF16)
 
     jobs = [prepare]
     for target, owner, after in (
@@ -619,28 +944,27 @@
     each(step, first, 1)
     for i in second[1:]:
         locals_[i] = begin(i)
-    work(3)
+    work(2)
     each(came, first, 0)
+    work(2)
+    each(step, first, 2)
     work(1)
-    each(step, first, 2)
+    each(came, first, 1)
     work(2)
-    each(came, first, 1)
-    work(1)
     each(step, second, 1)
     work(2)
     each(step, first, 3)
     each(spread, first)
     work(2)
     each(came, first, 2)
-    work(1)
+    work(2)
     each(step, second, 2)
     work(1)
     each(came, second, 0)
-    work(1)
+    work(len(jobs))
     for i in first:
         came(i, 3)
         spread_beside(i)
-    work(len(jobs))
     each(came, second, 1)
     each(step, second, 3)
     each(spread, second)
@@ -648,6 +972,7 @@
         if units[i][3]:
             x_came(i, "x")
     each(came, second, 2)
+    finish_rows()
     for i in first:
         if units[i][3]:
             x_came(i, "yx")
@@ -658,7 +983,6 @@
         if units[i][3]:
             x_came(i, "x")
             x_came(i, "yx")
-    finish_rows()
     for copy in sums.values():
         copy.wait_send()
 
@@ -686,13 +1010,15 @@
                         remote((i, side, k, "yx"), piece, piece, across).wait_send()
 
 
-def gather_weights(attend_in, attend_out, expand_weights, reduce_weights, wanted, table):
+def gather_weights(
+    plan, attend_in, attend_out, expand_weights, reduce_weights, wanted, table, row_lengths, gain
+):
     shards, rows_y = 8, 2
     rows_z = shards // rows_y
     rows = attend_in.shape[1]
     width = rows * shards
     tall = reduce_weights.shape[1]
-    share = wanted.shape[0] // 4
+    share = wanted.shape[1]
     valid = table.shape[0]
 
     def full(*tail):
@@ -703,16 +1029,19 @@
         + [full(rows, attend_out.shape[2])] * 3
         + [full(rows, expand_weights.shape[2])] * 2
         + [full(4, tall // 4, width)] * 2
-        + [jax.ShapeDtypeStruct((share, width), BF16)]
+        + [jax.ShapeDtypeStruct((n, width), BF16) for n in [plan.own] * 2 + [plan.heads] * 3]
     )
     copies = 10 * (1 + 4 * (rows_z - 1) + 2) + 4 * (1 + 4 * (rows_z - 1) + 2) + 3
-    anywhere = pl.BlockSpec(memory_space=pl.ANY)
+    anywhere, vmem, smem = [
+        pl.BlockSpec(memory_space=space) for space in (pl.ANY, pltpu.VMEM, pltpu.SMEM)
+    ]
     outs = pl.pallas_call(
-        functools.partial(gather_kernel, rows_z, rows_y),
+        functools.partial(gather_kernel, plan, rows_z, rows_y),
         out_shape=shapes,
-        in_specs=[anywhere] * 4 + [pl.BlockSpec(memory_space=pltpu.SMEM), anywhere],
-        out_specs=[anywhere] * 10 + [pl.BlockSpec(memory_space=pltpu.VMEM)],
+        in_specs=[anywhere] * 4 + [smem, anywhere, smem, vmem],
+        out_specs=[anywhere] * 10 + [vmem] * 5,
         scratch_shapes=[
+            pltpu.VMEM((share, width), BF16),
             pltpu.VMEM((valid, width), BF16),
             pltpu.VMEM((valid + 8, width), F32),
             pltpu.VMEM((share // 3, width), F32),
@@ -728,13 +1057,16 @@
             collective_id=0, has_side_effects=True, vmem_limit_bytes=60 * MIB
         ),
         cost_estimate=pl.CostEstimate(flops=0, bytes_accessed=400_000_000, transcendentals=0),
-    )(attend_in, attend_out, expand_weights, reduce_weights, wanted, table)
+    )(attend_in, attend_out, expand_weights, reduce_weights, wanted, table, row_lengths, gain[None])
     return [o.reshape(-1, o.shape[-1]) for o in outs]
 
 
-def vocab_exchange_kernel(tile, h_ref, target_ref, table_ref, grad_ref, stat_ref, *scratch):
+def vocab_exchange_kernel(plan, tile, *refs):
+    rows_ref, gain_ref, target_ref, table_ref, ids_ref, lengths_ref, tasks_ref = refs[:7]
+    grad_ref, stat_ref, *scratch = refs[7:]
     tail, held, logits_a, logits_b, powers_a, powers_b, scale_a, scale_b = scratch[:8]
-    maxima_ref, total_ref, parcel, arrived, send_sem, recv_sem = scratch[8:]
+    maxima_ref, total_ref, targets_ref, h_ref, columns, parcel, arrived = scratch[8:15]
+    stats_out, stats_in, send_sem, recv_sem = scratch[15:]
     rows, width = h_ref.shape
     valid = table_ref.shape[0]
     tiles = (valid + tile - 1) // tile
@@ -760,6 +1092,10 @@
             device_id_type=pl.DeviceIdType.MESH,
         )
 
+    values = rows_ref[...]
+    gain = gain_ref[...]
+    inverse = lax.rsqrt(jnp.mean(values * values, -1, keepdims=True) + NORM_EPS)
+    h_ref[...] = (values * inverse * gain * width ** (-0.5)).astype(BF16)
     to_twin = remote(h_ref, held.at[0], 0, twin)
     to_across = remote(h_ref, held.at[1], 1, across)
     passed_on = remote(held.at[1], held.at[2], 2, twin)
@@ -767,9 +1103,25 @@
         remote(parcel.at[k], arrived.at[k], 3 + k, peer)
         for k, peer in enumerate((twin, across, diagonal))
     ]
+    marks = [
+        remote(stats_out.at[k], stats_in.at[k], 6 + k, peer)
+        for k, peer in enumerate((twin, across, diagonal))
+    ]
     to_twin.start()
     to_across.start()
     held[3] = h_ref[...]
+
+    entry = lax.broadcasted_iota(jnp.int32, (8, rows), 1)
+    even = lax.rem(lax.broadcasted_iota(jnp.int32, (8, rows), 0), 2) == 0
+    for place in range(plan.group):
+        turns = [turn_of(plan, lengths_ref, m, place) for m in range(2)]
+        near, far = plan.near[place], plan.far[place]
+        picked = jnp.where(
+            entry < jnp.where(even, turns[0], turns[1]),
+            ids_ref[:, near : near + rows],
+            ids_ref[:, far : far + rows],
+        )
+        columns[place] = jnp.transpose(picked)
 
     short = padded - valid
     if short:
@@ -812,13 +1164,16 @@
             total_ref[...] = total_ref[...] * scale + jnp.sum(powers, -1, keepdims=True)
             scale_of[at % 2][...] = scale
             powers_of[at % 2][...] = jnp.where(
-                column == target_ref[owner] - at * tile, 0.0, powers
+                column == targets_ref[...] - at * tile, 0.0, powers
             ).astype(BF16)
 
         def gather(at):
             term = dot(powers_of[at % 2][...], part(at))
             grad_ref[...] = grad_ref[...] * scale_of[at % 2][...] + term
 
+        column_of = jnp.where(lax.rem(owner, 2) == 0, columns[0], columns[1])
+        target = jnp.where(owner < 2, column_of[:, 0:1], column_of[:, 1:2])
+        targets_ref[...] = target.astype(jnp.int32) - v * valid
         maxima_ref[...] = jnp.full((rows, 1), MASKED, F32)
         total_ref[...] = jnp.zeros((rows, 1), F32)
         grad_ref[...] = jnp.zeros_like(grad_ref)
@@ -832,73 +1187,95 @@
 
         @pl.when(k < 3)
         def _():
-            parcel[k, :, :width] = grad_ref[...].astype(BF16)
-            tail = jnp.zeros((rows, LANES), F32)
-            for first, value in ((0, maxima_ref[...]), (3, total_ref[...])):
-                for step in range(3):
-                    piece = value.astype(BF16).astype(F32)
-                    tail = jnp.where(lane == first + step, piece, tail)
-                    value = value - piece
-            parcel[k, :, width:] = tail.astype(BF16)
-
-        for index, result in enumerate(results):
-            pl.when(k == index)(result.start)
+            parcel[k] = grad_ref[...].astype(BF16)
+            side = lax.broadcasted_iota(jnp.int32, (rows, 8), 1)
+            pair = jnp.where(side == 0, maxima_ref[...], total_ref[...])
+            stats_out[k] = jnp.transpose(pair)
+
+        for index, (mark, result) in enumerate(zip(marks, results)):
+
+            @pl.when(k == index)
+            def _():
+                mark.start()
+                result.start()
+
         return 0
 
     lax.fori_loop(0, 4, turn, 0)
-    for result in results:
-        result.wait_recv()
-    tails = [arrived[k, :, width:].astype(F32) for k in range(3)]
-    highs = [t[:, 0:1] + t[:, 1:2] + t[:, 2:3] for t in tails] + [maxima_ref[...]]
-    totals = [t[:, 3:4] + t[:, 4:5] + t[:, 5:6] for t in tails] + [total_ref[...]]
+    for copy in [*marks, *results]:
+        copy.wait_recv()
+    pairs = [jnp.transpose(stats_in[k]) for k in range(3)]
+    highs = [pair[:, 0:1] for pair in pairs] + [maxima_ref[...]]
+    totals = [pair[:, 1:2] for pair in pairs] + [total_ref[...]]
     highest = functools.reduce(jnp.maximum, highs)
     log_total = highest + jnp.log(sum(t * jnp.exp(m - highest) for m, t in zip(highs, totals)))
     summed = grad_ref[...] * jnp.exp(highs[3] - log_total)
     for k in range(3):
-        summed = summed + arrived[k, :, :width].astype(F32) * jnp.exp(highs[k] - log_total)
-    grad_ref[...] = summed
-    stat_ref[...] = jnp.where(lane == 0, log_total, 0.0)
-    for copy in [to_twin, to_across, passed_on, *results]:
+        summed = summed + arrived[k].astype(F32) * jnp.exp(highs[k] - log_total)
+    target_rows = target_ref[...].astype(F32)
+    target_logit = jnp.sum(h_ref[...].astype(F32) * target_rows, -1, keepdims=True)
+    coefficient = (jnp.exp(target_logit - log_total) - 1.0).astype(BF16).astype(F32)
+    info = row_scalars(plan, lengths_ref, True)
+    position = row_positions(info, (rows, 1), 0)
+    in_second, in_third = position >= info[0], position >= info[1]
+    begin = jnp.where(in_third, info[1], jnp.where(in_second, info[0], 0))
+    task = jnp.where(in_third, tasks_ref[x, 2], jnp.where(in_second, tasks_ref[x, 1], tasks_ref[x, 0]))
+    counts = (position - begin >= P_SIZE) & (lax.broadcasted_iota(jnp.int32, (rows, 1), 0) < plan.half)
+    column_of = jnp.where(core == 0, columns[0], columns[1])
+    counted = jnp.where(counts, jnp.where(x == 0, column_of[:, 2:3], column_of[:, 3:4]), 0.0)
+    summed = counted * (summed + coefficient * target_rows)
+    grad_ref[...] = normed_back(rows_ref[...], gain_ref[...], inverse, summed * width ** (-0.5))
+    of_task = jnp.where(lane == task, counted, 0.0)
+    losses = jnp.sum(of_task * (log_total - target_logit), 0, keepdims=True)
+    counts = jnp.sum(of_task, 0, keepdims=True)
+    row = lax.broadcasted_iota(jnp.int32, stat_ref.shape, 0)
+    stat_ref[...] = jnp.where(row == 0, losses, jnp.where(row == 1, counts, 0.0))
+    for copy in [to_twin, to_across, passed_on, *marks, *results]:
         copy.wait_send()
 
 
-def vocab_exchange(hidden, target_local, embedding):
-    rows, width = hidden.shape
+def vocab_exchange(plan, rows, gain, target_rows, embedding, ids, row_lengths, row_tasks):
+    count, width = rows.shape
     valid = embedding.shape[0]
     tile = 2 * VOCAB_BLOCK
     padded = (valid + tile - 1) // tile * tile
     vmem = pl.BlockSpec(memory_space=pltpu.VMEM)
     return pl.pallas_call(
-        functools.partial(vocab_exchange_kernel, tile),
+        functools.partial(vocab_exchange_kernel, plan, tile),
         out_shape=[
-            jax.ShapeDtypeStruct((rows, width), F32),
-            jax.ShapeDtypeStruct((rows, LANES), F32),
+            jax.ShapeDtypeStruct((count, width), F32),
+            jax.ShapeDtypeStruct((8, LANES), F32),
         ],
-        in_specs=[vmem, vmem, vmem],
-        out_specs=[vmem, vmem],
+        in_specs=[vmem] * 5 + [pl.BlockSpec(memory_space=pltpu.SMEM)] * 2,
+        out_specs=[vmem] * 2,
         scratch_shapes=[
             pltpu.VMEM((tile, width), BF16),
-            pltpu.VMEM((4, rows, width), BF16),
-            pltpu.VMEM((rows, tile), F32),
-            pltpu.VMEM((rows, tile), F32),
-            pltpu.VMEM((rows, tile), BF16),
-            pltpu.VMEM((rows, tile), BF16),
-            pltpu.VMEM((rows, 1), F32),
-            pltpu.VMEM((rows, 1), F32),
-            pltpu.VMEM((rows, 1), F32),
-            pltpu.VMEM((rows, 1), F32),
-            pltpu.VMEM((3, rows, width + LANES), BF16),
-            pltpu.VMEM((3, rows, width + LANES), BF16),
-            pltpu.SemaphoreType.DMA((6,)),
-            pltpu.SemaphoreType.DMA((6,)),
+            pltpu.VMEM((4, count, width), BF16),
+            pltpu.VMEM((count, tile), F32),
+            pltpu.VMEM((count, tile), F32),
+            pltpu.VMEM((count, tile), BF16),
+            pltpu.VMEM((count, tile), BF16),
+            pltpu.VMEM((count, 1), F32),
+            pltpu.VMEM((count, 1), F32),
+            pltpu.VMEM((count, 1), F32),
+            pltpu.VMEM((count, 1), F32),
+            pltpu.VMEM((count, 1), jnp.int32),
+            pltpu.VMEM((count, width), BF16),
+            pltpu.VMEM((2, count, 8), F32),
+            pltpu.VMEM((3, count, width), BF16),
+            pltpu.VMEM((3, count, width), BF16),
+            pltpu.VMEM((3, 8, count), F32),
+            pltpu.VMEM((3, 8, count), F32),
+            pltpu.SemaphoreType.DMA((9,)),
+            pltpu.SemaphoreType.DMA((9,)),
         ],
         compiler_params=pltpu.CompilerParams(
-            collective_id=1, has_side_effects=True, vmem_limit_bytes=52 * MIB
+            collective_id=1, has_side_effects=True, vmem_limit_bytes=44 * MIB
         ),
         cost_estimate=pl.CostEstimate(
-            flops=16 * rows * padded * width, bytes_accessed=2 * valid * width, transcendentals=0
+            flops=30 * count * padded * width, bytes_accessed=2 * valid * width, transcendentals=0
         ),
-    )(hidden, target_local.reshape(4, rows, 1), embedding)
+    )(rows, gain[None], target_rows, embedding, ids, row_lengths, row_tasks)
 
 
 def reduce_kernel(rows_dp, task_ref, table_ref, stat_ref, out_ref, stats_out, squares_out, *scratch):
@@ -1107,30 +1484,29 @@
     ids = jnp.transpose(ids, (1, 2, 0, 3)).reshape(3, micros, length)
     enc_ids = ids[0].reshape(shards, own)
 
-    segments = seg_lengths.shape[-1]
-    row_lengths = seg_lengths[:, 0]
-    if group == 2 and segments == 3 and 2 * span + 2 * P_SIZE <= length - span:
-        half = (length - segments * P_SIZE) // group
+    row_lengths, row_tasks = seg_lengths[:, 0], task_ids[:, 0]
+    compact = group == 2 and 2 * span + 2 * P_SIZE <= length - span
+    if compact:
+        half = (length - SEGS * P_SIZE) // group
+        extra = (half + 2 * P_SIZE - own + HALO - 1) // HALO * HALO
         heads = (half + LANES - 1) // LANES * LANES
-        extra = (half + 2 * P_SIZE - own + HALO - 1) // HALO * HALO
-        starts = [0, own - extra]
-        near = [P_SIZE, half + 2 * P_SIZE]
-        far = [2 * P_SIZE, half + 3 * P_SIZE]
-        turns = [row_lengths[:, 0] - P_SIZE, length - row_lengths[:, 2] - near[1]]
+        near, far = (P_SIZE, half + 2 * P_SIZE), (2 * P_SIZE, half + 3 * P_SIZE)
+        plan = Plan(length, group, own, own + extra, heads, half, (0, own - extra), near, far)
     else:
-        half = heads = own
-        extra = 0
-        starts = near = far = [p * own for p in range(group)]
-        turns = [row_lengths[:, 0]] * group
-    held = own + extra
+        starts = tuple(p * own for p in range(group))
+        plan = Plan(length, group, own, own, own, own, starts, starts, starts)
+    held, heads, half, starts = plan.held, plan.heads, plan.half, plan.starts
+    turns = [
+        row_lengths[:, 0] - P_SIZE if p == 0 else length - row_lengths[:, 2] - plan.near[-1]
+        for p in range(group)
+    ]
     entries = jnp.arange(heads, dtype=jnp.int32)
 
     def of_rows(values, m, p):
-        values = jnp.pad(values, (0, heads + far[p]))
+        near, far = plan.near[p], plan.far[p]
+        values = jnp.pad(values, (0, heads + far))
         return jnp.where(
-            entries < turns[p][m],
-            values[near[p] : near[p] + heads],
-            values[far[p] : far[p] + heads],
+            entries < turns[p][m], values[near : near + heads], values[far : far + heads]
         )
 
     everyone = [(m, p) for m in range(micros) for p in range(group)]
@@ -1145,7 +1521,6 @@
             for m, p in everyone
         ]
     )
-    head_targets = jnp.stack([of_rows(ids[1, m], m, p) for m, p in everyone])
     first_row = me * shard_rows
 
     def here(wanted):
@@ -1153,16 +1528,22 @@
         inside = (local >= 0) & (local < shard_rows)
         return local, inside
 
-    prompt_all = lax.all_gather(prompt.astype(BF16), "vocab", axis=2, tiled=True)
-    prompt_flat = prompt_all.reshape(-1, width)
+    prompt_low = jnp.swapaxes(prompt, 1, 2).astype(BF16)
+    prompt_low = jnp.pad(prompt_low, ((0, 0), (0, 0), (0, LANES - P_SIZE)))
+    prompt_all = lax.all_gather(prompt_low, "vocab", axis=1, tiled=True)
+    lengths = lax.dynamic_index_in_dim(row_lengths, micro, 0, False)
+    tasks = lax.dynamic_index_in_dim(row_tasks, micro, 0, False)
     weights = (attend_in, attend_out, expand_weights, reduce_weights)
-    if lax.axis_size("dp") == 8 and shards == 4 and shard_rows % 32 == 0:
-        local, inside = here(jnp.concatenate([enc_ids, dec_ids], 1).reshape(-1))
+    on_links = lax.axis_size("dp") == 8 and shards == 4 and shard_rows % 32 == 0 and compact
+    if on_links:
+        local, inside = here(jnp.concatenate([enc_ids, dec_ids], 1))
         wanted = jnp.where(inside, local, shard_rows)
-        *flat, found = gather_weights(*weights, wanted, embedding)
+        *flat, enc_rows, keys_low, dec_input, heads_low, target_rows = gather_weights(
+            plan, *weights, wanted, embedding, row_lengths, norm_gains[3]
+        )
         attend_in, attend_out = flat[:3], flat[3:6]
-        expand_weights, reduce_weights = [[w] for w in flat[6:8]], [[w] for w in flat[8:]]
-        enc_rows, dec_rows = found[:own], found[own:]
+        expand_weights, reduce_weights = flat[6:8], flat[8:10]
+        dec_input = dec_input.astype(F32)
     else:
 
         def lookup(wanted):
@@ -1173,91 +1554,101 @@
 
         enc_rows, dec_rows = lookup(enc_ids), lookup(dec_ids)
         whole = [lax.all_gather(tensor, "dp", axis=1, tiled=True) for tensor in weights]
-        attend_in, attend_out = whole[:2]
-        expand_weights, reduce_weights = whole[2][:, None], whole[3][:, None]
-
-    lengths = lax.dynamic_index_in_dim(seg_lengths[:, 0], micro, 0, False)
-    tasks = lax.dynamic_index_in_dim(task_ids[:, 0], micro, 0, False)
-    steps = jnp.arange(own, dtype=jnp.int32)
-    positions = place * own + steps
-    segment, in_segment, task_of = layout(lengths, tasks, positions)
-    key_positions = jnp.concatenate(
-        [((place - k + group) % group) * own + steps for k in range(group)]
-    )
-    key_segment = layout(lengths, tasks, key_positions)[0]
-    rows_info = jnp.stack([segment, positions], 1)
-    keys_info = jnp.stack([key_segment, key_positions], 1)
-    turn = jnp.stack(turns)[place, micro]
-    near_row = jnp.asarray(near, jnp.int32)[place]
-    far_row = jnp.asarray(far, jnp.int32)[place]
-    first_held = jnp.asarray(starts, jnp.int32)[place]
-    head_positions = jnp.where(entries < turn, near_row, far_row) + entries
-    head_positions = jnp.minimum(head_positions, length - 1)
-    head_segment, head_in_segment, head_task = layout(lengths, tasks, head_positions)
-    heads_info = jnp.stack([head_segment, head_positions], 1)
-    head_mask_row = jnp.stack([of_rows(ids[2, m], m, p) for m, p in everyone])[me]
-    counted = (head_mask_row * ((head_in_segment >= P_SIZE) & (entries < half))).astype(F32)
-
-    def head_rows(values):
-        values = jnp.pad(values, ((0, heads), (0, 0)))
-        shape = (heads, values.shape[1])
-        return jnp.where(
-            (entries < turn)[:, None],
-            lax.dynamic_slice(values, (near_row - first_held, 0), shape),
-            lax.dynamic_slice(values, (far_row - first_held, 0), shape),
-        )
+        attend_in, attend_out, expand_weights, reduce_weights = whole
+        turn = jnp.stack(turns)[place, micro]
+        near_row = jnp.asarray(plan.near, jnp.int32)[place]
+        far_row = jnp.asarray(plan.far, jnp.int32)[place]
+        first_held = jnp.asarray(starts, jnp.int32)[place]
+        head_positions = jnp.where(entries < turn, near_row, far_row) + entries
+        head_positions = jnp.minimum(head_positions, length - 1)
+        _, head_in_segment, head_task = layout(lengths, tasks, head_positions)
+        head_mask_row = jnp.stack([of_rows(ids[2, m], m, p) for m, p in everyone])[me]
+        counted = (head_mask_row * ((head_in_segment >= P_SIZE) & (entries < half))).astype(F32)
+
+        def head_rows(values):
+            values = jnp.pad(values, ((0, heads), (0, 0)))
+            shape = (heads, values.shape[1])
+            return jnp.where(
+                (entries < turn)[:, None],
+                lax.dynamic_slice(values, (near_row - first_held, 0), shape),
+                lax.dynamic_slice(values, (far_row - first_held, 0), shape),
+            )
+
+        held_positions = first_held + jnp.arange(held, dtype=jnp.int32)
+        begun = layout(lengths, tasks, held_positions)[1] >= 1
+        dec_held = jnp.where(begun[:, None], dec_rows[HALO - 1 : HALO - 1 + held], dec_rows[:1])
+        dec_keys = lax.dynamic_slice(dec_held, (place * own - first_held, 0), (own, width))
+        keys_low = normed(dec_keys.astype(F32), norm_gains[3])[0].astype(BF16)
+        dec_input = head_rows(dec_held).astype(F32)
+        heads_low = normed(dec_input, norm_gains[3])[0].astype(BF16)
+        target_rows = head_rows(dec_rows[HALO:])
 
     def key_parts(source, weight):
         pair = dot(source, weight).astype(BF16)
         return [pair] + [around(pair, k) for k in range(1, group)]
 
-    def project(source, weight):
-        return dot(source, weight).astype(BF16)
-
+    positions = place * own + jnp.arange(own, dtype=jnp.int32)
+    segment, in_segment, _ = layout(lengths, tasks, positions)
     is_prompt = in_segment < P_SIZE
-    slot = task_of * P_SIZE + jnp.minimum(in_segment, P_SIZE - 1)
-    enc_input = jnp.where(
-        is_prompt[:, None], jnp.take(prompt_flat, slot, axis=0), enc_rows
-    ).astype(F32)
-    held_positions = first_held + jnp.arange(held, dtype=jnp.int32)
-    begun = layout(lengths, tasks, held_positions)[1] >= 1
-    dec_held = jnp.where(begun[:, None], dec_rows[HALO - 1 : HALO - 1 + held], dec_rows[:1])
-    dec_keys = lax.dynamic_slice(dec_held, (place * own - first_held, 0), (own, width)).astype(F32)
-    dec_input = head_rows(dec_held).astype(F32)
-    target_rows = head_rows(dec_rows[HALO:]).astype(F32)
-
-    normed_in, inverse_in = normed(enc_input, norm_gains[0])
-    normed_low = normed_in.astype(BF16)
-    enc_pairs = key_parts(normed_low, attend_in[0][:, width:])
-    enc_queries = project(normed_low, attend_in[0][:, :width])
-    normed_keys = normed(dec_keys, norm_gains[3])[0].astype(BF16)
-    dec_pairs = key_parts(normed_keys, attend_in[1][:, width:])
-    normed_dec = normed(dec_input, norm_gains[3])[0].astype(BF16)
-    dec_queries = project(normed_dec, attend_in[1][:, :width])
+    place_of = jnp.where(is_prompt, segment * LANES + in_segment, -1)
+    chosen_place = place_of[:, None] == jnp.arange(SEGS * LANES, dtype=jnp.int32)
+    chosen_low = chosen_place.astype(BF16)
+
+    if on_links:
+        enc_input, enc_queries, enc_pairs, dec_queries, dec_pairs = project(
+            plan,
+            enc_rows,
+            prompt_all,
+            keys_low,
+            heads_low,
+            norm_gains[0],
+            row_lengths,
+            row_tasks,
+            attend_in[0],
+            attend_in[1],
+        )
+    else:
+        prompts = jnp.concatenate(
+            [lax.dynamic_index_in_dim(prompt_all, tasks[j], 0, False) for j in range(SEGS)], 1
+        )
+        prompt_rows = dot_rows(chosen_low, prompts)
+        enc_input = jnp.where(is_prompt[:, None], prompt_rows, enc_rows.astype(F32))
+        normed_low = normed(enc_input, norm_gains[0])[0].astype(BF16)
+        enc_pairs = key_parts(normed_low, attend_in[0][:, width:])
+        enc_queries = dot(normed_low, attend_in[0][:, :width]).astype(BF16)
+        dec_pairs = key_parts(keys_low, attend_in[1][:, width:])
+        dec_queries = dot(heads_low, attend_in[1][:, :width]).astype(BF16)
     enc_mid, enc_mixed, enc_logs = attend(
-        enc_queries, enc_pairs, enc_input, attend_out[0], rows_info, keys_info, False
+        plan, enc_queries, enc_pairs, enc_input, attend_out[0], row_lengths, False, False
     )
     enc_last, enc_kept = feed(enc_mid, norm_gains[1], expand_weights[0], reduce_weights[0])
-    encoded, inverse_last = normed(enc_last, norm_gains[2])
-    cross_pairs = key_parts(encoded.astype(BF16), attend_in[2][:, width:])
+    encoded = normed(enc_last, norm_gains[2])[0].astype(BF16)
+    cross_pairs = key_parts(encoded, attend_in[2][:, width:])
 
     dec_first = attend(
-        dec_queries, dec_pairs, dec_input, attend_out[1], heads_info, keys_info, True
+        plan, dec_queries, dec_pairs, dec_input, attend_out[1], row_lengths, True, True
     )[0]
-    cross_queries = project(normed(dec_first, norm_gains[4])[0].astype(BF16), attend_in[2][:, :width])
+    cross_source = normed(dec_first, norm_gains[4])[0].astype(BF16)
+    cross_queries = dot(cross_source, attend_in[2][:, :width]).astype(BF16)
     dec_second, cross_mixed, cross_logs = attend(
-        cross_queries, cross_pairs, dec_first, attend_out[2], heads_info, keys_info, False
+        plan, cross_queries, cross_pairs, dec_first, attend_out[2], row_lengths, True, False
     )
     dec_last, dec_kept = feed(dec_second, norm_gains[5], expand_weights[1], reduce_weights[1])
-    output_norm, inverse_out = normed(dec_last, norm_gains[6])
-    hidden = (output_norm * width ** (-0.5)).astype(BF16)
-
-    target_local = head_targets.reshape(-1, 1) - first_row
-    if shards == 4:
-        summed, stats = vocab_exchange(hidden, target_local, embedding)
-        own_total = stats[:, 0]
+
+    if on_links:
+        wide = (plan.far[-1] + heads + LANES - 1) // LANES * LANES
+        marks = jnp.pad(
+            jnp.concatenate([ids[1], ids[2]]).astype(F32), ((0, 4), (0, wide - length))
+        )
+        dec_grad, stats = vocab_exchange(
+            plan, dec_last, norm_gains[6], target_rows, embedding, marks, row_lengths, row_tasks
+        )
     else:
+        output_norm, inverse_out = normed(dec_last, norm_gains[6])
+        hidden = (output_norm * width ** (-0.5)).astype(BF16)
         all_hidden = lax.all_gather(hidden, "vocab", axis=0, tiled=True)
+        head_targets = jnp.concatenate([of_rows(ids[1, m], m, p) for m, p in everyone])
+        target_local = head_targets[:, None] - first_row
         part, stats = vocab_pass(all_hidden, target_local, embedding, heads)
         gathered = lax.all_gather(stats[:, :2].T, "vocab")
         maxima = jnp.max(gathered[:, 0], 0)
@@ -1267,10 +1658,16 @@
         scaled = part * jnp.exp(stats[:, 0] - log_total)[:, None]
         summed = lax.psum_scatter(scaled, "vocab", scatter_dimension=0, tiled=True)
         own_total = lax.dynamic_slice(log_total, (me * heads,), (heads,))
-    target_logit = jnp.sum(hidden.astype(F32) * target_rows, -1)
-    token_loss = own_total - target_logit
-    target_coefficient = (jnp.exp(target_logit - own_total) - 1.0).astype(BF16).astype(F32)
-    hidden_grad = counted[:, None] * (summed + target_coefficient[:, None] * target_rows)
+        target_values = target_rows.astype(F32)
+        target_logit = jnp.sum(hidden.astype(F32) * target_values, -1)
+        coefficient = (jnp.exp(target_logit - own_total) - 1.0).astype(BF16).astype(F32)
+        hidden_grad = counted[:, None] * (summed + coefficient[:, None] * target_values)
+        dec_grad = normed_back(
+            dec_last, norm_gains[6], inverse_out, hidden_grad * width ** (-0.5)
+        )
+        losses = per_task(head_task, counted * (own_total - target_logit))
+        tallies = jnp.stack([losses, per_task(head_task, counted)])
+        stats = jnp.zeros((8, LANES), F32).at[:2, :TASKS].set(tallies)
 
     def keys_back(pairs, weight):
         total = pairs[0]
@@ -1280,59 +1677,63 @@
         rest = (total - high.astype(F32)).astype(BF16)
         return dot_rows(high, weight) + dot_rows(rest, weight)
 
-    dec_grad = normed_back(
-        dec_last, norm_gains[6], inverse_out, hidden_grad * width ** (-0.5)
-    )
     dec_grad = feed_back(
         dec_grad, dec_second, norm_gains[5], dec_kept, expand_weights[1], reduce_weights[1]
     )
     back = attend_back(
+        plan,
         cross_queries,
         cross_pairs,
         dec_grad,
         attend_out[2],
         cross_mixed,
         cross_logs,
-        heads_info,
-        keys_info,
+        row_lengths,
+        True,
         False,
+        (attend_in[2], enc_last, norm_gains[2], 3) if on_links else None,
     )
-    enc_grad = normed_back(
-        enc_last, norm_gains[2], inverse_last, keys_back(back, attend_in[2][:, width:])
-    )
+    if on_links:
+        enc_grad = back
+    else:
+        inverse_last = normed(enc_last, norm_gains[2])[1]
+        enc_grad = normed_back(
+            enc_last, norm_gains[2], inverse_last, keys_back(back, attend_in[2][:, width:])
+        )
     enc_grad = feed_back(
         enc_grad, enc_mid, norm_gains[1], enc_kept, expand_weights[0], reduce_weights[0]
     )
-    *back, back_queries = attend_back(
+    back = attend_back(
+        plan,
         enc_queries,
         enc_pairs,
         enc_grad,
         attend_out[0],
         enc_mixed,
         enc_logs,
-        rows_info,
-        keys_info,
+        row_lengths,
+        False,
         True,
+        (attend_in[0], enc_input, norm_gains[0], 4) if on_links else None,
     )
-    source_grad = keys_back(back, attend_in[0][:, width:]) + lax.dot_general(
-        back_queries,
-        attend_in[0][:, :width],
-        (((0,), (1,)), ((), ())),
-        preferred_element_type=F32,
-    )
-    enc_grad = enc_grad + normed_back(enc_input, norm_gains[0], inverse_in, source_grad)
-
-    place_of = segment * LANES + in_segment
-    chosen = (
-        (place_of[:, None] == jnp.arange(segments * LANES, dtype=jnp.int32)) & is_prompt[:, None]
-    ).astype(BF16)
+    if on_links:
+        enc_grad = back
+    else:
+        *back, back_queries = back
+        source_grad = keys_back(back, attend_in[0][:, width:]) + lax.dot_general(
+            back_queries,
+            attend_in[0][:, :width],
+            (((0,), (1,)), ((), ())),
+            preferred_element_type=F32,
+        )
+        inverse_in = normed(enc_input, norm_gains[0])[1]
+        enc_grad = enc_grad + normed_back(enc_input, norm_gains[0], inverse_in, source_grad)
+
     high = enc_grad.astype(BF16)
     rest = (enc_grad - high.astype(F32)).astype(BF16)
-    table = dot_columns(high, chosen) + dot_columns(rest, chosen)
-    tallies = jnp.stack([per_task(head_task, counted * token_loss), per_task(head_task, counted)])
-    stats = jnp.zeros((8, LANES), F32).at[:2, :TASKS].set(tallies)
-    if shards == 4 and lax.axis_size("dp") == TASKS:
-        gradient, stats, squares = reduce_over_devices(task_ids[:, 0], table, stats)
+    table = dot_columns(high, chosen_low) + dot_columns(rest, chosen_low)
+    if on_links:
+        gradient, stats, squares = reduce_over_devices(row_tasks, table, stats)
         full_grad = jnp.swapaxes(gradient[:, :, :P_SIZE], 1, 2)
         row_squares = squares[:, :P_SIZE]
         task_scale = 1.0 / (TASKS * jnp.maximum(stats[1, :TASKS], 1.0))
@@ -1340,7 +1741,7 @@
         hits = (tasks[:, None] == jnp.arange(TASKS, dtype=jnp.int32)).astype(F32)
         by_task = jnp.einsum(
             "fsp,st->tpf",
-            table.reshape(width, segments, LANES)[:, :, :P_SIZE],
+            table.reshape(width, SEGS, LANES)[:, :, :P_SIZE],
             hits,
             precision=lax.Precision.HIGHEST,
         )

time: 503 us -> 450 us (0.89)
  matrix products: 71.1 us -> 3.5 us
  Pallas kernels: 329 us -> 369 us
  other arithmetic: 37.8 us -> 7.68 us
  local copies, waits for them, and re-layouts: 24.3 us -> 43.3 us
  waiting for transfers between devices: 11.2 us -> 0.02 us
    dot_general x7 -> x0, matrix products: 40.5 us -> none  [the longest x6 39.3 us: dot_rows(): lax.dot_general(left, right, (((1,), (1,)), ((), ())), preferred_element_...]
    pallas_call x7 -> x12, Pallas kernels: 291 us -> 330 us  [the longest x1 151 us: gather_weights(): pl.pallas_call(functools.partial(gather_kernel, plan, rows_z, rows_y), ou...]
    unnamed x182 -> x146, local copies, waits for them, and re-layouts: 8.73 us -> 41 us
    dot_general x10 -> x2, matrix products: 28.5 us -> 2.13 us  [dot(): return jnp.dot(left, right, preferred_element_type=F32)]
    ppermute x5 -> x1, waiting for transfers between devices: 11.2 us -> 0.01 us  [around(): return lax.ppermute(array, 'vocab', pairs)]
    add x6 -> x1, other arithmetic: 6.07 us -> 0.01 us  [on_device(): positions = place * own + jnp.arange(own, dtype=jnp.int32)]
    another operation x10 -> x1, local copies, waits for them, and re-layouts: 5.23 us -> 0.01 us  [the longest x4 3.24 us: on_device(): head_targets = jnp.stack([of_rows(ids[1, m], m, p) for m, p in everyone])]
  transfers between devices with their start and end apart: 6 -> 2, of which waited for: 2 -> 0; matrix products, arithmetic and copies ran while one was open for 11% -> 1% of each run, Pallas kernels for 36% -> 37%
where the time goes in v5:
time: 450 us; the launch traced here: 446 us
  Pallas kernels  369 us (82%)
  local copies, waits for them, and re-layouts  43.3 us (10%)
  between operations  17 us (4%)
  other arithmetic  7.68 us (2%)
  blocking collectives  5.67 us (1%)
    pallas_call x1, Pallas kernels, gather_weights(): pl.pallas_call(functools.partial(gather_kernel, plan, rows_z, rows_y), ou...  151 us
    pallas_call x1, Pallas kernels, vocab_exchange(): pl.pallas_call(functools.partial(vocab_exchange_kernel, plan, tile), out_...  60.4 us
    pallas_call x2, Pallas kernels, attend_back(): pl.pallas_call(functools.partial(attend_back_kernel, plan, parts, decoder...  52.6 us
    unnamed x146, local copies, waits for them, and re-layouts  41 us
    pallas_call x1, Pallas kernels, reduce_over_devices(): pl.pallas_call(functools.partial(reduce_kernel, rows_dp), out_shape=[jax....  38.2 us
    pallas_call x3, Pallas kernels, attend(): pl.pallas_call(functools.partial(attend_kernel, plan, parts, decoder, cau...  35.9 us
    pallas_call x2, Pallas kernels, feed_back(): pl.pallas_call(feed_back_kernel, out_shape=jax.ShapeDtypeStruct((own, wid...  11.5 us
    pallas_call x1, Pallas kernels, project(): pl.pallas_call(functools.partial(project_kernel, plan), out_shape=[jax.Sh...  9.79 us
  transfers between devices with their start and end apart: 2, of which 0 were waited for; matrix products, arithmetic and copies ran while one was open for 1% of the time, Pallas kernels for 37%

profile of v5, /device:TPU:25, one launch (start us, length us, event | category | flops | bytes accessed | tf_op | source)
XLA Modules:
  0.0 445.8 jit_solution(11112556085650790335)
XLA Ops:
  7.3 1.2 convert_bitcast_fusion
  8.5 0.8 pad.23
  9.4 0.2 reduce-window.7
  9.6 5.7 %all-gather = s32[12,2,256]{2,1,0:T(2,128)S(1)} all-gather(s32[3,2,256]{2,1,0:T(2,128)S(1)} %pad_add_fusion), channel_id=2, replica_groups=mesh['dp'=8,'vocab'=4] {'vocab'}, dimensions={0}, use_global_device_ids=true | all-gather | bytes 30720 | tf_op jit(solution)/shard_map/all_gather | solution.py:1483
  15.6 0.1 slice_reduce_fusion.3
  15.9 0.6 and_select_fusion.refs_4_
  16.5 0.6 fusion.14
  17.1 150.9 %shard_map.198 = (bf16[4,2,96,2304]{3,2,1,0:T(8,128)(2,1)}, bf16[4,2,96,2304]{3,2,1,0:T(8,128)(2,1)}, bf16[4,2,96,2304]{3,2,1,0:T(8,128)(2,1)}, bf16[4,2,96,768]...) custom-call(bf16[3,96,2304]{2,1,0:T(8,128)(2,1)} %refs_0_.1, ...), custom_call_target="tpu_custom_call" | custom-call | bytes 400000000 | tf_op jit(solution)/shard_map/pallas_call | solution.py:1038
  168.0 1.3 convert_element_type.43.refs_3_
  169.6 0.6 add_select_fusion
  170.2 1.4 copy-done.20
  171.6 1.1 copy-done.32
  172.6 9.8 %shard_map.199 = (f32[512,768]{1,0:T(8,128)S(1)}, bf16[512,768]{1,0:T(8,128)(2,1)S(1)}, bf16[512,1536]{1,0:T(8,128)(2,1)S(1)}, bf16[512,1536]{1,0:T(8,128)(2,1)S...) custom-call(bf16[512,768]{1,0:T(8,128)(2,1)S(1)} %copy-done.29, ...), custom_call_target="tpu_custom_call" | custom-call | flops 3019898880 | bytes 7077888 | tf_op jit(solution)/shard_map/pallas_call | solution.py:578
  182.5 13.7 %shard_map.201 = (f32[512,768]{1,0:T(8,128)S(1)}, f32[512,768]{1,0:T(8,128)S(1)}, f32[512,128]{1,0:T(8,128)S(1)}) custom-call(bf16[512,768]{1,0:T(8,128)(2,1)S(1)} %get-tuple-element.50.refs_0_, bf16[512,1536]{1,0:T(8,128)(2,1)S(1)} %get-tuple-element.51.refs_1_, bf16[512,1536]{1,0:T(8,128)(2,1)S(1)} %get-tuple-element.52.refs_2_, ...), custom_call_target="tpu_custom_call" | custom-call | flops 17716740096 | bytes 2359296 | tf_op jit(solution)/shard_map/pallas_call | solution.py:223
  196.3 1.2 copy-done.50
  197.5 0.1 copy.41
  197.6 2.8 copy-done.5
  200.4 2.3 copy-done.6
  202.7 5.3 %shard_map.202 = (f32[512,768]{1,0:T(8,128)S(1)}, f32[512,3072]{1,0:T(8,128)S(1)}) custom-call(f32[512,768]{1,0:T(8,128)S(1)} %get-tuple-element.62.rows_ref, f32[1,768]{1,0:T(1,128)S(1)} %get-tuple-element.94.gain_ref, bf16[768,3072]{1,0:T(8,128)(2,1)S(1)} %bitcast.51, bf16[3072,768]{1,0:T(8,128)(2,1)S(1)} %bitcast.55), custom_call_target="tpu_custom_call" | custom-call | flops 4831838208 | bytes 9437184 | tf_op jit(solution)/shard_map/pallas_call | solution.py:448
  208.1 0.2 multiply_reduce_fusion
  208.3 1.4 convolution_convert_fusion.refs_1_
  209.8 1.4 copy-done
  211.2 0.8 copy-done.8
  211.9 0.1 collective-permute-start
  212.2 1.5 copy-done.41
  213.7 0.1 copy-done.45
  213.8 12.0 %shard_map.200 = (f32[384,768]{1,0:T(8,128)S(1)}, f32[384,768]{1,0:T(8,128)}, f32[384,128]{1,0:T(8,128)}) custom-call(bf16[384,768]{1,0:T(8,128)(2,1)S(1)} %copy-done.45, bf16[512,1536]{1,0:T(8,128)(2,1)S(1)} %copy-done.39, bf16[512,1536]{1,0:T(8,128)(2,1)S(1)} %copy-done.41, f32[384,768]{1,0:T(8,128)S(1)} %convert_element_type.43.refs_3_, ...), custom_call_target="tpu_custom_call" | custom-call | flops 13287555072 | bytes 1769472 | tf_op jit(solution)/shard_map/pallas_call | solution.py:223
  225.8 0.2 multiply_reduce_fusion.1
  226.0 0.7 convolution_convert_fusion.1.refs_0_
  226.7 0.5 copy-done.26
  227.2 10.2 %shard_map.203 = (f32[384,768]{1,0:T(8,128)S(1)}, f32[384,768]{1,0:T(8,128)S(1)}, f32[384,128]{1,0:T(8,128)S(1)}) custom-call(bf16[384,768]{1,0:T(8,128)(2,1)S(1)} %convolution_convert_fusion.1.refs_0_, bf16[512,1536]{1,0:T(8,128)(2,1)S(1)} %convolution_convert_fusion.refs_1_, bf16[512,1536]{1,0:T(8,128)(2,1)S(1)} %collective-permute-done.refs_2_, ...), custom_call_target="tpu_custom_call" | custom-call | flops 13287555072 | bytes 1769472 | tf_op jit(solution)/shard_map/pallas_call | solution.py:223
  237.5 1.0 copy-done.48
  238.5 0.1 copy.40
  238.6 2.3 copy-done.1
  241.0 2.3 copy-done.2
  243.3 4.1 shard_map.204
  247.4 2.2 copy-done.3
  249.6 60.4 %shard_map.205 = (f32[384,768]{1,0:T(8,128)S(1)}, f32[8,128]{1,0:T(8,128)S(1)}) custom-call(f32[384,768]{1,0:T(8,128)S(1)} %get-tuple-element.70.refs_0_, f32[1,768]{1,0:T(1,128)S(1)} %get-tuple-element.99.refs_1_, bf16[384,768]{1,0:T(8,128)(2,1)S(1)} %copy-done.31, bf16[8032,768]{1,0:T(8,128)(2,1)} %refs_3_.3, f32[8,1152]{1,0:T(8,128)S(1)} %pad.24.refs_4_, ...), custom_call_target="tpu_custom_call" | custom-call | flops 72477573120 | bytes 12337152 | tf_op jit(solution)/shard_map/pallas_call | solution.py:1243
  310.1 2.3 copy-done.4
  312.4 5.0 %shard_map.206.refs_3_ = f32[384,768]{1,0:T(8,128)S(1)} custom-call(f32[384,768]{1,0:T(8,128)S(1)} %get-tuple-element.72.grad_ref, f32[384,768]{1,0:T(8,128)S(1)} %get-tuple-element.67.rows_ref, f32[1,768]{1,0:T(1,128)S(1)} %get-tuple-element.100.gain_ref, f32[384,3072]{1,0:T(8,128)S(1)} %copy-done.4, bf16[768,3072]{1,0:T(8,128)(2,1)S(1)} %bitcast.46, ...), custom_call_target="tpu_custom_call" | custom-call | flops 3623878656 | bytes 9437184 | tf_op jit(solution)/shard_map/pallas_call | solution.py:499
  317.5 1.0 copy-done.13
  318.5 1.3 copy-done.14
  319.8 1.4 copy-done.22
  321.2 1.3 copy-done.27
  322.4 1.1 copy-done.47
  323.5 1.3 copy-done.49
  324.8 22.3 %shard_map.207.grad_ref = f32[512,768]{1,0:T(8,128)S(1)} custom-call(bf16[384,768]{1,0:T(8,128)(2,1)S(1)} %copy-done.47, bf16[512,1536]{1,0:T(8,128)(2,1)S(1)} %copy-done.22, bf16[512,1536]{1,0:T(8,128)(2,1)} %copy-done.23, f32[384,768]{1,0:T(8,128)S(1)} %copy-done.14, bf16[768,768]{1,0:T(8,128)(2,1)S(1)} %bitcast.71, f32[384,768]{1,0:T(8,128)S(1)} %copy-done.49, ...), custom_call_target="tpu_custom_call" | custom-call | flops 24159191040 | bytes 7864320 | tf_op jit(solution)/shard_map/pallas_call | solution.py:410
  347.1 2.3 copy-done.7
  349.5 1.4 copy-done.10
  350.9 6.4 %shard_map.208.refs_3_ = f32[512,768]{1,0:T(8,128)S(1)} custom-call(f32[512,768]{1,0:T(8,128)S(1)} %shard_map.207.grad_ref, f32[512,768]{1,0:T(8,128)S(1)} %copy-done.10, f32[1,768]{1,0:T(1,128)S(1)} %get-tuple-element.94.gain_ref, f32[512,3072]{1,0:T(8,128)S(1)} %bitcast.42, bf16[768,3072]{1,0:T(8,128)(2,1)S(1)} %bitcast.54, bf16[3072,768]{1,0:T(8,128)(2,1)S(1)} %bitcast.56), custom_call_target="tpu_custom_call" | custom-call | flops 4831838208 | bytes 9437184 | tf_op jit(solution)/shard_map/pallas_call | solution.py:499
  357.3 1.1 copy-done.11
  358.5 1.4 copy-done.12
  359.9 1.3 copy-done.25
  361.2 1.4 copy-done.35
  362.6 1.1 copy-done.43
  363.7 30.2 %shard_map.209 = f32[512,768]{1,0:T(8,128)S(1)} custom-call(bf16[512,768]{1,0:T(8,128)(2,1)S(1)} %copy-done.43, bf16[512,1536]{1,0:T(8,128)(2,1)S(1)} %copy-done.35, bf16[512,1536]{1,0:T(8,128)(2,1)S(1)} %copy-done.37, f32[512,768]{1,0:T(8,128)S(1)} %copy-done.12, bf16[768,768]{1,0:T(8,128)(2,1)S(1)} %bitcast.69, f32[512,768]{1,0:T(8,128)} %copy-done.50, ...), custom_call_target="tpu_custom_call" | custom-call | flops 32212254720 | bytes 7864320 | tf_op jit(solution)/shard_map/pallas_call | solution.py:410
  394.0 0.7 fusion.2
  394.7 0.7 convolution_add_fusion.table_ref
  395.4 38.2 %shard_map.210 = (f32[8,192,128]{2,1,0:T(8,128)S(1)}, f32[8,128]{1,0:T(8,128)S(1)}, f32[8,128]{1,0:T(8,128)S(1)}) custom-call(s32[2,3]{1,0:T(2,128)S(1)} %bitcast.67, f32[768,384]{1,0:T(8,128)S(1)} %convolution_add_fusion.table_ref, f32[8,128]{1,0:T(8,128)S(1)} %get-tuple-element.79.stat_ref), custom_call_target="tpu_custom_call" | custom-call | tf_op jit(solution)/shard_map/pallas_call | solution.py:1418
  433.6 0.6 slice_reduce_fusion
  434.9 0.6 fusion.11
  435.5 0.1 fusion.13
  435.7 0.4 multiply_reduce_fusion.2
  436.1 1.6 add_subtract_fusion
  (155 shorter events, 1.2 us)
Async XLA Ops:
  7.2 2.2 copy-start.61
  7.2 2.2 copy-start.62
  7.2 2.2 copy-start.17
  7.2 2.4 copy-start.60
  7.2 9.3 %copy-start.55 = (f32[7,768]{1,0:T(8,128)S(1)}, f32[7,768]{1,0:T(8,128)}, u32[]{:S(2)}) copy-start(f32[7,768]{1,0:T(8,128)} %param.25) | copy-start | bytes 64516
  7.2 162.9 %all-gather.3.cloned.1.call-start = ((), (), s32[]{:S(2)}) async-start(), calls=%async_computation | async-start | bytes 1966080 | tf_op jit(solution)/shard_map/all_gather | solution.py:1533
  17.1 153.0 %copy-start.15 = (f32[1,768]{1,0:T(1,128)}, f32[1,768]{1,0:T(1,128)S(1)}, u32[]{:S(2)}) copy-start(f32[1,768]{1,0:T(1,128)S(1)} %get-tuple-element.97.refs_4_.refs_10_) | copy-start | bytes 9220
  168.0 1.5 copy-start.18
  168.0 2.1 copy-start.19
  168.0 2.1 copy-start.29
  168.0 2.1 copy-start.30
  170.2 1.4 copy-start.20
  172.6 9.9 %copy-start.24 = (bf16[4,2,96,768]{3,2,1,0:T(8,128)(2,1)S(1)}, bf16[4,2,96,768]{3,2,1,0:T(8,128)(2,1)}, u32[]{:S(2)}) copy-start(bf16[4,2,96,768]{3,2,1,0:T(8,128)(2,1)} %get-tuple-element.61) | copy-start | bytes 3538948
  182.4 13.8 %copy-start.33 = (f32[512,768]{1,0:T(8,128)}, f32[512,768]{1,0:T(8,128)S(1)}, u32[]{:S(2)}) copy-start(f32[512,768]{1,0:T(8,128)S(1)} %get-tuple-element.60.refs_3_.refs_9_) | copy-start | bytes 4718596
  182.4 13.8 %copy-start.34 = (bf16[512,1536]{1,0:T(8,128)(2,1)}, bf16[512,1536]{1,0:T(8,128)(2,1)S(1)}, u32[]{:S(2)}) copy-start(bf16[512,1536]{1,0:T(8,128)(2,1)S(1)} %get-tuple-element.51.refs_1_) | copy-start | bytes 4718596
  182.5 13.8 %copy-start.36 = (bf16[512,1536]{1,0:T(8,128)(2,1)}, bf16[512,1536]{1,0:T(8,128)(2,1)S(1)}, u32[]{:S(2)}) copy-start(bf16[512,1536]{1,0:T(8,128)(2,1)S(1)} %get-tuple-element.52.refs_2_) | copy-start | bytes 4718596
  182.5 13.8 %copy-start.38 = (bf16[512,1536]{1,0:T(8,128)(2,1)}, bf16[512,1536]{1,0:T(8,128)(2,1)S(1)}, u32[]{:S(2)}) copy-start(bf16[512,1536]{1,0:T(8,128)(2,1)S(1)} %get-tuple-element.54.refs_1_) | copy-start | bytes 4718596
  182.5 13.8 %copy-start.40 = (bf16[512,1536]{1,0:T(8,128)(2,1)}, bf16[512,1536]{1,0:T(8,128)(2,1)S(1)}, u32[]{:S(2)}) copy-start(bf16[512,1536]{1,0:T(8,128)(2,1)S(1)} %get-tuple-element.55.refs_2_) | copy-start | bytes 4718596
  182.5 13.8 %copy-start.42 = (bf16[512,768]{1,0:T(8,128)(2,1)}, bf16[512,768]{1,0:T(8,128)(2,1)S(1)}, u32[]{:S(2)}) copy-start(bf16[512,768]{1,0:T(8,128)(2,1)S(1)} %get-tuple-element.50.refs_0_) | copy-start | bytes 2359300
  182.5 13.8 %copy-start.44 = (bf16[384,768]{1,0:T(8,128)(2,1)}, bf16[384,768]{1,0:T(8,128)(2,1)S(1)}, u32[]{:S(2)}) copy-start(bf16[384,768]{1,0:T(8,128)(2,1)S(1)} %get-tuple-element.53.refs_0_) | copy-start | bytes 1769476
  197.5 10.6 %copy-start.9 = (f32[512,768]{1,0:T(8,128)}, f32[512,768]{1,0:T(8,128)S(1)}, u32[]{:S(2)}) copy-start(f32[512,768]{1,0:T(8,128)S(1)} %get-tuple-element.62.rows_ref) | copy-start | bytes 4718596
  197.6 2.8 copy-start.5
  200.4 2.3 copy-start.6
  202.7 5.6 %copy-start.63 = (bf16[4,2,96,2304]{3,2,1,0:T(8,128)(2,1)S(1)}, bf16[4,2,96,2304]{3,2,1,0:T(8,128)(2,1)}, u32[]{:S(2)}) copy-start(bf16[4,2,96,2304]{3,2,1,0:T(8,128)(2,1)} %get-tuple-element.59) | copy-start | bytes 10616836
  208.1 3.1 copy-start
  208.1 3.8 copy-start.8
  208.3 3.8 copy-start.28
  208.3 3.8 copy-start.39
  208.3 5.4 %copy-start.41 = (bf16[512,1536]{1,0:T(8,128)(2,1)S(1)}, bf16[512,1536]{1,0:T(8,128)(2,1)}, u32[]{:S(2)}) copy-start(bf16[512,1536]{1,0:T(8,128)(2,1)} %copy-done.40) | copy-start | bytes 4718596
  208.3 5.5 %copy-start.45 = (bf16[384,768]{1,0:T(8,128)(2,1)S(1)}, bf16[384,768]{1,0:T(8,128)(2,1)}, u32[]{:S(2)}) copy-start(bf16[384,768]{1,0:T(8,128)(2,1)} %copy-done.44) | copy-start | bytes 1769476
  211.9 14.7 %copy-start.21 = (bf16[512,1536]{1,0:T(8,128)(2,1)}, bf16[512,1536]{1,0:T(8,128)(2,1)S(1)}, u32[]{:S(2)}) copy-start(bf16[512,1536]{1,0:T(8,128)(2,1)S(1)} %convolution_convert_fusion.refs_1_) | copy-start | bytes 4718596
  211.9 14.7 %collective-permute-start = (bf16[512,1536]{1,0:T(8,128)(2,1)S(1)}, bf16[512,1536]{1,0:T(8,128)(2,1)S(1)}, u32[]{:S(2)}, u32[]{:S(2)}) collective-permute-start(bf16[512,1536]{1,0:T(8,128)(2,1)S(1)} %convolution_convert_fusion.refs_1_), channel_id=1, source_target_pairs={{0,1},{1,0},{2,3},{3,2},{4,5},{5,4},{6,7},{7,6},{8,9},{9,8},{10,11... | collective-permute-start | bytes 4718600 | tf_op jit(solution)/shard_map/ppermute | solution.py:1481
  225.9 1.3 copy-start.26
  226.6 10.8 %copy-start.46 = (bf16[384,768]{1,0:T(8,128)(2,1)}, bf16[384,768]{1,0:T(8,128)(2,1)S(1)}, u32[]{:S(2)}) copy-start(bf16[384,768]{1,0:T(8,128)(2,1)S(1)} %convolution_convert_fusion.1.refs_0_) | copy-start | bytes 1769476
  226.7 10.8 %copy-start.23 = (bf16[512,1536]{1,0:T(8,128)(2,1)}, bf16[512,1536]{1,0:T(8,128)(2,1)S(1)}, u32[]{:S(2)}) copy-start(bf16[512,1536]{1,0:T(8,128)(2,1)S(1)} %collective-permute-done.refs_2_) | copy-start | bytes 4718596
  238.6 2.3 copy-start.1
  241.0 2.3 copy-start.2
  243.3 6.3 %copy-start.31 = (bf16[384,768]{1,0:T(8,128)(2,1)S(1)}, bf16[384,768]{1,0:T(8,128)(2,1)}, u32[]{:S(2)}) copy-start(bf16[384,768]{1,0:T(8,128)(2,1)} %get-tuple-element.71.refs_2_) | copy-start | bytes 1769476
  247.4 2.2 copy-start.3
  249.6 60.4 %slice-start.2 = ((s8[4718592]{0:T(1024)(128)(4,1)}), s8[4194304]{0:T(1024)(128)(4,1)S(1)}, s32[]{:S(2)}) async-start(s8[4718592]{0:T(1024)(128)(4,1)} %bitcast.44), calls=%async_computation.3 | async-start | bytes 8388608
  249.6 60.4 %slice-start.4 = ((s8[4718592]{0:T(1024)(128)(4,1)}), s8[4194304]{0:T(1024)(128)(4,1)S(1)}, s32[]{:S(2)}) async-start(s8[4718592]{0:T(1024)(128)(4,1)} %bitcast.48), calls=%async_computation.5 | async-start | bytes 8388608
  249.6 60.4 %slice-start.3 = ((s8[4718592]{0:T(1024)(128)(4,1)}), s8[524288]{0:T(1024)(128)(4,1)S(1)}, s32[]{:S(2)}) async-start(s8[4718592]{0:T(1024)(128)(4,1)} %bitcast.44), calls=%async_computation.4 | async-start | bytes 1048576
  249.6 60.4 %slice-start.5 = ((s8[4718592]{0:T(1024)(128)(4,1)}), s8[524288]{0:T(1024)(128)(4,1)S(1)}, s32[]{:S(2)}) async-start(s8[4718592]{0:T(1024)(128)(4,1)} %bitcast.48), calls=%async_computation.6 | async-start | bytes 1048576
  310.1 2.3 copy-start.4
  312.4 34.7 %slice-start = ((s8[6291456]{0:T(1024)(128)(4,1)}), s8[4194304]{0:T(1024)(128)(4,1)S(1)}, s32[]{:S(2)}) async-start(s8[6291456]{0:T(1024)(128)(4,1)} %bitcast.41), calls=%async_computation.1 | async-start | bytes 8388608
  312.4 34.7 %slice-start.6 = ((s8[4718592]{0:T(1024)(128)(4,1)}), s8[524288]{0:T(1024)(128)(4,1)S(1)}, s32[]{:S(2)}) async-start(s8[4718592]{0:T(1024)(128)(4,1)} %bitcast.52), calls=%async_computation.7 | async-start | bytes 1048576
  318.5 1.3 copy-start.14
  319.8 1.4 copy-start.22
  324.8 22.3 %slice-start.1 = ((s8[6291456]{0:T(1024)(128)(4,1)}), s8[2097152]{0:T(1024)(128)(4,1)S(1)}, s32[]{:S(2)}) async-start(s8[6291456]{0:T(1024)(128)(4,1)} %bitcast.41), calls=%async_computation.2 | async-start | bytes 4194304
  324.8 22.3 %slice-start.7 = ((s8[4718592]{0:T(1024)(128)(4,1)}), s8[4194304]{0:T(1024)(128)(4,1)S(1)}, s32[]{:S(2)}) async-start(s8[4718592]{0:T(1024)(128)(4,1)} %bitcast.52), calls=%async_computation.8 | async-start | bytes 8388608
  347.1 2.3 copy-start.7
  349.5 1.4 copy-start.10
  350.9 7.6 %copy-start.16 = (f32[1,768]{1,0:T(1,128)S(1)}, f32[1,768]{1,0:T(1,128)}, u32[]{:S(2)}) copy-start(f32[1,768]{1,0:T(1,128)} %copy-done.15) | copy-start | bytes 9220
  350.9 7.6 %copy-start.37 = (bf16[512,1536]{1,0:T(8,128)(2,1)S(1)}, bf16[512,1536]{1,0:T(8,128)(2,1)}, u32[]{:S(2)}) copy-start(bf16[512,1536]{1,0:T(8,128)(2,1)} %copy-done.36) | copy-start | bytes 4718596
  358.5 1.4 copy-start.12
  361.2 1.4 copy-start.35
  363.7 30.3 %copy-start.56 = (s32[512]{0:T(512)S(1)}, s32[512]{0:T(512)}, u32[]{:S(2)}) copy-start(s32[512]{0:T(512)} %add_select_fusion) | copy-start | bytes 6148
  394.7 40.9 %copy-start.59 = (f32[8,100]{1,0:T(8,128)S(1)}, f32[8,100]{1,0:T(8,128)}, u32[]{:S(2)}) copy-start(f32[8,100]{1,0:T(8,128)} %param.28) | copy-start | bytes 9604
  395.4 40.7 %copy-start.58 = (f32[8,192]{1,0:T(8,128)S(1)}, f32[8,192]{1,0:T(8,128)}, u32[]{:S(2)}) copy-start(f32[8,192]{1,0:T(8,128)} %param.29) | copy-start | bytes 18436
  395.4 40.7 %copy-start.51 = (f32[8,100,192]{1,2,0:T(8,128)S(1)}, f32[8,100,192]{1,2,0:T(8,128)}, u32[]{:S(2)}) copy-start(f32[8,100,192]{1,2,0:T(8,128)} %param.26) | copy-start | bytes 1843204
  395.4 40.7 %copy-start.53 = (f32[8,100,192]{1,2,0:T(8,128)S(1)}, f32[8,100,192]{1,2,0:T(8,128)}, u32[]{:S(2)}) copy-start(f32[8,100,192]{1,2,0:T(8,128)} %param.27) | copy-start | bytes 1843204
  435.6 2.0 copy-start.57
  436.0 1.7 copy-start.52
  436.1 1.6 copy-start.54
  (10 other events, 11.5 us)
Sparse Core Ops, SparseCore 0:
  10.2 21.0 all-gather.2

commit v6 on v5

--- a/solution.py
+++ b/solution.py
@@ -161,11 +161,41 @@
     mix(pairs - 1, 1)
 
 
-def attend_kernel(plan, parts, decoder, causal, *refs):
+def feed_pieces(rows_ref, gain_ref, one, two, out_ref, before_ref, source, held_of, active_of):
+    count = one.shape[1] // HIDDEN_PIECE
+    rows = rows_ref[...]
+    source[...] = normed(rows, gain_ref[...])[0].astype(BF16)
+    out_ref[...] = rows
+    for n in range(count + 2):
+        if n < count:
+            here = slice(n * HIDDEN_PIECE, (n + 1) * HIDDEN_PIECE)
+            before = dot(source[...], one[:, here])
+            held_of[n % 2][...] = before
+            before_ref[:, here] = before
+        if 0 < n <= count:
+            active_of[(n - 1) % 2][...] = smooth(held_of[(n - 1) % 2][...]).astype(BF16)
+        if n >= 2:
+            there = slice((n - 2) * HIDDEN_PIECE, (n - 1) * HIDDEN_PIECE)
+            out_ref[...] += dot(active_of[n % 2][...], two[there, :])
+
+
+def attend_kernel(plan, parts, decoder, causal, fed, *refs):
     q_ref, pair_refs = refs[0], refs[1 : 1 + parts]
-    residual_ref, weight_ref, lengths_ref, out_ref, mixed_ref, log_ref = refs[1 + parts : 7 + parts]
+    residual_ref, weight_ref, lengths_ref = refs[1 + parts : 4 + parts]
+    refs = refs[4 + parts :]
+    if fed:
+        gain_ref, one_hbm, two_hbm, out_ref, mixed_ref, log_ref, last_ref, before_ref = refs[:8]
+        *refs, one, two, source, held_a, held_b, active_a, active_b, sems = refs[8:]
+        loads = [
+            pltpu.make_async_copy(one_hbm, one, sems.at[0]),
+            pltpu.make_async_copy(two_hbm, two, sems.at[1]),
+        ]
+        for load in loads:
+            load.start()
+    else:
+        out_ref, mixed_ref, log_ref, *refs = refs
     info = row_scalars(plan, lengths_ref, decoder)
-    bias_ref, q_mark, k_mark, low_ref, scores_a, scores_b, powers_a, powers_b = refs[7 + parts :]
+    bias_ref, q_mark, k_mark, low_ref, scores_a, scores_b, powers_a, powers_b = refs
     width = q_ref.shape[1]
     own = pair_refs[0].shape[0]
     scores_of, powers_of = (scores_a, scores_b), (powers_a, powers_b)
@@ -214,36 +244,52 @@
 
     over_heads(width // LANES, scores, soften, mix)
     out_ref[...] = residual_ref[...] + dot(low_ref[...], weight_ref[...])
-
-
-def attend(plan, queries, pairs, residual, weight, row_lengths, decoder, causal):
+    if fed:
+        for load in loads:
+            load.wait()
+        feed_pieces(
+            out_ref, gain_ref, one, two, last_ref, before_ref, source, (held_a, held_b), (active_a, active_b)
+        )
+
+
+def attend(plan, queries, pairs, residual, weight, row_lengths, decoder, causal, feed=None):
     own, width = queries.shape
     parts, length = len(pairs), sum(pair.shape[0] for pair in pairs)
     vmem = pl.BlockSpec(memory_space=pltpu.VMEM)
+    operands = [queries, *pairs, residual, weight, row_lengths]
+    in_specs = [vmem] * (parts + 3) + [pl.BlockSpec(memory_space=pltpu.SMEM)]
+    rows = jax.ShapeDtypeStruct((own, width), F32)
+    shapes = [rows, rows, jax.ShapeDtypeStruct((own, LANES), F32)]
+    scratch = [
+        pltpu.VMEM((own, length) if causal else (8, LANES), F32),
+        pltpu.VMEM((own, LANES), BF16),
+        pltpu.VMEM((length, LANES), BF16),
+        pltpu.VMEM((own, width), BF16),
+        pltpu.VMEM((own, length), F32),
+        pltpu.VMEM((own, length), F32),
+        pltpu.VMEM((own, length), BF16),
+        pltpu.VMEM((own, length), BF16),
+    ]
+    if feed:
+        gain, one, two = feed
+        operands += [gain[None], one, two]
+        in_specs += [vmem] + [pl.BlockSpec(memory_space=pl.ANY)] * 2
+        shapes += [rows, jax.ShapeDtypeStruct((own, one.shape[1]), F32)]
+        scratch += [pltpu.VMEM(one.shape, BF16), pltpu.VMEM(two.shape, BF16)]
+        scratch += [pltpu.VMEM((own, width), BF16)]
+        scratch += [pltpu.VMEM((own, HIDDEN_PIECE), F32)] * 2
+        scratch += [pltpu.VMEM((own, HIDDEN_PIECE), BF16)] * 2 + [pltpu.SemaphoreType.DMA((2,))]
     return pl.pallas_call(
-        functools.partial(attend_kernel, plan, parts, decoder, causal),
-        out_shape=[
-            jax.ShapeDtypeStruct((own, width), F32),
-            jax.ShapeDtypeStruct((own, width), F32),
-            jax.ShapeDtypeStruct((own, LANES), F32),
-        ],
-        in_specs=[vmem] * (parts + 3) + [pl.BlockSpec(memory_space=pltpu.SMEM)],
-        out_specs=[vmem] * 3,
-        scratch_shapes=[
-            pltpu.VMEM((own, length) if causal else (8, LANES), F32),
-            pltpu.VMEM((own, LANES), BF16),
-            pltpu.VMEM((length, LANES), BF16),
-            pltpu.VMEM((own, width), BF16),
-            pltpu.VMEM((own, length), F32),
-            pltpu.VMEM((own, length), F32),
-            pltpu.VMEM((own, length), BF16),
-            pltpu.VMEM((own, length), BF16),
-        ],
-        compiler_params=pltpu.CompilerParams(vmem_limit_bytes=24 * MIB),
+        functools.partial(attend_kernel, plan, parts, decoder, causal, feed is not None),
+        out_shape=shapes,
+        in_specs=in_specs,
+        out_specs=[vmem] * len(shapes),
+        scratch_shapes=scratch,
+        compiler_params=pltpu.CompilerParams(vmem_limit_bytes=(26 + own // 32 if feed else 24) * MIB),
         cost_estimate=pl.CostEstimate(
             flops=44 * own * length * width, bytes_accessed=6 * own * width, transcendentals=0
         ),
-    )(queries, *pairs, residual, weight, row_lengths)
+    )(*operands)
 
 
 def attend_back_kernel(plan, parts, decoder, want_queries, exchange, *refs):
@@ -422,47 +468,6 @@
     )(*operands)
 
 
-def feed_kernel(rows_ref, gain_ref, one_ref, two_ref, out_ref, before_ref, source, *scratch):
-    held_of, active_of = scratch[0:2], scratch[2:4]
-    count = one_ref.shape[1] // HIDDEN_PIECE
-    rows = rows_ref[...]
-    source[...] = normed(rows, gain_ref[...])[0].astype(BF16)
-    out_ref[...] = rows
-    for n in range(count + 2):
-        if n < count:
-            here = slice(n * HIDDEN_PIECE, (n + 1) * HIDDEN_PIECE)
-            before = dot(source[...], one_ref[:, here])
-            held_of[n % 2][...] = before
-            before_ref[:, here] = before
-        if 0 < n <= count:
-            active_of[(n - 1) % 2][...] = smooth(held_of[(n - 1) % 2][...]).astype(BF16)
-        if n >= 2:
-            there = slice((n - 2) * HIDDEN_PIECE, (n - 1) * HIDDEN_PIECE)
-            out_ref[...] += dot(active_of[n % 2][...], two_ref[there, :])
-
-
-def feed(rows, gain, one, two):
-    own, width = rows.shape
-    hidden = one.shape[1]
-    vmem = pl.BlockSpec(memory_space=pltpu.VMEM)
-    return pl.pallas_call(
-        feed_kernel,
-        out_shape=[
-            jax.ShapeDtypeStruct((own, width), F32),
-            jax.ShapeDtypeStruct((own, hidden), F32),
-        ],
-        in_specs=[vmem] * 4,
-        out_specs=[vmem] * 2,
-        scratch_shapes=[pltpu.VMEM((own, width), BF16)]
-        + [pltpu.VMEM((own, HIDDEN_PIECE), F32)] * 2
-        + [pltpu.VMEM((own, HIDDEN_PIECE), BF16)] * 2,
-        compiler_params=pltpu.CompilerParams(vmem_limit_bytes=28 * MIB),
-        cost_estimate=pl.CostEstimate(
-            flops=4 * own * width * hidden, bytes_accessed=4 * width * hidden, transcendentals=0
-        ),
-    )(rows, gain[None], one, two)
-
-
 def smooth_slope(u):
     rate = (2.0 / jnp.pi) ** 0.5
     bend = jnp.tanh(rate * (u + 0.044715 * (u * u * u)))
@@ -909,7 +914,7 @@
             return jnp.where(before_turn, rows(plan.near), rows(plan.far))
 
         values = own_heads(held)
-        dec_rows[...] = values.astype(BF16)
+        dec_rows[...] = values
         dec_heads[...] = normed(values, gain)[0].astype(BF16)
         target_rows[...] = own_heads(base).astype(BF16)
 
@@ -1029,7 +1034,8 @@
         + [full(rows, attend_out.shape[2])] * 3
         + [full(rows, expand_weights.shape[2])] * 2
         + [full(4, tall // 4, width)] * 2
-        + [jax.ShapeDtypeStruct((n, width), BF16) for n in [plan.own] * 2 + [plan.heads] * 3]
+        + [jax.ShapeDtypeStruct((plan.own, width), BF16)] * 2
+        + [jax.ShapeDtypeStruct((plan.heads, width), kind) for kind in (F32, BF16, BF16)]
     )
     copies = 10 * (1 + 4 * (rows_z - 1) + 2) + 4 * (1 + 4 * (rows_z - 1) + 2) + 3
     anywhere, vmem, smem = [
@@ -1543,7 +1549,6 @@
         )
         attend_in, attend_out = flat[:3], flat[3:6]
         expand_weights, reduce_weights = flat[6:8], flat[8:10]
-        dec_input = dec_input.astype(F32)
     else:
 
         def lookup(wanted):
@@ -1618,10 +1623,17 @@
         enc_queries = dot(normed_low, attend_in[0][:, :width]).astype(BF16)
         dec_pairs = key_parts(keys_low, attend_in[1][:, width:])
         dec_queries = dot(heads_low, attend_in[1][:, :width]).astype(BF16)
-    enc_mid, enc_mixed, enc_logs = attend(
-        plan, enc_queries, enc_pairs, enc_input, attend_out[0], row_lengths, False, False
+    enc_mid, enc_mixed, enc_logs, enc_last, enc_kept = attend(
+        plan,
+        enc_queries,
+        enc_pairs,
+        enc_input,
+        attend_out[0],
+        row_lengths,
+        False,
+        False,
+        (norm_gains[1], expand_weights[0], reduce_weights[0]),
     )
-    enc_last, enc_kept = feed(enc_mid, norm_gains[1], expand_weights[0], reduce_weights[0])
     encoded = normed(enc_last, norm_gains[2])[0].astype(BF16)
     cross_pairs = key_parts(encoded, attend_in[2][:, width:])
 
@@ -1630,10 +1642,17 @@
     )[0]
     cross_source = normed(dec_first, norm_gains[4])[0].astype(BF16)
     cross_queries = dot(cross_source, attend_in[2][:, :width]).astype(BF16)
-    dec_second, cross_mixed, cross_logs = attend(
-        plan, cross_queries, cross_pairs, dec_first, attend_out[2], row_lengths, True, False
+    dec_second, cross_mixed, cross_logs, dec_last, dec_kept = attend(
+        plan,
+        cross_queries,
+        cross_pairs,
+        dec_first,
+        attend_out[2],
+        row_lengths,
+        True,
+        False,
+        (norm_gains[5], expand_weights[1], reduce_weights[1]),
     )
-    dec_last, dec_kept = feed(dec_second, norm_gains[5], expand_weights[1], reduce_weights[1])
 
     if on_links:
         wide = (plan.far[-1] + heads + LANES - 1) // LANES * LANES

time: 450 us -> 444 us (0.987)
  local copies, waits for them, and re-layouts: 43.3 us -> 33.1 us
    pallas_call x3, Pallas kernels: 35.9 us -> 47.1 us  [attend(): pl.pallas_call(functools.partial(attend_kernel, plan, parts, decoder, cau...]
    unnamed x146 -> x138, local copies, waits for them, and re-layouts: 41 us -> 30.8 us
    pallas_call x2 -> x0, Pallas kernels: 9.39 us -> none  [feed(): pl.pallas_call(feed_kernel, out_shape=[jax.ShapeDtypeStruct((own, width),...]
where the time goes in v6:
time: 444 us; the launch traced here: 440 us
  Pallas kernels  371 us (84%)
  local copies, waits for them, and re-layouts  33.1 us (7%)
  between operations  16.9 us (4%)
  matrix products  6.78 us (2%)
  other arithmetic  6.42 us (1%)
  blocking collectives  5.67 us (1%)
    pallas_call x1, Pallas kernels, gather_weights(): pl.pallas_call(functools.partial(gather_kernel, plan, rows_z, rows_y), ou...  151 us
    pallas_call x1, Pallas kernels, vocab_exchange(): pl.pallas_call(functools.partial(vocab_exchange_kernel, plan, tile), out_...  61 us
    pallas_call x2, Pallas kernels, attend_back(): pl.pallas_call(functools.partial(attend_back_kernel, plan, parts, decoder...  52.6 us
    pallas_call x3, Pallas kernels, attend(): pl.pallas_call(functools.partial(attend_kernel, plan, parts, decoder, cau...  47.1 us
    pallas_call x1, Pallas kernels, reduce_over_devices(): pl.pallas_call(functools.partial(reduce_kernel, rows_dp), out_shape=[jax....  38.1 us
    unnamed x138, local copies, waits for them, and re-layouts  30.8 us
    pallas_call x2, Pallas kernels, feed_back(): pl.pallas_call(feed_back_kernel, out_shape=jax.ShapeDtypeStruct((own, wid...  11.6 us
    pallas_call x1, Pallas kernels, project(): pl.pallas_call(functools.partial(project_kernel, plan), out_shape=[jax.Sh...  9.79 us
  transfers between devices with their start and end apart: 2, of which 0 were waited for; matrix products, arithmetic and copies ran while one was open for 1% of the time, Pallas kernels for 37%

profile of v6, /device:TPU:25, one launch (start us, length us, event | category | flops | bytes accessed | tf_op | source)
XLA Modules:
  0.0 440.4 jit_solution(1452564529873849767)
XLA Ops:
  7.3 1.2 convert_bitcast_fusion
  8.5 0.8 pad.23
  9.4 0.2 reduce-window.7
  9.6 5.7 %all-gather = s32[12,2,256]{2,1,0:T(2,128)S(1)} all-gather(s32[3,2,256]{2,1,0:T(2,128)S(1)} %pad_add_fusion), channel_id=2, replica_groups=mesh['dp'=8,'vocab'=4] {'vocab'}, dimensions={0}, use_global_device_ids=true | all-gather | bytes 30720 | tf_op jit(solution)/shard_map/all_gather | solution.py:1489
  15.3 0.1 pad_slice_fusion.1
  15.3 0.1 concatenate.18
  15.4 0.1 pad_slice_fusion
  15.5 0.1 concatenate.20
  15.6 0.1 slice_reduce_fusion.3
  15.7 0.1 concatenate.19
  15.8 0.1 concatenate.21
  15.9 0.6 and_select_fusion.refs_4_
  16.6 0.6 fusion.14
  17.2 151.1 %shard_map.198 = (bf16[4,2,96,2304]{3,2,1,0:T(8,128)(2,1)}, bf16[4,2,96,2304]{3,2,1,0:T(8,128)(2,1)}, bf16[4,2,96,2304]{3,2,1,0:T(8,128)(2,1)}, bf16[4,2,96,768]...) custom-call(bf16[3,96,2304]{2,1,0:T(8,128)(2,1)} %refs_0_.1, ...), custom_call_target="tpu_custom_call" | custom-call | bytes 400000000 | tf_op jit(solution)/shard_map/pallas_call | solution.py:1044
  168.3 0.1 convert_reduce_fusion
  168.4 0.1 select_reduce_fusion
  168.5 0.6 add_select_fusion
  169.1 1.4 copy-done.14
  170.5 1.1 copy-done.24
  171.6 1.1 copy-done.25
  172.7 1.1 copy-done.27
  173.8 9.8 %shard_map.199 = (f32[512,768]{1,0:T(8,128)S(1)}, bf16[512,768]{1,0:T(8,128)(2,1)S(1)}, bf16[512,1536]{1,0:T(8,128)(2,1)S(1)}, bf16[512,1536]{1,0:T(8,128)(2,1)S...) custom-call(bf16[512,768]{1,0:T(8,128)(2,1)S(1)} %copy-done.24, ...), custom_call_target="tpu_custom_call" | custom-call | flops 3019898880 | bytes 7077888 | tf_op jit(solution)/shard_map/pallas_call | solution.py:583
  183.6 1.1 copy-done.33
  184.7 1.1 copy-done.35
  185.9 20.5 %shard_map.201 = (f32[512,768]{1,0:T(8,128)S(1)}, f32[512,768]{1,0:T(8,128)S(1)}, f32[512,128]{1,0:T(8,128)S(1)}, f32[512,768]{1,0:T(8,128)S(1)}, f32[512,3072]{1,0:T(8,128)}) custom-call(bf16[512,768]{1,0:T(8,128)(2,1)S(1)} %get-tuple-element.50.refs_0_, bf16[512,1536]{1,0:T(8,128)(2,1)S(1)} %get-tuple-element.51.refs_1_, ...), custom_call_target="tpu_custom_call" | custom-call | flops 17716740096 | bytes 2359296 | tf_op jit(solution)/shard_map/pallas_call | solution.py:282
  206.4 1.1 copy-done.3
  207.5 1.2 copy-done.45
  208.7 0.2 multiply_reduce_fusion
  208.9 0.1 copy.41
  209.1 3.3 convolution_convert_fusion.refs_1_
  212.4 0.2 collective-permute-start
  212.7 12.0 %shard_map.200 = (f32[384,768]{1,0:T(8,128)S(1)}, f32[384,768]{1,0:T(8,128)}, f32[384,128]{1,0:T(8,128)}) custom-call(bf16[384,768]{1,0:T(8,128)(2,1)S(1)} %get-tuple-element.53.refs_0_, bf16[512,1536]{1,0:T(8,128)(2,1)S(1)} %copy-done.34, bf16[512,1536]{1,0:T(8,128)(2,1)S(1)} %copy-done.36, f32[384,768]{1,0:T(8,128)S(1)} %copy-done.23, ...), custom_call_target="tpu_custom_call" | custom-call | flops 13287555072 | bytes 1769472 | tf_op jit(solution)/shard_map/pallas_call | solution.py:282
  224.6 0.2 multiply_reduce_fusion.1
  224.8 2.1 convolution_convert_fusion.1.refs_0_
  226.9 14.7 %shard_map.202 = (f32[384,768]{1,0:T(8,128)S(1)}, f32[384,768]{1,0:T(8,128)S(1)}, f32[384,128]{1,0:T(8,128)S(1)}, f32[384,768]{1,0:T(8,128)S(1)}, f32[384,3072]{1,0:T(8,128)S(1)}) custom-call(bf16[384,768]{1,0:T(8,128)(2,1)S(1)} %convolution_convert_fusion.1.refs_0_, bf16[512,1536]{1,0:T(8,128)(2,1)S(1)} %convolution_convert_fusion.refs_1_, ...), custom_call_target="tpu_custom_call" | custom-call | flops 13287555072 | bytes 1769472 | tf_op jit(solution)/shard_map/pallas_call | solution.py:282
  241.7 2.3 copy-done
  243.9 1.0 copy-done.41
  244.9 1.0 copy-done.43
  246.0 0.1 copy.40
  246.1 1.4 copy-done.44
  247.6 61.0 %shard_map.203 = (f32[384,768]{1,0:T(8,128)S(1)}, f32[8,128]{1,0:T(8,128)S(1)}) custom-call(f32[384,768]{1,0:T(8,128)S(1)} %copy-done.44, f32[1,768]{1,0:T(1,128)S(1)} %get-tuple-element.99.refs_1_, bf16[384,768]{1,0:T(8,128)(2,1)S(1)} %copy-done.26, bf16[8032,768]{1,0:T(8,128)(2,1)} %refs_3_.3, f32[8,1152]{1,0:T(8,128)S(1)} %pad.24.refs_4_, ...), custom_call_target="tpu_custom_call" | custom-call | flops 72477573120 | bytes 12337152 | tf_op jit(solution)/shard_map/pallas_call | solution.py:1249
  308.7 5.0 %shard_map.204.refs_3_ = f32[384,768]{1,0:T(8,128)S(1)} custom-call(f32[384,768]{1,0:T(8,128)S(1)} %get-tuple-element.70.grad_ref, f32[384,768]{1,0:T(8,128)S(1)} %get-tuple-element.71.rows_ref, f32[1,768]{1,0:T(1,128)S(1)} %get-tuple-element.100.refs_6_.gain_ref, f32[384,3072]{1,0:T(8,128)S(1)} %bitcast.52, bf16[768,3072]{1,0:T(8,128)(2,1)S(1)} %bitcast.46, ...), custom_call_target="tpu_custom_call" | custom-call | flops 3623878656 | bytes 9437184 | tf_op jit(solution)/shard_map/pallas_call | solution.py:504
  313.7 1.0 copy-done.7
  314.7 1.4 copy-done.8
  316.1 2.1 copy-done.16
  318.2 1.3 copy-done.21
  319.5 1.1 copy-done.40
  320.6 1.3 copy-done.42
  321.8 22.3 %shard_map.205.grad_ref = f32[512,768]{1,0:T(8,128)S(1)} custom-call(bf16[384,768]{1,0:T(8,128)(2,1)S(1)} %copy-done.40, bf16[512,1536]{1,0:T(8,128)(2,1)S(1)} %copy-done.16, bf16[512,1536]{1,0:T(8,128)(2,1)} %copy-done.17, f32[384,768]{1,0:T(8,128)S(1)} %copy-done.8, bf16[768,768]{1,0:T(8,128)(2,1)S(1)} %bitcast.73, f32[384,768]{1,0:T(8,128)S(1)} %copy-done.42, ...), custom_call_target="tpu_custom_call" | custom-call | flops 24159191040 | bytes 7864320 | tf_op jit(solution)/shard_map/pallas_call | solution.py:456
  344.1 1.1 copy-done.5
  345.3 2.3 copy-done.1
  347.6 1.4 copy-done.4
  349.0 1.4 copy-done.6
  350.5 6.5 %shard_map.206.refs_3_ = f32[512,768]{1,0:T(8,128)S(1)} custom-call(f32[512,768]{1,0:T(8,128)S(1)} %copy-done.6, f32[512,768]{1,0:T(8,128)S(1)} %copy-done.4, f32[1,768]{1,0:T(1,128)S(1)} %get-tuple-element.94.refs_6_.gain_ref, f32[512,3072]{1,0:T(8,128)S(1)} %bitcast.42, bf16[768,3072]{1,0:T(8,128)(2,1)S(1)} %bitcast.56, bf16[3072,768]{1,0:T(8,128)(2,1)S(1)} %bitcast.58), custom_call_target="tpu_custom_call" | custom-call | flops 4831838208 | bytes 9437184 | tf_op jit(solution)/shard_map/pallas_call | solution.py:504
  357.1 1.3 copy-done.19
  358.3 30.3 %shard_map.207 = f32[512,768]{1,0:T(8,128)S(1)} custom-call(bf16[512,768]{1,0:T(8,128)(2,1)S(1)} %copy-done.38, bf16[512,1536]{1,0:T(8,128)(2,1)S(1)} %copy-done.30, bf16[512,1536]{1,0:T(8,128)(2,1)S(1)} %copy-done.32, f32[512,768]{1,0:T(8,128)S(1)} %shard_map.206.refs_3_, bf16[768,768]{1,0:T(8,128)(2,1)S(1)} %bitcast.71, f32[512,768]{1,0:T(8,128)} %copy-done.45, ...), custom_call_target="tpu_custom_call" | custom-call | flops 32212254720 | bytes 7864320 | tf_op jit(solution)/shard_map/pallas_call | solution.py:456
  388.6 0.7 fusion.2
  389.3 0.7 convolution_add_fusion.table_ref
  390.0 38.1 %shard_map.208 = (f32[8,192,128]{2,1,0:T(8,128)S(1)}, f32[8,128]{1,0:T(8,128)S(1)}, f32[8,128]{1,0:T(8,128)S(1)}) custom-call(s32[2,3]{1,0:T(2,128)S(1)} %bitcast.69, f32[768,384]{1,0:T(8,128)S(1)} %convolution_add_fusion.table_ref, f32[8,128]{1,0:T(8,128)S(1)} %get-tuple-element.79.stat_ref), custom_call_target="tpu_custom_call" | custom-call | tf_op jit(solution)/shard_map/pallas_call | solution.py:1424
  428.2 0.6 slice_reduce_fusion
  429.5 0.6 fusion.11
  430.1 0.1 fusion.13
  430.2 0.4 multiply_reduce_fusion.2
  430.7 1.6 add_subtract_fusion
  (145 shorter events, 0.5 us)
Async XLA Ops:
  7.2 2.2 copy-start.56
  7.2 2.2 copy-start.57
  7.2 2.2 copy-start.11
  7.2 2.4 copy-start.55
  7.2 9.3 %copy-start.50 = (f32[7,768]{1,0:T(8,128)S(1)}, f32[7,768]{1,0:T(8,128)}, u32[]{:S(2)}) copy-start(f32[7,768]{1,0:T(8,128)} %param.25) | copy-start | bytes 64516
  7.2 161.8 %all-gather.3.cloned.1.call-start = ((), (), s32[]{:S(2)}) async-start(), calls=%async_computation | async-start | bytes 1966080 | tf_op jit(solution)/shard_map/all_gather | solution.py:1539
  17.1 151.9 %copy-start.9 = (f32[1,768]{1,0:T(1,128)}, f32[1,768]{1,0:T(1,128)S(1)}, u32[]{:S(2)}) copy-start(f32[1,768]{1,0:T(1,128)S(1)} %get-tuple-element.97.refs_4_.refs_10_) | copy-start | bytes 9220
  17.1 151.2 %copy-start.12 = (s32[2,1,3]{2,1,0:T(1,128)S(1)}, s32[2,1,3]{2,1,0:T(1,128)}, u32[]{:S(2)}) copy-start(s32[2,1,3]{2,1,0:T(1,128)} %param.18) | copy-start | bytes 76
  17.2 151.9 %copy-start.13 = (s32[2,1,3]{2,1,0:T(1,128)S(1)}, s32[2,1,3]{2,1,0:T(1,128)}, u32[]{:S(2)}) copy-start(s32[2,1,3]{2,1,0:T(1,128)} %param.19) | copy-start | bytes 76
  169.0 1.4 copy-start.14
  170.5 1.1 copy-start.24
  171.6 1.1 copy-start.25
  173.8 12.1 %copy-start.18 = (bf16[4,2,96,768]{3,2,1,0:T(8,128)(2,1)S(1)}, bf16[4,2,96,768]{3,2,1,0:T(8,128)(2,1)}, u32[]{:S(2)}) copy-start(bf16[4,2,96,768]{3,2,1,0:T(8,128)(2,1)} %get-tuple-element.61) | copy-start | bytes 3538948
  183.6 1.2 copy-start.33
  184.7 1.1 copy-start.35
  185.9 20.5 %copy-start.28 = (f32[512,768]{1,0:T(8,128)}, f32[512,768]{1,0:T(8,128)S(1)}, u32[]{:S(2)}) copy-start(f32[512,768]{1,0:T(8,128)S(1)} %get-tuple-element.60.refs_3_.refs_9_) | copy-start | bytes 4718596
  185.9 20.5 %copy-start.29 = (bf16[512,1536]{1,0:T(8,128)(2,1)}, bf16[512,1536]{1,0:T(8,128)(2,1)S(1)}, u32[]{:S(2)}) copy-start(bf16[512,1536]{1,0:T(8,128)(2,1)S(1)} %get-tuple-element.51.refs_1_) | copy-start | bytes 4718596
  185.9 20.5 %copy-start.31 = (bf16[512,1536]{1,0:T(8,128)(2,1)}, bf16[512,1536]{1,0:T(8,128)(2,1)S(1)}, u32[]{:S(2)}) copy-start(bf16[512,1536]{1,0:T(8,128)(2,1)S(1)} %get-tuple-element.52.refs_2_) | copy-start | bytes 4718596
  185.9 20.5 %copy-start.37 = (bf16[512,768]{1,0:T(8,128)(2,1)}, bf16[512,768]{1,0:T(8,128)(2,1)S(1)}, u32[]{:S(2)}) copy-start(bf16[512,768]{1,0:T(8,128)(2,1)S(1)} %get-tuple-element.50.refs_0_) | copy-start | bytes 2359300
  207.5 1.2 copy-start.45
  208.7 3.7 copy-start.2
  209.0 3.6 copy-start.22
  209.0 3.6 copy-start.23
  209.0 3.6 copy-start.34
  209.1 3.6 copy-start.36
  212.4 14.5 %copy-start.15 = (bf16[512,1536]{1,0:T(8,128)(2,1)}, bf16[512,1536]{1,0:T(8,128)(2,1)S(1)}, u32[]{:S(2)}) copy-start(bf16[512,1536]{1,0:T(8,128)(2,1)S(1)} %convolution_convert_fusion.refs_1_) | copy-start | bytes 4718596
  212.4 14.5 %collective-permute-start = (bf16[512,1536]{1,0:T(8,128)(2,1)S(1)}, bf16[512,1536]{1,0:T(8,128)(2,1)S(1)}, u32[]{:S(2)}, u32[]{:S(2)}) collective-permute-start(bf16[512,1536]{1,0:T(8,128)(2,1)S(1)} %convolution_convert_fusion.refs_1_), channel_id=1, source_target_pairs={{0,1},{1,0},{2,3},{3,2},{4,5},{5,4},{6,7},{7,6},{8,9},{9,8},{10,11... | collective-permute-start | bytes 4718600 | tf_op jit(solution)/shard_map/ppermute | solution.py:1487
  224.8 2.1 copy-start.20
  226.9 14.8 %copy-start.39 = (bf16[384,768]{1,0:T(8,128)(2,1)}, bf16[384,768]{1,0:T(8,128)(2,1)S(1)}, u32[]{:S(2)}) copy-start(bf16[384,768]{1,0:T(8,128)(2,1)S(1)} %convolution_convert_fusion.1.refs_0_) | copy-start | bytes 1769476
  226.9 14.7 %copy-start.17 = (bf16[512,1536]{1,0:T(8,128)(2,1)}, bf16[512,1536]{1,0:T(8,128)(2,1)S(1)}, u32[]{:S(2)}) copy-start(bf16[512,1536]{1,0:T(8,128)(2,1)S(1)} %collective-permute-done.refs_2_) | copy-start | bytes 4718596
  226.9 19.2 %copy-start.26 = (bf16[384,768]{1,0:T(8,128)(2,1)S(1)}, bf16[384,768]{1,0:T(8,128)(2,1)}, u32[]{:S(2)}) copy-start(bf16[384,768]{1,0:T(8,128)(2,1)} %get-tuple-element.69.refs_2_) | copy-start | bytes 1769476
  241.7 2.3 copy-start
  246.1 62.5 %slice-start.2 = ((s8[4718592]{0:T(1024)(128)(4,1)}), s8[4194304]{0:T(1024)(128)(4,1)S(1)}, s32[]{:S(2)}) async-start(s8[4718592]{0:T(1024)(128)(4,1)} %bitcast.44), calls=%async_computation.3 | async-start | bytes 8388608
  246.1 62.5 %slice-start.4 = ((s8[4718592]{0:T(1024)(128)(4,1)}), s8[4194304]{0:T(1024)(128)(4,1)S(1)}, s32[]{:S(2)}) async-start(s8[4718592]{0:T(1024)(128)(4,1)} %bitcast.48), calls=%async_computation.5 | async-start | bytes 8388608
  246.1 62.5 %slice-start.6 = ((s8[4718592]{0:T(1024)(128)(4,1)}), s8[4194304]{0:T(1024)(128)(4,1)S(1)}, s32[]{:S(2)}) async-start(s8[4718592]{0:T(1024)(128)(4,1)} %bitcast.51), calls=%async_computation.7 | async-start | bytes 8388608
  246.1 1.4 copy-start.44
  247.6 61.0 %slice-start.3 = ((s8[4718592]{0:T(1024)(128)(4,1)}), s8[524288]{0:T(1024)(128)(4,1)S(1)}, s32[]{:S(2)}) async-start(s8[4718592]{0:T(1024)(128)(4,1)} %bitcast.44), calls=%async_computation.4 | async-start | bytes 1048576
  247.6 61.1 %slice-start.5 = ((s8[4718592]{0:T(1024)(128)(4,1)}), s8[524288]{0:T(1024)(128)(4,1)S(1)}, s32[]{:S(2)}) async-start(s8[4718592]{0:T(1024)(128)(4,1)} %bitcast.48), calls=%async_computation.6 | async-start | bytes 1048576
  247.6 61.1 %slice-start.7 = ((s8[4718592]{0:T(1024)(128)(4,1)}), s8[524288]{0:T(1024)(128)(4,1)S(1)}, s32[]{:S(2)}) async-start(s8[4718592]{0:T(1024)(128)(4,1)} %bitcast.51), calls=%async_computation.8 | async-start | bytes 1048576
  314.7 30.6 %slice-start = ((s8[6291456]{0:T(1024)(128)(4,1)}), s8[4194304]{0:T(1024)(128)(4,1)S(1)}, s32[]{:S(2)}) async-start(s8[6291456]{0:T(1024)(128)(4,1)} %bitcast.41), calls=%async_computation.1 | async-start | bytes 8388608
  314.7 30.6 %slice-start.8 = ((s8[4718592]{0:T(1024)(128)(4,1)}), s8[4194304]{0:T(1024)(128)(4,1)S(1)}, s32[]{:S(2)}) async-start(s8[4718592]{0:T(1024)(128)(4,1)} %bitcast.54), calls=%async_computation.9 | async-start | bytes 8388608
  314.7 1.4 copy-start.8
  316.1 2.1 copy-start.16
  318.2 1.3 copy-start.21
  320.6 1.3 copy-start.42
  321.8 23.5 %slice-start.1 = ((s8[6291456]{0:T(1024)(128)(4,1)}), s8[2097152]{0:T(1024)(128)(4,1)S(1)}, s32[]{:S(2)}) async-start(s8[6291456]{0:T(1024)(128)(4,1)} %bitcast.41), calls=%async_computation.2 | async-start | bytes 4194304
  321.8 23.5 %slice-start.9 = ((s8[4718592]{0:T(1024)(128)(4,1)}), s8[524288]{0:T(1024)(128)(4,1)S(1)}, s32[]{:S(2)}) async-start(s8[4718592]{0:T(1024)(128)(4,1)} %bitcast.54), calls=%async_computation.10 | async-start | bytes 1048576
  344.1 1.1 copy-start.5
  345.3 2.3 copy-start.1
  347.6 1.4 copy-start.4
  349.0 1.4 copy-start.6
  350.5 6.6 %copy-start.10 = (f32[1,768]{1,0:T(1,128)S(1)}, f32[1,768]{1,0:T(1,128)}, u32[]{:S(2)}) copy-start(f32[1,768]{1,0:T(1,128)} %copy-done.9) | copy-start | bytes 9220
  350.5 6.6 %copy-start.30 = (bf16[512,1536]{1,0:T(8,128)(2,1)S(1)}, bf16[512,1536]{1,0:T(8,128)(2,1)}, u32[]{:S(2)}) copy-start(bf16[512,1536]{1,0:T(8,128)(2,1)} %copy-done.29) | copy-start | bytes 4718596
  350.5 6.6 %copy-start.32 = (bf16[512,1536]{1,0:T(8,128)(2,1)S(1)}, bf16[512,1536]{1,0:T(8,128)(2,1)}, u32[]{:S(2)}) copy-start(bf16[512,1536]{1,0:T(8,128)(2,1)} %copy-done.31) | copy-start | bytes 4718596
  350.5 6.6 %copy-start.38 = (bf16[512,768]{1,0:T(8,128)(2,1)S(1)}, bf16[512,768]{1,0:T(8,128)(2,1)}, u32[]{:S(2)}) copy-start(bf16[512,768]{1,0:T(8,128)(2,1)} %copy-done.37) | copy-start | bytes 2359300
  357.0 1.3 copy-start.19
  358.3 30.3 %copy-start.51 = (s32[512]{0:T(512)S(1)}, s32[512]{0:T(512)}, u32[]{:S(2)}) copy-start(s32[512]{0:T(512)} %add_select_fusion) | copy-start | bytes 6148
  389.3 40.8 %copy-start.54 = (f32[8,100]{1,0:T(8,128)S(1)}, f32[8,100]{1,0:T(8,128)}, u32[]{:S(2)}) copy-start(f32[8,100]{1,0:T(8,128)} %param.28) | copy-start | bytes 9604
  390.0 40.6 %copy-start.53 = (f32[8,192]{1,0:T(8,128)S(1)}, f32[8,192]{1,0:T(8,128)}, u32[]{:S(2)}) copy-start(f32[8,192]{1,0:T(8,128)} %param.29) | copy-start | bytes 18436
  390.0 40.7 %copy-start.46 = (f32[8,100,192]{1,2,0:T(8,128)S(1)}, f32[8,100,192]{1,2,0:T(8,128)}, u32[]{:S(2)}) copy-start(f32[8,100,192]{1,2,0:T(8,128)} %param.26) | copy-start | bytes 1843204
  390.0 40.7 %copy-start.48 = (f32[8,100,192]{1,2,0:T(8,128)S(1)}, f32[8,100,192]{1,2,0:T(8,128)}, u32[]{:S(2)}) copy-start(f32[8,100,192]{1,2,0:T(8,128)} %param.27) | copy-start | bytes 1843204
  430.2 2.0 copy-start.52
  430.6 1.7 copy-start.47
  430.6 1.6 copy-start.49
  (6 other events, 6.3 us)
Sparse Core Ops, SparseCore 0:
  10.2 21.0 all-gather.2

commit v7 on v6

--- a/solution.py
+++ b/solution.py
@@ -445,7 +445,9 @@
             + scratch
         )
         params = pltpu.CompilerParams(
-            collective_id=collective_id, has_side_effects=True, vmem_limit_bytes=46 * MIB
+            collective_id=collective_id,
+            has_side_effects=True,
+            vmem_limit_bytes=(30 + heads // 32) * MIB,
         )
     else:
         shapes = [jax.ShapeDtypeStruct(pair.shape, F32) for pair in pairs]
@@ -1285,8 +1287,8 @@
 
 
 def reduce_kernel(rows_dp, task_ref, table_ref, stat_ref, out_ref, stats_out, squares_out, *scratch):
-    cast, crossed, swap, swapped, own, outgoing, pieces, result, results = scratch[:9]
-    stats, squares, send_sem, recv_sem = scratch[9:]
+    cast, crossed, swap, swapped, own, others, outgoing, pieces, result, results = scratch[:10]
+    stats, squares, send_sem, recv_sem = scratch[10:]
     features = own.shape[1]
     at, v = lax.axis_index("dp"), lax.axis_index("vocab")
     x, core = v // 2, lax.rem(v, 2)
@@ -1318,34 +1320,37 @@
     stat_x = remote(stats.at[0], stats.at[1], 1, 1, {"vocab": across})
     over_x.start()
     stat_x.start()
-    over_x.wait_recv()
+    tasks = [[task_ref[m, s] for s in range(task_ref.shape[1])] for m in range(2)]
+
+    def by_task(part, t, came):
+        total = jnp.zeros((features, LANES), F32)
+        if came:
+            start = pl.multiple_of(part * features, features)
+            rows = crossed[pl.ds(start, features), :].astype(F32)
+            order = tasks[::-1]
+        else:
+            start = pl.multiple_of(x * half + part * features, features)
+            rows = table_ref[pl.ds(start, features), :]
+            order = tasks
+        for s in range(task_ref.shape[1]):
+            task = jnp.where(x == 0, order[0][s], order[1][s])
+            total = total + jnp.where(task == t, rows[:, s * LANES : (s + 1) * LANES], 0.0)
+        return total
+
+    for t in range(TASKS):
+        others[t] = by_task(1 - core, t, False)
+        own[t] = by_task(core, t, False)
     stat_x.wait_recv()
-
     stats[2] = stats[0] + stats[1]
     stat_core = remote(stats.at[2], stats.at[3], 2, 2, {"vocab": twin})
     stat_core.start()
-    tasks = [[task_ref[m, s] for s in range(task_ref.shape[1])] for m in range(2)]
-    other = jnp.where(x == 0, 1, 0)
-
-    def by_task(part, t):
-        start = pl.multiple_of(part * features, features)
-        mine = table_ref[pl.ds(pl.multiple_of(x * half + part * features, features), features), :]
-        theirs = crossed[pl.ds(start, features), :].astype(F32)
-        total = jnp.zeros((features, LANES), F32)
-        for s in range(task_ref.shape[1]):
-            lanes = slice(s * LANES, (s + 1) * LANES)
-            mine_task = jnp.where(x == 0, tasks[0][s], tasks[1][s])
-            their_task = jnp.where(x == 0, tasks[1][s], tasks[0][s])
-            total = total + jnp.where(mine_task == t, mine[:, lanes], 0.0)
-            total = total + jnp.where(their_task == t, theirs[:, lanes], 0.0)
-        return total
-
+    over_x.wait_recv()
     for t in range(TASKS):
-        swap[t] = by_task(1 - core, t).astype(BF16)
+        swap[t] = (others[t] + by_task(1 - core, t, True)).astype(BF16)
     over_core = remote(swap, swapped, 3, 3, {"vocab": twin})
     over_core.start()
     for t in range(TASKS):
-        own[t] = by_task(core, t)
+        own[t] = own[t] + by_task(core, t, True)
     over_core.wait_recv()
     stat_core.wait_recv()
     stats[4 + at] = stats[2] + stats[3]
@@ -1435,6 +1440,7 @@
             pltpu.VMEM((2 * features, table.shape[1]), BF16),
             pltpu.VMEM((TASKS, features, LANES), BF16),
             pltpu.VMEM((TASKS, features, LANES), BF16),
+            pltpu.VMEM((TASKS, features, LANES), F32),
             pltpu.VMEM((TASKS, features, LANES), F32),
             pltpu.VMEM((TASKS, features, LANES), BF16),
             pltpu.VMEM((rows_dp, features, LANES), BF16),

time: 444 us -> 443 us (level)
    unnamed x138 -> x142, local copies, waits for them, and re-layouts: 30.8 us -> 30.4 us
where the time goes in v7:
time: 443 us; the launch traced here: 439 us
  Pallas kernels  370 us (84%)
  local copies, waits for them, and re-layouts  32.7 us (7%)
  between operations  17 us (4%)
  matrix products  6.78 us (2%)
  other arithmetic  6.42 us (1%)
  blocking collectives  5.67 us (1%)
    pallas_call x1, Pallas kernels, gather_weights(): pl.pallas_call(functools.partial(gather_kernel, plan, rows_z, rows_y), ou...  151 us
    pallas_call x1, Pallas kernels, vocab_exchange(): pl.pallas_call(functools.partial(vocab_exchange_kernel, plan, tile), out_...  61.1 us
    pallas_call x2, Pallas kernels, attend_back(): pl.pallas_call(functools.partial(attend_back_kernel, plan, parts, decoder...  51.7 us
    pallas_call x3, Pallas kernels, attend(): pl.pallas_call(functools.partial(attend_kernel, plan, parts, decoder, cau...  47.2 us
    pallas_call x1, Pallas kernels, reduce_over_devices(): pl.pallas_call(functools.partial(reduce_kernel, rows_dp), out_shape=[jax....  38 us
    unnamed x142, local copies, waits for them, and re-layouts  30.4 us
    pallas_call x2, Pallas kernels, feed_back(): pl.pallas_call(feed_back_kernel, out_shape=jax.ShapeDtypeStruct((own, wid...  11.5 us
    pallas_call x1, Pallas kernels, project(): pl.pallas_call(functools.partial(project_kernel, plan), out_shape=[jax.Sh...  9.79 us
  transfers between devices with their start and end apart: 2, of which 0 were waited for; matrix products, arithmetic and copies ran while one was open for 1% of the time, Pallas kernels for 37%

profile of v7, /device:TPU:25, one launch (start us, length us, event | category | flops | bytes accessed | tf_op | source)
XLA Modules:
  0.0 439.1 jit_solution(11543869534440052205)
XLA Ops:
  7.2 0.0 all-gather.3.cloned.1.call-start
  7.3 1.2 convert_bitcast_fusion
  8.5 0.8 pad.23
  9.4 0.2 reduce-window.7
  9.6 5.7 %all-gather = s32[12,2,256]{2,1,0:T(2,128)S(1)} all-gather(s32[3,2,256]{2,1,0:T(2,128)S(1)} %pad_add_fusion), channel_id=2, replica_groups=mesh['dp'=8,'vocab'=4] {'vocab'}, dimensions={0}, use_global_device_ids=true | all-gather | bytes 30720 | tf_op jit(solution)/shard_map/all_gather | solution.py:1495
  15.3 0.1 pad_slice_fusion.1
  15.3 0.1 concatenate.18
  15.4 0.1 pad_slice_fusion
  15.5 0.1 concatenate.20
  15.6 0.1 slice_reduce_fusion.3
  15.7 0.1 concatenate.19
  15.8 0.1 concatenate.21
  15.9 0.6 and_select_fusion.refs_4_
  16.6 0.6 fusion.14
  17.2 151.1 %shard_map.198 = (bf16[4,2,96,2304]{3,2,1,0:T(8,128)(2,1)}, bf16[4,2,96,2304]{3,2,1,0:T(8,128)(2,1)}, bf16[4,2,96,2304]{3,2,1,0:T(8,128)(2,1)}, bf16[4,2,96,768]...) custom-call(bf16[3,96,2304]{2,1,0:T(8,128)(2,1)} %refs_0_.1, ...), custom_call_target="tpu_custom_call" | custom-call | bytes 400000000 | tf_op jit(solution)/shard_map/pallas_call | solution.py:1046
  168.2 0.1 convert_reduce_fusion
  168.4 0.1 select_reduce_fusion
  168.4 0.6 add_select_fusion
  169.0 1.4 copy-done.13
  170.4 1.1 copy-done.24
  171.6 1.1 copy-done.25
  172.7 1.1 copy-done.27
  173.8 9.8 %shard_map.199 = (f32[512,768]{1,0:T(8,128)S(1)}, bf16[512,768]{1,0:T(8,128)(2,1)S(1)}, bf16[512,1536]{1,0:T(8,128)(2,1)S(1)}, bf16[512,1536]{1,0:T(8,128)(2,1)S...) custom-call(bf16[512,768]{1,0:T(8,128)(2,1)S(1)} %copy-done.24, ...), custom_call_target="tpu_custom_call" | custom-call | flops 3019898880 | bytes 7077888 | tf_op jit(solution)/shard_map/pallas_call | solution.py:585
  183.6 1.2 copy-done.33
  184.7 1.1 copy-done.35
  185.9 0.8 copy-done.39
  186.7 20.5 %shard_map.201 = (f32[512,768]{1,0:T(8,128)S(1)}, f32[512,768]{1,0:T(8,128)S(1)}, f32[512,128]{1,0:T(8,128)S(1)}, f32[512,768]{1,0:T(8,128)S(1)}, f32[512,3072]{1,0:T(8,128)}) custom-call(bf16[512,768]{1,0:T(8,128)(2,1)S(1)} %get-tuple-element.50.refs_0_, bf16[512,1536]{1,0:T(8,128)(2,1)S(1)} %get-tuple-element.51.refs_1_, ...), custom_call_target="tpu_custom_call" | custom-call | flops 17716740096 | bytes 2359296 | tf_op jit(solution)/shard_map/pallas_call | solution.py:282
  207.3 1.1 copy-done.4
  208.4 1.2 copy-done.47
  209.6 0.2 multiply_reduce_fusion
  209.8 0.1 copy.41
  210.0 3.3 convolution_convert_fusion.refs_1_
  213.3 0.2 collective-permute-start
  213.6 12.0 %shard_map.200 = (f32[384,768]{1,0:T(8,128)S(1)}, f32[384,768]{1,0:T(8,128)}, f32[384,128]{1,0:T(8,128)}) custom-call(bf16[384,768]{1,0:T(8,128)(2,1)S(1)} %copy-done.40, bf16[512,1536]{1,0:T(8,128)(2,1)S(1)} %copy-done.34, bf16[512,1536]{1,0:T(8,128)(2,1)S(1)} %copy-done.36, f32[384,768]{1,0:T(8,128)S(1)} %copy-done.23, bf16[768,768]{1,0:T(8,128)(2,1)S(1)} %bitcast.74, ...), custom_call_target="tpu_custom_call" | custom-call | flops 13287555072 | bytes 1769472 | tf_op jit(solution)/shard_map/pallas_call | solution.py:282
  225.6 0.2 multiply_reduce_fusion.1
  225.7 2.1 convolution_convert_fusion.1.refs_0_
  227.9 14.7 %shard_map.202 = (f32[384,768]{1,0:T(8,128)S(1)}, f32[384,768]{1,0:T(8,128)S(1)}, f32[384,128]{1,0:T(8,128)S(1)}, f32[384,768]{1,0:T(8,128)S(1)}, f32[384,3072]{1,0:T(8,128)S(1)}) custom-call(bf16[384,768]{1,0:T(8,128)(2,1)S(1)} %convolution_convert_fusion.1.refs_0_, bf16[512,1536]{1,0:T(8,128)(2,1)S(1)} %convolution_convert_fusion.refs_1_, ...), custom_call_target="tpu_custom_call" | custom-call | flops 13287555072 | bytes 1769472 | tf_op jit(solution)/shard_map/pallas_call | solution.py:282
  242.6 2.2 copy-done
  244.8 1.0 copy-done.43
  245.8 1.0 copy-done.45
  246.9 0.1 copy.40
  247.1 1.2 copy-done.26
  248.3 1.9 copy-done.46
  250.1 61.1 %shard_map.203 = (f32[384,768]{1,0:T(8,128)S(1)}, f32[8,128]{1,0:T(8,128)S(1)}) custom-call(f32[384,768]{1,0:T(8,128)S(1)} %copy-done.46, f32[1,768]{1,0:T(1,128)S(1)} %get-tuple-element.99.refs_1_, bf16[384,768]{1,0:T(8,128)(2,1)S(1)} %copy-done.26, bf16[8032,768]{1,0:T(8,128)(2,1)} %refs_3_.3, f32[8,1152]{1,0:T(8,128)S(1)} %pad.24.refs_4_, ...), custom_call_target="tpu_custom_call" | custom-call | flops 72477573120 | bytes 12337152 | tf_op jit(solution)/shard_map/pallas_call | solution.py:1251
  311.4 5.0 %shard_map.204.refs_3_ = f32[384,768]{1,0:T(8,128)S(1)} custom-call(f32[384,768]{1,0:T(8,128)S(1)} %get-tuple-element.70.grad_ref, f32[384,768]{1,0:T(8,128)S(1)} %get-tuple-element.71.rows_ref, f32[1,768]{1,0:T(1,128)S(1)} %get-tuple-element.100.refs_6_.gain_ref, f32[384,3072]{1,0:T(8,128)S(1)} %bitcast.52, bf16[768,3072]{1,0:T(8,128)(2,1)S(1)} %bitcast.46, ...), custom_call_target="tpu_custom_call" | custom-call | flops 3623878656 | bytes 9437184 | tf_op jit(solution)/shard_map/pallas_call | solution.py:506
  316.4 1.5 copy-done.15
  318.0 2.2 copy-done.17
  320.2 1.3 copy-done.44
  321.4 21.4 %shard_map.205.grad_ref = f32[512,768]{1,0:T(8,128)S(1)} custom-call(bf16[384,768]{1,0:T(8,128)(2,1)S(1)} %copy-done.42, bf16[512,1536]{1,0:T(8,128)(2,1)S(1)} %copy-done.15, bf16[512,1536]{1,0:T(8,128)(2,1)S(1)} %copy-done.17, f32[384,768]{1,0:T(8,128)S(1)} %shard_map.204.refs_3_, bf16[768,768]{1,0:T(8,128)(2,1)S(1)} %bitcast.73, ...), custom_call_target="tpu_custom_call" | custom-call | flops 24159191040 | bytes 7864320 | tf_op jit(solution)/shard_map/pallas_call | solution.py:458
  342.9 2.3 copy-done.1
  345.2 1.4 copy-done.5
  346.7 6.5 %shard_map.206.refs_3_ = f32[512,768]{1,0:T(8,128)S(1)} custom-call(f32[512,768]{1,0:T(8,128)S(1)} %shard_map.205.grad_ref, f32[512,768]{1,0:T(8,128)S(1)} %copy-done.5, f32[1,768]{1,0:T(1,128)S(1)} %get-tuple-element.94.refs_6_.gain_ref, f32[512,3072]{1,0:T(8,128)S(1)} %bitcast.42, bf16[768,3072]{1,0:T(8,128)(2,1)S(1)} %bitcast.56, ...), custom_call_target="tpu_custom_call" | custom-call | flops 4831838208 | bytes 9437184 | tf_op jit(solution)/shard_map/pallas_call | solution.py:506
  353.1 1.1 copy-done.6
  354.3 1.4 copy-done.7
  355.7 1.4 copy-done.32
  357.1 30.3 %shard_map.207 = f32[512,768]{1,0:T(8,128)S(1)} custom-call(bf16[512,768]{1,0:T(8,128)(2,1)S(1)} %copy-done.38, bf16[512,1536]{1,0:T(8,128)(2,1)S(1)} %copy-done.30, bf16[512,1536]{1,0:T(8,128)(2,1)S(1)} %copy-done.32, f32[512,768]{1,0:T(8,128)S(1)} %copy-done.7, bf16[768,768]{1,0:T(8,128)(2,1)S(1)} %bitcast.71, f32[512,768]{1,0:T(8,128)} %copy-done.47, ...), custom_call_target="tpu_custom_call" | custom-call | flops 32212254720 | bytes 7864320 | tf_op jit(solution)/shard_map/pallas_call | solution.py:458
  387.4 0.7 fusion.2
  388.1 0.7 convolution_add_fusion.table_ref
  388.8 38.0 %shard_map.208 = (f32[8,192,128]{2,1,0:T(8,128)S(1)}, f32[8,128]{1,0:T(8,128)S(1)}, f32[8,128]{1,0:T(8,128)S(1)}) custom-call(s32[2,3]{1,0:T(2,128)S(1)} %bitcast.69, f32[768,384]{1,0:T(8,128)S(1)} %convolution_add_fusion.table_ref, f32[8,128]{1,0:T(8,128)S(1)} %get-tuple-element.79.stat_ref), custom_call_target="tpu_custom_call" | custom-call | tf_op jit(solution)/shard_map/pallas_call | solution.py:1429
  426.8 0.6 slice_reduce_fusion
  428.2 0.6 fusion.11
  428.8 0.1 fusion.13
  428.9 0.4 multiply_reduce_fusion.2
  429.4 1.6 add_subtract_fusion
  (149 shorter events, 0.4 us)
Async XLA Ops:
  7.2 2.2 copy-start.58
  7.2 2.2 copy-start.59
  7.2 2.2 copy-start.10
  7.2 2.4 copy-start.57
  7.2 9.3 %copy-start.52 = (f32[7,768]{1,0:T(8,128)S(1)}, f32[7,768]{1,0:T(8,128)}, u32[]{:S(2)}) copy-start(f32[7,768]{1,0:T(8,128)} %param.25) | copy-start | bytes 64516
  7.2 161.8 %all-gather.3.cloned.1.call-start = ((), (), s32[]{:S(2)}) async-start(), calls=%async_computation | async-start | bytes 1966080 | tf_op jit(solution)/shard_map/all_gather | solution.py:1545
  17.1 151.9 %copy-start.8 = (f32[1,768]{1,0:T(1,128)}, f32[1,768]{1,0:T(1,128)S(1)}, u32[]{:S(2)}) copy-start(f32[1,768]{1,0:T(1,128)S(1)} %get-tuple-element.97.refs_4_.refs_10_) | copy-start | bytes 9220
  17.1 151.2 %copy-start.11 = (s32[2,1,3]{2,1,0:T(1,128)S(1)}, s32[2,1,3]{2,1,0:T(1,128)}, u32[]{:S(2)}) copy-start(s32[2,1,3]{2,1,0:T(1,128)} %param.18) | copy-start | bytes 76
  17.2 151.9 %copy-start.12 = (s32[2,1,3]{2,1,0:T(1,128)S(1)}, s32[2,1,3]{2,1,0:T(1,128)}, u32[]{:S(2)}) copy-start(s32[2,1,3]{2,1,0:T(1,128)} %param.19) | copy-start | bytes 76
  169.0 1.4 copy-start.13
  173.8 12.9 %copy-start.18 = (bf16[4,2,96,768]{3,2,1,0:T(8,128)(2,1)S(1)}, bf16[4,2,96,768]{3,2,1,0:T(8,128)(2,1)}, u32[]{:S(2)}) copy-start(bf16[4,2,96,768]{3,2,1,0:T(8,128)(2,1)} %get-tuple-element.61) | copy-start | bytes 3538948
  183.6 1.2 copy-start.33
  186.7 20.5 %copy-start.28 = (f32[512,768]{1,0:T(8,128)}, f32[512,768]{1,0:T(8,128)S(1)}, u32[]{:S(2)}) copy-start(f32[512,768]{1,0:T(8,128)S(1)} %get-tuple-element.60.refs_3_.refs_9_) | copy-start | bytes 4718596
  186.7 20.5 %copy-start.29 = (bf16[512,1536]{1,0:T(8,128)(2,1)}, bf16[512,1536]{1,0:T(8,128)(2,1)S(1)}, u32[]{:S(2)}) copy-start(bf16[512,1536]{1,0:T(8,128)(2,1)S(1)} %get-tuple-element.51.refs_1_) | copy-start | bytes 4718596
  186.7 20.5 %copy-start.31 = (bf16[512,1536]{1,0:T(8,128)(2,1)}, bf16[512,1536]{1,0:T(8,128)(2,1)S(1)}, u32[]{:S(2)}) copy-start(bf16[512,1536]{1,0:T(8,128)(2,1)S(1)} %get-tuple-element.52.refs_2_) | copy-start | bytes 4718596
  186.7 20.5 %copy-start.37 = (bf16[512,768]{1,0:T(8,128)(2,1)}, bf16[512,768]{1,0:T(8,128)(2,1)S(1)}, u32[]{:S(2)}) copy-start(bf16[512,768]{1,0:T(8,128)(2,1)S(1)} %get-tuple-element.50.refs_0_) | copy-start | bytes 2359300
  208.4 1.2 copy-start.47
  209.6 3.8 copy-start.2
  209.9 3.6 copy-start.22
  209.9 3.6 copy-start.23
  209.9 3.6 copy-start.34
  209.9 3.6 copy-start.36
  210.0 3.6 copy-start.40
  213.3 14.5 %copy-start.14 = (bf16[512,1536]{1,0:T(8,128)(2,1)}, bf16[512,1536]{1,0:T(8,128)(2,1)S(1)}, u32[]{:S(2)}) copy-start(bf16[512,1536]{1,0:T(8,128)(2,1)S(1)} %convolution_convert_fusion.refs_1_) | copy-start | bytes 4718596
  213.3 14.5 %collective-permute-start = (bf16[512,1536]{1,0:T(8,128)(2,1)S(1)}, bf16[512,1536]{1,0:T(8,128)(2,1)S(1)}, u32[]{:S(2)}, u32[]{:S(2)}) collective-permute-start(bf16[512,1536]{1,0:T(8,128)(2,1)S(1)} %convolution_convert_fusion.refs_1_), channel_id=1, source_target_pairs={{0,1},{1,0},{2,3},{3,2},{4,5},{5,4},{6,7},{7,6},{8,9},{9,8},{10,11... | collective-permute-start | bytes 4718600 | tf_op jit(solution)/shard_map/ppermute | solution.py:1493
  225.7 2.1 copy-start.20
  227.8 14.7 %copy-start.41 = (bf16[384,768]{1,0:T(8,128)(2,1)}, bf16[384,768]{1,0:T(8,128)(2,1)S(1)}, u32[]{:S(2)}) copy-start(bf16[384,768]{1,0:T(8,128)(2,1)S(1)} %convolution_convert_fusion.1.refs_0_) | copy-start | bytes 1769476
  227.8 14.7 %copy-start.16 = (bf16[512,1536]{1,0:T(8,128)(2,1)}, bf16[512,1536]{1,0:T(8,128)(2,1)S(1)}, u32[]{:S(2)}) copy-start(bf16[512,1536]{1,0:T(8,128)(2,1)S(1)} %collective-permute-done.refs_2_) | copy-start | bytes 4718596
  242.6 2.3 copy-start
  247.0 64.2 %slice-start.2 = ((s8[4718592]{0:T(1024)(128)(4,1)}), s8[4194304]{0:T(1024)(128)(4,1)S(1)}, s32[]{:S(2)}) async-start(s8[4718592]{0:T(1024)(128)(4,1)} %bitcast.44), calls=%async_computation.3 | async-start | bytes 8388608
  247.0 64.2 %slice-start.4 = ((s8[4718592]{0:T(1024)(128)(4,1)}), s8[4194304]{0:T(1024)(128)(4,1)S(1)}, s32[]{:S(2)}) async-start(s8[4718592]{0:T(1024)(128)(4,1)} %bitcast.48), calls=%async_computation.5 | async-start | bytes 8388608
  247.0 64.2 %slice-start.6 = ((s8[4718592]{0:T(1024)(128)(4,1)}), s8[4194304]{0:T(1024)(128)(4,1)S(1)}, s32[]{:S(2)}) async-start(s8[4718592]{0:T(1024)(128)(4,1)} %bitcast.51), calls=%async_computation.7 | async-start | bytes 8388608
  247.0 1.2 copy-start.26
  248.3 1.9 copy-start.46
  250.1 61.2 %slice-start.3 = ((s8[4718592]{0:T(1024)(128)(4,1)}), s8[524288]{0:T(1024)(128)(4,1)S(1)}, s32[]{:S(2)}) async-start(s8[4718592]{0:T(1024)(128)(4,1)} %bitcast.44), calls=%async_computation.4 | async-start | bytes 1048576
  250.1 61.2 %slice-start.5 = ((s8[4718592]{0:T(1024)(128)(4,1)}), s8[524288]{0:T(1024)(128)(4,1)S(1)}, s32[]{:S(2)}) async-start(s8[4718592]{0:T(1024)(128)(4,1)} %bitcast.48), calls=%async_computation.6 | async-start | bytes 1048576
  250.1 61.2 %slice-start.7 = ((s8[4718592]{0:T(1024)(128)(4,1)}), s8[524288]{0:T(1024)(128)(4,1)S(1)}, s32[]{:S(2)}) async-start(s8[4718592]{0:T(1024)(128)(4,1)} %bitcast.51), calls=%async_computation.8 | async-start | bytes 1048576
  311.3 5.1 %copy-start.3 = (f32[512,768]{1,0:T(8,128)S(1)}, f32[512,768]{1,0:T(8,128)}, u32[]{:S(2)}) copy-start(f32[512,768]{1,0:T(8,128)} %copy-done.2) | copy-start | bytes 4718596
  311.3 5.1 %copy-start.21 = (bf16[4,2,96,768]{3,2,1,0:T(8,128)(2,1)S(1)}, bf16[4,2,96,768]{3,2,1,0:T(8,128)(2,1)}, u32[]{:S(2)}) copy-start(bf16[4,2,96,768]{3,2,1,0:T(8,128)(2,1)} %get-tuple-element.65) | copy-start | bytes 3538948
  311.3 5.1 %copy-start.42 = (bf16[384,768]{1,0:T(8,128)(2,1)S(1)}, bf16[384,768]{1,0:T(8,128)(2,1)}, u32[]{:S(2)}) copy-start(bf16[384,768]{1,0:T(8,128)(2,1)} %copy-done.41) | copy-start | bytes 1769476
  316.4 26.5 %slice-start = ((s8[6291456]{0:T(1024)(128)(4,1)}), s8[4194304]{0:T(1024)(128)(4,1)S(1)}, s32[]{:S(2)}) async-start(s8[6291456]{0:T(1024)(128)(4,1)} %bitcast.41), calls=%async_computation.1 | async-start | bytes 8388608
  316.4 26.5 %slice-start.8 = ((s8[4718592]{0:T(1024)(128)(4,1)}), s8[4194304]{0:T(1024)(128)(4,1)S(1)}, s32[]{:S(2)}) async-start(s8[4718592]{0:T(1024)(128)(4,1)} %bitcast.54), calls=%async_computation.9 | async-start | bytes 8388608
  316.4 1.6 copy-start.15
  318.0 2.2 copy-start.17
  320.2 1.3 copy-start.44
  321.4 21.5 %slice-start.1 = ((s8[6291456]{0:T(1024)(128)(4,1)}), s8[2097152]{0:T(1024)(128)(4,1)S(1)}, s32[]{:S(2)}) async-start(s8[6291456]{0:T(1024)(128)(4,1)} %bitcast.41), calls=%async_computation.2 | async-start | bytes 4194304
  321.4 21.5 %slice-start.9 = ((s8[4718592]{0:T(1024)(128)(4,1)}), s8[524288]{0:T(1024)(128)(4,1)S(1)}, s32[]{:S(2)}) async-start(s8[4718592]{0:T(1024)(128)(4,1)} %bitcast.54), calls=%async_computation.10 | async-start | bytes 1048576
  342.9 2.3 copy-start.1
  345.2 1.4 copy-start.5
  346.6 7.7 %copy-start.9 = (f32[1,768]{1,0:T(1,128)S(1)}, f32[1,768]{1,0:T(1,128)}, u32[]{:S(2)}) copy-start(f32[1,768]{1,0:T(1,128)} %copy-done.8) | copy-start | bytes 9220
  346.6 7.7 %copy-start.19 = (bf16[4,2,96,768]{3,2,1,0:T(8,128)(2,1)S(1)}, bf16[4,2,96,768]{3,2,1,0:T(8,128)(2,1)}, u32[]{:S(2)}) copy-start(bf16[4,2,96,768]{3,2,1,0:T(8,128)(2,1)} %get-tuple-element.61) | copy-start | bytes 3538948
  346.6 7.7 %copy-start.30 = (bf16[512,1536]{1,0:T(8,128)(2,1)S(1)}, bf16[512,1536]{1,0:T(8,128)(2,1)}, u32[]{:S(2)}) copy-start(bf16[512,1536]{1,0:T(8,128)(2,1)} %copy-done.29) | copy-start | bytes 4718596
  346.7 7.6 %copy-start.38 = (bf16[512,768]{1,0:T(8,128)(2,1)S(1)}, bf16[512,768]{1,0:T(8,128)(2,1)}, u32[]{:S(2)}) copy-start(bf16[512,768]{1,0:T(8,128)(2,1)} %copy-done.37) | copy-start | bytes 2359300
  353.1 1.2 copy-start.6
  354.3 1.4 copy-start.7
  355.7 1.4 copy-start.32
  357.1 30.3 %copy-start.53 = (s32[512]{0:T(512)S(1)}, s32[512]{0:T(512)}, u32[]{:S(2)}) copy-start(s32[512]{0:T(512)} %add_select_fusion) | copy-start | bytes 6148
  388.1 40.7 %copy-start.56 = (f32[8,100]{1,0:T(8,128)S(1)}, f32[8,100]{1,0:T(8,128)}, u32[]{:S(2)}) copy-start(f32[8,100]{1,0:T(8,128)} %param.28) | copy-start | bytes 9604
  388.8 40.5 %copy-start.55 = (f32[8,192]{1,0:T(8,128)S(1)}, f32[8,192]{1,0:T(8,128)}, u32[]{:S(2)}) copy-start(f32[8,192]{1,0:T(8,128)} %param.29) | copy-start | bytes 18436
  388.8 40.5 %copy-start.48 = (f32[8,100,192]{1,2,0:T(8,128)S(1)}, f32[8,100,192]{1,2,0:T(8,128)}, u32[]{:S(2)}) copy-start(f32[8,100,192]{1,2,0:T(8,128)} %param.26) | copy-start | bytes 1843204
  388.8 40.5 %copy-start.50 = (f32[8,100,192]{1,2,0:T(8,128)S(1)}, f32[8,100,192]{1,2,0:T(8,128)}, u32[]{:S(2)}) copy-start(f32[8,100,192]{1,2,0:T(8,128)} %param.27) | copy-start | bytes 1843204
  428.9 2.0 copy-start.54
  429.3 1.7 copy-start.49
  429.3 1.6 copy-start.51
  (8 other events, 8.4 us)
Sparse Core Ops, SparseCore 0:
  10.2 21.0 all-gather.2
